TPU v7x, 32 devices: a whole 2x2x4 slice. The times are simulated.
32 devices in a mesh: band: 8 (over y, x, core), ga: 4 (over z).
Axes of the slice: x: 2, y: 2, z: 4, core: 2. Of those that a mesh axis runs over, the one named last changes fastest.
Arguments:
- waves: bfloat16 [2, 64, 4, 147456], P(None, 'band', None, 'ga'), as said below
- ionic_field: float32 [384, 1536], P('ga'), may hold values from -1 to 3
- point_charge: float32 [8192], P(('band', 'ga')), may hold values from -6 to 6
- charge_place: float32 [3, 8192], P(None, ('band', 'ga')), may hold values from 0 to 1
- charge_slab: int32 [8192, 1], P(('band', 'ga')), may hold values from 0 to 3; in each aligned block of 256 rows (0 to 255, 256 to 511, ...) at most 128 rows name the same one
Outputs:
- applied_waves: bfloat16 [2, 64, 4, 147456], P(None, 'band', None, 'ga')
- subspace: float32 [2, 64, 64], P(None, 'band', 'ga')
Inputs may be any that keep to these rules, and one draw needn't show every extreme that they name: `waves`: entries are of order one. `charge_slab`: among the 256 rows of one device at most 128 name the same slab, and in every draw some device has exactly 128 rows naming one slab.
All inputs are finite; a program needn't handle non-finite values.
Results may differ from a plain program's by a relative error of at most 0.0073.
Values may be sent and summed in bfloat16 or wider, within the bound.
No kernel may reach another device: no remote copies, remote signals or barrier semaphores. Data moves between devices by JAX's collectives and lax.ppermute only.
A program may use at most 192 MiB of HBM per device.

v0:
```python
import functools

import jax
import jax.numpy as jnp
from jax import lax
from jax.experimental import pallas as pl
from jax.experimental.pallas import tpu as pltpu
from jax.sharding import PartitionSpec as P

NX = 384
NY = 384
LANES = 128

width_cells = 1.5


def tables(length):
    indices = jnp.arange(length, dtype=jnp.int32)
    phases = indices[:, None] * indices[None, :] % length
    angles = phases.astype(jnp.float32) * (2.0 * jnp.pi / length)
    factor = 1.0 / jnp.sqrt(jnp.float32(length))
    return (
        (jnp.cos(angles) * factor).astype(jnp.bfloat16),
        (jnp.sin(angles) * factor).astype(jnp.bfloat16),
    )


def gaussian(distance):
    return jnp.exp(-distance * distance / (2.0 * width_cells * width_cells))


def frequency(indices, length):
    return jnp.where(indices < length // 2, indices, indices - length).astype(jnp.float32)


def dot(left, right):
    return jnp.dot(left, right, preferred_element_type=jnp.float32)


def lasting(microseconds):
    return pl.CostEstimate(
        flops=0, bytes_accessed=int(microseconds * 3.69e6), transcendentals=0
    )


def pack_body(place, *refs):
    halves = len(refs) - 1 - refs[-1].shape[0]
    sources, messages, held = refs[:halves], refs[halves:-1], refs[-1]
    groups, count, rows, _ = held.shape
    planes = groups // halves
    for h, source in enumerate(sources):
        for i in range(count):
            split = source[0, i].reshape(planes, rows, NY)
            for p in range(planes):
                held[p * halves + h, i] = split[p]
    for s, message in enumerate(messages):
        message[0] = held[lax.rem(place[0] + s, groups)]


def pack(waves, place, first, count, rows, groups):
    planes = waves.shape[2]
    halves = groups // planes
    own = waves.shape[1] // halves
    return pl.pallas_call(
        pack_body,
        grid=(2, count),
        in_specs=[pl.BlockSpec(memory_space=pltpu.SMEM)]
        + [
            pl.BlockSpec((1, 1, planes, rows * NY), functools.partial(block_at, h * own + first))
            for h in range(halves)
        ],
        out_specs=[pl.BlockSpec((1, 1, rows, NY), lambda c, n: (c, n, 0, 0))] * groups,
        out_shape=[jax.ShapeDtypeStruct((2, count, rows, NY), jnp.bfloat16)] * groups,
        scratch_shapes=[pltpu.VMEM((groups, 1, rows, NY), jnp.bfloat16)],
        compiler_params=pltpu.CompilerParams(vmem_limit_bytes=56 << 20),
        cost_estimate=lasting(1.0 * count),
        name="pack_planes",
    )(place, *[waves] * halves)


def block_at(base, c, n):
    return (c, base + n, 0, 0)


def mix_waves_body(w_ref, z_ref, mixed):
    _, bands, planes, width = w_ref.shape
    rows = width // NY
    per = 2 * bands
    for c in range(2):
        for n in range(bands):
            wide = w_ref[c, n].reshape(planes, rows, NY).astype(jnp.float32)
            for p in range(planes):
                at = pl.ds(p * rows * per + c * bands + n, rows, stride=per)
                for t in range(NY // LANES):
                    mixed[t, at, :] = wide[p, :, t * LANES : (t + 1) * LANES]
    for t in range(NY // LANES):
        z_ref[0, :, t * LANES : (t + 1) * LANES] = mixed[t].astype(jnp.bfloat16)


def mix_waves(waves, rows, shares):
    _, bands, planes, _ = waves.shape
    own = rows // shares
    depth = planes * own * 2 * bands
    return pl.pallas_call(
        mix_waves_body,
        grid=(shares,),
        in_specs=[pl.BlockSpec((2, bands, planes, own * NY), lambda d: (0, 0, 0, d))],
        out_specs=pl.BlockSpec((1, depth, NY), lambda d: (d, 0, 0)),
        out_shape=jax.ShapeDtypeStruct((shares, depth, NY), jnp.bfloat16),
        scratch_shapes=[pltpu.VMEM((NY // LANES, depth, LANES), jnp.float32)],
        compiler_params=pltpu.CompilerParams(vmem_limit_bytes=56 << 20),
        cost_estimate=lasting(8.0),
        name="mix_waves",
    )(waves)


def mix_space_body(*refs):
    sources, z_ref, mixed = refs[:-2], refs[-2], refs[-1]
    bands = sum(source.shape[0] for source in sources)
    rows = sources[0].shape[2]
    for c in range(2):
        row = c * bands
        for source in sources:
            for n in range(source.shape[0]):
                wide = source[n, c].astype(jnp.float32)
                for t in range(NY // LANES):
                    mixed[t, pl.ds(row, rows, stride=2 * bands), :] = wide[
                        :, t * LANES : (t + 1) * LANES
                    ]
                row += 1
    for t in range(NY // LANES):
        z_ref[:, :, t * LANES : (t + 1) * LANES] = (
            mixed[t].astype(jnp.bfloat16).reshape(z_ref.shape[:2] + (LANES,))
        )


def mix_space(sources, shares):
    bands = sum(source.shape[0] for source in sources)
    own = NX // shares
    depth = own * 2 * bands
    group = max(1, 48 // own)
    return pl.pallas_call(
        mix_space_body,
        grid=(shares // group,),
        in_specs=[
            pl.BlockSpec((source.shape[0], 2, group * own, NY), lambda d: (0, 0, d, 0))
            for source in sources
        ],
        out_specs=pl.BlockSpec((group, depth, NY), lambda d: (d, 0, 0)),
        out_shape=jax.ShapeDtypeStruct((shares, depth, NY), jnp.bfloat16),
        scratch_shapes=[pltpu.VMEM((NY // LANES, group * depth, LANES), jnp.float32)],
        compiler_params=pltpu.CompilerParams(vmem_limit_bytes=56 << 20),
        cost_estimate=lasting(8.0),
        name="mix_space",
    )(*sources)


def unpack_body(groups, place, *refs):
    messages, o_ref, held = refs[:groups], refs[-2], refs[-1]
    halves, planes, count, rows, _ = held.shape
    for s, message in enumerate(messages):
        source = lax.rem(place[0] + groups - s, groups)
        held[lax.rem(source, halves), source // halves] = message[0]
    half = pl.program_id(1)
    for i in range(count):
        o_ref[0, i] = held[half, :, i].reshape(planes, rows * NY)


def unpack(messages, place, base, first, bands, planes):
    groups = len(messages)
    _, count, rows, _ = messages[0].shape
    halves = groups // planes
    own = bands // halves
    in_specs = [pl.BlockSpec(memory_space=pltpu.SMEM)] + [
        pl.BlockSpec((1, 1, rows, NY), lambda c, h, n: (c, n, 0, 0))
    ] * groups
    operands = [place, *messages]
    aliases = {}
    if base is not None:
        in_specs.append(pl.BlockSpec(memory_space=pl.ANY))
        operands.append(base)
        aliases = {groups + 1: 0}
    return pl.pallas_call(
        functools.partial(unpack_body, groups),
        grid=(2, halves, count),
        in_specs=in_specs,
        out_specs=pl.BlockSpec(
            (1, 1, planes, rows * NY), lambda c, h, n: (c, h * own + first + n, 0, 0)
        ),
        out_shape=jax.ShapeDtypeStruct((2, bands, planes, rows * NY), jnp.bfloat16),
        scratch_shapes=[pltpu.VMEM((halves, planes, 1, rows, NY), jnp.bfloat16)],
        input_output_aliases=aliases,
        compiler_params=pltpu.CompilerParams(vmem_limit_bytes=56 << 20),
        cost_estimate=lasting(1.2 * count),
        name="unpack_planes",
    )(*operands)


def forward_body(groups, place, *refs):
    messages, (f_ref, b_ref, s_ref, held) = refs[:groups], refs[groups:]
    for s, message in enumerate(messages):
        held[lax.rem(place[0] + groups - s, groups)] = message[:, 0]
    parts = [held[:, c].reshape(NX, NY) for c in range(2)]
    first = dot(jnp.concatenate(parts, axis=1), f_ref[...]).astype(jnp.bfloat16)
    first = jnp.concatenate([first[:, :NY], first[:, NY:]], axis=0)
    in_space = dot(b_ref[...], first).astype(jnp.bfloat16)
    s_ref[0, 0] = in_space[:NX]
    s_ref[0, 1] = in_space[NX:]


def forward(messages, place, forth, back):
    groups = len(messages)
    _, bands, rows, _ = messages[0].shape
    square = pl.BlockSpec((2 * NX, 2 * NX), lambda n: (0, 0))
    return pl.pallas_call(
        functools.partial(forward_body, groups),
        grid=(bands,),
        in_specs=[pl.BlockSpec(memory_space=pltpu.SMEM)]
        + [pl.BlockSpec((2, 1, rows, NY), lambda n: (0, n, 0, 0))] * groups
        + [square, square],
        out_specs=pl.BlockSpec((1, 2, NX, NY), lambda n: (n, 0, 0, 0)),
        out_shape=jax.ShapeDtypeStruct((bands, 2, NX, NY), jnp.bfloat16),
        scratch_shapes=[pltpu.VMEM((groups, 2, rows, NY), jnp.bfloat16)],
        compiler_params=pltpu.CompilerParams(vmem_limit_bytes=56 << 20),
        cost_estimate=lasting(1.5 * bands + 1.0),
        name="forward",
    )(place, *messages, forth, back)


def inverse_body(groups, place, *refs):
    messages, (s_ref, v_ref, f_ref, b_ref) = refs[:groups], refs[groups : groups + 4]
    held = refs[-1]
    results = refs[-1 - groups : -1]
    rows = held.shape[2]
    freq_x = frequency(lax.broadcasted_iota(jnp.int32, (NX, 1), 0), NX)
    freq_y = frequency(lax.broadcasted_iota(jnp.int32, (1, NY), 1), NY)
    kinetic = 2.0 * (freq_x * freq_x / (NX * NX) + freq_y * freq_y / (NY * NY))
    for s, message in enumerate(messages):
        held[lax.rem(place[0] + groups - s, groups)] = message[:, 0]
    weighted = jnp.concatenate(
        [v_ref[...] * s_ref[0, c].astype(jnp.float32) for c in range(2)],
        axis=0,
    ).astype(jnp.bfloat16)
    back = dot(f_ref[...], weighted).astype(jnp.bfloat16)
    recip = dot(jnp.concatenate([back[:NX], back[NX:]], axis=1), b_ref[...])
    for c in range(2):
        wide = held[:, c].reshape(NX, NY).astype(jnp.float32)
        applied = kinetic * wide + recip[:, c * NY : (c + 1) * NY]
        held[:, c] = applied.astype(jnp.bfloat16).reshape(groups, rows, NY)
    for s, result in enumerate(results):
        result[:, 0] = held[lax.rem(place[0] + s, groups)]


def inverse(messages, place, in_space, potential, forth, back):
    groups = len(messages)
    shape = messages[0].shape
    _, bands, rows, _ = shape
    square = pl.BlockSpec((2 * NX, 2 * NX), lambda n: (0, 0))
    return pl.pallas_call(
        functools.partial(inverse_body, groups),
        grid=(bands,),
        in_specs=[pl.BlockSpec(memory_space=pltpu.SMEM)]
        + [pl.BlockSpec((2, 1, rows, NY), lambda n: (0, n, 0, 0))] * groups
        + [
            pl.BlockSpec((1, 2, NX, NY), lambda n: (n, 0, 0, 0)),
            pl.BlockSpec((NX, NY), lambda n: (0, 0)),
            square,
            square,
        ],
        out_specs=[pl.BlockSpec((2, 1, rows, NY), lambda n: (0, n, 0, 0))] * groups,
        out_shape=[jax.ShapeDtypeStruct(shape, jnp.bfloat16)] * groups,
        scratch_shapes=[pltpu.VMEM((groups, 2, rows, NY), jnp.bfloat16)],
        compiler_params=pltpu.CompilerParams(vmem_limit_bytes=56 << 20),
        cost_estimate=lasting(1.8 * bands + 1.0),
        name="inverse",
    )(place, *messages, in_space, potential, forth, back)


def overlap_body(scale, per, z_ref, w_ref, *refs):
    g_ref, total = refs[-2:]
    shares = z_ref.shape[0]
    if len(refs) == 3:
        total[...] = refs[0][...]
    else:
        total[...] = jnp.zeros_like(total)

    @pl.loop(0, w_ref.shape[0] // 2)
    def _(pair):
        plain, scaled = [], []
        for k in range(2):
            point = pair * 2 + k
            at = pl.multiple_of(point * per, per)
            rows = jnp.concatenate([z_ref[d, pl.ds(at, per), :] for d in range(shares)], axis=0)
            plain.append(rows)
            scaled.append(
                (rows.astype(jnp.float32) * w_ref[pl.ds(point, 1), :]).astype(jnp.bfloat16)
            )
        total[...] += lax.dot_general(
            jnp.concatenate(plain, axis=1),
            jnp.concatenate(scaled, axis=1),
            (((1,), (1,)), ((), ())),
            preferred_element_type=jnp.float32,
        )

    if len(refs) == 2:
        g_ref[...] = total[...]
        return
    half = per // 2

    def picked(rows, c):
        return jnp.concatenate(
            [rows[d * per + c * half : d * per + (c + 1) * half] for d in range(shares)], axis=0
        )

    grams = total[...]
    parts = [[picked(picked(grams, c).T, d) for d in range(2)] for c in range(2)]
    g_ref[0] = (parts[0][0] + parts[1][1]).T * scale
    g_ref[1] = (parts[0][1] - parts[1][0]).T * scale


def overlap(pieces, weights, per, scale, before=None):
    shares = pieces.shape[0]
    size = shares * per
    whole = pl.BlockSpec(memory_space=pltpu.VMEM)
    last = before is not None
    shape = (2, size // 2, size // 2) if last else (size, size)
    operands = [pieces, weights] + ([before] if last else [])
    return pl.pallas_call(
        functools.partial(overlap_body, scale, per),
        in_specs=[whole] * len(operands),
        out_specs=whole,
        out_shape=jax.ShapeDtypeStruct(shape, jnp.float32),
        scratch_shapes=[pltpu.VMEM((size, size), jnp.float32)],
        compiler_params=pltpu.CompilerParams(vmem_limit_bytes=56 << 20),
        cost_estimate=lasting(8.0),
        name="overlap",
    )(*operands)


def shifted(messages):
    groups = len(messages)
    return [
        lax.ppermute(message, "ga", [(i, (i + s) % groups) for i in range(groups)]) if s else message
        for s, message in enumerate(messages)
    ]


def split(wide):
    high = wide.astype(jnp.bfloat16)
    return high, (wide - high.astype(jnp.float32)).astype(jnp.bfloat16)


def charges_body(planes, slab_rows, place, c_ref, i_ref, o_ref):
    share = o_ref.shape[0]
    first = place[0].astype(jnp.float32)
    plane = place[1].astype(jnp.float32)
    own_x = lax.broadcasted_iota(jnp.int32, (share, 1), 0).astype(jnp.float32) + first
    cells_y = lax.broadcasted_iota(jnp.int32, (NY, 1), 0)
    slab_y = (cells_y // slab_rows).astype(jnp.float32)
    cells_y = cells_y.astype(jnp.float32)
    o_ref[...] = i_ref[...]

    @pl.loop(0, c_ref.shape[0])
    def _(device):
        along_u, along_v, along_w, amount, slab = [c_ref[device, k : k + 1, :] for k in range(5)]
        kernel_x = gaussian(own_x - NX * along_u) * (amount * gaussian(plane - planes * along_w))
        kernel_y = gaussian(cells_y - (slab * slab_rows + slab_rows * along_v))
        kernel_y = jnp.where(slab_y == slab, kernel_y, 0.0)
        (x_high, x_low), (y_high, y_low) = split(kernel_x), split(kernel_y)
        total = o_ref[...]
        for left, right in ((x_high, y_low), (x_low, y_high), (x_high, y_high)):
            total = total + lax.dot_general(
                left, right, (((1,), (1,)), ((), ())), preferred_element_type=jnp.float32
            )
        o_ref[...] = total


def potential_message(ionic_field, point_charge, charge_place, charge_slab, planes, halves):
    ga_count = lax.axis_size("ga")
    band_groups = lax.axis_size("band")
    devices = band_groups * ga_count
    slab_rows = NY // ga_count
    share = NX // band_groups
    piece = share * slab_rows // band_groups
    atoms = point_charge.shape[0]
    spare = -(-piece // atoms)
    band_at = lax.axis_index("band")
    charges = jnp.concatenate(
        [charge_place, point_charge[None], charge_slab[:, 0][None].astype(jnp.float32)], axis=0
    )
    ionic = ionic_field.T.reshape(planes, band_groups, band_groups, piece)
    ionic = lax.dynamic_index_in_dim(ionic, band_at, 2, keepdims=False)
    ionic = jnp.broadcast_to(
        ionic.transpose(1, 0, 2)[:, :, None], (band_groups, planes, halves, piece)
    )
    ionic = jnp.pad(ionic.reshape(devices, piece), ((0, 0), (0, spare * atoms - piece)))
    return jnp.concatenate(
        [
            jnp.broadcast_to(charges[None], (devices, 5, atoms)),
            ionic.reshape(devices, spare, atoms),
        ],
        axis=1,
    )


def own_share(message, planes, halves):
    ga_count = lax.axis_size("ga")
    band_groups = lax.axis_size("band")
    slab_rows = NY // ga_count
    share = NX // band_groups
    piece = share * slab_rows // band_groups
    atoms = message.shape[2]
    spare = message.shape[1] - 5
    band_at = lax.axis_index("band")
    ionic = message[:, 5:].reshape(band_groups, ga_count, spare * atoms)[:, :, :piece]
    ionic = ionic.transpose(1, 0, 2).reshape(ga_count, share, slab_rows)
    ionic = ionic.transpose(1, 0, 2).reshape(share, NY)
    place = jnp.stack([band_at * share, lax.axis_index("ga") // halves]).astype(jnp.int32)
    return pl.pallas_call(
        functools.partial(charges_body, planes, slab_rows),
        in_specs=[
            pl.BlockSpec(memory_space=pltpu.SMEM),
            pl.BlockSpec(memory_space=pltpu.VMEM),
            pl.BlockSpec(memory_space=pltpu.VMEM),
        ],
        out_specs=pl.BlockSpec(memory_space=pltpu.VMEM),
        out_shape=jax.ShapeDtypeStruct((share, NY), jnp.float32),
        compiler_params=pltpu.CompilerParams(vmem_limit_bytes=56 << 20),
        cost_estimate=lasting(12.0),
        name="charge_potential",
    )(place, message, ionic)


def shards(waves, ionic_field, point_charge, charge_place, charge_slab):
    ga_count = lax.axis_size("ga")
    band_groups = lax.axis_size("band")
    bands = waves.shape[1]
    planes = waves.shape[2]
    rows = NX // ga_count
    halves = ga_count // planes
    own_bands = bands // halves
    chunks = [(0, 2), (2, own_bands - 3), (own_bands - 1, 1)]
    per = 2 * bands
    pairs = [[p * halves + h for h in range(halves)] for p in range(planes)]
    ga_at, band_at = lax.axis_index("ga"), lax.axis_index("band")
    place = ga_at.astype(jnp.int32)[None]

    packed = [pack(waves, place, first, count, rows, ga_count) for first, count in chunks]
    message = potential_message(
        ionic_field, point_charge, charge_place, charge_slab, planes, halves
    )
    cosine, sine = tables(NX)
    forth = jnp.concatenate(
        [jnp.concatenate([cosine, sine], axis=1), jnp.concatenate([-sine, cosine], axis=1)], axis=0
    )
    back = jnp.concatenate(
        [jnp.concatenate([cosine, -sine], axis=1), jnp.concatenate([sine, cosine], axis=1)], axis=0
    )

    arrived = [shifted(packed[0])]
    message = lax.all_to_all(message, ("band", "ga"), 0, 0, tiled=True)
    mixed = mix_waves(waves, rows, band_groups)
    arrived[0], message, packed[1], mixed = lax.optimization_barrier(
        (arrived[0], message, packed[1], mixed)
    )

    arrived.append(shifted(packed[1]))
    met_waves = lax.all_to_all(mixed, "band", 0, 0, tiled=True)
    own_potential = own_share(message, planes, halves)
    copies = jnp.broadcast_to(own_potential[None], (band_groups,) + own_potential.shape)
    in_space = [forward(arrived[0], place, forth, back)]
    arrived[1], met_waves, packed[2], copies, in_space[0], forth, back = (
        lax.optimization_barrier(
            (arrived[1], met_waves, packed[2], copies, in_space[0], forth, back)
        )
    )

    arrived.append(shifted(packed[2]))
    potential = lax.all_to_all(copies, "band", 0, 0, tiled=True).reshape(NX, NY)
    in_space.append(forward(arrived[1], place, forth, back))
    applied = []
    for j in range(2):
        result = inverse(arrived[j], place, in_space[j], potential, forth, back)
        result, place = lax.optimization_barrier((result, place))
        applied.append(result)
    returned = [shifted(result) for result in applied]
    in_space.append(forward(arrived[2], place, forth, back))
    mixed = mix_space(in_space, band_groups * halves)
    mixed = mixed.reshape(band_groups, halves, -1, NY)
    if halves > 1:
        mixed = lax.all_to_all(mixed, "ga", 1, 1, axis_index_groups=pairs, tiled=True)
    met_space = lax.all_to_all(mixed, "band", 0, 0, tiled=True)
    if halves > 1:
        met_space = met_space.reshape(band_groups, halves, -1, 2, own_bands, NY)
        met_space = met_space.transpose(0, 2, 3, 1, 4, 5)
    met_space = met_space.reshape(band_groups, -1, NY)
    space_weights = own_potential
    if halves > 1:
        space_weights = lax.dynamic_slice_in_dim(
            own_potential, ga_at % halves * (NX // band_groups // halves),
            NX // band_groups // halves, 0,
        )

    share = rows // band_groups
    own_x = ga_at * rows + band_at * share + jnp.arange(share, dtype=jnp.int32)
    freq_x, freq_y = frequency(own_x, NX), frequency(jnp.arange(NY, dtype=jnp.int32), NY)
    kinetic = 2.0 * (
        freq_x[:, None] * freq_x[:, None] / (NX * NX)
        + freq_y[None, :] * freq_y[None, :] / (NY * NY)
    )
    kinetic = jnp.broadcast_to(kinetic[None], (planes, share, NY)).reshape(planes * share, NY)

    scale = 1.0 / (planes * NX * NY)
    grams = overlap(met_waves, kinetic, per, scale)
    grams, place = lax.optimization_barrier((grams, place))
    returned.append(shifted(inverse(arrived[2], place, in_space[2], potential, forth, back)))
    full_matrix = overlap(met_space, space_weights, per, scale, grams)
    all_bands = bands * band_groups
    col_width = all_bands // ga_count
    blocks = full_matrix.reshape(2, band_groups, bands, ga_count, col_width)
    blocks = blocks.transpose(1, 3, 0, 2, 4).reshape(
        band_groups * ga_count, 2, bands, col_width
    )
    subspace = lax.all_to_all(blocks, ("band", "ga"), 0, 0, tiled=True).sum(0)

    applied_waves = None
    for j, (first, _) in enumerate(chunks):
        if j == 2:
            place, subspace = lax.optimization_barrier((place, subspace))
        applied_waves = unpack(returned[j], place, applied_waves, first, bands, planes)
    return (applied_waves, subspace)


def solution(mesh):
    placed = (
        P(None, "band", None, "ga"),
        P("ga", None),
        P(("band", "ga")),
        P(None, ("band", "ga")),
        P(("band", "ga"), None),
    )
    return jax.shard_map(
        shards,
        mesh=mesh,
        in_specs=placed,
        out_specs=(P(None, "band", None, "ga"), P(None, "band", "ga")),
        check_vma=False,
    )
```

profile of v0, /device:TPU:0, one launch (start us, length us, event | category | flops | bytes accessed | tf_op | source)
XLA Modules:
  0.0 303.2 jit_solution(342442500124550454)
XLA Ops:
  4.0 7.3 %all-to-all-start = ((f32[32,8,256]{2,1,0:T(8,128)}), f32[32,8,256]{2,1,0:T(8,128)S(1)}, u32[]{:S(2)}, u32[]{:S(2)}) async-start(f32[32,8,256]{2,1,0:T(8,128)} %pad_maximum_fusion.4), calls=%async_computation | async-start | bytes 524288 | tf_op jit(solution)/shard_map/all_to_all | solution.py:461
  11.3 3.7 %pack_planes.3 = (bf16[2,2,96,384]{3,2,1,0:T(8,128)(2,1)}, bf16[2,2,96,384]{3,2,1,0:T(8,128)(2,1)}, bf16[2,2,96,384]{3,2,1,0:T(8,128)(2,1)}, bf16[2,2,96,384]{3,2,1,0:T(8,128)(2,1)}) custom-call(s32[1]{0:T(128)} %bitcast.place, bf16[2,8,4,36864]{3,2,1,0:T(4,128)(2,1)} %refs_0_.5), custom_call_target="tpu_custom_call" | custom-call | bytes 7380000 | tf_op jit(solution)/shard_map/pack_planes/pallas_call | solution.py:64
  16.8 2.4 collective-permute-start.1
  20.6 7.5 %pack_planes.4 = (bf16[2,5,96,384]{3,2,1,0:T(8,128)(2,1)}, bf16[2,5,96,384]{3,2,1,0:T(8,128)(2,1)}, bf16[2,5,96,384]{3,2,1,0:T(8,128)(2,1)}, bf16[2,5,96,384]{3,2,1,0:T(8,128)(2,1)}) custom-call(s32[1]{0:T(128)} %bitcast.place, bf16[2,8,4,36864]{3,2,1,0:T(4,128)(2,1)} %refs_0_.5), custom_call_target="tpu_custom_call" | custom-call | bytes 18450000 | tf_op jit(solution)/shard_map/pack_planes/pallas_call | solution.py:64
  28.1 10.0 %mix_waves.1 = bf16[8,768,384]{2,1,0:T(8,128)(2,1)} custom-call(bf16[2,8,4,36864]{3,2,1,0:T(4,128)(2,1)} %refs_0_.5), custom_call_target="tpu_custom_call" | custom-call | bytes 29520000 | tf_op jit(solution)/shard_map/mix_waves/pallas_call | solution.py:104
  41.0 4.6 %all-to-all-start.1 = ((bf16[8,768,384]{2,1,0:T(8,128)(2,1)}), bf16[8,768,384]{2,1,0:T(8,128)(2,1)}, u32[]{:S(2)}, u32[]{:S(2)}) async-start(bf16[8,768,384]{2,1,0:T(8,128)(2,1)} %mix_waves.1), calls=%async_computation.1 | async-start | bytes 9437184 | tf_op jit(solution)/shard_map/all_to_all | solution.py:468
  47.7 6.3 %collective-permute-start.3 = (bf16[2,5,96,384]{3,2,1,0:T(8,128)(2,1)}, bf16[2,5,96,384]{3,2,1,0:T(8,128)(2,1)S(1)}, u32[]{:S(2)}, u32[]{:S(2)}) collective-permute-start(bf16[2,5,96,384]{3,2,1,0:T(8,128)(2,1)} %get-tuple-element.72), channel_id=1, source_target_pairs={{0,1},{1,2},{2,3},{3,0},{4,5},{5,6},{6,7},{7,4},{8,9},{9,10},{10,1... | collective-permute-start | bytes 2211848 | tf_op jit(solution)/shard_map/ppermute | solution.py:343
  57.1 2.3 fusion.7
  59.4 2.6 multiply_convert_fusion
  64.7 13.6 %charge_potential.1.w_ref = f32[48,384]{1,0:T(8,128)} custom-call(s32[2]{0:T(128)} %pad_add_fusion.place, f32[32,8,256]{2,1,0:T(8,128)} %copy-done.4, f32[48,384]{1,0:T(8,128)} %reshape.109.i_ref), custom_call_target="tpu_custom_call" | custom-call | bytes 44280000 | tf_op jit(solution)/shard_map/charge_potential/pallas_call | solution.py:419
  78.3 5.7 %forward.3.refs_4_.refs_0_ = bf16[2,2,384,384]{3,2,1,0:T(8,128)(2,1)} custom-call(s32[1]{0:T(128)} %bitcast.place, bf16[2,2,96,384]{3,2,1,0:T(8,128)(2,1)} %get-tuple-element.81.refs_0_, bf16[2,2,96,384]{3,2,1,0:T(8,128)(2,1)} %copy-done.5, bf16[2,2,96,384]{3,2,1,0:T(8,128)(2,1)} %copy-done.6, bf16[2,2,96,384]{3,2,1,0:T(8,128)(2,1)} %copy-done.7, ...), custom_call_target="tpu_custom_call" | custom-call | bytes 14760000 | tf_op jit(solution)/shard_map/forward/pallas_call | solution.py:215
  84.0 19.9 %collective-permute-done.4.refs_2_ = bf16[2,5,96,384]{3,2,1,0:T(8,128)(2,1)S(1)} collective-permute-done((bf16[2,5,96,384]{3,2,1,0:T(8,128)(2,1)}, bf16[2,5,96,384]{3,2,1,0:T(8,128)(2,1)S(1)}, u32[]{:S(2)}, u32[]{:S(2)}) %collective-permute-start.4) | collective-permute-done | bytes 737312 | tf_op jit(solution)/shard_map/ppermute | solution.py:343
  104.8 3.9 %all-to-all-start.2 = ((f32[8,48,384]{2,1,0:T(8,128)}), f32[8,48,384]{2,1,0:T(8,128)S(1)}, u32[]{:S(2)}, u32[]{:S(2)}) async-start(f32[8,48,384]{2,1,0:T(8,128)} %broadcast_in_dim.13), calls=%async_computation.2 | async-start | bytes 1179648 | tf_op jit(solution)/shard_map/all_to_all | solution.py:479
  108.7 16.2 %collective-permute-start.6 = (bf16[2,1,96,384]{3,2,1,0:T(8,128)(2,1)}, bf16[2,1,96,384]{3,2,1,0:T(8,128)(2,1)S(1)}, u32[]{:S(2)}, u32[]{:S(2)}) collective-permute-start(bf16[2,1,96,384]{3,2,1,0:T(8,128)(2,1)} %get-tuple-element.106), channel_id=1, source_target_pairs={{0,1},{1,2},{2,3},{3,0},{4,5},{5,6},{6,7},{7,4},{8,9},{9,10},{10,1... | collective-permute-start | bytes 442376 | tf_op jit(solution)/shard_map/ppermute | solution.py:343
  127.4 10.0 %forward.4.refs_4_.refs_1_ = bf16[5,2,384,384]{3,2,1,0:T(8,128)(2,1)} custom-call(s32[1]{0:T(128)} %bitcast.place, bf16[2,5,96,384]{3,2,1,0:T(8,128)(2,1)} %get-tuple-element.95.refs_0_, bf16[2,5,96,384]{3,2,1,0:T(8,128)(2,1)} %copy-done.1, bf16[2,5,96,384]{3,2,1,0:T(8,128)(2,1)} %copy-done.2, bf16[2,5,96,384]{3,2,1,0:T(8,128)(2,1)} %copy-done.3, ...), custom_call_target="tpu_custom_call" | custom-call | bytes 31365000 | tf_op jit(solution)/shard_map/forward/pallas_call | solution.py:215
  138.2 6.2 %inverse.3 = (bf16[2,2,96,384]{3,2,1,0:T(8,128)(2,1)}, bf16[2,2,96,384]{3,2,1,0:T(8,128)(2,1)}, bf16[2,2,96,384]{3,2,1,0:T(8,128)(2,1)}, bf16[2,2,96,384]{3,2,1,0:T(8,128)(2,1)}) custom-call(s32[1]{0:T(128)} %bitcast.place, bf16[2,2,96,384]{3,2,1,0:T(8,128)(2,1)} %get-tuple-element.81.refs_0_, bf16[2,2,96,384]{3,2,1,0:T(8,128)(2,1)} %copy-done.5, ...), custom_call_target="tpu_custom_call" | custom-call | bytes 16974000 | tf_op jit(solution)/shard_map/inverse/pallas_call | solution.py:259
  144.4 11.0 %inverse.4 = (bf16[2,5,96,384]{3,2,1,0:T(8,128)(2,1)}, bf16[2,5,96,384]{3,2,1,0:T(8,128)(2,1)}, bf16[2,5,96,384]{3,2,1,0:T(8,128)(2,1)}, bf16[2,5,96,384]{3,2,1,0:T(8,128)(2,1)}) custom-call(s32[1]{0:T(128)} %bitcast.place, bf16[2,5,96,384]{3,2,1,0:T(8,128)(2,1)} %get-tuple-element.95.refs_0_, bf16[2,5,96,384]{3,2,1,0:T(8,128)(2,1)} %copy-done.1, ...), custom_call_target="tpu_custom_call" | custom-call | bytes 36900000 | tf_op jit(solution)/shard_map/inverse/pallas_call | solution.py:259
  156.8 4.1 %forward.5.refs_2_.refs_4_ = bf16[1,2,384,384]{3,2,1,0:T(8,128)(2,1)} custom-call(s32[1]{0:T(128)} %bitcast.place, bf16[2,1,96,384]{3,2,1,0:T(8,128)(2,1)} %get-tuple-element.105.refs_0_, bf16[2,1,96,384]{3,2,1,0:T(8,128)(2,1)} %copy-done.12, bf16[2,1,96,384]{3,2,1,0:T(8,128)(2,1)} %copy-done.13, bf16[2,1,96,384]{3,2,1,0:T(8,128)(2,1)} %copy-done.14, ...), custom_call_target="tpu_custom_call" | custom-call | bytes 9225000 | tf_op jit(solution)/shard_map/forward/pallas_call | solution.py:215
  160.9 9.3 %mix_space.1 = bf16[8,768,384]{2,1,0:T(8,128)(2,1)} custom-call(bf16[2,2,384,384]{3,2,1,0:T(8,128)(2,1)} %forward.3.refs_4_.refs_0_, bf16[5,2,384,384]{3,2,1,0:T(8,128)(2,1)} %forward.4.refs_4_.refs_1_, bf16[1,2,384,384]{3,2,1,0:T(8,128)(2,1)} %forward.5.refs_2_.refs_4_), custom_call_target="tpu_custom_call" | custom-call | bytes 29520000 | tf_op jit(solution)/shard_map/mix_space/pallas_call | solution.py:142
  170.2 4.7 %all-to-all-start.3 = ((bf16[8,1,768,384]{3,2,1,0:T(8,128)(2,1)}), bf16[8,1,768,384]{3,2,1,0:T(8,128)(2,1)}, u32[]{:S(2)}, u32[]{:S(2)}) async-start(bf16[8,1,768,384]{3,2,1,0:T(8,128)(2,1)} %bitcast.22), calls=%async_computation.3 | async-start | bytes 9437184 | tf_op jit(solution)/shard_map/all_to_all | solution.py:492
  176.2 3.2 %collective-permute-start.13 = (bf16[2,5,96,384]{3,2,1,0:T(8,128)(2,1)}, bf16[2,5,96,384]{3,2,1,0:T(8,128)(2,1)S(1)}, u32[]{:S(2)}, u32[]{:S(2)}) collective-permute-start(bf16[2,5,96,384]{3,2,1,0:T(8,128)(2,1)} %get-tuple-element.117), channel_id=1, source_target_pairs={{0,2},{1,3},{2,0},{3,1},{4,6},{5,7},{6,4},{7,5},{8,10},{9,11},{10,... | collective-permute-start | bytes 2211848 | tf_op jit(solution)/shard_map/ppermute | solution.py:343
  182.0 20.8 %collective-permute-done.15.refs_1_ = bf16[2,2,96,384]{3,2,1,0:T(8,128)(2,1)S(1)} collective-permute-done((bf16[2,2,96,384]{3,2,1,0:T(8,128)(2,1)S(1)}, bf16[2,2,96,384]{3,2,1,0:T(8,128)(2,1)S(1)}, u32[]{:S(2)}, u32[]{:S(2)}) %collective-permute-start.15) | collective-permute-done | bytes 294944 | tf_op jit(solution)/shard_map/ppermute | solution.py:343
  203.8 8.3 %overlap.2.refs_0_ = f32[128,128]{1,0:T(8,128)} custom-call(bf16[8,768,384]{2,1,0:T(8,128)(2,1)} %all-to-all-done.1.z_ref, f32[48,384]{1,0:T(8,128)} %reshape.110.w_ref), custom_call_target="tpu_custom_call" | custom-call | bytes 29520000 | tf_op jit(solution)/shard_map/overlap/pallas_call | solution.py:328
  212.2 4.6 %inverse.5 = (bf16[2,1,96,384]{3,2,1,0:T(8,128)(2,1)}, bf16[2,1,96,384]{3,2,1,0:T(8,128)(2,1)}, bf16[2,1,96,384]{3,2,1,0:T(8,128)(2,1)}, bf16[2,1,96,384]{3,2,1,0:T(8,128)(2,1)}) custom-call(s32[1]{0:T(128)} %bitcast.place, bf16[2,1,96,384]{3,2,1,0:T(8,128)(2,1)} %get-tuple-element.105.refs_0_, bf16[2,1,96,384]{3,2,1,0:T(8,128)(2,1)} %copy-done.12, ...), custom_call_target="tpu_custom_call" | custom-call | bytes 10332000 | tf_op jit(solution)/shard_map/inverse/pallas_call | solution.py:259
  216.7 45.6 %collective-permute-done.16.refs_2_ = bf16[2,2,96,384]{3,2,1,0:T(8,128)(2,1)S(1)} collective-permute-done((bf16[2,2,96,384]{3,2,1,0:T(8,128)(2,1)}, bf16[2,2,96,384]{3,2,1,0:T(8,128)(2,1)S(1)}, u32[]{:S(2)}, u32[]{:S(2)}) %collective-permute-start.16) | collective-permute-done | bytes 294944 | tf_op jit(solution)/shard_map/ppermute | solution.py:343
  262.3 3.4 %collective-permute-start.9 = (bf16[2,1,96,384]{3,2,1,0:T(8,128)(2,1)}, bf16[2,1,96,384]{3,2,1,0:T(8,128)(2,1)S(1)}, u32[]{:S(2)}, u32[]{:S(2)}) collective-permute-start(bf16[2,1,96,384]{3,2,1,0:T(8,128)(2,1)} %get-tuple-element.112), channel_id=1, source_target_pairs={{0,1},{1,2},{2,3},{3,0},{4,5},{5,6},{6,7},{7,4},{8,9},{9,10},{10,1... | collective-permute-start | bytes 442376 | tf_op jit(solution)/shard_map/ppermute | solution.py:343
  265.7 3.3 %collective-permute-start.10 = (bf16[2,1,96,384]{3,2,1,0:T(8,128)(2,1)}, bf16[2,1,96,384]{3,2,1,0:T(8,128)(2,1)S(1)}, u32[]{:S(2)}, u32[]{:S(2)}) collective-permute-start(bf16[2,1,96,384]{3,2,1,0:T(8,128)(2,1)} %get-tuple-element.113), channel_id=1, source_target_pairs={{0,2},{1,3},{2,0},{3,1},{4,6},{5,7},{6,4},{7,5},{8,10},{9,11},{10,... | collective-permute-start | bytes 442376 | tf_op jit(solution)/shard_map/ppermute | solution.py:343
  269.0 2.5 collective-permute-start.11
  271.5 8.5 %overlap.3 = f32[2,64,64]{2,1,0:T(8,128)} custom-call(bf16[8,768,384]{2,1,0:T(8,128)(2,1)} %bitcast.11.z_ref, f32[48,384]{1,0:T(8,128)} %charge_potential.1.w_ref, f32[128,128]{1,0:T(8,128)} %overlap.2.refs_0_), custom_call_target="tpu_custom_call" | custom-call | bytes 29520000 | tf_op jit(solution)/shard_map/overlap/pallas_call | solution.py:328
  281.8 3.0 all-to-all-start.4
  284.8 3.8 %unpack_planes.3.refs_4_ = bf16[2,8,4,36864]{3,2,1,0:T(4,128)(2,1)} custom-call(s32[1]{0:T(128)} %bitcast.place, bf16[2,2,96,384]{3,2,1,0:T(8,128)(2,1)} %get-tuple-element.119.refs_0_, bf16[2,2,96,384]{3,2,1,0:T(8,128)(2,1)} %copy-done.15, bf16[2,2,96,384]{3,2,1,0:T(8,128)(2,1)} %copy-done.16, bf16[2,2,96,384]{3,2,1,0:T(8,128)(2,1)} %copy-done.17), custom_call_target="tpu_custom_call" | custom-call | bytes 8856000 | tf_op jit(solution)/shard_map/unpack_planes/pallas_call | solution.py:183
  290.4 7.9 %unpack_planes.4.refs_4_ = bf16[2,8,4,36864]{3,2,1,0:T(4,128)(2,1)} custom-call(s32[1]{0:T(128)} %bitcast.place, bf16[2,5,96,384]{3,2,1,0:T(8,128)(2,1)} %get-tuple-element.115.refs_0_, bf16[2,5,96,384]{3,2,1,0:T(8,128)(2,1)} %copy-done.8, bf16[2,5,96,384]{3,2,1,0:T(8,128)(2,1)} %copy-done.9, ...), custom_call_target="tpu_custom_call", output_to_operand_aliasing={{}: (5, {})} | custom-call | bytes 22140000 | tf_op jit(solution)/shard_map/unpack_planes/pallas_call | solution.py:183
  (121 shorter events, 35.8 us)
Async XLA Ops:
  4.0 36.1 %all-to-all-start = ((f32[32,8,256]{2,1,0:T(8,128)}), f32[32,8,256]{2,1,0:T(8,128)S(1)}, u32[]{:S(2)}, u32[]{:S(2)}) async-start(f32[32,8,256]{2,1,0:T(8,128)} %pad_maximum_fusion.4), calls=%async_computation | async-start | bytes 524288 | tf_op jit(solution)/shard_map/all_to_all | solution.py:461
  15.1 23.1 %collective-permute-start = (bf16[2,2,96,384]{3,2,1,0:T(8,128)(2,1)}, bf16[2,2,96,384]{3,2,1,0:T(8,128)(2,1)S(1)}, u32[]{:S(2)}, u32[]{:S(2)}) collective-permute-start(bf16[2,2,96,384]{3,2,1,0:T(8,128)(2,1)} %get-tuple-element.64), channel_id=1, source_target_pairs={{0,1},{1,2},{2,3},{3,0},{4,5},{5,6},{6,7},{7,4},{8,9},{9,10},{10,1... | collective-permute-start | bytes 884744 | tf_op jit(solution)/shard_map/ppermute | solution.py:343
  16.8 23.3 %collective-permute-start.1 = (bf16[2,2,96,384]{3,2,1,0:T(8,128)(2,1)}, bf16[2,2,96,384]{3,2,1,0:T(8,128)(2,1)S(1)}, u32[]{:S(2)}, u32[]{:S(2)}) collective-permute-start(bf16[2,2,96,384]{3,2,1,0:T(8,128)(2,1)} %get-tuple-element.65), channel_id=1, source_target_pairs={{0,2},{1,3},{2,0},{3,1},{4,6},{5,7},{6,4},{7,5},{8,10},{9,11},{10,... | collective-permute-start | bytes 884744 | tf_op jit(solution)/shard_map/ppermute | solution.py:343
  19.2 20.9 %collective-permute-start.2 = (bf16[2,2,96,384]{3,2,1,0:T(8,128)(2,1)}, bf16[2,2,96,384]{3,2,1,0:T(8,128)(2,1)S(1)}, u32[]{:S(2)}, u32[]{:S(2)}) collective-permute-start(bf16[2,2,96,384]{3,2,1,0:T(8,128)(2,1)} %get-tuple-element.66), channel_id=1, source_target_pairs={{0,3},{1,0},{2,1},{3,2},{4,7},{5,4},{6,5},{7,6},{8,11},{9,8},{10,9... | collective-permute-start | bytes 884744 | tf_op jit(solution)/shard_map/ppermute | solution.py:343
  40.2 23.4 %copy-start.4 = (f32[32,8,256]{2,1,0:T(8,128)}, f32[32,8,256]{2,1,0:T(8,128)S(1)}, u32[]{:S(2)}) copy-start(f32[32,8,256]{2,1,0:T(8,128)S(1)} %all-to-all-done.c_ref) | copy-start | bytes 786436
  41.0 62.9 %all-to-all-start.1 = ((bf16[8,768,384]{2,1,0:T(8,128)(2,1)}), bf16[8,768,384]{2,1,0:T(8,128)(2,1)}, u32[]{:S(2)}, u32[]{:S(2)}) async-start(bf16[8,768,384]{2,1,0:T(8,128)(2,1)} %mix_waves.1), calls=%async_computation.1 | async-start | bytes 9437184 | tf_op jit(solution)/shard_map/all_to_all | solution.py:468
  47.7 36.3 %collective-permute-start.3 = (bf16[2,5,96,384]{3,2,1,0:T(8,128)(2,1)}, bf16[2,5,96,384]{3,2,1,0:T(8,128)(2,1)S(1)}, u32[]{:S(2)}, u32[]{:S(2)}) collective-permute-start(bf16[2,5,96,384]{3,2,1,0:T(8,128)(2,1)} %get-tuple-element.72), channel_id=1, source_target_pairs={{0,1},{1,2},{2,3},{3,0},{4,5},{5,6},{6,7},{7,4},{8,9},{9,10},{10,1... | collective-permute-start | bytes 2211848 | tf_op jit(solution)/shard_map/ppermute | solution.py:343
  54.0 49.8 %collective-permute-start.4 = (bf16[2,5,96,384]{3,2,1,0:T(8,128)(2,1)}, bf16[2,5,96,384]{3,2,1,0:T(8,128)(2,1)S(1)}, u32[]{:S(2)}, u32[]{:S(2)}) collective-permute-start(bf16[2,5,96,384]{3,2,1,0:T(8,128)(2,1)} %get-tuple-element.73), channel_id=1, source_target_pairs={{0,2},{1,3},{2,0},{3,1},{4,6},{5,7},{6,4},{7,5},{8,10},{9,11},{10,... | collective-permute-start | bytes 2211848 | tf_op jit(solution)/shard_map/ppermute | solution.py:343
  55.5 48.4 %collective-permute-start.5 = (bf16[2,5,96,384]{3,2,1,0:T(8,128)(2,1)S(1)}, bf16[2,5,96,384]{3,2,1,0:T(8,128)(2,1)S(1)}, u32[]{:S(2)}, u32[]{:S(2)}) collective-permute-start(bf16[2,5,96,384]{3,2,1,0:T(8,128)(2,1)S(1)} %copy-done.23), channel_id=1, source_target_pairs={{0,3},{1,0},{2,1},{3,2},{4,7},{5,4},{6,5},{7,6},{8,11},{9,8},{10,9... | collective-permute-start | bytes 2211848 | tf_op jit(solution)/shard_map/ppermute | solution.py:343
  78.3 25.6 %copy-start.11 = (f32[48,384]{1,0:T(8,128)S(1)}, f32[48,384]{1,0:T(8,128)}, u32[]{:S(2)}) copy-start(f32[48,384]{1,0:T(8,128)} %charge_potential.1.w_ref) | copy-start | bytes 221188
  78.3 48.1 %copy-start.26 = (bf16[2,1,96,384]{3,2,1,0:T(8,128)(2,1)S(1)}, bf16[2,1,96,384]{3,2,1,0:T(8,128)(2,1)}, u32[]{:S(2)}) copy-start(bf16[2,1,96,384]{3,2,1,0:T(8,128)(2,1)} %get-tuple-element.108) | copy-start | bytes 442372
  84.0 43.4 %copy-start.1 = (bf16[2,5,96,384]{3,2,1,0:T(8,128)(2,1)}, bf16[2,5,96,384]{3,2,1,0:T(8,128)(2,1)S(1)}, u32[]{:S(2)}) copy-start(bf16[2,5,96,384]{3,2,1,0:T(8,128)(2,1)S(1)} %collective-permute-done.3.refs_1_) | copy-start | bytes 2211844
  103.8 23.5 %copy-start.2 = (bf16[2,5,96,384]{3,2,1,0:T(8,128)(2,1)}, bf16[2,5,96,384]{3,2,1,0:T(8,128)(2,1)S(1)}, u32[]{:S(2)}) copy-start(bf16[2,5,96,384]{3,2,1,0:T(8,128)(2,1)S(1)} %collective-permute-done.4.refs_2_) | copy-start | bytes 2211844
  103.8 23.5 %copy-start.3 = (bf16[2,5,96,384]{3,2,1,0:T(8,128)(2,1)}, bf16[2,5,96,384]{3,2,1,0:T(8,128)(2,1)S(1)}, u32[]{:S(2)}) copy-start(bf16[2,5,96,384]{3,2,1,0:T(8,128)(2,1)S(1)} %collective-permute-done.5.refs_3_) | copy-start | bytes 2211844
  104.8 32.6 %all-to-all-start.2 = ((f32[8,48,384]{2,1,0:T(8,128)}), f32[8,48,384]{2,1,0:T(8,128)S(1)}, u32[]{:S(2)}, u32[]{:S(2)}) async-start(f32[8,48,384]{2,1,0:T(8,128)} %broadcast_in_dim.13), calls=%async_computation.2 | async-start | bytes 1179648 | tf_op jit(solution)/shard_map/all_to_all | solution.py:479
  108.7 46.7 %collective-permute-start.6 = (bf16[2,1,96,384]{3,2,1,0:T(8,128)(2,1)}, bf16[2,1,96,384]{3,2,1,0:T(8,128)(2,1)S(1)}, u32[]{:S(2)}, u32[]{:S(2)}) collective-permute-start(bf16[2,1,96,384]{3,2,1,0:T(8,128)(2,1)} %get-tuple-element.106), channel_id=1, source_target_pairs={{0,1},{1,2},{2,3},{3,0},{4,5},{5,6},{6,7},{7,4},{8,9},{9,10},{10,1... | collective-permute-start | bytes 442376 | tf_op jit(solution)/shard_map/ppermute | solution.py:343
  124.9 30.5 %collective-permute-start.7 = (bf16[2,1,96,384]{3,2,1,0:T(8,128)(2,1)}, bf16[2,1,96,384]{3,2,1,0:T(8,128)(2,1)S(1)}, u32[]{:S(2)}, u32[]{:S(2)}) collective-permute-start(bf16[2,1,96,384]{3,2,1,0:T(8,128)(2,1)} %get-tuple-element.107), channel_id=1, source_target_pairs={{0,2},{1,3},{2,0},{3,1},{4,6},{5,7},{6,4},{7,5},{8,10},{9,11},{10,... | collective-permute-start | bytes 442376 | tf_op jit(solution)/shard_map/ppermute | solution.py:343
  126.4 29.0 %collective-permute-start.8 = (bf16[2,1,96,384]{3,2,1,0:T(8,128)(2,1)S(1)}, bf16[2,1,96,384]{3,2,1,0:T(8,128)(2,1)S(1)}, u32[]{:S(2)}, u32[]{:S(2)}) collective-permute-start(bf16[2,1,96,384]{3,2,1,0:T(8,128)(2,1)S(1)} %copy-done.26), channel_id=1, source_target_pairs={{0,3},{1,0},{2,1},{3,2},{4,7},{5,4},{6,5},{7,6},{8,11},{9,8},{10,9... | collective-permute-start | bytes 442376 | tf_op jit(solution)/shard_map/ppermute | solution.py:343
  170.2 32.6 %copy-start.24 = (bf16[2,2,96,384]{3,2,1,0:T(8,128)(2,1)S(1)}, bf16[2,2,96,384]{3,2,1,0:T(8,128)(2,1)}, u32[]{:S(2)}) copy-start(bf16[2,2,96,384]{3,2,1,0:T(8,128)(2,1)} %get-tuple-element.122) | copy-start | bytes 884740
  170.2 101.2 %all-to-all-start.3 = ((bf16[8,1,768,384]{3,2,1,0:T(8,128)(2,1)}), bf16[8,1,768,384]{3,2,1,0:T(8,128)(2,1)}, u32[]{:S(2)}, u32[]{:S(2)}) async-start(bf16[8,1,768,384]{3,2,1,0:T(8,128)(2,1)} %bitcast.22), calls=%async_computation.3 | async-start | bytes 9437184 | tf_op jit(solution)/shard_map/all_to_all | solution.py:492
  175.0 94.0 %collective-permute-start.12 = (bf16[2,5,96,384]{3,2,1,0:T(8,128)(2,1)}, bf16[2,5,96,384]{3,2,1,0:T(8,128)(2,1)S(1)}, u32[]{:S(2)}, u32[]{:S(2)}) collective-permute-start(bf16[2,5,96,384]{3,2,1,0:T(8,128)(2,1)} %get-tuple-element.116), channel_id=1, source_target_pairs={{0,1},{1,2},{2,3},{3,0},{4,5},{5,6},{6,7},{7,4},{8,9},{9,10},{10,1... | collective-permute-start | bytes 2211848 | tf_op jit(solution)/shard_map/ppermute | solution.py:343
  176.2 26.7 %collective-permute-start.15 = (bf16[2,2,96,384]{3,2,1,0:T(8,128)(2,1)S(1)}, bf16[2,2,96,384]{3,2,1,0:T(8,128)(2,1)S(1)}, u32[]{:S(2)}, u32[]{:S(2)}) collective-permute-start(bf16[2,2,96,384]{3,2,1,0:T(8,128)(2,1)S(1)} %copy-done.25), channel_id=1, source_target_pairs={{0,1},{1,2},{2,3},{3,0},{4,5},{5,6},{6,7},{7,4},{8,9},{9,10},{10,1... | collective-permute-start | bytes 884744 | tf_op jit(solution)/shard_map/ppermute | solution.py:343
  176.2 112.4 %collective-permute-start.13 = (bf16[2,5,96,384]{3,2,1,0:T(8,128)(2,1)}, bf16[2,5,96,384]{3,2,1,0:T(8,128)(2,1)S(1)}, u32[]{:S(2)}, u32[]{:S(2)}) collective-permute-start(bf16[2,5,96,384]{3,2,1,0:T(8,128)(2,1)} %get-tuple-element.117), channel_id=1, source_target_pairs={{0,2},{1,3},{2,0},{3,1},{4,6},{5,7},{6,4},{7,5},{8,10},{9,11},{10,... | collective-permute-start | bytes 2211848 | tf_op jit(solution)/shard_map/ppermute | solution.py:343
  179.4 109.2 %collective-permute-start.14 = (bf16[2,5,96,384]{3,2,1,0:T(8,128)(2,1)}, bf16[2,5,96,384]{3,2,1,0:T(8,128)(2,1)S(1)}, u32[]{:S(2)}, u32[]{:S(2)}) collective-permute-start(bf16[2,5,96,384]{3,2,1,0:T(8,128)(2,1)} %get-tuple-element.118), channel_id=1, source_target_pairs={{0,3},{1,0},{2,1},{3,2},{4,7},{5,4},{6,5},{7,6},{8,11},{9,8},{10,9... | collective-permute-start | bytes 2211848 | tf_op jit(solution)/shard_map/ppermute | solution.py:343
  180.5 81.8 %collective-permute-start.16 = (bf16[2,2,96,384]{3,2,1,0:T(8,128)(2,1)}, bf16[2,2,96,384]{3,2,1,0:T(8,128)(2,1)S(1)}, u32[]{:S(2)}, u32[]{:S(2)}) collective-permute-start(bf16[2,2,96,384]{3,2,1,0:T(8,128)(2,1)} %get-tuple-element.121), channel_id=1, source_target_pairs={{0,2},{1,3},{2,0},{3,1},{4,6},{5,7},{6,4},{7,5},{8,10},{9,11},{10,... | collective-permute-start | bytes 884744 | tf_op jit(solution)/shard_map/ppermute | solution.py:343
  202.8 62.8 %collective-permute-start.17 = (bf16[2,2,96,384]{3,2,1,0:T(8,128)(2,1)S(1)}, bf16[2,2,96,384]{3,2,1,0:T(8,128)(2,1)S(1)}, u32[]{:S(2)}, u32[]{:S(2)}) collective-permute-start(bf16[2,2,96,384]{3,2,1,0:T(8,128)(2,1)S(1)} %copy-done.24), channel_id=1, source_target_pairs={{0,3},{1,0},{2,1},{3,2},{4,7},{5,4},{6,5},{7,6},{8,11},{9,8},{10,9... | collective-permute-start | bytes 884744 | tf_op jit(solution)/shard_map/ppermute | solution.py:343
  262.3 17.7 %copy-start.16 = (bf16[2,2,96,384]{3,2,1,0:T(8,128)(2,1)}, bf16[2,2,96,384]{3,2,1,0:T(8,128)(2,1)S(1)}, u32[]{:S(2)}) copy-start(bf16[2,2,96,384]{3,2,1,0:T(8,128)(2,1)S(1)} %collective-permute-done.16.refs_2_) | copy-start | bytes 884740
  262.3 38.0 %collective-permute-start.9 = (bf16[2,1,96,384]{3,2,1,0:T(8,128)(2,1)}, bf16[2,1,96,384]{3,2,1,0:T(8,128)(2,1)S(1)}, u32[]{:S(2)}, u32[]{:S(2)}) collective-permute-start(bf16[2,1,96,384]{3,2,1,0:T(8,128)(2,1)} %get-tuple-element.112), channel_id=1, source_target_pairs={{0,1},{1,2},{2,3},{3,0},{4,5},{5,6},{6,7},{7,4},{8,9},{9,10},{10,1... | collective-permute-start | bytes 442376 | tf_op jit(solution)/shard_map/ppermute | solution.py:343
  265.7 34.6 %collective-permute-start.10 = (bf16[2,1,96,384]{3,2,1,0:T(8,128)(2,1)}, bf16[2,1,96,384]{3,2,1,0:T(8,128)(2,1)S(1)}, u32[]{:S(2)}, u32[]{:S(2)}) collective-permute-start(bf16[2,1,96,384]{3,2,1,0:T(8,128)(2,1)} %get-tuple-element.113), channel_id=1, source_target_pairs={{0,2},{1,3},{2,0},{3,1},{4,6},{5,7},{6,4},{7,5},{8,10},{9,11},{10,... | collective-permute-start | bytes 442376 | tf_op jit(solution)/shard_map/ppermute | solution.py:343
  269.0 11.1 %copy-start.8 = (bf16[2,5,96,384]{3,2,1,0:T(8,128)(2,1)}, bf16[2,5,96,384]{3,2,1,0:T(8,128)(2,1)S(1)}, u32[]{:S(2)}) copy-start(bf16[2,5,96,384]{3,2,1,0:T(8,128)(2,1)S(1)} %collective-permute-done.12.refs_1_) | copy-start | bytes 2211844
  269.0 31.3 %collective-permute-start.11 = (bf16[2,1,96,384]{3,2,1,0:T(8,128)(2,1)}, bf16[2,1,96,384]{3,2,1,0:T(8,128)(2,1)S(1)}, u32[]{:S(2)}, u32[]{:S(2)}) collective-permute-start(bf16[2,1,96,384]{3,2,1,0:T(8,128)(2,1)} %get-tuple-element.114), channel_id=1, source_target_pairs={{0,3},{1,0},{2,1},{3,2},{4,7},{5,4},{6,5},{7,6},{8,11},{9,8},{10,9... | collective-permute-start | bytes 442376 | tf_op jit(solution)/shard_map/ppermute | solution.py:343
  281.8 16.4 %all-to-all-start.4 = ((f32[32,1,256]{2,1,0:T(1,128)}), f32[32,1,256]{2,1,0:T(1,128)S(1)}, u32[]{:S(2)}, u32[]{:S(2)}) async-start(f32[32,1,256]{2,1,0:T(1,128)} %reshape.116), calls=%async_computation.4 | async-start | bytes 65536 | tf_op jit(solution)/shard_map/all_to_all | solution.py:524
  (18 other events, 46.4 us)
where the time goes:
time: 305 us; the launch traced here: 303 us
  Pallas kernels  119 us (39%)
  waiting for transfers between devices  88.3 us (29%)
  starting transfers between devices  72.9 us (24%)
  local copies, waits for them, and re-layouts  12.3 us (4%)
  other arithmetic  10.1 us (3%)
    ppermute x18, waiting for transfers between devices, shifted(): lax.ppermute(message, 'ga', [(i, (i + s) % groups) for i in range(groups)])  88.3 us
    ppermute x18, starting transfers between devices, shifted(): lax.ppermute(message, 'ga', [(i, (i + s) % groups) for i in range(groups)])  49.4 us
    pallas_call x3, Pallas kernels, inverse(): pl.pallas_call(functools.partial(inverse_body, groups), grid=(bands,), in...  21.7 us
    pallas_call x3, Pallas kernels, forward(): pl.pallas_call(functools.partial(forward_body, groups), grid=(bands,), in...  19.9 us
    pallas_call x2, Pallas kernels, overlap(): pl.pallas_call(functools.partial(overlap_body, scale, per), in_specs=[who...  16.9 us
    pallas_call x3, Pallas kernels, unpack(): pl.pallas_call(functools.partial(unpack_body, groups), grid=(2, halves, c...  13.8 us
    pallas_call x1, Pallas kernels, own_share(): pl.pallas_call(functools.partial(charges_body, planes, slab_rows), in_spe...  13.6 us
    pallas_call x3, Pallas kernels, pack(): pl.pallas_call(pack_body, grid=(2, count), in_specs=[pl.BlockSpec(memory_...  13.3 us
  transfers between devices with their start and end apart: 23, of which 4 were waited for; matrix products, arithmetic and copies ran while one was open for 4% of the time, Pallas kernels for 34%

commit v1 on v0

--- a/solution.py
+++ b/solution.py
@@ -10,12 +10,13 @@
 NX = 384
 NY = 384
 LANES = 128
+STEP = 2
 
 width_cells = 1.5
 
 
-def tables(length):
-    indices = jnp.arange(length, dtype=jnp.int32)
+def tables(indices):
+    length = indices.shape[0]
     phases = indices[:, None] * indices[None, :] % length
     angles = phases.astype(jnp.float32) * (2.0 * jnp.pi / length)
     factor = 1.0 / jnp.sqrt(jnp.float32(length))
@@ -63,17 +64,20 @@
     own = waves.shape[1] // halves
     return pl.pallas_call(
         pack_body,
-        grid=(2, count),
+        grid=(2, count // STEP),
         in_specs=[pl.BlockSpec(memory_space=pltpu.SMEM)]
         + [
-            pl.BlockSpec((1, 1, planes, rows * NY), functools.partial(block_at, h * own + first))
+            pl.BlockSpec(
+                (1, STEP, planes, rows * NY),
+                functools.partial(block_at, (h * own + first) // STEP),
+            )
             for h in range(halves)
         ],
-        out_specs=[pl.BlockSpec((1, 1, rows, NY), lambda c, n: (c, n, 0, 0))] * groups,
+        out_specs=[pl.BlockSpec((1, STEP, rows, NY), lambda c, n: (c, n, 0, 0))] * groups,
         out_shape=[jax.ShapeDtypeStruct((2, count, rows, NY), jnp.bfloat16)] * groups,
-        scratch_shapes=[pltpu.VMEM((groups, 1, rows, NY), jnp.bfloat16)],
-        compiler_params=pltpu.CompilerParams(vmem_limit_bytes=56 << 20),
-        cost_estimate=lasting(1.0 * count),
+        scratch_shapes=[pltpu.VMEM((groups, STEP, rows, NY), jnp.bfloat16)],
+        compiler_params=pltpu.CompilerParams(vmem_limit_bytes=56 << 20),
+        cost_estimate=lasting(0.01),
         name="pack_planes",
     )(place, *[waves] * halves)
 
@@ -109,7 +113,7 @@
         out_shape=jax.ShapeDtypeStruct((shares, depth, NY), jnp.bfloat16),
         scratch_shapes=[pltpu.VMEM((NY // LANES, depth, LANES), jnp.float32)],
         compiler_params=pltpu.CompilerParams(vmem_limit_bytes=56 << 20),
-        cost_estimate=lasting(8.0),
+        cost_estimate=lasting(0.01),
         name="mix_waves",
     )(waves)
 
@@ -150,7 +154,7 @@
         out_shape=jax.ShapeDtypeStruct((shares, depth, NY), jnp.bfloat16),
         scratch_shapes=[pltpu.VMEM((NY // LANES, group * depth, LANES), jnp.float32)],
         compiler_params=pltpu.CompilerParams(vmem_limit_bytes=56 << 20),
-        cost_estimate=lasting(8.0),
+        cost_estimate=lasting(0.01),
         name="mix_space",
     )(*sources)
 
@@ -222,7 +226,7 @@
         out_shape=jax.ShapeDtypeStruct((bands, 2, NX, NY), jnp.bfloat16),
         scratch_shapes=[pltpu.VMEM((groups, 2, rows, NY), jnp.bfloat16)],
         compiler_params=pltpu.CompilerParams(vmem_limit_bytes=56 << 20),
-        cost_estimate=lasting(1.5 * bands + 1.0),
+        cost_estimate=lasting(0.01),
         name="forward",
     )(place, *messages, forth, back)
 
@@ -251,18 +255,18 @@
         result[:, 0] = held[lax.rem(place[0] + s, groups)]
 
 
-def inverse(messages, place, in_space, potential, forth, back):
+def inverse(messages, base, bands, place, in_space, potential, forth, back):
     groups = len(messages)
-    shape = messages[0].shape
-    _, bands, rows, _ = shape
+    rows = messages[0].shape[2]
+    shape = (2, bands, rows, NY)
     square = pl.BlockSpec((2 * NX, 2 * NX), lambda n: (0, 0))
     return pl.pallas_call(
         functools.partial(inverse_body, groups),
         grid=(bands,),
         in_specs=[pl.BlockSpec(memory_space=pltpu.SMEM)]
-        + [pl.BlockSpec((2, 1, rows, NY), lambda n: (0, n, 0, 0))] * groups
+        + [pl.BlockSpec((2, 1, rows, NY), lambda n: (0, base + n, 0, 0))] * groups
         + [
-            pl.BlockSpec((1, 2, NX, NY), lambda n: (n, 0, 0, 0)),
+            pl.BlockSpec((1, 2, NX, NY), lambda n: (base + n, 0, 0, 0)),
             pl.BlockSpec((NX, NY), lambda n: (0, 0)),
             square,
             square,
@@ -271,7 +275,7 @@
         out_shape=[jax.ShapeDtypeStruct(shape, jnp.bfloat16)] * groups,
         scratch_shapes=[pltpu.VMEM((groups, 2, rows, NY), jnp.bfloat16)],
         compiler_params=pltpu.CompilerParams(vmem_limit_bytes=56 << 20),
-        cost_estimate=lasting(1.8 * bands + 1.0),
+        cost_estimate=lasting(0.01),
         name="inverse",
     )(place, *messages, in_space, potential, forth, back)
 
@@ -426,7 +430,7 @@
         out_specs=pl.BlockSpec(memory_space=pltpu.VMEM),
         out_shape=jax.ShapeDtypeStruct((share, NY), jnp.float32),
         compiler_params=pltpu.CompilerParams(vmem_limit_bytes=56 << 20),
-        cost_estimate=lasting(12.0),
+        cost_estimate=lasting(0.01),
         name="charge_potential",
     )(place, message, ionic)
 
@@ -439,7 +443,8 @@
     rows = NX // ga_count
     halves = ga_count // planes
     own_bands = bands // halves
-    chunks = [(0, 2), (2, own_bands - 3), (own_bands - 1, 1)]
+    half = own_bands // 2
+    chunks = [(0, half), (half, half)]
     per = 2 * bands
     pairs = [[p * halves + h for h in range(halves)] for p in range(planes)]
     ga_at, band_at = lax.axis_index("ga"), lax.axis_index("band")
@@ -449,43 +454,36 @@
     message = potential_message(
         ionic_field, point_charge, charge_place, charge_slab, planes, halves
     )
-    cosine, sine = tables(NX)
+
+    arrived = [shifted(packed[0])]
+    message = lax.all_to_all(message, ("band", "ga"), 0, 0, tiled=True)
+    own_potential = own_share(message, planes, halves)
+    copies = jnp.broadcast_to(own_potential[None], (band_groups,) + own_potential.shape)
+    potential = lax.all_to_all(copies, "band", 0, 0, tiled=True).reshape(NX, NY)
+    mixed = mix_waves(waves, rows, band_groups)
+    cells = jnp.arange(NX, dtype=jnp.int32)
+    arrived[0], potential, packed[1], mixed, cells = lax.optimization_barrier(
+        (arrived[0], potential, packed[1], mixed, cells)
+    )
+
+    arrived.append(shifted(packed[1]))
+    met_waves = lax.all_to_all(mixed, "band", 0, 0, tiled=True)
+    cosine, sine = tables(cells)
     forth = jnp.concatenate(
         [jnp.concatenate([cosine, sine], axis=1), jnp.concatenate([-sine, cosine], axis=1)], axis=0
     )
     back = jnp.concatenate(
         [jnp.concatenate([cosine, -sine], axis=1), jnp.concatenate([sine, cosine], axis=1)], axis=0
     )
-
-    arrived = [shifted(packed[0])]
-    message = lax.all_to_all(message, ("band", "ga"), 0, 0, tiled=True)
-    mixed = mix_waves(waves, rows, band_groups)
-    arrived[0], message, packed[1], mixed = lax.optimization_barrier(
-        (arrived[0], message, packed[1], mixed)
-    )
-
-    arrived.append(shifted(packed[1]))
-    met_waves = lax.all_to_all(mixed, "band", 0, 0, tiled=True)
-    own_potential = own_share(message, planes, halves)
-    copies = jnp.broadcast_to(own_potential[None], (band_groups,) + own_potential.shape)
     in_space = [forward(arrived[0], place, forth, back)]
-    arrived[1], met_waves, packed[2], copies, in_space[0], forth, back = (
-        lax.optimization_barrier(
-            (arrived[1], met_waves, packed[2], copies, in_space[0], forth, back)
-        )
-    )
-
-    arrived.append(shifted(packed[2]))
-    potential = lax.all_to_all(copies, "band", 0, 0, tiled=True).reshape(NX, NY)
+    result = inverse(arrived[0], 0, half, place, in_space[0], potential, forth, back)
+    arrived[1], met_waves, result = lax.optimization_barrier((arrived[1], met_waves, result))
+
+    returned = [shifted(result)]
     in_space.append(forward(arrived[1], place, forth, back))
-    applied = []
-    for j in range(2):
-        result = inverse(arrived[j], place, in_space[j], potential, forth, back)
-        result, place = lax.optimization_barrier((result, place))
-        applied.append(result)
-    returned = [shifted(result) for result in applied]
-    in_space.append(forward(arrived[2], place, forth, back))
     mixed = mix_space(in_space, band_groups * halves)
+    middle = ga_count // 2
+    mixed, returned[0][middle] = lax.optimization_barrier((mixed, returned[0][middle]))
     mixed = mixed.reshape(band_groups, halves, -1, NY)
     if halves > 1:
         mixed = lax.all_to_all(mixed, "ga", 1, 1, axis_index_groups=pairs, tiled=True)
@@ -512,8 +510,10 @@
 
     scale = 1.0 / (planes * NX * NY)
     grams = overlap(met_waves, kinetic, per, scale)
+    spectrum = (in_space[1], potential, forth, back)
+    returned.append(shifted(inverse(arrived[1], 0, half - 1, place, *spectrum)))
     grams, place = lax.optimization_barrier((grams, place))
-    returned.append(shifted(inverse(arrived[2], place, in_space[2], potential, forth, back)))
+    returned.append(shifted(inverse(arrived[1], half - 1, 1, place, *spectrum)))
     full_matrix = overlap(met_space, space_weights, per, scale, grams)
     all_bands = bands * band_groups
     col_width = all_bands // ga_count
@@ -524,7 +524,7 @@
     subspace = lax.all_to_all(blocks, ("band", "ga"), 0, 0, tiled=True).sum(0)
 
     applied_waves = None
-    for j, (first, _) in enumerate(chunks):
+    for j, first in enumerate((0, half, own_bands - 1)):
         if j == 2:
             place, subspace = lax.optimization_barrier((place, subspace))
         applied_waves = unpack(returned[j], place, applied_waves, first, bands, planes)

time: 305 us -> 252 us (0.83)
  waiting for transfers between devices: 88.3 us -> 47 us
  Pallas kernels: 119 us -> 111 us
  starting transfers between devices: 72.9 us -> 69 us
    ppermute x18 -> x15, waiting for transfers between devices: 88.3 us -> 33.9 us  [shifted(): lax.ppermute(message, 'ga', [(i, (i + s) % groups) for i in range(groups)])]
    all_to_all x1, waiting for transfers between devices: 0.01 us -> 10.6 us  [shards(): met_space = lax.all_to_all(mixed, 'band', 0, 0, tiled=True)]
    ppermute x18 -> x15, starting transfers between devices: 49.4 us -> 44.8 us  [shifted(): lax.ppermute(message, 'ga', [(i, (i + s) % groups) for i in range(groups)])]
    pallas_call x3 -> x2, Pallas kernels: 13.3 us -> 8.84 us  [pack(): pl.pallas_call(pack_body, grid=(2, count // STEP), in_specs=[pl.BlockSpec...]
    pallas_call x3 -> x2, Pallas kernels: 19.9 us -> 17.1 us  [forward(): pl.pallas_call(functools.partial(forward_body, groups), grid=(bands,), in...]
    unnamed x57 -> x47, local copies, waits for them, and re-layouts: 6.37 us -> 4.53 us
  transfers between devices with their start and end apart: 23 -> 20, of which waited for: 4 -> 7; matrix products, arithmetic and copies ran while one was open for 4% -> 6% of each run, Pallas kernels for 34% -> 44%
where the time goes in v1:
time: 252 us; the launch traced here: 250 us
  Pallas kernels  111 us (44%)
  starting transfers between devices  69 us (27%)
  waiting for transfers between devices  47 us (19%)
  local copies, waits for them, and re-layouts  11.3 us (4%)
  other arithmetic  10.5 us (4%)
    ppermute x15, starting transfers between devices, shifted(): lax.ppermute(message, 'ga', [(i, (i + s) % groups) for i in range(groups)])  44.8 us
    ppermute x15, waiting for transfers between devices, shifted(): lax.ppermute(message, 'ga', [(i, (i + s) % groups) for i in range(groups)])  33.9 us
    pallas_call x3, Pallas kernels, inverse(): pl.pallas_call(functools.partial(inverse_body, groups), grid=(bands,), in...  21.7 us
    pallas_call x2, Pallas kernels, forward(): pl.pallas_call(functools.partial(forward_body, groups), grid=(bands,), in...  17.1 us
    pallas_call x2, Pallas kernels, overlap(): pl.pallas_call(functools.partial(overlap_body, scale, per), in_specs=[who...  16.9 us
    pallas_call x3, Pallas kernels, unpack(): pl.pallas_call(functools.partial(unpack_body, groups), grid=(2, halves, c...  13.9 us
    pallas_call x1, Pallas kernels, own_share(): pl.pallas_call(functools.partial(charges_body, planes, slab_rows), in_spe...  13.6 us
    all_to_all x1, waiting for transfers between devices, shards(): met_space = lax.all_to_all(mixed, 'band', 0, 0, tiled=True)  10.6 us
  transfers between devices with their start and end apart: 20, of which 7 were waited for; matrix products, arithmetic and copies ran while one was open for 6% of the time, Pallas kernels for 44%

profile of v1, /device:TPU:0, one launch (start us, length us, event | category | flops | bytes accessed | tf_op | source)
XLA Modules:
  0.0 250.2 jit_solution(6560018032550454299)
XLA Ops:
  4.0 7.3 %all-to-all-start = ((f32[32,8,256]{2,1,0:T(8,128)}), f32[32,8,256]{2,1,0:T(8,128)S(1)}, u32[]{:S(2)}, u32[]{:S(2)}) async-start(f32[32,8,256]{2,1,0:T(8,128)} %pad_maximum_fusion.4), calls=%async_computation | async-start | bytes 524288 | tf_op jit(solution)/shard_map/all_to_all | solution.py:459
  11.3 4.5 %pack_planes.2 = (bf16[2,4,96,384]{3,2,1,0:T(8,128)(2,1)}, bf16[2,4,96,384]{3,2,1,0:T(8,128)(2,1)}, bf16[2,4,96,384]{3,2,1,0:T(8,128)(2,1)}, bf16[2,4,96,384]{3,2,1,0:T(8,128)(2,1)}) custom-call(s32[1]{0:T(128)} %bitcast.place, bf16[2,8,4,36864]{3,2,1,0:T(4,128)(2,1)} %w_ref.1), custom_call_target="tpu_custom_call" | custom-call | bytes 36900 | tf_op jit(solution)/shard_map/pack_planes/pallas_call | solution.py:65
  17.6 2.4 collective-permute-start.1
  23.0 13.6 %charge_potential.1.w_ref = f32[48,384]{1,0:T(8,128)} custom-call(s32[2]{0:T(128)} %pad_add_fusion.place, f32[32,8,256]{2,1,0:T(8,128)} %copy-done.7, f32[48,384]{1,0:T(8,128)} %reshape.111.i_ref), custom_call_target="tpu_custom_call" | custom-call | bytes 36900 | tf_op jit(solution)/shard_map/charge_potential/pallas_call | solution.py:423
  38.4 3.7 %all-to-all-start.1 = ((f32[8,48,384]{2,1,0:T(8,128)}), f32[8,48,384]{2,1,0:T(8,128)S(1)}, u32[]{:S(2)}, u32[]{:S(2)}) async-start(f32[8,48,384]{2,1,0:T(8,128)} %broadcast_in_dim.13), calls=%async_computation.1 | async-start | bytes 1179648 | tf_op jit(solution)/shard_map/all_to_all | solution.py:462
  42.1 4.4 %pack_planes.3 = (bf16[2,4,96,384]{3,2,1,0:T(8,128)(2,1)}, bf16[2,4,96,384]{3,2,1,0:T(8,128)(2,1)}, bf16[2,4,96,384]{3,2,1,0:T(8,128)(2,1)}, bf16[2,4,96,384]{3,2,1,0:T(8,128)(2,1)}) custom-call(s32[1]{0:T(128)} %bitcast.place, bf16[2,8,4,36864]{3,2,1,0:T(4,128)(2,1)} %w_ref.1), custom_call_target="tpu_custom_call" | custom-call | bytes 36900 | tf_op jit(solution)/shard_map/pack_planes/pallas_call | solution.py:65
  46.5 10.0 %mix_waves.1 = bf16[8,768,384]{2,1,0:T(8,128)(2,1)} custom-call(bf16[2,8,4,36864]{3,2,1,0:T(4,128)(2,1)} %w_ref.1), custom_call_target="tpu_custom_call" | custom-call | bytes 36900 | tf_op jit(solution)/shard_map/mix_waves/pallas_call | solution.py:108
  56.5 2.2 collective-permute-done.1.refs_2_
  59.9 4.6 %all-to-all-start.2 = ((bf16[8,768,384]{2,1,0:T(8,128)(2,1)}), bf16[8,768,384]{2,1,0:T(8,128)(2,1)}, u32[]{:S(2)}, u32[]{:S(2)}) async-start(bf16[8,768,384]{2,1,0:T(8,128)(2,1)} %mix_waves.1), calls=%async_computation.2 | async-start | bytes 9437184 | tf_op jit(solution)/shard_map/all_to_all | solution.py:470
  64.5 13.1 %collective-permute-start.3 = (bf16[2,4,96,384]{3,2,1,0:T(8,128)(2,1)}, bf16[2,4,96,384]{3,2,1,0:T(8,128)(2,1)S(1)}, u32[]{:S(2)}, u32[]{:S(2)}) collective-permute-start(bf16[2,4,96,384]{3,2,1,0:T(8,128)(2,1)} %get-tuple-element.57), channel_id=1, source_target_pairs={{0,1},{1,2},{2,3},{3,0},{4,5},{5,6},{6,7},{7,4},{8,9},{9,10},{10,1... | collective-permute-start | bytes 1769480 | tf_op jit(solution)/shard_map/ppermute | solution.py:347
  80.0 2.6 %fusion.7 = bf16[384,384]{1,0:T(8,128)(2,1)S(1)} fusion(s32[384]{0:T(512)S(1)} %iota.13), kind=kLoop, calls=%fused_computation.18 | loop fusion | flops 2064384 | bytes 296448 | tf_op jit(solution)/shard_map/neg | solution.py:473
  82.5 2.9 %multiply_convert_fusion = (bf16[384,384]{1,0:T(8,128)(2,1)S(1)}, bf16[384,384]{1,0:T(8,128)(2,1)S(1)}) fusion(s32[384]{0:T(512)S(1)} %iota.13), kind=kLoop, calls=%fused_computation.9 | loop fusion | flops 1916928 | bytes 591360 | tf_op jit(solution)/shard_map/convert_element_type | solution.py:25
  87.0 8.5 %forward.2.refs_4_.refs_0_ = bf16[4,2,384,384]{3,2,1,0:T(8,128)(2,1)} custom-call(s32[1]{0:T(128)} %bitcast.place, bf16[2,4,96,384]{3,2,1,0:T(8,128)(2,1)} %get-tuple-element.61.refs_0_, bf16[2,4,96,384]{3,2,1,0:T(8,128)(2,1)} %copy-done.4, bf16[2,4,96,384]{3,2,1,0:T(8,128)(2,1)} %copy-done.5, bf16[2,4,96,384]{3,2,1,0:T(8,128)(2,1)} %copy-done.6, ...), custom_call_target="tpu_custom_call" | custom-call | bytes 36900 | tf_op jit(solution)/shard_map/forward/pallas_call | solution.py:219
  95.5 9.4 %inverse.3 = (bf16[2,4,96,384]{3,2,1,0:T(8,128)(2,1)}, bf16[2,4,96,384]{3,2,1,0:T(8,128)(2,1)}, bf16[2,4,96,384]{3,2,1,0:T(8,128)(2,1)}, bf16[2,4,96,384]{3,2,1,0:T(8,128)(2,1)}) custom-call(s32[1]{0:T(128)} %bitcast.place, bf16[2,4,96,384]{3,2,1,0:T(8,128)(2,1)} %get-tuple-element.61.refs_0_, bf16[2,4,96,384]{3,2,1,0:T(8,128)(2,1)} %copy-done.4, ...), custom_call_target="tpu_custom_call" | custom-call | bytes 36900 | tf_op jit(solution)/shard_map/inverse/pallas_call | solution.py:263
  104.9 13.3 %collective-permute-done.4.refs_2_ = bf16[2,4,96,384]{3,2,1,0:T(8,128)(2,1)S(1)} collective-permute-done((bf16[2,4,96,384]{3,2,1,0:T(8,128)(2,1)S(1)}, bf16[2,4,96,384]{3,2,1,0:T(8,128)(2,1)S(1)}, u32[]{:S(2)}, u32[]{:S(2)}) %collective-permute-start.4) | collective-permute-done | bytes 589856 | tf_op jit(solution)/shard_map/ppermute | solution.py:347
  119.2 12.1 %collective-permute-start.6 = (bf16[2,4,96,384]{3,2,1,0:T(8,128)(2,1)}, bf16[2,4,96,384]{3,2,1,0:T(8,128)(2,1)S(1)}, u32[]{:S(2)}, u32[]{:S(2)}) collective-permute-start(bf16[2,4,96,384]{3,2,1,0:T(8,128)(2,1)} %get-tuple-element.77), channel_id=1, source_target_pairs={{0,2},{1,3},{2,0},{3,1},{4,6},{5,7},{6,4},{7,5},{8,10},{9,11},{10,... | collective-permute-start | bytes 1769480 | tf_op jit(solution)/shard_map/ppermute | solution.py:347
  131.3 8.6 %forward.3.refs_1_.refs_4_ = bf16[4,2,384,384]{3,2,1,0:T(8,128)(2,1)} custom-call(s32[1]{0:T(128)} %bitcast.place, bf16[2,4,96,384]{3,2,1,0:T(8,128)(2,1)} %get-tuple-element.73.refs_0_, bf16[2,4,96,384]{3,2,1,0:T(8,128)(2,1)} %copy-done.1, bf16[2,4,96,384]{3,2,1,0:T(8,128)(2,1)} %copy-done.2, bf16[2,4,96,384]{3,2,1,0:T(8,128)(2,1)} %copy-done.3, ...), custom_call_target="tpu_custom_call" | custom-call | bytes 36900 | tf_op jit(solution)/shard_map/forward/pallas_call | solution.py:219
  139.9 9.3 %mix_space.1 = bf16[8,768,384]{2,1,0:T(8,128)(2,1)} custom-call(bf16[4,2,384,384]{3,2,1,0:T(8,128)(2,1)} %forward.2.refs_4_.refs_0_, bf16[4,2,384,384]{3,2,1,0:T(8,128)(2,1)} %forward.3.refs_1_.refs_4_), custom_call_target="tpu_custom_call" | custom-call | bytes 36900 | tf_op jit(solution)/shard_map/mix_space/pallas_call | solution.py:146
  149.2 7.5 %collective-permute-done.6.refs_2_ = bf16[2,4,96,384]{3,2,1,0:T(8,128)(2,1)S(1)} collective-permute-done((bf16[2,4,96,384]{3,2,1,0:T(8,128)(2,1)}, bf16[2,4,96,384]{3,2,1,0:T(8,128)(2,1)S(1)}, u32[]{:S(2)}, u32[]{:S(2)}) %collective-permute-start.6) | collective-permute-done | bytes 589856 | tf_op jit(solution)/shard_map/ppermute | solution.py:347
  157.5 4.6 %all-to-all-start.3 = ((bf16[8,1,768,384]{3,2,1,0:T(8,128)(2,1)}), bf16[8,1,768,384]{3,2,1,0:T(8,128)(2,1)}, u32[]{:S(2)}, u32[]{:S(2)}) async-start(bf16[8,1,768,384]{3,2,1,0:T(8,128)(2,1)} %bitcast.22), calls=%async_computation.3 | async-start | bytes 9437184 | tf_op jit(solution)/shard_map/all_to_all | solution.py:490
  163.0 3.0 %collective-permute-start.14 = (bf16[2,4,96,384]{3,2,1,0:T(8,128)(2,1)}, bf16[2,4,96,384]{3,2,1,0:T(8,128)(2,1)S(1)}, u32[]{:S(2)}, u32[]{:S(2)}) collective-permute-start(bf16[2,4,96,384]{3,2,1,0:T(8,128)(2,1)} %get-tuple-element.92), channel_id=1, source_target_pairs={{0,3},{1,0},{2,1},{3,2},{4,7},{5,4},{6,5},{7,6},{8,11},{9,8},{10,9... | collective-permute-start | bytes 1769480 | tf_op jit(solution)/shard_map/ppermute | solution.py:347
  166.0 7.8 %inverse.5 = (bf16[2,3,96,384]{3,2,1,0:T(8,128)(2,1)}, bf16[2,3,96,384]{3,2,1,0:T(8,128)(2,1)}, bf16[2,3,96,384]{3,2,1,0:T(8,128)(2,1)}, bf16[2,3,96,384]{3,2,1,0:T(8,128)(2,1)}) custom-call(s32[1]{0:T(128)} %bitcast.place, bf16[2,4,96,384]{3,2,1,0:T(8,128)(2,1)} %get-tuple-element.73.refs_0_, bf16[2,4,96,384]{3,2,1,0:T(8,128)(2,1)} %copy-done.1, ...), custom_call_target="tpu_custom_call" | custom-call | bytes 36900 | tf_op jit(solution)/shard_map/inverse/pallas_call | solution.py:263
  173.8 2.3 collective-permute-start.11
  178.4 8.3 %overlap.2.refs_0_ = f32[128,128]{1,0:T(8,128)} custom-call(bf16[8,768,384]{2,1,0:T(8,128)(2,1)} %all-to-all-done.2.z_ref, f32[48,384]{1,0:T(8,128)} %reshape.113.w_ref), custom_call_target="tpu_custom_call" | custom-call | bytes 29520000 | tf_op jit(solution)/shard_map/overlap/pallas_call | solution.py:332
  186.7 4.6 %inverse.4 = (bf16[2,1,96,384]{3,2,1,0:T(8,128)(2,1)}, bf16[2,1,96,384]{3,2,1,0:T(8,128)(2,1)}, bf16[2,1,96,384]{3,2,1,0:T(8,128)(2,1)}, bf16[2,1,96,384]{3,2,1,0:T(8,128)(2,1)}) custom-call(s32[1]{0:T(128)} %bitcast.place, bf16[2,4,96,384]{3,2,1,0:T(8,128)(2,1)} %get-tuple-element.73.refs_0_, bf16[2,4,96,384]{3,2,1,0:T(8,128)(2,1)} %copy-done.1, ...), custom_call_target="tpu_custom_call" | custom-call | bytes 36900 | tf_op jit(solution)/shard_map/inverse/pallas_call | solution.py:263
  191.3 11.1 %collective-permute-done.10.refs_1_ = bf16[2,3,96,384]{3,2,1,0:T(8,128)(2,1)S(1)} collective-permute-done((bf16[2,3,96,384]{3,2,1,0:T(8,128)(2,1)}, bf16[2,3,96,384]{3,2,1,0:T(8,128)(2,1)S(1)}, u32[]{:S(2)}, u32[]{:S(2)}) %collective-permute-start.10) | collective-permute-done | bytes 442400 | tf_op jit(solution)/shard_map/ppermute | solution.py:347
  202.4 2.9 %collective-permute-start.8 = (bf16[2,1,96,384]{3,2,1,0:T(8,128)(2,1)}, bf16[2,1,96,384]{3,2,1,0:T(8,128)(2,1)S(1)}, u32[]{:S(2)}, u32[]{:S(2)}) collective-permute-start(bf16[2,1,96,384]{3,2,1,0:T(8,128)(2,1)} %get-tuple-element.83), channel_id=1, source_target_pairs={{0,2},{1,3},{2,0},{3,1},{4,6},{5,7},{6,4},{7,5},{8,10},{9,11},{10,... | collective-permute-start | bytes 442376 | tf_op jit(solution)/shard_map/ppermute | solution.py:347
  206.3 10.6 %all-to-all-done.3 = bf16[8,1,768,384]{3,2,1,0:T(8,128)(2,1)} async-done(((bf16[8,1,768,384]{3,2,1,0:T(8,128)(2,1)}), bf16[8,1,768,384]{3,2,1,0:T(8,128)(2,1)}, u32[]{:S(2)}, u32[]{:S(2)}) %all-to-all-start.3) | async-done | bytes 4718624 | tf_op jit(solution)/shard_map/all_to_all | solution.py:490
  216.8 8.5 %overlap.3 = f32[2,64,64]{2,1,0:T(8,128)} custom-call(bf16[8,768,384]{2,1,0:T(8,128)(2,1)} %bitcast.11.z_ref, f32[48,384]{1,0:T(8,128)} %charge_potential.1.w_ref, f32[128,128]{1,0:T(8,128)} %overlap.2.refs_0_), custom_call_target="tpu_custom_call" | custom-call | bytes 29520000 | tf_op jit(solution)/shard_map/overlap/pallas_call | solution.py:332
  227.2 3.9 %all-to-all-start.4 = ((f32[32,1,256]{2,1,0:T(1,128)}), f32[32,1,256]{2,1,0:T(1,128)S(1)}, u32[]{:S(2)}, u32[]{:S(2)}) async-start(f32[32,1,256]{2,1,0:T(1,128)} %reshape.118), calls=%async_computation.4 | async-start | bytes 65536 | tf_op jit(solution)/shard_map/all_to_all | solution.py:524
  231.1 6.6 %unpack_planes.3.refs_4_ = bf16[2,8,4,36864]{3,2,1,0:T(4,128)(2,1)} custom-call(s32[1]{0:T(128)} %bitcast.place, bf16[2,4,96,384]{3,2,1,0:T(8,128)(2,1)} %get-tuple-element.89.refs_0_, bf16[2,4,96,384]{3,2,1,0:T(8,128)(2,1)} %copy-done.9, bf16[2,4,96,384]{3,2,1,0:T(8,128)(2,1)} %copy-done.8, bf16[2,4,96,384]{3,2,1,0:T(8,128)(2,1)} %copy-done.10), custom_call_target="tpu_custom_call" | custom-call | bytes 17712000 | tf_op jit(solution)/shard_map/unpack_planes/pallas_call | solution.py:187
  238.6 5.2 %unpack_planes.4.refs_4_ = bf16[2,8,4,36864]{3,2,1,0:T(4,128)(2,1)} custom-call(s32[1]{0:T(128)} %bitcast.place, bf16[2,3,96,384]{3,2,1,0:T(8,128)(2,1)} %get-tuple-element.85.refs_0_, bf16[2,3,96,384]{3,2,1,0:T(8,128)(2,1)} %copy-done.11, bf16[2,3,96,384]{3,2,1,0:T(8,128)(2,1)} %copy-done.12, ...), custom_call_target="tpu_custom_call", output_to_operand_aliasing={{}: (5, {})} | custom-call | bytes 13283999 | tf_op jit(solution)/shard_map/unpack_planes/pallas_call | solution.py:187
  (104 shorter events, 30.1 us)
Async XLA Ops:
  0.6 2.6 %copy-start.17 = (f32[3,256]{1,0:T(4,128)S(1)}, f32[3,256]{1,0:T(4,128)}, u32[]{:S(2)}) copy-start(f32[3,256]{1,0:T(4,128)} %param.8) | copy-start | bytes 9220
  0.6 2.6 %copy-start.18 = (f32[256]{0:T(256)S(1)}, f32[256]{0:T(256)}, u32[]{:S(2)}) copy-start(f32[256]{0:T(256)} %param.7) | copy-start | bytes 3076
  4.0 17.9 %all-to-all-start = ((f32[32,8,256]{2,1,0:T(8,128)}), f32[32,8,256]{2,1,0:T(8,128)S(1)}, u32[]{:S(2)}, u32[]{:S(2)}) async-start(f32[32,8,256]{2,1,0:T(8,128)} %pad_maximum_fusion.4), calls=%async_computation | async-start | bytes 524288 | tf_op jit(solution)/shard_map/all_to_all | solution.py:459
  15.8 40.7 %collective-permute-start = (bf16[2,4,96,384]{3,2,1,0:T(8,128)(2,1)}, bf16[2,4,96,384]{3,2,1,0:T(8,128)(2,1)S(1)}, u32[]{:S(2)}, u32[]{:S(2)}) collective-permute-start(bf16[2,4,96,384]{3,2,1,0:T(8,128)(2,1)} %get-tuple-element.49), channel_id=1, source_target_pairs={{0,1},{1,2},{2,3},{3,0},{4,5},{5,6},{6,7},{7,4},{8,9},{9,10},{10,1... | collective-permute-start | bytes 1769480 | tf_op jit(solution)/shard_map/ppermute | solution.py:347
  17.6 41.1 %collective-permute-start.1 = (bf16[2,4,96,384]{3,2,1,0:T(8,128)(2,1)}, bf16[2,4,96,384]{3,2,1,0:T(8,128)(2,1)S(1)}, u32[]{:S(2)}, u32[]{:S(2)}) collective-permute-start(bf16[2,4,96,384]{3,2,1,0:T(8,128)(2,1)} %get-tuple-element.50), channel_id=1, source_target_pairs={{0,2},{1,3},{2,0},{3,1},{4,6},{5,7},{6,4},{7,5},{8,10},{9,11},{10,... | collective-permute-start | bytes 1769480 | tf_op jit(solution)/shard_map/ppermute | solution.py:347
  20.0 38.7 %collective-permute-start.2 = (bf16[2,4,96,384]{3,2,1,0:T(8,128)(2,1)}, bf16[2,4,96,384]{3,2,1,0:T(8,128)(2,1)S(1)}, u32[]{:S(2)}, u32[]{:S(2)}) collective-permute-start(bf16[2,4,96,384]{3,2,1,0:T(8,128)(2,1)} %get-tuple-element.51), channel_id=1, source_target_pairs={{0,3},{1,0},{2,1},{3,2},{4,7},{5,4},{6,5},{7,6},{8,11},{9,8},{10,9... | collective-permute-start | bytes 1769480 | tf_op jit(solution)/shard_map/ppermute | solution.py:347
  38.4 20.3 %all-to-all-start.1 = ((f32[8,48,384]{2,1,0:T(8,128)}), f32[8,48,384]{2,1,0:T(8,128)S(1)}, u32[]{:S(2)}, u32[]{:S(2)}) async-start(f32[8,48,384]{2,1,0:T(8,128)} %broadcast_in_dim.13), calls=%async_computation.1 | async-start | bytes 1179648 | tf_op jit(solution)/shard_map/all_to_all | solution.py:462
  56.5 2.2 copy-start.4
  58.7 18.8 %copy-start.21 = (bf16[2,4,96,384]{3,2,1,0:T(8,128)(2,1)S(1)}, bf16[2,4,96,384]{3,2,1,0:T(8,128)(2,1)}, u32[]{:S(2)}) copy-start(bf16[2,4,96,384]{3,2,1,0:T(8,128)(2,1)} %get-tuple-element.58) | copy-start | bytes 1769476
  58.7 20.6 %copy-start.20 = (bf16[2,4,96,384]{3,2,1,0:T(8,128)(2,1)S(1)}, bf16[2,4,96,384]{3,2,1,0:T(8,128)(2,1)}, u32[]{:S(2)}) copy-start(bf16[2,4,96,384]{3,2,1,0:T(8,128)(2,1)} %get-tuple-element.59) | copy-start | bytes 1769476
  59.9 59.3 %all-to-all-start.2 = ((bf16[8,768,384]{2,1,0:T(8,128)(2,1)}), bf16[8,768,384]{2,1,0:T(8,128)(2,1)}, u32[]{:S(2)}, u32[]{:S(2)}) async-start(bf16[8,768,384]{2,1,0:T(8,128)(2,1)} %mix_waves.1), calls=%async_computation.2 | async-start | bytes 9437184 | tf_op jit(solution)/shard_map/all_to_all | solution.py:470
  64.5 40.4 %collective-permute-start.3 = (bf16[2,4,96,384]{3,2,1,0:T(8,128)(2,1)}, bf16[2,4,96,384]{3,2,1,0:T(8,128)(2,1)S(1)}, u32[]{:S(2)}, u32[]{:S(2)}) collective-permute-start(bf16[2,4,96,384]{3,2,1,0:T(8,128)(2,1)} %get-tuple-element.57), channel_id=1, source_target_pairs={{0,1},{1,2},{2,3},{3,0},{4,5},{5,6},{6,7},{7,4},{8,9},{9,10},{10,1... | collective-permute-start | bytes 1769480 | tf_op jit(solution)/shard_map/ppermute | solution.py:347
  77.5 40.6 %collective-permute-start.4 = (bf16[2,4,96,384]{3,2,1,0:T(8,128)(2,1)S(1)}, bf16[2,4,96,384]{3,2,1,0:T(8,128)(2,1)S(1)}, u32[]{:S(2)}, u32[]{:S(2)}) collective-permute-start(bf16[2,4,96,384]{3,2,1,0:T(8,128)(2,1)S(1)} %copy-done.21), channel_id=1, source_target_pairs={{0,2},{1,3},{2,0},{3,1},{4,6},{5,7},{6,4},{7,5},{8,10},{9,11},{10,... | collective-permute-start | bytes 1769480 | tf_op jit(solution)/shard_map/ppermute | solution.py:347
  79.3 38.9 %collective-permute-start.5 = (bf16[2,4,96,384]{3,2,1,0:T(8,128)(2,1)S(1)}, bf16[2,4,96,384]{3,2,1,0:T(8,128)(2,1)S(1)}, u32[]{:S(2)}, u32[]{:S(2)}) collective-permute-start(bf16[2,4,96,384]{3,2,1,0:T(8,128)(2,1)S(1)} %copy-done.20), channel_id=1, source_target_pairs={{0,3},{1,0},{2,1},{3,2},{4,7},{5,4},{6,5},{7,6},{8,11},{9,8},{10,9... | collective-permute-start | bytes 1769480 | tf_op jit(solution)/shard_map/ppermute | solution.py:347
  104.9 26.4 %copy-start.1 = (bf16[2,4,96,384]{3,2,1,0:T(8,128)(2,1)}, bf16[2,4,96,384]{3,2,1,0:T(8,128)(2,1)S(1)}, u32[]{:S(2)}) copy-start(bf16[2,4,96,384]{3,2,1,0:T(8,128)(2,1)S(1)} %collective-permute-done.3.refs_1_) | copy-start | bytes 1769476
  118.2 13.1 %copy-start.2 = (bf16[2,4,96,384]{3,2,1,0:T(8,128)(2,1)}, bf16[2,4,96,384]{3,2,1,0:T(8,128)(2,1)S(1)}, u32[]{:S(2)}) copy-start(bf16[2,4,96,384]{3,2,1,0:T(8,128)(2,1)S(1)} %collective-permute-done.4.refs_2_) | copy-start | bytes 1769476
  118.2 13.1 %copy-start.3 = (bf16[2,4,96,384]{3,2,1,0:T(8,128)(2,1)}, bf16[2,4,96,384]{3,2,1,0:T(8,128)(2,1)S(1)}, u32[]{:S(2)}) copy-start(bf16[2,4,96,384]{3,2,1,0:T(8,128)(2,1)S(1)} %collective-permute-done.5.refs_3_) | copy-start | bytes 1769476
  119.2 37.4 %collective-permute-start.6 = (bf16[2,4,96,384]{3,2,1,0:T(8,128)(2,1)}, bf16[2,4,96,384]{3,2,1,0:T(8,128)(2,1)S(1)}, u32[]{:S(2)}, u32[]{:S(2)}) collective-permute-start(bf16[2,4,96,384]{3,2,1,0:T(8,128)(2,1)} %get-tuple-element.77), channel_id=1, source_target_pairs={{0,2},{1,3},{2,0},{3,1},{4,6},{5,7},{6,4},{7,5},{8,10},{9,11},{10,... | collective-permute-start | bytes 1769480 | tf_op jit(solution)/shard_map/ppermute | solution.py:347
  156.6 5.5 %copy-start.19 = (bf16[2,4,96,384]{3,2,1,0:T(8,128)(2,1)S(1)}, bf16[2,4,96,384]{3,2,1,0:T(8,128)(2,1)}, u32[]{:S(2)}) copy-start(bf16[2,4,96,384]{3,2,1,0:T(8,128)(2,1)} %get-tuple-element.90) | copy-start | bytes 1769476
  157.5 59.4 %all-to-all-start.3 = ((bf16[8,1,768,384]{3,2,1,0:T(8,128)(2,1)}), bf16[8,1,768,384]{3,2,1,0:T(8,128)(2,1)}, u32[]{:S(2)}, u32[]{:S(2)}) async-start(bf16[8,1,768,384]{3,2,1,0:T(8,128)(2,1)} %bitcast.22), calls=%async_computation.3 | async-start | bytes 9437184 | tf_op jit(solution)/shard_map/all_to_all | solution.py:490
  162.1 40.3 %collective-permute-start.13 = (bf16[2,4,96,384]{3,2,1,0:T(8,128)(2,1)S(1)}, bf16[2,4,96,384]{3,2,1,0:T(8,128)(2,1)S(1)}, u32[]{:S(2)}, u32[]{:S(2)}) collective-permute-start(bf16[2,4,96,384]{3,2,1,0:T(8,128)(2,1)S(1)} %copy-done.19), channel_id=1, source_target_pairs={{0,1},{1,2},{2,3},{3,0},{4,5},{5,6},{6,7},{7,4},{8,9},{9,10},{10,1... | collective-permute-start | bytes 1769480 | tf_op jit(solution)/shard_map/ppermute | solution.py:347
  163.0 42.3 %collective-permute-start.14 = (bf16[2,4,96,384]{3,2,1,0:T(8,128)(2,1)}, bf16[2,4,96,384]{3,2,1,0:T(8,128)(2,1)S(1)}, u32[]{:S(2)}, u32[]{:S(2)}) collective-permute-start(bf16[2,4,96,384]{3,2,1,0:T(8,128)(2,1)} %get-tuple-element.92), channel_id=1, source_target_pairs={{0,3},{1,0},{2,1},{3,2},{4,7},{5,4},{6,5},{7,6},{8,11},{9,8},{10,9... | collective-permute-start | bytes 1769480 | tf_op jit(solution)/shard_map/ppermute | solution.py:347
  173.7 28.6 %collective-permute-start.10 = (bf16[2,3,96,384]{3,2,1,0:T(8,128)(2,1)}, bf16[2,3,96,384]{3,2,1,0:T(8,128)(2,1)S(1)}, u32[]{:S(2)}, u32[]{:S(2)}) collective-permute-start(bf16[2,3,96,384]{3,2,1,0:T(8,128)(2,1)} %get-tuple-element.86), channel_id=1, source_target_pairs={{0,1},{1,2},{2,3},{3,0},{4,5},{5,6},{6,7},{7,4},{8,9},{9,10},{10,1... | collective-permute-start | bytes 1327112 | tf_op jit(solution)/shard_map/ppermute | solution.py:347
  173.8 63.9 %collective-permute-start.11 = (bf16[2,3,96,384]{3,2,1,0:T(8,128)(2,1)}, bf16[2,3,96,384]{3,2,1,0:T(8,128)(2,1)S(1)}, u32[]{:S(2)}, u32[]{:S(2)}) collective-permute-start(bf16[2,3,96,384]{3,2,1,0:T(8,128)(2,1)} %get-tuple-element.87), channel_id=1, source_target_pairs={{0,2},{1,3},{2,0},{3,1},{4,6},{5,7},{6,4},{7,5},{8,10},{9,11},{10,... | collective-permute-start | bytes 1327112 | tf_op jit(solution)/shard_map/ppermute | solution.py:347
  176.1 61.6 %collective-permute-start.12 = (bf16[2,3,96,384]{3,2,1,0:T(8,128)(2,1)}, bf16[2,3,96,384]{3,2,1,0:T(8,128)(2,1)S(1)}, u32[]{:S(2)}, u32[]{:S(2)}) collective-permute-start(bf16[2,3,96,384]{3,2,1,0:T(8,128)(2,1)} %get-tuple-element.88), channel_id=1, source_target_pairs={{0,3},{1,0},{2,1},{3,2},{4,7},{5,4},{6,5},{7,6},{8,11},{9,8},{10,9... | collective-permute-start | bytes 1327112 | tf_op jit(solution)/shard_map/ppermute | solution.py:347
  202.4 23.0 %copy-start.11 = (bf16[2,3,96,384]{3,2,1,0:T(8,128)(2,1)}, bf16[2,3,96,384]{3,2,1,0:T(8,128)(2,1)S(1)}, u32[]{:S(2)}) copy-start(bf16[2,3,96,384]{3,2,1,0:T(8,128)(2,1)S(1)} %collective-permute-done.10.refs_1_) | copy-start | bytes 1327108
  202.4 44.9 %collective-permute-start.7 = (bf16[2,1,96,384]{3,2,1,0:T(8,128)(2,1)}, bf16[2,1,96,384]{3,2,1,0:T(8,128)(2,1)S(1)}, u32[]{:S(2)}, u32[]{:S(2)}) collective-permute-start(bf16[2,1,96,384]{3,2,1,0:T(8,128)(2,1)} %get-tuple-element.82), channel_id=1, source_target_pairs={{0,1},{1,2},{2,3},{3,0},{4,5},{5,6},{6,7},{7,4},{8,9},{9,10},{10,1... | collective-permute-start | bytes 442376 | tf_op jit(solution)/shard_map/ppermute | solution.py:347
  202.4 23.0 %copy-start.9 = (bf16[2,4,96,384]{3,2,1,0:T(8,128)(2,1)}, bf16[2,4,96,384]{3,2,1,0:T(8,128)(2,1)S(1)}, u32[]{:S(2)}) copy-start(bf16[2,4,96,384]{3,2,1,0:T(8,128)(2,1)S(1)} %collective-permute-done.13.refs_1_) | copy-start | bytes 1769476
  202.4 44.9 %collective-permute-start.8 = (bf16[2,1,96,384]{3,2,1,0:T(8,128)(2,1)}, bf16[2,1,96,384]{3,2,1,0:T(8,128)(2,1)S(1)}, u32[]{:S(2)}, u32[]{:S(2)}) collective-permute-start(bf16[2,1,96,384]{3,2,1,0:T(8,128)(2,1)} %get-tuple-element.83), channel_id=1, source_target_pairs={{0,2},{1,3},{2,0},{3,1},{4,6},{5,7},{6,4},{7,5},{8,10},{9,11},{10,... | collective-permute-start | bytes 442376 | tf_op jit(solution)/shard_map/ppermute | solution.py:347
  205.3 20.1 %copy-start.10 = (bf16[2,4,96,384]{3,2,1,0:T(8,128)(2,1)}, bf16[2,4,96,384]{3,2,1,0:T(8,128)(2,1)S(1)}, u32[]{:S(2)}) copy-start(bf16[2,4,96,384]{3,2,1,0:T(8,128)(2,1)S(1)} %collective-permute-done.14.refs_3_) | copy-start | bytes 1769476
  205.3 42.0 %collective-permute-start.9 = (bf16[2,1,96,384]{3,2,1,0:T(8,128)(2,1)}, bf16[2,1,96,384]{3,2,1,0:T(8,128)(2,1)S(1)}, u32[]{:S(2)}, u32[]{:S(2)}) collective-permute-start(bf16[2,1,96,384]{3,2,1,0:T(8,128)(2,1)} %get-tuple-element.84), channel_id=1, source_target_pairs={{0,3},{1,0},{2,1},{3,2},{4,7},{5,4},{6,5},{7,6},{8,11},{9,8},{10,9... | collective-permute-start | bytes 442376 | tf_op jit(solution)/shard_map/ppermute | solution.py:347
  227.2 18.1 %all-to-all-start.4 = ((f32[32,1,256]{2,1,0:T(1,128)}), f32[32,1,256]{2,1,0:T(1,128)S(1)}, u32[]{:S(2)}, u32[]{:S(2)}) async-start(f32[32,1,256]{2,1,0:T(1,128)} %reshape.118), calls=%async_computation.4 | async-start | bytes 65536 | tf_op jit(solution)/shard_map/all_to_all | solution.py:524
  (10 other events, 8.7 us)

commit v2 on v1

--- a/solution.py
+++ b/solution.py
@@ -118,45 +118,46 @@
     )(waves)
 
 
-def mix_space_body(*refs):
-    sources, z_ref, mixed = refs[:-2], refs[-2], refs[-1]
-    bands = sum(source.shape[0] for source in sources)
-    rows = sources[0].shape[2]
+def mix_space_body(s_ref, *refs):
+    z_ref, mixed = refs[-2:]
+    bands, _, rows, _ = s_ref.shape
     for c in range(2):
-        row = c * bands
-        for source in sources:
-            for n in range(source.shape[0]):
-                wide = source[n, c].astype(jnp.float32)
-                for t in range(NY // LANES):
-                    mixed[t, pl.ds(row, rows, stride=2 * bands), :] = wide[
-                        :, t * LANES : (t + 1) * LANES
-                    ]
-                row += 1
+        for n in range(bands):
+            wide = s_ref[n, c].astype(jnp.float32)
+            for t in range(NY // LANES):
+                mixed[t, pl.ds(c * bands + n, rows, stride=2 * bands), :] = wide[
+                    :, t * LANES : (t + 1) * LANES
+                ]
     for t in range(NY // LANES):
-        z_ref[:, :, t * LANES : (t + 1) * LANES] = (
-            mixed[t].astype(jnp.bfloat16).reshape(z_ref.shape[:2] + (LANES,))
+        z_ref[:, 0, :, t * LANES : (t + 1) * LANES] = (
+            mixed[t].astype(jnp.bfloat16).reshape(z_ref.shape[0], -1, LANES)
         )
 
 
-def mix_space(sources, shares):
-    bands = sum(source.shape[0] for source in sources)
+def mix_space(in_space, part, base, shares):
+    bands = in_space.shape[0]
     own = NX // shares
     depth = own * 2 * bands
     group = max(1, 48 // own)
+    in_specs = [pl.BlockSpec((bands, 2, group * own, NY), lambda d: (0, 0, d, 0))]
+    operands = [in_space]
+    aliases = {}
+    if base is not None:
+        in_specs.append(pl.BlockSpec(memory_space=pl.ANY))
+        operands.append(base)
+        aliases = {1: 0}
     return pl.pallas_call(
         mix_space_body,
         grid=(shares // group,),
-        in_specs=[
-            pl.BlockSpec((source.shape[0], 2, group * own, NY), lambda d: (0, 0, d, 0))
-            for source in sources
-        ],
-        out_specs=pl.BlockSpec((group, depth, NY), lambda d: (d, 0, 0)),
-        out_shape=jax.ShapeDtypeStruct((shares, depth, NY), jnp.bfloat16),
+        in_specs=in_specs,
+        out_specs=pl.BlockSpec((group, 1, depth, NY), lambda d: (d, part, 0, 0)),
+        out_shape=jax.ShapeDtypeStruct((shares, 2, depth, NY), jnp.bfloat16),
         scratch_shapes=[pltpu.VMEM((NY // LANES, group * depth, LANES), jnp.float32)],
+        input_output_aliases=aliases,
         compiler_params=pltpu.CompilerParams(vmem_limit_bytes=56 << 20),
         cost_estimate=lasting(0.01),
         name="mix_space",
-    )(*sources)
+    )(*operands)
 
 
 def unpack_body(groups, place, *refs):
@@ -176,7 +177,7 @@
     halves = groups // planes
     own = bands // halves
     in_specs = [pl.BlockSpec(memory_space=pltpu.SMEM)] + [
-        pl.BlockSpec((1, 1, rows, NY), lambda c, h, n: (c, n, 0, 0))
+        pl.BlockSpec((1, STEP, rows, NY), lambda c, h, n: (c, n, 0, 0))
     ] * groups
     operands = [place, *messages]
     aliases = {}
@@ -186,13 +187,13 @@
         aliases = {groups + 1: 0}
     return pl.pallas_call(
         functools.partial(unpack_body, groups),
-        grid=(2, halves, count),
+        grid=(2, halves, count // STEP),
         in_specs=in_specs,
         out_specs=pl.BlockSpec(
-            (1, 1, planes, rows * NY), lambda c, h, n: (c, h * own + first + n, 0, 0)
+            (1, STEP, planes, rows * NY), lambda c, h, n: (c, (h * own + first) // STEP + n, 0, 0)
         ),
         out_shape=jax.ShapeDtypeStruct((2, bands, planes, rows * NY), jnp.bfloat16),
-        scratch_shapes=[pltpu.VMEM((halves, planes, 1, rows, NY), jnp.bfloat16)],
+        scratch_shapes=[pltpu.VMEM((halves, planes, STEP, rows, NY), jnp.bfloat16)],
         input_output_aliases=aliases,
         compiler_params=pltpu.CompilerParams(vmem_limit_bytes=56 << 20),
         cost_estimate=lasting(1.2 * count),
@@ -203,13 +204,14 @@
 def forward_body(groups, place, *refs):
     messages, (f_ref, b_ref, s_ref, held) = refs[:groups], refs[groups:]
     for s, message in enumerate(messages):
-        held[lax.rem(place[0] + groups - s, groups)] = message[:, 0]
-    parts = [held[:, c].reshape(NX, NY) for c in range(2)]
-    first = dot(jnp.concatenate(parts, axis=1), f_ref[...]).astype(jnp.bfloat16)
-    first = jnp.concatenate([first[:, :NY], first[:, NY:]], axis=0)
-    in_space = dot(b_ref[...], first).astype(jnp.bfloat16)
-    s_ref[0, 0] = in_space[:NX]
-    s_ref[0, 1] = in_space[NX:]
+        held[lax.rem(place[0] + groups - s, groups)] = message[...]
+    for i in range(STEP):
+        parts = [held[:, c, i].reshape(NX, NY) for c in range(2)]
+        first = dot(jnp.concatenate(parts, axis=1), f_ref[...]).astype(jnp.bfloat16)
+        first = jnp.concatenate([first[:, :NY], first[:, NY:]], axis=0)
+        in_space = dot(b_ref[...], first).astype(jnp.bfloat16)
+        s_ref[i, 0] = in_space[:NX]
+        s_ref[i, 1] = in_space[NX:]
 
 
 def forward(messages, place, forth, back):
@@ -218,13 +220,13 @@
     square = pl.BlockSpec((2 * NX, 2 * NX), lambda n: (0, 0))
     return pl.pallas_call(
         functools.partial(forward_body, groups),
-        grid=(bands,),
+        grid=(bands // STEP,),
         in_specs=[pl.BlockSpec(memory_space=pltpu.SMEM)]
-        + [pl.BlockSpec((2, 1, rows, NY), lambda n: (0, n, 0, 0))] * groups
+        + [pl.BlockSpec((2, STEP, rows, NY), lambda n: (0, n, 0, 0))] * groups
         + [square, square],
-        out_specs=pl.BlockSpec((1, 2, NX, NY), lambda n: (n, 0, 0, 0)),
+        out_specs=pl.BlockSpec((STEP, 2, NX, NY), lambda n: (n, 0, 0, 0)),
         out_shape=jax.ShapeDtypeStruct((bands, 2, NX, NY), jnp.bfloat16),
-        scratch_shapes=[pltpu.VMEM((groups, 2, rows, NY), jnp.bfloat16)],
+        scratch_shapes=[pltpu.VMEM((groups, 2, STEP, rows, NY), jnp.bfloat16)],
         compiler_params=pltpu.CompilerParams(vmem_limit_bytes=56 << 20),
         cost_estimate=lasting(0.01),
         name="forward",
@@ -235,24 +237,24 @@
     messages, (s_ref, v_ref, f_ref, b_ref) = refs[:groups], refs[groups : groups + 4]
     held = refs[-1]
     results = refs[-1 - groups : -1]
-    rows = held.shape[2]
+    rows = held.shape[3]
     freq_x = frequency(lax.broadcasted_iota(jnp.int32, (NX, 1), 0), NX)
     freq_y = frequency(lax.broadcasted_iota(jnp.int32, (1, NY), 1), NY)
     kinetic = 2.0 * (freq_x * freq_x / (NX * NX) + freq_y * freq_y / (NY * NY))
     for s, message in enumerate(messages):
-        held[lax.rem(place[0] + groups - s, groups)] = message[:, 0]
-    weighted = jnp.concatenate(
-        [v_ref[...] * s_ref[0, c].astype(jnp.float32) for c in range(2)],
-        axis=0,
-    ).astype(jnp.bfloat16)
-    back = dot(f_ref[...], weighted).astype(jnp.bfloat16)
-    recip = dot(jnp.concatenate([back[:NX], back[NX:]], axis=1), b_ref[...])
-    for c in range(2):
-        wide = held[:, c].reshape(NX, NY).astype(jnp.float32)
-        applied = kinetic * wide + recip[:, c * NY : (c + 1) * NY]
-        held[:, c] = applied.astype(jnp.bfloat16).reshape(groups, rows, NY)
+        held[lax.rem(place[0] + groups - s, groups)] = message[...]
+    for i in range(STEP):
+        weighted = jnp.concatenate(
+            [v_ref[...] * s_ref[i, c].astype(jnp.float32) for c in range(2)], axis=0
+        ).astype(jnp.bfloat16)
+        back = dot(f_ref[...], weighted).astype(jnp.bfloat16)
+        recip = dot(jnp.concatenate([back[:NX], back[NX:]], axis=1), b_ref[...])
+        for c in range(2):
+            wide = held[:, c, i].reshape(NX, NY).astype(jnp.float32)
+            applied = kinetic * wide + recip[:, c * NY : (c + 1) * NY]
+            held[:, c, i] = applied.astype(jnp.bfloat16).reshape(groups, rows, NY)
     for s, result in enumerate(results):
-        result[:, 0] = held[lax.rem(place[0] + s, groups)]
+        result[...] = held[lax.rem(place[0] + s, groups)]
 
 
 def inverse(messages, base, bands, place, in_space, potential, forth, back):
@@ -262,18 +264,18 @@
     square = pl.BlockSpec((2 * NX, 2 * NX), lambda n: (0, 0))
     return pl.pallas_call(
         functools.partial(inverse_body, groups),
-        grid=(bands,),
+        grid=(bands // STEP,),
         in_specs=[pl.BlockSpec(memory_space=pltpu.SMEM)]
-        + [pl.BlockSpec((2, 1, rows, NY), lambda n: (0, base + n, 0, 0))] * groups
+        + [pl.BlockSpec((2, STEP, rows, NY), lambda n: (0, base // STEP + n, 0, 0))] * groups
         + [
-            pl.BlockSpec((1, 2, NX, NY), lambda n: (base + n, 0, 0, 0)),
+            pl.BlockSpec((STEP, 2, NX, NY), lambda n: (base // STEP + n, 0, 0, 0)),
             pl.BlockSpec((NX, NY), lambda n: (0, 0)),
             square,
             square,
         ],
-        out_specs=[pl.BlockSpec((2, 1, rows, NY), lambda n: (0, n, 0, 0))] * groups,
+        out_specs=[pl.BlockSpec((2, STEP, rows, NY), lambda n: (0, n, 0, 0))] * groups,
         out_shape=[jax.ShapeDtypeStruct(shape, jnp.bfloat16)] * groups,
-        scratch_shapes=[pltpu.VMEM((groups, 2, rows, NY), jnp.bfloat16)],
+        scratch_shapes=[pltpu.VMEM((groups, 2, STEP, rows, NY), jnp.bfloat16)],
         compiler_params=pltpu.CompilerParams(vmem_limit_bytes=56 << 20),
         cost_estimate=lasting(0.01),
         name="inverse",
@@ -281,24 +283,21 @@
 
 
 def overlap_body(scale, per, z_ref, w_ref, *refs):
-    g_ref, total = refs[-2:]
-    shares = z_ref.shape[0]
-    if len(refs) == 3:
-        total[...] = refs[0][...]
-    else:
-        total[...] = jnp.zeros_like(total)
+    o_ref, total = refs[-2:]
+    shares, parts, _, _ = z_ref.shape
+    bands = per // 2
+    total[...] = jnp.zeros_like(total)
+    pieces = [(d, h) for d in range(shares) for h in range(parts)]
 
     @pl.loop(0, w_ref.shape[0] // 2)
     def _(pair):
         plain, scaled = [], []
+        at = pl.multiple_of(pair * 2 * per, 2 * per)
+        both = [z_ref[d, h, pl.ds(at, 2 * per), :].astype(jnp.float32) for d, h in pieces]
         for k in range(2):
-            point = pair * 2 + k
-            at = pl.multiple_of(point * per, per)
-            rows = jnp.concatenate([z_ref[d, pl.ds(at, per), :] for d in range(shares)], axis=0)
-            plain.append(rows)
-            scaled.append(
-                (rows.astype(jnp.float32) * w_ref[pl.ds(point, 1), :]).astype(jnp.bfloat16)
-            )
+            wide = jnp.concatenate([rows[k * per : (k + 1) * per] for rows in both], axis=0)
+            plain.append(wide.astype(jnp.bfloat16))
+            scaled.append((wide * w_ref[pl.ds(pair * 2 + k, 1), :]).astype(jnp.bfloat16))
         total[...] += lax.dot_general(
             jnp.concatenate(plain, axis=1),
             jnp.concatenate(scaled, axis=1),
@@ -306,34 +305,40 @@
             preferred_element_type=jnp.float32,
         )
 
-    if len(refs) == 2:
-        g_ref[...] = total[...]
-        return
-    half = per // 2
-
-    def picked(rows, c):
-        return jnp.concatenate(
-            [rows[d * per + c * half : d * per + (c + 1) * half] for d in range(shares)], axis=0
-        )
-
-    grams = total[...]
-    parts = [[picked(picked(grams, c).T, d) for d in range(2)] for c in range(2)]
-    g_ref[0] = (parts[0][0] + parts[1][1]).T * scale
-    g_ref[1] = (parts[0][1] - parts[1][0]).T * scale
+    size = total.shape[0]
+    half = size // 2
+    to = lax.broadcasted_iota(jnp.int32, (size, size), 0)
+    at = lax.broadcasted_iota(jnp.int32, (size, size), 1)
+    order = at % per // bands * half + at // per * bands + at % bands
+    chosen = (to == order).astype(jnp.float32)
+    grams = jnp.dot(
+        chosen, total[...], precision=lax.Precision.HIGHEST, preferred_element_type=jnp.float32
+    )
+    grams = lax.dot_general(
+        grams,
+        chosen,
+        (((1,), (1,)), ((), ())),
+        precision=lax.Precision.HIGHEST,
+        preferred_element_type=jnp.float32,
+    )
+    real = (grams[:half, :half] + grams[half:, half:]) * scale
+    imaginary = (grams[:half, half:] - grams[half:, :half]) * scale
+    if len(refs) == 3:
+        real, imaginary = real + refs[0][0], imaginary + refs[0][1]
+    o_ref[0] = real
+    o_ref[1] = imaginary
 
 
 def overlap(pieces, weights, per, scale, before=None):
-    shares = pieces.shape[0]
-    size = shares * per
+    shares, parts, _, _ = pieces.shape
+    size = shares * parts * per
     whole = pl.BlockSpec(memory_space=pltpu.VMEM)
-    last = before is not None
-    shape = (2, size // 2, size // 2) if last else (size, size)
-    operands = [pieces, weights] + ([before] if last else [])
+    operands = [pieces, weights] + ([] if before is None else [before])
     return pl.pallas_call(
         functools.partial(overlap_body, scale, per),
         in_specs=[whole] * len(operands),
         out_specs=whole,
-        out_shape=jax.ShapeDtypeStruct(shape, jnp.float32),
+        out_shape=jax.ShapeDtypeStruct((2, size // 2, size // 2), jnp.float32),
         scratch_shapes=[pltpu.VMEM((size, size), jnp.float32)],
         compiler_params=pltpu.CompilerParams(vmem_limit_bytes=56 << 20),
         cost_estimate=lasting(8.0),
@@ -476,22 +481,25 @@
         [jnp.concatenate([cosine, -sine], axis=1), jnp.concatenate([sine, cosine], axis=1)], axis=0
     )
     in_space = [forward(arrived[0], place, forth, back)]
+    shares = band_groups * halves
+    mixed = mix_space(in_space[0], 0, None, shares)
     result = inverse(arrived[0], 0, half, place, in_space[0], potential, forth, back)
-    arrived[1], met_waves, result = lax.optimization_barrier((arrived[1], met_waves, result))
+    arrived[1], met_waves, result, mixed = lax.optimization_barrier(
+        (arrived[1], met_waves, result, mixed)
+    )
 
     returned = [shifted(result)]
     in_space.append(forward(arrived[1], place, forth, back))
-    mixed = mix_space(in_space, band_groups * halves)
-    middle = ga_count // 2
-    mixed, returned[0][middle] = lax.optimization_barrier((mixed, returned[0][middle]))
-    mixed = mixed.reshape(band_groups, halves, -1, NY)
+    mixed = mix_space(in_space[1], 1, mixed, shares)
+    mixed, returned[0][1] = lax.optimization_barrier((mixed, returned[0][1]))
     if halves > 1:
+        mixed = mixed.reshape(band_groups, halves, -1, NY)
         mixed = lax.all_to_all(mixed, "ga", 1, 1, axis_index_groups=pairs, tiled=True)
     met_space = lax.all_to_all(mixed, "band", 0, 0, tiled=True)
     if halves > 1:
-        met_space = met_space.reshape(band_groups, halves, -1, 2, own_bands, NY)
-        met_space = met_space.transpose(0, 2, 3, 1, 4, 5)
-    met_space = met_space.reshape(band_groups, -1, NY)
+        met_space = met_space.reshape(band_groups, halves, 2, -1, 2, half, NY)
+        met_space = met_space.transpose(0, 3, 4, 1, 2, 5, 6)
+        met_space = met_space.reshape(band_groups, 1, -1, NY)
     space_weights = own_potential
     if halves > 1:
         space_weights = lax.dynamic_slice_in_dim(
@@ -509,12 +517,18 @@
     kinetic = jnp.broadcast_to(kinetic[None], (planes, share, NY)).reshape(planes * share, NY)
 
     scale = 1.0 / (planes * NX * NY)
-    grams = overlap(met_waves, kinetic, per, scale)
+    applied_waves = unpack(returned[0], place, None, 0, bands, planes)
+    grams = overlap(met_waves[:, None], kinetic, per, scale)
     spectrum = (in_space[1], potential, forth, back)
-    returned.append(shifted(inverse(arrived[1], 0, half - 1, place, *spectrum)))
-    grams, place = lax.optimization_barrier((grams, place))
-    returned.append(shifted(inverse(arrived[1], half - 1, 1, place, *spectrum)))
-    full_matrix = overlap(met_space, space_weights, per, scale, grams)
+    firsts = list(range(0, half, STEP))
+    for first in firsts:
+        if first == firsts[-1]:
+            grams, place = lax.optimization_barrier((grams, place))
+        returned.append(shifted(inverse(arrived[1], first, STEP, place, *spectrum)))
+    grams, applied_waves = lax.optimization_barrier((grams, applied_waves))
+    full_matrix = overlap(
+        met_space, space_weights, per // met_space.shape[1], scale, grams
+    )
     all_bands = bands * band_groups
     col_width = all_bands // ga_count
     blocks = full_matrix.reshape(2, band_groups, bands, ga_count, col_width)
@@ -523,11 +537,10 @@
     )
     subspace = lax.all_to_all(blocks, ("band", "ga"), 0, 0, tiled=True).sum(0)
 
-    applied_waves = None
-    for j, first in enumerate((0, half, own_bands - 1)):
-        if j == 2:
+    for j, first in enumerate(firsts):
+        if first == firsts[-1]:
             place, subspace = lax.optimization_barrier((place, subspace))
-        applied_waves = unpack(returned[j], place, applied_waves, first, bands, planes)
+        applied_waves = unpack(returned[j + 1], place, applied_waves, half + first, bands, planes)
     return (applied_waves, subspace)
 
 

time: 252 us -> 263 us (1.044)
  starting transfers between devices: 69 us -> 92.2 us
  waiting for transfers between devices: 47 us -> 35.3 us
    all_to_all x1, starting transfers between devices: 3.67 us -> 26.3 us  [shards(): potential = lax.all_to_all(copies, 'band', 0, 0, tiled=True).reshape(NX, NY)]
    ppermute x15, waiting for transfers between devices: 33.9 us -> 14.9 us  [shifted(): lax.ppermute(message, 'ga', [(i, (i + s) % groups) for i in range(groups)])]
    all_to_all x1, waiting for transfers between devices: 1.03 us -> 12.2 us  [shards(): met_waves = lax.all_to_all(mixed, 'band', 0, 0, tiled=True)]
    all_to_all x1, waiting for transfers between devices: 10.6 us -> 0.01 us  [shards(): met_space = lax.all_to_all(mixed, 'band', 0, 0, tiled=True)]
    all_to_all x1, waiting for transfers between devices: 1.47 us -> 8.25 us  [shards(): subspace = lax.all_to_all(blocks, ('band', 'ga'), 0, 0, tiled=True).sum(0)]
    pallas_call x3, Pallas kernels: 13.9 us -> 10 us  [unpack(): pl.pallas_call(functools.partial(unpack_body, groups), grid=(2, halves, c...]
    pallas_call x6 -> x7, Pallas kernels: 48.1 us -> 50.7 us  [the longest x3 21.7 us: inverse(): pl.pallas_call(functools.partial(inverse_body, groups), grid=(bands // ST...]
  transfers between devices with their start and end apart: 20 -> 20, of which waited for: 7 -> 4; matrix products, arithmetic and copies ran while one was open for 6% -> 6% of each run, Pallas kernels for 44% -> 41%
where the time goes in v2:
time: 263 us; the launch traced here: 261 us
  Pallas kernels  111 us (42%)
  starting transfers between devices  92.2 us (35%)
  waiting for transfers between devices  35.3 us (13%)
  local copies, waits for them, and re-layouts  11.6 us (4%)
  other arithmetic  9.85 us (4%)
    ppermute x15, starting transfers between devices, shifted(): lax.ppermute(message, 'ga', [(i, (i + s) % groups) for i in range(groups)])  46.2 us
    all_to_all x1, starting transfers between devices, shards(): potential = lax.all_to_all(copies, 'band', 0, 0, tiled=True).reshape(NX, NY)  26.3 us
    pallas_call x3, Pallas kernels, inverse(): pl.pallas_call(functools.partial(inverse_body, groups), grid=(bands // ST...  21.7 us
    pallas_call x2, Pallas kernels, overlap(): pl.pallas_call(functools.partial(overlap_body, scale, per), in_specs=[who...  17.9 us
    pallas_call x2, Pallas kernels, forward(): pl.pallas_call(functools.partial(forward_body, groups), grid=(bands // ST...  16.3 us
    ppermute x15, waiting for transfers between devices, shifted(): lax.ppermute(message, 'ga', [(i, (i + s) % groups) for i in range(groups)])  14.9 us
    pallas_call x1, Pallas kernels, own_share(): pl.pallas_call(functools.partial(charges_body, planes, slab_rows), in_spe...  13.6 us
    pallas_call x2, Pallas kernels, mix_space(): pl.pallas_call(mix_space_body, grid=(shares // group,), in_specs=in_specs...  12.7 us
  transfers between devices with their start and end apart: 20, of which 4 were waited for; matrix products, arithmetic and copies ran while one was open for 6% of the time, Pallas kernels for 41%

profile of v2, /device:TPU:0, one launch (start us, length us, event | category | flops | bytes accessed | tf_op | source)
XLA Modules:
  0.0 261.2 jit_solution(13879853925833698007)
XLA Ops:
  3.4 7.3 %all-to-all-start = ((f32[32,8,256]{2,1,0:T(8,128)}), f32[32,8,256]{2,1,0:T(8,128)S(1)}, u32[]{:S(2)}, u32[]{:S(2)}) async-start(f32[32,8,256]{2,1,0:T(8,128)} %pad_maximum_fusion.4), calls=%async_computation | async-start | bytes 524288 | tf_op jit(solution)/shard_map/all_to_all | solution.py:464
  10.7 4.4 %pack_planes.2 = (bf16[2,4,96,384]{3,2,1,0:T(8,128)(2,1)}, bf16[2,4,96,384]{3,2,1,0:T(8,128)(2,1)}, bf16[2,4,96,384]{3,2,1,0:T(8,128)(2,1)}, bf16[2,4,96,384]{3,2,1,0:T(8,128)(2,1)}) custom-call(s32[1]{0:T(128)} %bitcast.place, bf16[2,8,4,36864]{3,2,1,0:T(4,128)(2,1)} %w_ref.1), custom_call_target="tpu_custom_call" | custom-call | bytes 36900 | tf_op jit(solution)/shard_map/pack_planes/pallas_call | solution.py:65
  22.4 13.6 %charge_potential.1.w_ref = f32[48,384]{1,0:T(8,128)} custom-call(s32[2]{0:T(128)} %pad_add_fusion.place, f32[32,8,256]{2,1,0:T(8,128)} %copy-done.7, f32[48,384]{1,0:T(8,128)} %reshape.105.i_ref), custom_call_target="tpu_custom_call" | custom-call | bytes 36900 | tf_op jit(solution)/shard_map/charge_potential/pallas_call | solution.py:428
  37.8 26.3 %all-to-all-start.1 = ((f32[8,48,384]{2,1,0:T(8,128)}), f32[8,48,384]{2,1,0:T(8,128)S(1)}, u32[]{:S(2)}, u32[]{:S(2)}) async-start(f32[8,48,384]{2,1,0:T(8,128)} %broadcast_in_dim.15), calls=%async_computation.1 | async-start | bytes 1179648 | tf_op jit(solution)/shard_map/all_to_all | solution.py:467
  64.1 4.4 %pack_planes.3 = (bf16[2,4,96,384]{3,2,1,0:T(8,128)(2,1)}, bf16[2,4,96,384]{3,2,1,0:T(8,128)(2,1)}, bf16[2,4,96,384]{3,2,1,0:T(8,128)(2,1)}, bf16[2,4,96,384]{3,2,1,0:T(8,128)(2,1)}) custom-call(s32[1]{0:T(128)} %bitcast.place, bf16[2,8,4,36864]{3,2,1,0:T(4,128)(2,1)} %w_ref.1), custom_call_target="tpu_custom_call" | custom-call | bytes 36900 | tf_op jit(solution)/shard_map/pack_planes/pallas_call | solution.py:65
  68.5 10.0 %mix_waves.1 = bf16[8,768,384]{2,1,0:T(8,128)(2,1)} custom-call(bf16[2,8,4,36864]{3,2,1,0:T(4,128)(2,1)} %w_ref.1), custom_call_target="tpu_custom_call" | custom-call | bytes 36900 | tf_op jit(solution)/shard_map/mix_waves/pallas_call | solution.py:108
  80.0 4.6 %all-to-all-start.2 = ((bf16[8,768,384]{2,1,0:T(8,128)(2,1)}), bf16[8,768,384]{2,1,0:T(8,128)(2,1)}, u32[]{:S(2)}, u32[]{:S(2)}) async-start(bf16[8,768,384]{2,1,0:T(8,128)(2,1)} %mix_waves.1), calls=%async_computation.2 | async-start | bytes 9437184 | tf_op jit(solution)/shard_map/all_to_all | solution.py:475
  84.9 3.8 %collective-permute-start.5 = (bf16[2,4,96,384]{3,2,1,0:T(8,128)(2,1)S(1)}, bf16[2,4,96,384]{3,2,1,0:T(8,128)(2,1)S(1)}, u32[]{:S(2)}, u32[]{:S(2)}) collective-permute-start(bf16[2,4,96,384]{3,2,1,0:T(8,128)(2,1)S(1)} %copy-done.21), channel_id=1, source_target_pairs={{0,3},{1,0},{2,1},{3,2},{4,7},{5,4},{6,5},{7,6},{8,11},{9,8},{10,9... | collective-permute-start | bytes 1769480 | tf_op jit(solution)/shard_map/ppermute | solution.py:352
  88.6 2.6 fusion.7
  91.2 2.9 %multiply_convert_fusion = (bf16[384,384]{1,0:T(8,128)(2,1)S(1)}, bf16[384,384]{1,0:T(8,128)(2,1)S(1)}) fusion(s32[384]{0:T(512)S(1)} %iota.13), kind=kLoop, calls=%fused_computation.9 | loop fusion | flops 1916928 | bytes 591360 | tf_op jit(solution)/shard_map/convert_element_type | solution.py:25
  95.6 8.1 %forward.2.refs_4_.s_ref = bf16[4,2,384,384]{3,2,1,0:T(8,128)(2,1)} custom-call(s32[1]{0:T(128)} %bitcast.place, bf16[2,4,96,384]{3,2,1,0:T(8,128)(2,1)} %get-tuple-element.64.refs_0_, bf16[2,4,96,384]{3,2,1,0:T(8,128)(2,1)} %copy-done.4, bf16[2,4,96,384]{3,2,1,0:T(8,128)(2,1)} %copy-done.5, bf16[2,4,96,384]{3,2,1,0:T(8,128)(2,1)} %copy-done.6, ...), custom_call_target="tpu_custom_call" | custom-call | bytes 36900 | tf_op jit(solution)/shard_map/forward/pallas_call | solution.py:221
  103.7 6.4 %mix_space.2.refs_0_ = bf16[8,2,384,384]{3,2,1,0:T(8,128)(2,1)} custom-call(bf16[4,2,384,384]{3,2,1,0:T(8,128)(2,1)} %forward.2.refs_4_.s_ref), custom_call_target="tpu_custom_call" | custom-call | bytes 36900 | tf_op jit(solution)/shard_map/mix_space/pallas_call | solution.py:149
  110.1 9.1 %inverse.3 = (bf16[2,4,96,384]{3,2,1,0:T(8,128)(2,1)}, bf16[2,4,96,384]{3,2,1,0:T(8,128)(2,1)}, bf16[2,4,96,384]{3,2,1,0:T(8,128)(2,1)}, bf16[2,4,96,384]{3,2,1,0:T(8,128)(2,1)}) custom-call(s32[1]{0:T(128)} %bitcast.place, bf16[2,4,96,384]{3,2,1,0:T(8,128)(2,1)} %get-tuple-element.64.refs_0_, bf16[2,4,96,384]{3,2,1,0:T(8,128)(2,1)} %copy-done.4, ...), custom_call_target="tpu_custom_call" | custom-call | bytes 36900 | tf_op jit(solution)/shard_map/inverse/pallas_call | solution.py:265
  119.2 8.1 %collective-permute-done.4.refs_2_ = bf16[2,4,96,384]{3,2,1,0:T(8,128)(2,1)S(1)} collective-permute-done((bf16[2,4,96,384]{3,2,1,0:T(8,128)(2,1)S(1)}, bf16[2,4,96,384]{3,2,1,0:T(8,128)(2,1)S(1)}, u32[]{:S(2)}, u32[]{:S(2)}) %collective-permute-start.4) | collective-permute-done | bytes 589856 | tf_op jit(solution)/shard_map/ppermute | solution.py:352
  127.3 12.2 %all-to-all-done.2 = bf16[8,768,384]{2,1,0:T(8,128)(2,1)} async-done(((bf16[8,768,384]{2,1,0:T(8,128)(2,1)}), bf16[8,768,384]{2,1,0:T(8,128)(2,1)}, u32[]{:S(2)}, u32[]{:S(2)}) %all-to-all-start.2) | async-done | bytes 4718624 | tf_op jit(solution)/shard_map/all_to_all | solution.py:475
  140.5 8.1 %forward.3.s_ref.refs_4_ = bf16[4,2,384,384]{3,2,1,0:T(8,128)(2,1)} custom-call(s32[1]{0:T(128)} %bitcast.place, bf16[2,4,96,384]{3,2,1,0:T(8,128)(2,1)} %get-tuple-element.76.refs_0_, bf16[2,4,96,384]{3,2,1,0:T(8,128)(2,1)} %copy-done.1, bf16[2,4,96,384]{3,2,1,0:T(8,128)(2,1)} %copy-done.2, bf16[2,4,96,384]{3,2,1,0:T(8,128)(2,1)} %copy-done.3, ...), custom_call_target="tpu_custom_call" | custom-call | bytes 36900 | tf_op jit(solution)/shard_map/forward/pallas_call | solution.py:221
  148.6 6.4 %mix_space.3 = bf16[8,2,384,384]{3,2,1,0:T(8,128)(2,1)} custom-call(bf16[4,2,384,384]{3,2,1,0:T(8,128)(2,1)} %forward.3.s_ref.refs_4_, bf16[8,2,384,384]{3,2,1,0:T(8,128)(2,1)} %mix_space.2.refs_0_), custom_call_target="tpu_custom_call", output_to_operand_aliasing={{}: (1, {})} | custom-call | bytes 36900 | tf_op jit(solution)/shard_map/mix_space/pallas_call | solution.py:149
  155.8 4.6 %all-to-all-start.3 = ((bf16[8,2,384,384]{3,2,1,0:T(8,128)(2,1)}), bf16[8,2,384,384]{3,2,1,0:T(8,128)(2,1)}, u32[]{:S(2)}, u32[]{:S(2)}) async-start(bf16[8,2,384,384]{3,2,1,0:T(8,128)(2,1)} %mix_space.3), calls=%async_computation.3 | async-start | bytes 9437184 | tf_op jit(solution)/shard_map/all_to_all | solution.py:498
  161.2 2.6 %collective-permute-start.8 = (bf16[2,4,96,384]{3,2,1,0:T(8,128)(2,1)S(1)}, bf16[2,4,96,384]{3,2,1,0:T(8,128)(2,1)S(1)}, u32[]{:S(2)}, u32[]{:S(2)}) collective-permute-start(bf16[2,4,96,384]{3,2,1,0:T(8,128)(2,1)S(1)} %copy-done.20), channel_id=1, source_target_pairs={{0,3},{1,0},{2,1},{3,2},{4,7},{5,4},{6,5},{7,6},{8,11},{9,8},{10,9... | collective-permute-start | bytes 1769480 | tf_op jit(solution)/shard_map/ppermute | solution.py:352
  163.9 6.3 %inverse.5 = (bf16[2,2,96,384]{3,2,1,0:T(8,128)(2,1)}, bf16[2,2,96,384]{3,2,1,0:T(8,128)(2,1)}, bf16[2,2,96,384]{3,2,1,0:T(8,128)(2,1)}, bf16[2,2,96,384]{3,2,1,0:T(8,128)(2,1)}) custom-call(s32[1]{0:T(128)} %bitcast.place, bf16[2,4,96,384]{3,2,1,0:T(8,128)(2,1)} %get-tuple-element.76.refs_0_, bf16[2,4,96,384]{3,2,1,0:T(8,128)(2,1)} %copy-done.1, ...), custom_call_target="tpu_custom_call" | custom-call | bytes 36900 | tf_op jit(solution)/shard_map/inverse/pallas_call | solution.py:265
  172.5 2.8 %collective-permute-start.14 = (bf16[2,2,96,384]{3,2,1,0:T(8,128)(2,1)}, bf16[2,2,96,384]{3,2,1,0:T(8,128)(2,1)S(1)}, u32[]{:S(2)}, u32[]{:S(2)}) collective-permute-start(bf16[2,2,96,384]{3,2,1,0:T(8,128)(2,1)} %get-tuple-element.97), channel_id=1, source_target_pairs={{0,3},{1,0},{2,1},{3,2},{4,7},{5,4},{6,5},{7,6},{8,11},{9,8},{10,9... | collective-permute-start | bytes 884744 | tf_op jit(solution)/shard_map/ppermute | solution.py:352
  175.3 8.9 %overlap.2.refs_0_ = f32[2,64,64]{2,1,0:T(8,128)} custom-call(bf16[8,1,768,384]{3,2,1,0:T(8,128)(2,1)} %bitcast.9.z_ref, f32[48,384]{1,0:T(8,128)} %reshape.107.w_ref), custom_call_target="tpu_custom_call" | custom-call | bytes 29520000 | tf_op jit(solution)/shard_map/overlap/pallas_call | solution.py:337
  184.2 6.3 %inverse.4 = (bf16[2,2,96,384]{3,2,1,0:T(8,128)(2,1)}, bf16[2,2,96,384]{3,2,1,0:T(8,128)(2,1)}, bf16[2,2,96,384]{3,2,1,0:T(8,128)(2,1)}, bf16[2,2,96,384]{3,2,1,0:T(8,128)(2,1)}) custom-call(s32[1]{0:T(128)} %bitcast.place, bf16[2,4,96,384]{3,2,1,0:T(8,128)(2,1)} %get-tuple-element.76.refs_0_, bf16[2,4,96,384]{3,2,1,0:T(8,128)(2,1)} %copy-done.1, ...), custom_call_target="tpu_custom_call" | custom-call | bytes 36900 | tf_op jit(solution)/shard_map/inverse/pallas_call | solution.py:265
  190.5 6.8 %collective-permute-done.12.refs_1_ = bf16[2,2,96,384]{3,2,1,0:T(8,128)(2,1)S(1)} collective-permute-done((bf16[2,2,96,384]{3,2,1,0:T(8,128)(2,1)}, bf16[2,2,96,384]{3,2,1,0:T(8,128)(2,1)S(1)}, u32[]{:S(2)}, u32[]{:S(2)}) %collective-permute-start.12) | collective-permute-done | bytes 294944 | tf_op jit(solution)/shard_map/ppermute | solution.py:352
  197.3 23.1 %collective-permute-start.9 = (bf16[2,2,96,384]{3,2,1,0:T(8,128)(2,1)}, bf16[2,2,96,384]{3,2,1,0:T(8,128)(2,1)S(1)}, u32[]{:S(2)}, u32[]{:S(2)}) collective-permute-start(bf16[2,2,96,384]{3,2,1,0:T(8,128)(2,1)} %get-tuple-element.91), channel_id=1, source_target_pairs={{0,1},{1,2},{2,3},{3,0},{4,5},{5,6},{6,7},{7,4},{8,9},{9,10},{10,1... | collective-permute-start | bytes 884744 | tf_op jit(solution)/shard_map/ppermute | solution.py:352
  222.3 2.8 %collective-permute-start.11 = (bf16[2,2,96,384]{3,2,1,0:T(8,128)(2,1)}, bf16[2,2,96,384]{3,2,1,0:T(8,128)(2,1)S(1)}, u32[]{:S(2)}, u32[]{:S(2)}) collective-permute-start(bf16[2,2,96,384]{3,2,1,0:T(8,128)(2,1)} %get-tuple-element.93), channel_id=1, source_target_pairs={{0,3},{1,0},{2,1},{3,2},{4,7},{5,4},{6,5},{7,6},{8,11},{9,8},{10,9... | collective-permute-start | bytes 884744 | tf_op jit(solution)/shard_map/ppermute | solution.py:352
  225.2 4.6 %unpack_planes.3.refs_4_ = bf16[2,8,4,36864]{3,2,1,0:T(4,128)(2,1)} custom-call(s32[1]{0:T(128)} %bitcast.place, bf16[2,4,96,384]{3,2,1,0:T(8,128)(2,1)} %get-tuple-element.84.refs_0_, bf16[2,4,96,384]{3,2,1,0:T(8,128)(2,1)} %copy-done.8, bf16[2,4,96,384]{3,2,1,0:T(8,128)(2,1)} %copy-done.9, bf16[2,4,96,384]{3,2,1,0:T(8,128)(2,1)} %copy-done.10), custom_call_target="tpu_custom_call" | custom-call | bytes 17712000 | tf_op jit(solution)/shard_map/unpack_planes/pallas_call | solution.py:188
  229.8 9.0 %overlap.3 = f32[2,64,64]{2,1,0:T(8,128)} custom-call(bf16[8,2,384,384]{3,2,1,0:T(8,128)(2,1)} %all-to-all-done.3.z_ref, f32[48,384]{1,0:T(8,128)} %charge_potential.1.w_ref, f32[2,64,64]{2,1,0:T(8,128)} %overlap.2.refs_0_), custom_call_target="tpu_custom_call" | custom-call | bytes 29520000 | tf_op jit(solution)/shard_map/overlap/pallas_call | solution.py:337
  240.6 3.2 %all-to-all-start.4 = ((f32[32,1,256]{2,1,0:T(1,128)}), f32[32,1,256]{2,1,0:T(1,128)S(1)}, u32[]{:S(2)}, u32[]{:S(2)}) async-start(f32[32,1,256]{2,1,0:T(1,128)} %reshape.110), calls=%async_computation.4 | async-start | bytes 65536 | tf_op jit(solution)/shard_map/all_to_all | solution.py:538
  244.6 2.7 %unpack_planes.4.refs_4_ = bf16[2,8,4,36864]{3,2,1,0:T(4,128)(2,1)} custom-call(s32[1]{0:T(128)} %bitcast.place, bf16[2,2,96,384]{3,2,1,0:T(8,128)(2,1)} %get-tuple-element.94.refs_0_, bf16[2,2,96,384]{3,2,1,0:T(8,128)(2,1)} %copy-done.11, bf16[2,2,96,384]{3,2,1,0:T(8,128)(2,1)} %copy-done.13, ...), custom_call_target="tpu_custom_call", output_to_operand_aliasing={{}: (5, {})} | custom-call | bytes 8856000 | tf_op jit(solution)/shard_map/unpack_planes/pallas_call | solution.py:188
  247.3 8.2 %all-to-all-done.4 = f32[32,1,256]{2,1,0:T(1,128)S(1)} async-done(((f32[32,1,256]{2,1,0:T(1,128)}), f32[32,1,256]{2,1,0:T(1,128)S(1)}, u32[]{:S(2)}, u32[]{:S(2)}) %all-to-all-start.4) | async-done | bytes 32800 | tf_op jit(solution)/shard_map/all_to_all | solution.py:538
  258.5 2.7 %unpack_planes.5 = bf16[2,8,4,36864]{3,2,1,0:T(4,128)(2,1)} custom-call(s32[1]{0:T(128)} %bitcast.place, bf16[2,2,96,384]{3,2,1,0:T(8,128)(2,1)} %get-tuple-element.90.refs_0_, bf16[2,2,96,384]{3,2,1,0:T(8,128)(2,1)} %copy-done.12, bf16[2,2,96,384]{3,2,1,0:T(8,128)(2,1)} %copy-done.14, ...), custom_call_target="tpu_custom_call", output_to_operand_aliasing={{}: (5, {})} | custom-call | bytes 8856000 | tf_op jit(solution)/shard_map/unpack_planes/pallas_call | solution.py:188
  (107 shorter events, 27.1 us)
Async XLA Ops:
  0.6 1.9 copy-start.19
  0.6 1.9 copy-start.18
  0.7 1.9 copy-start.17
  3.4 18.0 %all-to-all-start = ((f32[32,8,256]{2,1,0:T(8,128)}), f32[32,8,256]{2,1,0:T(8,128)S(1)}, u32[]{:S(2)}, u32[]{:S(2)}) async-start(f32[32,8,256]{2,1,0:T(8,128)} %pad_maximum_fusion.4), calls=%async_computation | async-start | bytes 524288 | tf_op jit(solution)/shard_map/all_to_all | solution.py:464
  15.1 63.5 %collective-permute-start = (bf16[2,4,96,384]{3,2,1,0:T(8,128)(2,1)}, bf16[2,4,96,384]{3,2,1,0:T(8,128)(2,1)S(1)}, u32[]{:S(2)}, u32[]{:S(2)}) collective-permute-start(bf16[2,4,96,384]{3,2,1,0:T(8,128)(2,1)} %get-tuple-element.52), channel_id=1, source_target_pairs={{0,1},{1,2},{2,3},{3,0},{4,5},{5,6},{6,7},{7,4},{8,9},{9,10},{10,1... | collective-permute-start | bytes 1769480 | tf_op jit(solution)/shard_map/ppermute | solution.py:352
  16.9 61.7 %collective-permute-start.1 = (bf16[2,4,96,384]{3,2,1,0:T(8,128)(2,1)}, bf16[2,4,96,384]{3,2,1,0:T(8,128)(2,1)S(1)}, u32[]{:S(2)}, u32[]{:S(2)}) collective-permute-start(bf16[2,4,96,384]{3,2,1,0:T(8,128)(2,1)} %get-tuple-element.53), channel_id=1, source_target_pairs={{0,2},{1,3},{2,0},{3,1},{4,6},{5,7},{6,4},{7,5},{8,10},{9,11},{10,... | collective-permute-start | bytes 1769480 | tf_op jit(solution)/shard_map/ppermute | solution.py:352
  19.3 59.3 %collective-permute-start.2 = (bf16[2,4,96,384]{3,2,1,0:T(8,128)(2,1)}, bf16[2,4,96,384]{3,2,1,0:T(8,128)(2,1)S(1)}, u32[]{:S(2)}, u32[]{:S(2)}) collective-permute-start(bf16[2,4,96,384]{3,2,1,0:T(8,128)(2,1)} %get-tuple-element.54), channel_id=1, source_target_pairs={{0,3},{1,0},{2,1},{3,2},{4,7},{5,4},{6,5},{7,6},{8,11},{9,8},{10,9... | collective-permute-start | bytes 1769480 | tf_op jit(solution)/shard_map/ppermute | solution.py:352
  37.8 40.8 %all-to-all-start.1 = ((f32[8,48,384]{2,1,0:T(8,128)}), f32[8,48,384]{2,1,0:T(8,128)S(1)}, u32[]{:S(2)}, u32[]{:S(2)}) async-start(f32[8,48,384]{2,1,0:T(8,128)} %broadcast_in_dim.15), calls=%async_computation.1 | async-start | bytes 1179648 | tf_op jit(solution)/shard_map/all_to_all | solution.py:467
  78.6 6.1 %copy-start.22 = (bf16[2,4,96,384]{3,2,1,0:T(8,128)(2,1)S(1)}, bf16[2,4,96,384]{3,2,1,0:T(8,128)(2,1)}, u32[]{:S(2)}) copy-start(bf16[2,4,96,384]{3,2,1,0:T(8,128)(2,1)} %get-tuple-element.61) | copy-start | bytes 1769476
  78.6 6.2 %copy-start.21 = (bf16[2,4,96,384]{3,2,1,0:T(8,128)(2,1)S(1)}, bf16[2,4,96,384]{3,2,1,0:T(8,128)(2,1)}, u32[]{:S(2)}) copy-start(bf16[2,4,96,384]{3,2,1,0:T(8,128)(2,1)} %get-tuple-element.62) | copy-start | bytes 1769476
  80.0 59.4 %all-to-all-start.2 = ((bf16[8,768,384]{2,1,0:T(8,128)(2,1)}), bf16[8,768,384]{2,1,0:T(8,128)(2,1)}, u32[]{:S(2)}, u32[]{:S(2)}) async-start(bf16[8,768,384]{2,1,0:T(8,128)(2,1)} %mix_waves.1), calls=%async_computation.2 | async-start | bytes 9437184 | tf_op jit(solution)/shard_map/all_to_all | solution.py:475
  84.7 34.5 %collective-permute-start.3 = (bf16[2,4,96,384]{3,2,1,0:T(8,128)(2,1)}, bf16[2,4,96,384]{3,2,1,0:T(8,128)(2,1)S(1)}, u32[]{:S(2)}, u32[]{:S(2)}) collective-permute-start(bf16[2,4,96,384]{3,2,1,0:T(8,128)(2,1)} %get-tuple-element.60), channel_id=1, source_target_pairs={{0,1},{1,2},{2,3},{3,0},{4,5},{5,6},{6,7},{7,4},{8,9},{9,10},{10,1... | collective-permute-start | bytes 1769480 | tf_op jit(solution)/shard_map/ppermute | solution.py:352
  84.8 42.5 %collective-permute-start.4 = (bf16[2,4,96,384]{3,2,1,0:T(8,128)(2,1)S(1)}, bf16[2,4,96,384]{3,2,1,0:T(8,128)(2,1)S(1)}, u32[]{:S(2)}, u32[]{:S(2)}) collective-permute-start(bf16[2,4,96,384]{3,2,1,0:T(8,128)(2,1)S(1)} %copy-done.22), channel_id=1, source_target_pairs={{0,2},{1,3},{2,0},{3,1},{4,6},{5,7},{6,4},{7,5},{8,10},{9,11},{10,... | collective-permute-start | bytes 1769480 | tf_op jit(solution)/shard_map/ppermute | solution.py:352
  84.9 42.4 %collective-permute-start.5 = (bf16[2,4,96,384]{3,2,1,0:T(8,128)(2,1)S(1)}, bf16[2,4,96,384]{3,2,1,0:T(8,128)(2,1)S(1)}, u32[]{:S(2)}, u32[]{:S(2)}) collective-permute-start(bf16[2,4,96,384]{3,2,1,0:T(8,128)(2,1)S(1)} %copy-done.21), channel_id=1, source_target_pairs={{0,3},{1,0},{2,1},{3,2},{4,7},{5,4},{6,5},{7,6},{8,11},{9,8},{10,9... | collective-permute-start | bytes 1769480 | tf_op jit(solution)/shard_map/ppermute | solution.py:352
  119.2 21.3 %copy-start.1 = (bf16[2,4,96,384]{3,2,1,0:T(8,128)(2,1)}, bf16[2,4,96,384]{3,2,1,0:T(8,128)(2,1)S(1)}, u32[]{:S(2)}) copy-start(bf16[2,4,96,384]{3,2,1,0:T(8,128)(2,1)S(1)} %collective-permute-done.3.refs_1_) | copy-start | bytes 1769476
  127.2 13.2 %copy-start.2 = (bf16[2,4,96,384]{3,2,1,0:T(8,128)(2,1)}, bf16[2,4,96,384]{3,2,1,0:T(8,128)(2,1)S(1)}, u32[]{:S(2)}) copy-start(bf16[2,4,96,384]{3,2,1,0:T(8,128)(2,1)S(1)} %collective-permute-done.4.refs_2_) | copy-start | bytes 1769476
  127.3 13.2 %copy-start.3 = (bf16[2,4,96,384]{3,2,1,0:T(8,128)(2,1)}, bf16[2,4,96,384]{3,2,1,0:T(8,128)(2,1)S(1)}, u32[]{:S(2)}) copy-start(bf16[2,4,96,384]{3,2,1,0:T(8,128)(2,1)S(1)} %collective-permute-done.5.refs_3_) | copy-start | bytes 1769476
  139.4 15.5 %collective-permute-start.6 = (bf16[2,4,96,384]{3,2,1,0:T(8,128)(2,1)}, bf16[2,4,96,384]{3,2,1,0:T(8,128)(2,1)S(1)}, u32[]{:S(2)}, u32[]{:S(2)}) collective-permute-start(bf16[2,4,96,384]{3,2,1,0:T(8,128)(2,1)} %get-tuple-element.81), channel_id=1, source_target_pairs={{0,1},{1,2},{2,3},{3,0},{4,5},{5,6},{6,7},{7,4},{8,9},{9,10},{10,1... | collective-permute-start | bytes 1769480 | tf_op jit(solution)/shard_map/ppermute | solution.py:352
  155.0 6.3 %copy-start.20 = (bf16[2,4,96,384]{3,2,1,0:T(8,128)(2,1)S(1)}, bf16[2,4,96,384]{3,2,1,0:T(8,128)(2,1)}, u32[]{:S(2)}) copy-start(bf16[2,4,96,384]{3,2,1,0:T(8,128)(2,1)} %get-tuple-element.87) | copy-start | bytes 1769476
  155.8 74.0 %all-to-all-start.3 = ((bf16[8,2,384,384]{3,2,1,0:T(8,128)(2,1)}), bf16[8,2,384,384]{3,2,1,0:T(8,128)(2,1)}, u32[]{:S(2)}, u32[]{:S(2)}) async-start(bf16[8,2,384,384]{3,2,1,0:T(8,128)(2,1)} %mix_space.3), calls=%async_computation.3 | async-start | bytes 9437184 | tf_op jit(solution)/shard_map/all_to_all | solution.py:498
  160.4 60.0 %collective-permute-start.7 = (bf16[2,4,96,384]{3,2,1,0:T(8,128)(2,1)}, bf16[2,4,96,384]{3,2,1,0:T(8,128)(2,1)S(1)}, u32[]{:S(2)}, u32[]{:S(2)}) collective-permute-start(bf16[2,4,96,384]{3,2,1,0:T(8,128)(2,1)} %get-tuple-element.86), channel_id=1, source_target_pairs={{0,2},{1,3},{2,0},{3,1},{4,6},{5,7},{6,4},{7,5},{8,10},{9,11},{10,... | collective-permute-start | bytes 1769480 | tf_op jit(solution)/shard_map/ppermute | solution.py:352
  161.2 61.1 %collective-permute-start.8 = (bf16[2,4,96,384]{3,2,1,0:T(8,128)(2,1)S(1)}, bf16[2,4,96,384]{3,2,1,0:T(8,128)(2,1)S(1)}, u32[]{:S(2)}, u32[]{:S(2)}) collective-permute-start(bf16[2,4,96,384]{3,2,1,0:T(8,128)(2,1)S(1)} %copy-done.20), channel_id=1, source_target_pairs={{0,3},{1,0},{2,1},{3,2},{4,7},{5,4},{6,5},{7,6},{8,11},{9,8},{10,9... | collective-permute-start | bytes 1769480 | tf_op jit(solution)/shard_map/ppermute | solution.py:352
  170.2 27.1 %collective-permute-start.12 = (bf16[2,2,96,384]{3,2,1,0:T(8,128)(2,1)}, bf16[2,2,96,384]{3,2,1,0:T(8,128)(2,1)S(1)}, u32[]{:S(2)}, u32[]{:S(2)}) collective-permute-start(bf16[2,2,96,384]{3,2,1,0:T(8,128)(2,1)} %get-tuple-element.95), channel_id=1, source_target_pairs={{0,1},{1,2},{2,3},{3,0},{4,5},{5,6},{6,7},{7,4},{8,9},{9,10},{10,1... | collective-permute-start | bytes 884744 | tf_op jit(solution)/shard_map/ppermute | solution.py:352
  170.9 72.9 %collective-permute-start.13 = (bf16[2,2,96,384]{3,2,1,0:T(8,128)(2,1)}, bf16[2,2,96,384]{3,2,1,0:T(8,128)(2,1)S(1)}, u32[]{:S(2)}, u32[]{:S(2)}) collective-permute-start(bf16[2,2,96,384]{3,2,1,0:T(8,128)(2,1)} %get-tuple-element.96), channel_id=1, source_target_pairs={{0,2},{1,3},{2,0},{3,1},{4,6},{5,7},{6,4},{7,5},{8,10},{9,11},{10,... | collective-permute-start | bytes 884744 | tf_op jit(solution)/shard_map/ppermute | solution.py:352
  172.5 71.4 %collective-permute-start.14 = (bf16[2,2,96,384]{3,2,1,0:T(8,128)(2,1)}, bf16[2,2,96,384]{3,2,1,0:T(8,128)(2,1)S(1)}, u32[]{:S(2)}, u32[]{:S(2)}) collective-permute-start(bf16[2,2,96,384]{3,2,1,0:T(8,128)(2,1)} %get-tuple-element.97), channel_id=1, source_target_pairs={{0,3},{1,0},{2,1},{3,2},{4,7},{5,4},{6,5},{7,6},{8,11},{9,8},{10,9... | collective-permute-start | bytes 884744 | tf_op jit(solution)/shard_map/ppermute | solution.py:352
  197.3 46.5 %copy-start.11 = (bf16[2,2,96,384]{3,2,1,0:T(8,128)(2,1)}, bf16[2,2,96,384]{3,2,1,0:T(8,128)(2,1)S(1)}, u32[]{:S(2)}) copy-start(bf16[2,2,96,384]{3,2,1,0:T(8,128)(2,1)S(1)} %collective-permute-done.12.refs_1_) | copy-start | bytes 884740
  197.3 60.3 %collective-permute-start.9 = (bf16[2,2,96,384]{3,2,1,0:T(8,128)(2,1)}, bf16[2,2,96,384]{3,2,1,0:T(8,128)(2,1)S(1)}, u32[]{:S(2)}, u32[]{:S(2)}) collective-permute-start(bf16[2,2,96,384]{3,2,1,0:T(8,128)(2,1)} %get-tuple-element.91), channel_id=1, source_target_pairs={{0,1},{1,2},{2,3},{3,0},{4,5},{5,6},{6,7},{7,4},{8,9},{9,10},{10,1... | collective-permute-start | bytes 884744 | tf_op jit(solution)/shard_map/ppermute | solution.py:352
  220.4 4.7 %copy-start.9 = (bf16[2,4,96,384]{3,2,1,0:T(8,128)(2,1)}, bf16[2,4,96,384]{3,2,1,0:T(8,128)(2,1)S(1)}, u32[]{:S(2)}) copy-start(bf16[2,4,96,384]{3,2,1,0:T(8,128)(2,1)S(1)} %collective-permute-done.7.refs_2_) | copy-start | bytes 1769476
  220.4 37.2 %collective-permute-start.10 = (bf16[2,2,96,384]{3,2,1,0:T(8,128)(2,1)}, bf16[2,2,96,384]{3,2,1,0:T(8,128)(2,1)S(1)}, u32[]{:S(2)}, u32[]{:S(2)}) collective-permute-start(bf16[2,2,96,384]{3,2,1,0:T(8,128)(2,1)} %get-tuple-element.92), channel_id=1, source_target_pairs={{0,2},{1,3},{2,0},{3,1},{4,6},{5,7},{6,4},{7,5},{8,10},{9,11},{10,... | collective-permute-start | bytes 884744 | tf_op jit(solution)/shard_map/ppermute | solution.py:352
  222.3 2.9 %copy-start.10 = (bf16[2,4,96,384]{3,2,1,0:T(8,128)(2,1)}, bf16[2,4,96,384]{3,2,1,0:T(8,128)(2,1)S(1)}, u32[]{:S(2)}) copy-start(bf16[2,4,96,384]{3,2,1,0:T(8,128)(2,1)S(1)} %collective-permute-done.8.refs_3_) | copy-start | bytes 1769476
  222.3 35.3 %collective-permute-start.11 = (bf16[2,2,96,384]{3,2,1,0:T(8,128)(2,1)}, bf16[2,2,96,384]{3,2,1,0:T(8,128)(2,1)S(1)}, u32[]{:S(2)}, u32[]{:S(2)}) collective-permute-start(bf16[2,2,96,384]{3,2,1,0:T(8,128)(2,1)} %get-tuple-element.93), channel_id=1, source_target_pairs={{0,3},{1,0},{2,1},{3,2},{4,7},{5,4},{6,5},{7,6},{8,11},{9,8},{10,9... | collective-permute-start | bytes 884744 | tf_op jit(solution)/shard_map/ppermute | solution.py:352
  240.6 15.0 %all-to-all-start.4 = ((f32[32,1,256]{2,1,0:T(1,128)}), f32[32,1,256]{2,1,0:T(1,128)S(1)}, u32[]{:S(2)}, u32[]{:S(2)}) async-start(f32[32,1,256]{2,1,0:T(1,128)} %reshape.110), calls=%async_computation.4 | async-start | bytes 65536 | tf_op jit(solution)/shard_map/all_to_all | solution.py:538
  (11 other events, 10.3 us)

commit v3 on v2

--- a/solution.py
+++ b/solution.py
@@ -11,6 +11,7 @@
 NY = 384
 LANES = 128
 STEP = 2
+UNIT = 48
 
 width_cells = 1.5
 
@@ -119,27 +120,30 @@
 
 
 def mix_space_body(s_ref, *refs):
-    z_ref, mixed = refs[-2:]
+    z_ref = refs[-1]
     bands, _, rows, _ = s_ref.shape
-    for c in range(2):
-        for n in range(bands):
-            wide = s_ref[n, c].astype(jnp.float32)
-            for t in range(NY // LANES):
-                mixed[t, pl.ds(c * bands + n, rows, stride=2 * bands), :] = wide[
-                    :, t * LANES : (t + 1) * LANES
-                ]
-    for t in range(NY // LANES):
-        z_ref[:, 0, :, t * LANES : (t + 1) * LANES] = (
-            mixed[t].astype(jnp.bfloat16).reshape(z_ref.shape[0], -1, LANES)
+    size = 2 * bands * UNIT
+    to = lax.broadcasted_iota(jnp.int32, (size, size), 0)
+    at = lax.broadcasted_iota(jnp.int32, (size, size), 1)
+    band, part, row = at // (2 * UNIT), at // UNIT % 2, at % UNIT
+    chosen = (to == row * 2 * bands + part * bands + band).astype(jnp.bfloat16)
+    shares, _, depth, _ = z_ref.shape
+    each = shares * UNIT // rows
+    for unit in range(rows // UNIT):
+        cut = slice(unit * UNIT, (unit + 1) * UNIT)
+        stacked = jnp.concatenate(
+            [s_ref[n, c, cut] for n in range(bands) for c in range(2)], axis=0
         )
+        mixed = dot(chosen, stacked).astype(jnp.bfloat16)
+        z_ref[unit * each : (unit + 1) * each, 0] = mixed.reshape(each, depth, NY)
 
 
 def mix_space(in_space, part, base, shares):
     bands = in_space.shape[0]
     own = NX // shares
     depth = own * 2 * bands
-    group = max(1, 48 // own)
-    in_specs = [pl.BlockSpec((bands, 2, group * own, NY), lambda d: (0, 0, d, 0))]
+    rows = 2 * UNIT
+    in_specs = [pl.BlockSpec((bands, 2, rows, NY), lambda d: (0, 0, d, 0))]
     operands = [in_space]
     aliases = {}
     if base is not None:
@@ -148,11 +152,10 @@
         aliases = {1: 0}
     return pl.pallas_call(
         mix_space_body,
-        grid=(shares // group,),
+        grid=(NX // rows,),
         in_specs=in_specs,
-        out_specs=pl.BlockSpec((group, 1, depth, NY), lambda d: (d, part, 0, 0)),
+        out_specs=pl.BlockSpec((rows // own, 1, depth, NY), lambda d: (d, part, 0, 0)),
         out_shape=jax.ShapeDtypeStruct((shares, 2, depth, NY), jnp.bfloat16),
-        scratch_shapes=[pltpu.VMEM((NY // LANES, group * depth, LANES), jnp.float32)],
         input_output_aliases=aliases,
         compiler_params=pltpu.CompilerParams(vmem_limit_bytes=56 << 20),
         cost_estimate=lasting(0.01),
@@ -359,29 +362,36 @@
     return high, (wide - high.astype(jnp.float32)).astype(jnp.bfloat16)
 
 
-def charges_body(planes, slab_rows, place, c_ref, i_ref, o_ref):
-    share = o_ref.shape[0]
+def charges_body(planes, slab_rows, place, c_ref, i_ref, o_ref, total):
     first = place[0].astype(jnp.float32)
     plane = place[1].astype(jnp.float32)
-    own_x = lax.broadcasted_iota(jnp.int32, (share, 1), 0).astype(jnp.float32) + first
+    own_x = lax.broadcasted_iota(jnp.int32, (LANES, 1), 0).astype(jnp.float32) + first
     cells_y = lax.broadcasted_iota(jnp.int32, (NY, 1), 0)
     slab_y = (cells_y // slab_rows).astype(jnp.float32)
     cells_y = cells_y.astype(jnp.float32)
-    o_ref[...] = i_ref[...]
-
-    @pl.loop(0, c_ref.shape[0])
-    def _(device):
-        along_u, along_v, along_w, amount, slab = [c_ref[device, k : k + 1, :] for k in range(5)]
-        kernel_x = gaussian(own_x - NX * along_u) * (amount * gaussian(plane - planes * along_w))
-        kernel_y = gaussian(cells_y - (slab * slab_rows + slab_rows * along_v))
-        kernel_y = jnp.where(slab_y == slab, kernel_y, 0.0)
-        (x_high, x_low), (y_high, y_low) = split(kernel_x), split(kernel_y)
-        total = o_ref[...]
-        for left, right in ((x_high, y_low), (x_low, y_high), (x_high, y_high)):
-            total = total + lax.dot_general(
-                left, right, (((1,), (1,)), ((), ())), preferred_element_type=jnp.float32
-            )
-        o_ref[...] = total
+    total[...] = jnp.zeros_like(total)
+
+    @pl.loop(0, c_ref.shape[0] // 2)
+    def _(pair):
+        lefts, rights = [], []
+        for k in range(2):
+            along_u, along_v, along_w, amount, slab = [
+                c_ref[pair * 2 + k, row : row + 1, :] for row in range(5)
+            ]
+            weight = amount * gaussian(plane - planes * along_w)
+            x_high, x_low = split(gaussian(own_x - NX * along_u) * weight)
+            kernel_y = gaussian(cells_y - (slab * slab_rows + slab_rows * along_v))
+            y_high, y_low = split(jnp.where(slab_y == slab, kernel_y, 0.0))
+            lefts += [y_low, y_high, y_high]
+            rights += [x_high, x_low, x_high]
+        total[...] += lax.dot_general(
+            jnp.concatenate(lefts, axis=1),
+            jnp.concatenate(rights, axis=1),
+            (((1,), (1,)), ((), ())),
+            preferred_element_type=jnp.float32,
+        )
+
+    o_ref[...] = i_ref[...] + total[...].T[: o_ref.shape[0]]
 
 
 def potential_message(ionic_field, point_charge, charge_place, charge_slab, planes, halves):
@@ -434,6 +444,7 @@
         ],
         out_specs=pl.BlockSpec(memory_space=pltpu.VMEM),
         out_shape=jax.ShapeDtypeStruct((share, NY), jnp.float32),
+        scratch_shapes=[pltpu.VMEM((NY, LANES), jnp.float32)],
         compiler_params=pltpu.CompilerParams(vmem_limit_bytes=56 << 20),
         cost_estimate=lasting(0.01),
         name="charge_potential",
@@ -462,10 +473,11 @@
 
     arrived = [shifted(packed[0])]
     message = lax.all_to_all(message, ("band", "ga"), 0, 0, tiled=True)
+    mixed = mix_waves(waves, rows, band_groups)
+    message, packed[1], mixed = lax.optimization_barrier((message, packed[1], mixed))
     own_potential = own_share(message, planes, halves)
     copies = jnp.broadcast_to(own_potential[None], (band_groups,) + own_potential.shape)
     potential = lax.all_to_all(copies, "band", 0, 0, tiled=True).reshape(NX, NY)
-    mixed = mix_waves(waves, rows, band_groups)
     cells = jnp.arange(NX, dtype=jnp.int32)
     arrived[0], potential, packed[1], mixed, cells = lax.optimization_barrier(
         (arrived[0], potential, packed[1], mixed, cells)
@@ -517,15 +529,11 @@
     kinetic = jnp.broadcast_to(kinetic[None], (planes, share, NY)).reshape(planes * share, NY)
 
     scale = 1.0 / (planes * NX * NY)
+    spectrum = (in_space[1], potential, forth, back)
+    place, returned[0][-1] = lax.optimization_barrier((place, returned[0][-1]))
+    returned.append(shifted(inverse(arrived[1], 0, half, place, *spectrum)))
+    grams = overlap(met_waves[:, None], kinetic, per, scale)
     applied_waves = unpack(returned[0], place, None, 0, bands, planes)
-    grams = overlap(met_waves[:, None], kinetic, per, scale)
-    spectrum = (in_space[1], potential, forth, back)
-    firsts = list(range(0, half, STEP))
-    for first in firsts:
-        if first == firsts[-1]:
-            grams, place = lax.optimization_barrier((grams, place))
-        returned.append(shifted(inverse(arrived[1], first, STEP, place, *spectrum)))
-    grams, applied_waves = lax.optimization_barrier((grams, applied_waves))
     full_matrix = overlap(
         met_space, space_weights, per // met_space.shape[1], scale, grams
     )
@@ -537,10 +545,8 @@
     )
     subspace = lax.all_to_all(blocks, ("band", "ga"), 0, 0, tiled=True).sum(0)
 
-    for j, first in enumerate(firsts):
-        if first == firsts[-1]:
-            place, subspace = lax.optimization_barrier((place, subspace))
-        applied_waves = unpack(returned[j + 1], place, applied_waves, half + first, bands, planes)
+    place, subspace = lax.optimization_barrier((place, subspace))
+    applied_waves = unpack(returned[1], place, applied_waves, half, bands, planes)
     return (applied_waves, subspace)
 
 

time: 263 us -> 257 us (0.977)
  waiting for transfers between devices: 35.3 us -> 70.9 us
  starting transfers between devices: 92.2 us -> 59.9 us
  Pallas kernels: 111 us -> 102 us
    ppermute x15 -> x12, starting transfers between devices: 46.2 us -> 28.4 us  [shifted(): lax.ppermute(message, 'ga', [(i, (i + s) % groups) for i in range(groups)])]
    all_to_all x1, starting transfers between devices: 26.3 us -> 12 us  [shards(): potential = lax.all_to_all(copies, 'band', 0, 0, tiled=True).reshape(NX, NY)]
    all_to_all x1, waiting for transfers between devices: 8.25 us -> 20.7 us  [shards(): subspace = lax.all_to_all(blocks, ('band', 'ga'), 0, 0, tiled=True).sum(0)]
    all_to_all x1, waiting for transfers between devices: 0.01 us -> 10.4 us  [shards(): potential = lax.all_to_all(copies, 'band', 0, 0, tiled=True).reshape(NX, NY)]
    ppermute x15 -> x12, waiting for transfers between devices: 14.9 us -> 23.9 us  [shifted(): lax.ppermute(message, 'ga', [(i, (i + s) % groups) for i in range(groups)])]
    all_to_all x1, waiting for transfers between devices: 0.01 us -> 3.67 us  [shards(): met_space = lax.all_to_all(mixed, 'band', 0, 0, tiled=True)]
    pallas_call x3 -> x2, Pallas kernels: 21.7 us -> 18.4 us  [inverse(): pl.pallas_call(functools.partial(inverse_body, groups), grid=(bands // ST...]
    pallas_call x2, Pallas kernels: 12.7 us -> 9.69 us  [mix_space(): pl.pallas_call(mix_space_body, grid=(NX // rows,), in_specs=in_specs, out...]
  transfers between devices with their start and end apart: 20 -> 17, of which waited for: 4 -> 7; matrix products, arithmetic and copies ran while one was open for 6% -> 6% of each run, Pallas kernels for 41% -> 38%
where the time goes in v3:
time: 257 us; the launch traced here: 256 us
  Pallas kernels  102 us (40%)
  waiting for transfers between devices  70.9 us (28%)
  starting transfers between devices  59.9 us (23%)
  local copies, waits for them, and re-layouts  11.3 us (4%)
  other arithmetic  10.6 us (4%)
    ppermute x12, starting transfers between devices, shifted(): lax.ppermute(message, 'ga', [(i, (i + s) % groups) for i in range(groups)])  28.4 us
    ppermute x12, waiting for transfers between devices, shifted(): lax.ppermute(message, 'ga', [(i, (i + s) % groups) for i in range(groups)])  23.9 us
    all_to_all x1, waiting for transfers between devices, shards(): subspace = lax.all_to_all(blocks, ('band', 'ga'), 0, 0, tiled=True).sum(0)  20.7 us
    pallas_call x2, Pallas kernels, inverse(): pl.pallas_call(functools.partial(inverse_body, groups), grid=(bands // ST...  18.4 us
    pallas_call x2, Pallas kernels, overlap(): pl.pallas_call(functools.partial(overlap_body, scale, per), in_specs=[who...  17.9 us
    pallas_call x2, Pallas kernels, forward(): pl.pallas_call(functools.partial(forward_body, groups), grid=(bands // ST...  16.2 us
    all_to_all x1, waiting for transfers between devices, shards(): met_waves = lax.all_to_all(mixed, 'band', 0, 0, tiled=True)  12.2 us
    pallas_call x1, Pallas kernels, own_share(): pl.pallas_call(functools.partial(charges_body, planes, slab_rows), in_spe...  12 us
  transfers between devices with their start and end apart: 17, of which 7 were waited for; matrix products, arithmetic and copies ran while one was open for 6% of the time, Pallas kernels for 38%

profile of v3, /device:TPU:0, one launch (start us, length us, event | category | flops | bytes accessed | tf_op | source)
XLA Modules:
  0.0 256.0 jit_solution(5346400347509106566)
XLA Ops:
  4.0 7.3 %all-to-all-start = ((f32[32,8,256]{2,1,0:T(8,128)}), f32[32,8,256]{2,1,0:T(8,128)S(1)}, u32[]{:S(2)}, u32[]{:S(2)}) async-start(f32[32,8,256]{2,1,0:T(8,128)} %pad_maximum_fusion.4), calls=%async_computation | async-start | bytes 524288 | tf_op jit(solution)/shard_map/all_to_all | solution.py:475
  11.3 4.4 %pack_planes.2 = (bf16[2,4,96,384]{3,2,1,0:T(8,128)(2,1)}, bf16[2,4,96,384]{3,2,1,0:T(8,128)(2,1)}, bf16[2,4,96,384]{3,2,1,0:T(8,128)(2,1)}, bf16[2,4,96,384]{3,2,1,0:T(8,128)(2,1)}) custom-call(s32[1]{0:T(128)} %bitcast.place, bf16[2,8,4,36864]{3,2,1,0:T(4,128)(2,1)} %w_ref.1), custom_call_target="tpu_custom_call" | custom-call | bytes 36900 | tf_op jit(solution)/shard_map/pack_planes/pallas_call | solution.py:66
  17.5 2.4 collective-permute-start.1
  21.3 4.3 %pack_planes.3 = (bf16[2,4,96,384]{3,2,1,0:T(8,128)(2,1)}, bf16[2,4,96,384]{3,2,1,0:T(8,128)(2,1)}, bf16[2,4,96,384]{3,2,1,0:T(8,128)(2,1)}, bf16[2,4,96,384]{3,2,1,0:T(8,128)(2,1)}) custom-call(s32[1]{0:T(128)} %bitcast.place, bf16[2,8,4,36864]{3,2,1,0:T(4,128)(2,1)} %w_ref.1), custom_call_target="tpu_custom_call" | custom-call | bytes 36900 | tf_op jit(solution)/shard_map/pack_planes/pallas_call | solution.py:66
  25.7 10.0 %mix_waves.1 = bf16[8,768,384]{2,1,0:T(8,128)(2,1)} custom-call(bf16[2,8,4,36864]{3,2,1,0:T(4,128)(2,1)} %w_ref.1), custom_call_target="tpu_custom_call" | custom-call | bytes 36900 | tf_op jit(solution)/shard_map/mix_waves/pallas_call | solution.py:109
  37.4 12.0 %charge_potential.1.w_ref = f32[48,384]{1,0:T(8,128)} custom-call(s32[2]{0:T(128)} %pad_add_fusion.place, f32[32,8,256]{2,1,0:T(8,128)} %copy-done.7, f32[48,384]{1,0:T(8,128)} %reshape.105.i_ref), custom_call_target="tpu_custom_call" | custom-call | bytes 36900 | tf_op jit(solution)/shard_map/charge_potential/pallas_call | solution.py:438
  51.1 12.0 %all-to-all-start.1 = ((f32[8,48,384]{2,1,0:T(8,128)}), f32[8,48,384]{2,1,0:T(8,128)S(1)}, u32[]{:S(2)}, u32[]{:S(2)}) async-start(f32[8,48,384]{2,1,0:T(8,128)} %broadcast_in_dim.15), calls=%async_computation.1 | async-start | bytes 1179648 | tf_op jit(solution)/shard_map/all_to_all | solution.py:480
  63.2 10.4 %all-to-all-done.1 = f32[8,48,384]{2,1,0:T(8,128)S(1)} async-done(((f32[8,48,384]{2,1,0:T(8,128)}), f32[8,48,384]{2,1,0:T(8,128)S(1)}, u32[]{:S(2)}, u32[]{:S(2)}) %all-to-all-start.1) | async-done | bytes 589856 | tf_op jit(solution)/shard_map/all_to_all | solution.py:480
  74.4 4.6 %all-to-all-start.2 = ((bf16[8,768,384]{2,1,0:T(8,128)(2,1)}), bf16[8,768,384]{2,1,0:T(8,128)(2,1)}, u32[]{:S(2)}, u32[]{:S(2)}) async-start(bf16[8,768,384]{2,1,0:T(8,128)(2,1)} %mix_waves.1), calls=%async_computation.2 | async-start | bytes 9437184 | tf_op jit(solution)/shard_map/all_to_all | solution.py:487
  79.3 3.6 %collective-permute-start.5 = (bf16[2,4,96,384]{3,2,1,0:T(8,128)(2,1)S(1)}, bf16[2,4,96,384]{3,2,1,0:T(8,128)(2,1)S(1)}, u32[]{:S(2)}, u32[]{:S(2)}) collective-permute-start(bf16[2,4,96,384]{3,2,1,0:T(8,128)(2,1)S(1)} %copy-done.17), channel_id=1, source_target_pairs={{0,3},{1,0},{2,1},{3,2},{4,7},{5,4},{6,5},{7,6},{8,11},{9,8},{10,9... | collective-permute-start | bytes 1769480 | tf_op jit(solution)/shard_map/ppermute | solution.py:355
  82.9 2.6 fusion.7
  85.5 2.9 %multiply_convert_fusion = (bf16[384,384]{1,0:T(8,128)(2,1)S(1)}, bf16[384,384]{1,0:T(8,128)(2,1)S(1)}) fusion(s32[384]{0:T(512)S(1)} %iota.13), kind=kLoop, calls=%fused_computation.9 | loop fusion | flops 1916928 | bytes 591360 | tf_op jit(solution)/shard_map/convert_element_type | solution.py:26
  90.0 8.1 %forward.2.refs_4_.s_ref = bf16[4,2,384,384]{3,2,1,0:T(8,128)(2,1)} custom-call(s32[1]{0:T(128)} %bitcast.place, bf16[2,4,96,384]{3,2,1,0:T(8,128)(2,1)} %get-tuple-element.70.refs_0_, bf16[2,4,96,384]{3,2,1,0:T(8,128)(2,1)} %copy-done.1, bf16[2,4,96,384]{3,2,1,0:T(8,128)(2,1)} %copy-done.2, bf16[2,4,96,384]{3,2,1,0:T(8,128)(2,1)} %copy-done.3, ...), custom_call_target="tpu_custom_call" | custom-call | bytes 36900 | tf_op jit(solution)/shard_map/forward/pallas_call | solution.py:224
  98.1 4.8 %mix_space.2.refs_0_ = bf16[8,2,384,384]{3,2,1,0:T(8,128)(2,1)} custom-call(bf16[4,2,384,384]{3,2,1,0:T(8,128)(2,1)} %forward.2.refs_4_.s_ref), custom_call_target="tpu_custom_call" | custom-call | bytes 36900 | tf_op jit(solution)/shard_map/mix_space/pallas_call | solution.py:153
  102.9 9.1 %inverse.2 = (bf16[2,4,96,384]{3,2,1,0:T(8,128)(2,1)}, bf16[2,4,96,384]{3,2,1,0:T(8,128)(2,1)}, bf16[2,4,96,384]{3,2,1,0:T(8,128)(2,1)}, bf16[2,4,96,384]{3,2,1,0:T(8,128)(2,1)}) custom-call(s32[1]{0:T(128)} %bitcast.place, bf16[2,4,96,384]{3,2,1,0:T(8,128)(2,1)} %get-tuple-element.70.refs_0_, bf16[2,4,96,384]{3,2,1,0:T(8,128)(2,1)} %copy-done.1, ...), custom_call_target="tpu_custom_call" | custom-call | bytes 36900 | tf_op jit(solution)/shard_map/inverse/pallas_call | solution.py:268
  112.0 9.5 %collective-permute-done.4.refs_2_ = bf16[2,4,96,384]{3,2,1,0:T(8,128)(2,1)S(1)} collective-permute-done((bf16[2,4,96,384]{3,2,1,0:T(8,128)(2,1)S(1)}, bf16[2,4,96,384]{3,2,1,0:T(8,128)(2,1)S(1)}, u32[]{:S(2)}, u32[]{:S(2)}) %collective-permute-start.4) | collective-permute-done | bytes 589856 | tf_op jit(solution)/shard_map/ppermute | solution.py:355
  121.5 12.2 %all-to-all-done.2 = bf16[8,768,384]{2,1,0:T(8,128)(2,1)} async-done(((bf16[8,768,384]{2,1,0:T(8,128)(2,1)}), bf16[8,768,384]{2,1,0:T(8,128)(2,1)}, u32[]{:S(2)}, u32[]{:S(2)}) %all-to-all-start.2) | async-done | bytes 4718624 | tf_op jit(solution)/shard_map/all_to_all | solution.py:487
  134.1 8.1 %forward.3.s_ref.refs_4_ = bf16[4,2,384,384]{3,2,1,0:T(8,128)(2,1)} custom-call(s32[1]{0:T(128)} %bitcast.place, bf16[2,4,96,384]{3,2,1,0:T(8,128)(2,1)} %get-tuple-element.82.refs_0_, bf16[2,4,96,384]{3,2,1,0:T(8,128)(2,1)} %copy-done.4, bf16[2,4,96,384]{3,2,1,0:T(8,128)(2,1)} %copy-done.5, bf16[2,4,96,384]{3,2,1,0:T(8,128)(2,1)} %copy-done.6, ...), custom_call_target="tpu_custom_call" | custom-call | bytes 36900 | tf_op jit(solution)/shard_map/forward/pallas_call | solution.py:224
  142.2 4.8 %mix_space.3 = bf16[8,2,384,384]{3,2,1,0:T(8,128)(2,1)} custom-call(bf16[4,2,384,384]{3,2,1,0:T(8,128)(2,1)} %forward.3.s_ref.refs_4_, bf16[8,2,384,384]{3,2,1,0:T(8,128)(2,1)} %mix_space.2.refs_0_), custom_call_target="tpu_custom_call", output_to_operand_aliasing={{}: (1, {})} | custom-call | bytes 36900 | tf_op jit(solution)/shard_map/mix_space/pallas_call | solution.py:153
  148.7 5.0 %all-to-all-start.3 = ((bf16[8,2,384,384]{3,2,1,0:T(8,128)(2,1)}), bf16[8,2,384,384]{3,2,1,0:T(8,128)(2,1)}, u32[]{:S(2)}, u32[]{:S(2)}) async-start(bf16[8,2,384,384]{3,2,1,0:T(8,128)(2,1)} %mix_space.3), calls=%async_computation.3 | async-start | bytes 9437184 | tf_op jit(solution)/shard_map/all_to_all | solution.py:510
  153.7 2.4 collective-permute-start.6
  156.1 13.7 %collective-permute-done.6.refs_3_ = bf16[2,4,96,384]{3,2,1,0:T(8,128)(2,1)S(1)} collective-permute-done((bf16[2,4,96,384]{3,2,1,0:T(8,128)(2,1)S(1)}, bf16[2,4,96,384]{3,2,1,0:T(8,128)(2,1)S(1)}, u32[]{:S(2)}, u32[]{:S(2)}) %collective-permute-start.6) | collective-permute-done | bytes 589856 | tf_op jit(solution)/shard_map/ppermute | solution.py:355
  169.8 9.3 %inverse.3 = (bf16[2,4,96,384]{3,2,1,0:T(8,128)(2,1)}, bf16[2,4,96,384]{3,2,1,0:T(8,128)(2,1)}, bf16[2,4,96,384]{3,2,1,0:T(8,128)(2,1)}, bf16[2,4,96,384]{3,2,1,0:T(8,128)(2,1)}) custom-call(s32[1]{0:T(128)} %bitcast.place, bf16[2,4,96,384]{3,2,1,0:T(8,128)(2,1)} %get-tuple-element.82.refs_0_, bf16[2,4,96,384]{3,2,1,0:T(8,128)(2,1)} %copy-done.4, ...), custom_call_target="tpu_custom_call" | custom-call | bytes 36900 | tf_op jit(solution)/shard_map/inverse/pallas_call | solution.py:268
  179.1 13.6 %collective-permute-start.8 = (bf16[2,4,96,384]{3,2,1,0:T(8,128)(2,1)}, bf16[2,4,96,384]{3,2,1,0:T(8,128)(2,1)S(1)}, u32[]{:S(2)}, u32[]{:S(2)}) collective-permute-start(bf16[2,4,96,384]{3,2,1,0:T(8,128)(2,1)} %get-tuple-element.92), channel_id=1, source_target_pairs={{0,1},{1,2},{2,3},{3,0},{4,5},{5,6},{6,7},{7,4},{8,9},{9,10},{10,1... | collective-permute-start | bytes 1769480 | tf_op jit(solution)/shard_map/ppermute | solution.py:355
  192.7 2.4 collective-permute-start.10
  195.9 8.9 %overlap.2.refs_0_ = f32[2,64,64]{2,1,0:T(8,128)} custom-call(bf16[8,1,768,384]{3,2,1,0:T(8,128)(2,1)} %bitcast.9.z_ref, f32[48,384]{1,0:T(8,128)} %reshape.107.w_ref), custom_call_target="tpu_custom_call" | custom-call | bytes 29520000 | tf_op jit(solution)/shard_map/overlap/pallas_call | solution.py:340
  204.8 3.7 %all-to-all-done.3.z_ref = bf16[8,2,384,384]{3,2,1,0:T(8,128)(2,1)} async-done(((bf16[8,2,384,384]{3,2,1,0:T(8,128)(2,1)}), bf16[8,2,384,384]{3,2,1,0:T(8,128)(2,1)}, u32[]{:S(2)}, u32[]{:S(2)}) %all-to-all-start.3) | async-done | bytes 4718624 | tf_op jit(solution)/shard_map/all_to_all | solution.py:510
  208.5 9.0 %overlap.3 = f32[2,64,64]{2,1,0:T(8,128)} custom-call(bf16[8,2,384,384]{3,2,1,0:T(8,128)(2,1)} %all-to-all-done.3.z_ref, f32[48,384]{1,0:T(8,128)} %charge_potential.1.w_ref, f32[2,64,64]{2,1,0:T(8,128)} %overlap.2.refs_0_), custom_call_target="tpu_custom_call" | custom-call | bytes 29520000 | tf_op jit(solution)/shard_map/overlap/pallas_call | solution.py:340
  219.3 2.6 %all-to-all-start.4 = ((f32[32,1,256]{2,1,0:T(1,128)}), f32[32,1,256]{2,1,0:T(1,128)S(1)}, u32[]{:S(2)}, u32[]{:S(2)}) async-start(f32[32,1,256]{2,1,0:T(1,128)} %reshape.110), calls=%async_computation.4 | async-start | bytes 65536 | tf_op jit(solution)/shard_map/all_to_all | solution.py:546
  222.7 4.6 %unpack_planes.2.refs_4_ = bf16[2,8,4,36864]{3,2,1,0:T(4,128)(2,1)} custom-call(s32[1]{0:T(128)} %bitcast.place, bf16[2,4,96,384]{3,2,1,0:T(8,128)(2,1)} %get-tuple-element.95.refs_0_, bf16[2,4,96,384]{3,2,1,0:T(8,128)(2,1)} %copy-done.8, bf16[2,4,96,384]{3,2,1,0:T(8,128)(2,1)} %copy-done.13, bf16[2,4,96,384]{3,2,1,0:T(8,128)(2,1)} %copy-done.12), custom_call_target="tpu_custom_call" | custom-call | bytes 17712000 | tf_op jit(solution)/shard_map/unpack_planes/pallas_call | solution.py:191
  227.4 20.7 %all-to-all-done.4 = f32[32,1,256]{2,1,0:T(1,128)S(1)} async-done(((f32[32,1,256]{2,1,0:T(1,128)}), f32[32,1,256]{2,1,0:T(1,128)S(1)}, u32[]{:S(2)}, u32[]{:S(2)}) %all-to-all-start.4) | async-done | bytes 32800 | tf_op jit(solution)/shard_map/all_to_all | solution.py:546
  251.3 4.6 %unpack_planes.3 = bf16[2,8,4,36864]{3,2,1,0:T(4,128)(2,1)} custom-call(s32[1]{0:T(128)} %bitcast.place, bf16[2,4,96,384]{3,2,1,0:T(8,128)(2,1)} %get-tuple-element.91.refs_0_, bf16[2,4,96,384]{3,2,1,0:T(8,128)(2,1)} %copy-done.9, bf16[2,4,96,384]{3,2,1,0:T(8,128)(2,1)} %copy-done.10, ...), custom_call_target="tpu_custom_call", output_to_operand_aliasing={{}: (5, {})} | custom-call | bytes 17712000 | tf_op jit(solution)/shard_map/unpack_planes/pallas_call | solution.py:191
  (93 shorter events, 21.1 us)
Async XLA Ops:
  0.6 2.6 %copy-start.14 = (f32[3,256]{1,0:T(4,128)S(1)}, f32[3,256]{1,0:T(4,128)}, u32[]{:S(2)}) copy-start(f32[3,256]{1,0:T(4,128)} %param.8) | copy-start | bytes 9220
  0.6 2.6 %copy-start.15 = (f32[256]{0:T(256)S(1)}, f32[256]{0:T(256)}, u32[]{:S(2)}) copy-start(f32[256]{0:T(256)} %param.7) | copy-start | bytes 3076
  4.0 32.3 %all-to-all-start = ((f32[32,8,256]{2,1,0:T(8,128)}), f32[32,8,256]{2,1,0:T(8,128)S(1)}, u32[]{:S(2)}, u32[]{:S(2)}) async-start(f32[32,8,256]{2,1,0:T(8,128)} %pad_maximum_fusion.4), calls=%async_computation | async-start | bytes 524288 | tf_op jit(solution)/shard_map/all_to_all | solution.py:475
  15.7 47.4 %collective-permute-start = (bf16[2,4,96,384]{3,2,1,0:T(8,128)(2,1)}, bf16[2,4,96,384]{3,2,1,0:T(8,128)(2,1)S(1)}, u32[]{:S(2)}, u32[]{:S(2)}) collective-permute-start(bf16[2,4,96,384]{3,2,1,0:T(8,128)(2,1)} %get-tuple-element.52), channel_id=1, source_target_pairs={{0,1},{1,2},{2,3},{3,0},{4,5},{5,6},{6,7},{7,4},{8,9},{9,10},{10,1... | collective-permute-start | bytes 1769480 | tf_op jit(solution)/shard_map/ppermute | solution.py:355
  17.5 45.6 %collective-permute-start.1 = (bf16[2,4,96,384]{3,2,1,0:T(8,128)(2,1)}, bf16[2,4,96,384]{3,2,1,0:T(8,128)(2,1)S(1)}, u32[]{:S(2)}, u32[]{:S(2)}) collective-permute-start(bf16[2,4,96,384]{3,2,1,0:T(8,128)(2,1)} %get-tuple-element.53), channel_id=1, source_target_pairs={{0,2},{1,3},{2,0},{3,1},{4,6},{5,7},{6,4},{7,5},{8,10},{9,11},{10,... | collective-permute-start | bytes 1769480 | tf_op jit(solution)/shard_map/ppermute | solution.py:355
  19.9 43.2 %collective-permute-start.2 = (bf16[2,4,96,384]{3,2,1,0:T(8,128)(2,1)}, bf16[2,4,96,384]{3,2,1,0:T(8,128)(2,1)S(1)}, u32[]{:S(2)}, u32[]{:S(2)}) collective-permute-start(bf16[2,4,96,384]{3,2,1,0:T(8,128)(2,1)} %get-tuple-element.54), channel_id=1, source_target_pairs={{0,3},{1,0},{2,1},{3,2},{4,7},{5,4},{6,5},{7,6},{8,11},{9,8},{10,9... | collective-permute-start | bytes 1769480 | tf_op jit(solution)/shard_map/ppermute | solution.py:355
  36.3 1.1 copy-start.7
  51.1 22.4 %all-to-all-start.1 = ((f32[8,48,384]{2,1,0:T(8,128)}), f32[8,48,384]{2,1,0:T(8,128)S(1)}, u32[]{:S(2)}, u32[]{:S(2)}) async-start(f32[8,48,384]{2,1,0:T(8,128)} %broadcast_in_dim.15), calls=%async_computation.1 | async-start | bytes 1179648 | tf_op jit(solution)/shard_map/all_to_all | solution.py:480
  63.1 10.5 %copy-start.1 = (bf16[2,4,96,384]{3,2,1,0:T(8,128)(2,1)}, bf16[2,4,96,384]{3,2,1,0:T(8,128)(2,1)S(1)}, u32[]{:S(2)}) copy-start(bf16[2,4,96,384]{3,2,1,0:T(8,128)(2,1)S(1)} %collective-permute-done.refs_1_) | copy-start | bytes 1769476
  63.1 10.4 %copy-start.2 = (bf16[2,4,96,384]{3,2,1,0:T(8,128)(2,1)}, bf16[2,4,96,384]{3,2,1,0:T(8,128)(2,1)S(1)}, u32[]{:S(2)}) copy-start(bf16[2,4,96,384]{3,2,1,0:T(8,128)(2,1)S(1)} %collective-permute-done.1.refs_2_) | copy-start | bytes 1769476
  63.1 10.4 %copy-start.3 = (bf16[2,4,96,384]{3,2,1,0:T(8,128)(2,1)}, bf16[2,4,96,384]{3,2,1,0:T(8,128)(2,1)S(1)}, u32[]{:S(2)}) copy-start(bf16[2,4,96,384]{3,2,1,0:T(8,128)(2,1)S(1)} %collective-permute-done.2.refs_3_) | copy-start | bytes 1769476
  73.5 5.5 %copy-start.18 = (bf16[2,4,96,384]{3,2,1,0:T(8,128)(2,1)S(1)}, bf16[2,4,96,384]{3,2,1,0:T(8,128)(2,1)}, u32[]{:S(2)}) copy-start(bf16[2,4,96,384]{3,2,1,0:T(8,128)(2,1)} %get-tuple-element.67) | copy-start | bytes 1769476
  73.5 5.7 %copy-start.17 = (bf16[2,4,96,384]{3,2,1,0:T(8,128)(2,1)S(1)}, bf16[2,4,96,384]{3,2,1,0:T(8,128)(2,1)}, u32[]{:S(2)}) copy-start(bf16[2,4,96,384]{3,2,1,0:T(8,128)(2,1)} %get-tuple-element.68) | copy-start | bytes 1769476
  74.4 59.4 %all-to-all-start.2 = ((bf16[8,768,384]{2,1,0:T(8,128)(2,1)}), bf16[8,768,384]{2,1,0:T(8,128)(2,1)}, u32[]{:S(2)}, u32[]{:S(2)}) async-start(bf16[8,768,384]{2,1,0:T(8,128)(2,1)} %mix_waves.1), calls=%async_computation.2 | async-start | bytes 9437184 | tf_op jit(solution)/shard_map/all_to_all | solution.py:487
  79.0 33.1 %collective-permute-start.3 = (bf16[2,4,96,384]{3,2,1,0:T(8,128)(2,1)}, bf16[2,4,96,384]{3,2,1,0:T(8,128)(2,1)S(1)}, u32[]{:S(2)}, u32[]{:S(2)}) collective-permute-start(bf16[2,4,96,384]{3,2,1,0:T(8,128)(2,1)} %get-tuple-element.66), channel_id=1, source_target_pairs={{0,1},{1,2},{2,3},{3,0},{4,5},{5,6},{6,7},{7,4},{8,9},{9,10},{10,1... | collective-permute-start | bytes 1769480 | tf_op jit(solution)/shard_map/ppermute | solution.py:355
  79.1 42.4 %collective-permute-start.4 = (bf16[2,4,96,384]{3,2,1,0:T(8,128)(2,1)S(1)}, bf16[2,4,96,384]{3,2,1,0:T(8,128)(2,1)S(1)}, u32[]{:S(2)}, u32[]{:S(2)}) collective-permute-start(bf16[2,4,96,384]{3,2,1,0:T(8,128)(2,1)S(1)} %copy-done.18), channel_id=1, source_target_pairs={{0,2},{1,3},{2,0},{3,1},{4,6},{5,7},{6,4},{7,5},{8,10},{9,11},{10,... | collective-permute-start | bytes 1769480 | tf_op jit(solution)/shard_map/ppermute | solution.py:355
  79.3 42.2 %collective-permute-start.5 = (bf16[2,4,96,384]{3,2,1,0:T(8,128)(2,1)S(1)}, bf16[2,4,96,384]{3,2,1,0:T(8,128)(2,1)S(1)}, u32[]{:S(2)}, u32[]{:S(2)}) collective-permute-start(bf16[2,4,96,384]{3,2,1,0:T(8,128)(2,1)S(1)} %copy-done.17), channel_id=1, source_target_pairs={{0,3},{1,0},{2,1},{3,2},{4,7},{5,4},{6,5},{7,6},{8,11},{9,8},{10,9... | collective-permute-start | bytes 1769480 | tf_op jit(solution)/shard_map/ppermute | solution.py:355
  112.0 22.1 %copy-start.4 = (bf16[2,4,96,384]{3,2,1,0:T(8,128)(2,1)}, bf16[2,4,96,384]{3,2,1,0:T(8,128)(2,1)S(1)}, u32[]{:S(2)}) copy-start(bf16[2,4,96,384]{3,2,1,0:T(8,128)(2,1)S(1)} %collective-permute-done.3.refs_1_) | copy-start | bytes 1769476
  121.5 12.6 %copy-start.5 = (bf16[2,4,96,384]{3,2,1,0:T(8,128)(2,1)}, bf16[2,4,96,384]{3,2,1,0:T(8,128)(2,1)S(1)}, u32[]{:S(2)}) copy-start(bf16[2,4,96,384]{3,2,1,0:T(8,128)(2,1)S(1)} %collective-permute-done.4.refs_2_) | copy-start | bytes 1769476
  121.5 12.6 %copy-start.6 = (bf16[2,4,96,384]{3,2,1,0:T(8,128)(2,1)}, bf16[2,4,96,384]{3,2,1,0:T(8,128)(2,1)S(1)}, u32[]{:S(2)}) copy-start(bf16[2,4,96,384]{3,2,1,0:T(8,128)(2,1)S(1)} %collective-permute-done.5.refs_3_) | copy-start | bytes 1769476
  133.7 14.1 %collective-permute-start.7 = (bf16[2,4,96,384]{3,2,1,0:T(8,128)(2,1)}, bf16[2,4,96,384]{3,2,1,0:T(8,128)(2,1)S(1)}, u32[]{:S(2)}, u32[]{:S(2)}) collective-permute-start(bf16[2,4,96,384]{3,2,1,0:T(8,128)(2,1)} %get-tuple-element.87), channel_id=1, source_target_pairs={{0,1},{1,2},{2,3},{3,0},{4,5},{5,6},{6,7},{7,4},{8,9},{9,10},{10,1... | collective-permute-start | bytes 1769480 | tf_op jit(solution)/shard_map/ppermute | solution.py:355
  147.1 6.6 %copy-start.19 = (bf16[2,4,96,384]{3,2,1,0:T(8,128)(2,1)S(1)}, bf16[2,4,96,384]{3,2,1,0:T(8,128)(2,1)}, u32[]{:S(2)}) copy-start(bf16[2,4,96,384]{3,2,1,0:T(8,128)(2,1)} %get-tuple-element.80) | copy-start | bytes 1769476
  147.1 9.0 %copy-start.16 = (bf16[2,4,96,384]{3,2,1,0:T(8,128)(2,1)S(1)}, bf16[2,4,96,384]{3,2,1,0:T(8,128)(2,1)}, u32[]{:S(2)}) copy-start(bf16[2,4,96,384]{3,2,1,0:T(8,128)(2,1)} %get-tuple-element.97) | copy-start | bytes 1769476
  148.7 59.8 %all-to-all-start.3 = ((bf16[8,2,384,384]{3,2,1,0:T(8,128)(2,1)}), bf16[8,2,384,384]{3,2,1,0:T(8,128)(2,1)}, u32[]{:S(2)}, u32[]{:S(2)}) async-start(bf16[8,2,384,384]{3,2,1,0:T(8,128)(2,1)} %mix_space.3), calls=%async_computation.3 | async-start | bytes 9437184 | tf_op jit(solution)/shard_map/all_to_all | solution.py:510
  153.7 16.1 %collective-permute-start.6 = (bf16[2,4,96,384]{3,2,1,0:T(8,128)(2,1)S(1)}, bf16[2,4,96,384]{3,2,1,0:T(8,128)(2,1)S(1)}, u32[]{:S(2)}, u32[]{:S(2)}) collective-permute-start(bf16[2,4,96,384]{3,2,1,0:T(8,128)(2,1)S(1)} %copy-done.19), channel_id=1, source_target_pairs={{0,3},{1,0},{2,1},{3,2},{4,7},{5,4},{6,5},{7,6},{8,11},{9,8},{10,9... | collective-permute-start | bytes 1769480 | tf_op jit(solution)/shard_map/ppermute | solution.py:355
  156.1 65.8 %collective-permute-start.11 = (bf16[2,4,96,384]{3,2,1,0:T(8,128)(2,1)S(1)}, bf16[2,4,96,384]{3,2,1,0:T(8,128)(2,1)S(1)}, u32[]{:S(2)}, u32[]{:S(2)}) collective-permute-start(bf16[2,4,96,384]{3,2,1,0:T(8,128)(2,1)S(1)} %copy-done.16), channel_id=1, source_target_pairs={{0,2},{1,3},{2,0},{3,1},{4,6},{5,7},{6,4},{7,5},{8,10},{9,11},{10,... | collective-permute-start | bytes 1769480 | tf_op jit(solution)/shard_map/ppermute | solution.py:355
  169.8 9.3 %copy-start.12 = (bf16[2,4,96,384]{3,2,1,0:T(8,128)(2,1)}, bf16[2,4,96,384]{3,2,1,0:T(8,128)(2,1)S(1)}, u32[]{:S(2)}) copy-start(bf16[2,4,96,384]{3,2,1,0:T(8,128)(2,1)S(1)} %collective-permute-done.6.refs_3_) | copy-start | bytes 1769476
  179.1 71.0 %collective-permute-start.8 = (bf16[2,4,96,384]{3,2,1,0:T(8,128)(2,1)}, bf16[2,4,96,384]{3,2,1,0:T(8,128)(2,1)S(1)}, u32[]{:S(2)}, u32[]{:S(2)}) collective-permute-start(bf16[2,4,96,384]{3,2,1,0:T(8,128)(2,1)} %get-tuple-element.92), channel_id=1, source_target_pairs={{0,1},{1,2},{2,3},{3,0},{4,5},{5,6},{6,7},{7,4},{8,9},{9,10},{10,1... | collective-permute-start | bytes 1769480 | tf_op jit(solution)/shard_map/ppermute | solution.py:355
  192.7 57.4 %collective-permute-start.9 = (bf16[2,4,96,384]{3,2,1,0:T(8,128)(2,1)}, bf16[2,4,96,384]{3,2,1,0:T(8,128)(2,1)S(1)}, u32[]{:S(2)}, u32[]{:S(2)}) collective-permute-start(bf16[2,4,96,384]{3,2,1,0:T(8,128)(2,1)} %get-tuple-element.93), channel_id=1, source_target_pairs={{0,2},{1,3},{2,0},{3,1},{4,6},{5,7},{6,4},{7,5},{8,10},{9,11},{10,... | collective-permute-start | bytes 1769480 | tf_op jit(solution)/shard_map/ppermute | solution.py:355
  192.7 57.4 %collective-permute-start.10 = (bf16[2,4,96,384]{3,2,1,0:T(8,128)(2,1)}, bf16[2,4,96,384]{3,2,1,0:T(8,128)(2,1)S(1)}, u32[]{:S(2)}, u32[]{:S(2)}) collective-permute-start(bf16[2,4,96,384]{3,2,1,0:T(8,128)(2,1)} %get-tuple-element.94), channel_id=1, source_target_pairs={{0,3},{1,0},{2,1},{3,2},{4,7},{5,4},{6,5},{7,6},{8,11},{9,8},{10,9... | collective-permute-start | bytes 1769480 | tf_op jit(solution)/shard_map/ppermute | solution.py:355
  219.3 28.8 %all-to-all-start.4 = ((f32[32,1,256]{2,1,0:T(1,128)}), f32[32,1,256]{2,1,0:T(1,128)S(1)}, u32[]{:S(2)}, u32[]{:S(2)}) async-start(f32[32,1,256]{2,1,0:T(1,128)} %reshape.110), calls=%async_computation.4 | async-start | bytes 65536 | tf_op jit(solution)/shard_map/all_to_all | solution.py:546
  250.1 1.2 copy-start.11
  (5 other events, 4.3 us)

commit v4 on v3

--- a/solution.py
+++ b/solution.py
@@ -10,7 +10,6 @@
 NX = 384
 NY = 384
 LANES = 128
-STEP = 2
 UNIT = 48
 
 width_cells = 1.5
@@ -37,6 +36,10 @@
 
 def dot(left, right):
     return jnp.dot(left, right, preferred_element_type=jnp.float32)
+
+
+def step_of(count):
+    return 1 if count % 2 else 2
 
 
 def lasting(microseconds):
@@ -56,7 +59,7 @@
             for p in range(planes):
                 held[p * halves + h, i] = split[p]
     for s, message in enumerate(messages):
-        message[0] = held[lax.rem(place[0] + s, groups)]
+        message[0] = held[place[0] ^ s]
 
 
 def pack(waves, place, first, count, rows, groups):
@@ -65,18 +68,18 @@
     own = waves.shape[1] // halves
     return pl.pallas_call(
         pack_body,
-        grid=(2, count // STEP),
+        grid=(2, 1),
         in_specs=[pl.BlockSpec(memory_space=pltpu.SMEM)]
         + [
             pl.BlockSpec(
-                (1, STEP, planes, rows * NY),
-                functools.partial(block_at, (h * own + first) // STEP),
+                (1, count, planes, rows * NY),
+                functools.partial(block_at, (h * own + first) // count),
             )
             for h in range(halves)
         ],
-        out_specs=[pl.BlockSpec((1, STEP, rows, NY), lambda c, n: (c, n, 0, 0))] * groups,
+        out_specs=[pl.BlockSpec((1, count, rows, NY), lambda c, n: (c, n, 0, 0))] * groups,
         out_shape=[jax.ShapeDtypeStruct((2, count, rows, NY), jnp.bfloat16)] * groups,
-        scratch_shapes=[pltpu.VMEM((groups, STEP, rows, NY), jnp.bfloat16)],
+        scratch_shapes=[pltpu.VMEM((groups, count, rows, NY), jnp.bfloat16)],
         compiler_params=pltpu.CompilerParams(vmem_limit_bytes=56 << 20),
         cost_estimate=lasting(0.01),
         name="pack_planes",
@@ -167,7 +170,7 @@
     messages, o_ref, held = refs[:groups], refs[-2], refs[-1]
     halves, planes, count, rows, _ = held.shape
     for s, message in enumerate(messages):
-        source = lax.rem(place[0] + groups - s, groups)
+        source = place[0] ^ s
         held[lax.rem(source, halves), source // halves] = message[0]
     half = pl.program_id(1)
     for i in range(count):
@@ -178,9 +181,10 @@
     groups = len(messages)
     _, count, rows, _ = messages[0].shape
     halves = groups // planes
+    step = step_of(count)
     own = bands // halves
     in_specs = [pl.BlockSpec(memory_space=pltpu.SMEM)] + [
-        pl.BlockSpec((1, STEP, rows, NY), lambda c, h, n: (c, n, 0, 0))
+        pl.BlockSpec((1, step, rows, NY), lambda c, h, n: (c, n, 0, 0))
     ] * groups
     operands = [place, *messages]
     aliases = {}
@@ -190,13 +194,13 @@
         aliases = {groups + 1: 0}
     return pl.pallas_call(
         functools.partial(unpack_body, groups),
-        grid=(2, halves, count // STEP),
+        grid=(2, halves, count // step),
         in_specs=in_specs,
         out_specs=pl.BlockSpec(
-            (1, STEP, planes, rows * NY), lambda c, h, n: (c, (h * own + first) // STEP + n, 0, 0)
+            (1, step, planes, rows * NY), lambda c, h, n: (c, (h * own + first) // step + n, 0, 0)
         ),
         out_shape=jax.ShapeDtypeStruct((2, bands, planes, rows * NY), jnp.bfloat16),
-        scratch_shapes=[pltpu.VMEM((halves, planes, STEP, rows, NY), jnp.bfloat16)],
+        scratch_shapes=[pltpu.VMEM((halves, planes, step, rows, NY), jnp.bfloat16)],
         input_output_aliases=aliases,
         compiler_params=pltpu.CompilerParams(vmem_limit_bytes=56 << 20),
         cost_estimate=lasting(1.2 * count),
@@ -207,8 +211,8 @@
 def forward_body(groups, place, *refs):
     messages, (f_ref, b_ref, s_ref, held) = refs[:groups], refs[groups:]
     for s, message in enumerate(messages):
-        held[lax.rem(place[0] + groups - s, groups)] = message[...]
-    for i in range(STEP):
+        held[place[0] ^ s] = message[...]
+    for i in range(held.shape[2]):
         parts = [held[:, c, i].reshape(NX, NY) for c in range(2)]
         first = dot(jnp.concatenate(parts, axis=1), f_ref[...]).astype(jnp.bfloat16)
         first = jnp.concatenate([first[:, :NY], first[:, NY:]], axis=0)
@@ -220,16 +224,17 @@
 def forward(messages, place, forth, back):
     groups = len(messages)
     _, bands, rows, _ = messages[0].shape
+    step = step_of(bands)
     square = pl.BlockSpec((2 * NX, 2 * NX), lambda n: (0, 0))
     return pl.pallas_call(
         functools.partial(forward_body, groups),
-        grid=(bands // STEP,),
+        grid=(bands // step,),
         in_specs=[pl.BlockSpec(memory_space=pltpu.SMEM)]
-        + [pl.BlockSpec((2, STEP, rows, NY), lambda n: (0, n, 0, 0))] * groups
+        + [pl.BlockSpec((2, step, rows, NY), lambda n: (0, n, 0, 0))] * groups
         + [square, square],
-        out_specs=pl.BlockSpec((STEP, 2, NX, NY), lambda n: (n, 0, 0, 0)),
+        out_specs=pl.BlockSpec((step, 2, NX, NY), lambda n: (n, 0, 0, 0)),
         out_shape=jax.ShapeDtypeStruct((bands, 2, NX, NY), jnp.bfloat16),
-        scratch_shapes=[pltpu.VMEM((groups, 2, STEP, rows, NY), jnp.bfloat16)],
+        scratch_shapes=[pltpu.VMEM((groups, 2, step, rows, NY), jnp.bfloat16)],
         compiler_params=pltpu.CompilerParams(vmem_limit_bytes=56 << 20),
         cost_estimate=lasting(0.01),
         name="forward",
@@ -245,8 +250,8 @@
     freq_y = frequency(lax.broadcasted_iota(jnp.int32, (1, NY), 1), NY)
     kinetic = 2.0 * (freq_x * freq_x / (NX * NX) + freq_y * freq_y / (NY * NY))
     for s, message in enumerate(messages):
-        held[lax.rem(place[0] + groups - s, groups)] = message[...]
-    for i in range(STEP):
+        held[place[0] ^ s] = message[...]
+    for i in range(held.shape[2]):
         weighted = jnp.concatenate(
             [v_ref[...] * s_ref[i, c].astype(jnp.float32) for c in range(2)], axis=0
         ).astype(jnp.bfloat16)
@@ -257,28 +262,29 @@
             applied = kinetic * wide + recip[:, c * NY : (c + 1) * NY]
             held[:, c, i] = applied.astype(jnp.bfloat16).reshape(groups, rows, NY)
     for s, result in enumerate(results):
-        result[...] = held[lax.rem(place[0] + s, groups)]
+        result[...] = held[place[0] ^ s]
 
 
 def inverse(messages, base, bands, place, in_space, potential, forth, back):
     groups = len(messages)
     rows = messages[0].shape[2]
     shape = (2, bands, rows, NY)
+    step = 1 if base % 2 else step_of(bands)
     square = pl.BlockSpec((2 * NX, 2 * NX), lambda n: (0, 0))
     return pl.pallas_call(
         functools.partial(inverse_body, groups),
-        grid=(bands // STEP,),
+        grid=(bands // step,),
         in_specs=[pl.BlockSpec(memory_space=pltpu.SMEM)]
-        + [pl.BlockSpec((2, STEP, rows, NY), lambda n: (0, base // STEP + n, 0, 0))] * groups
+        + [pl.BlockSpec((2, step, rows, NY), lambda n: (0, base // step + n, 0, 0))] * groups
         + [
-            pl.BlockSpec((STEP, 2, NX, NY), lambda n: (base // STEP + n, 0, 0, 0)),
+            pl.BlockSpec((step, 2, NX, NY), lambda n: (base // step + n, 0, 0, 0)),
             pl.BlockSpec((NX, NY), lambda n: (0, 0)),
             square,
             square,
         ],
-        out_specs=[pl.BlockSpec((2, STEP, rows, NY), lambda n: (0, n, 0, 0))] * groups,
+        out_specs=[pl.BlockSpec((2, step, rows, NY), lambda n: (0, n, 0, 0))] * groups,
         out_shape=[jax.ShapeDtypeStruct(shape, jnp.bfloat16)] * groups,
-        scratch_shapes=[pltpu.VMEM((groups, 2, STEP, rows, NY), jnp.bfloat16)],
+        scratch_shapes=[pltpu.VMEM((groups, 2, step, rows, NY), jnp.bfloat16)],
         compiler_params=pltpu.CompilerParams(vmem_limit_bytes=56 << 20),
         cost_estimate=lasting(0.01),
         name="inverse",
@@ -352,7 +358,7 @@
 def shifted(messages):
     groups = len(messages)
     return [
-        lax.ppermute(message, "ga", [(i, (i + s) % groups) for i in range(groups)]) if s else message
+        lax.ppermute(message, "ga", [(i, i ^ s) for i in range(groups)]) if s else message
         for s, message in enumerate(messages)
     ]
 
@@ -503,7 +509,8 @@
     returned = [shifted(result)]
     in_space.append(forward(arrived[1], place, forth, back))
     mixed = mix_space(in_space[1], 1, mixed, shares)
-    mixed, returned[0][1] = lax.optimization_barrier((mixed, returned[0][1]))
+    middle = ga_count // 2
+    mixed, returned[0][middle] = lax.optimization_barrier((mixed, returned[0][middle]))
     if halves > 1:
         mixed = mixed.reshape(band_groups, halves, -1, NY)
         mixed = lax.all_to_all(mixed, "ga", 1, 1, axis_index_groups=pairs, tiled=True)
@@ -529,11 +536,13 @@
     kinetic = jnp.broadcast_to(kinetic[None], (planes, share, NY)).reshape(planes * share, NY)
 
     scale = 1.0 / (planes * NX * NY)
+    applied_waves = unpack(returned[0], place, None, 0, bands, planes)
+    grams = overlap(met_waves[:, None], kinetic, per, scale)
     spectrum = (in_space[1], potential, forth, back)
-    place, returned[0][-1] = lax.optimization_barrier((place, returned[0][-1]))
-    returned.append(shifted(inverse(arrived[1], 0, half, place, *spectrum)))
-    grams = overlap(met_waves[:, None], kinetic, per, scale)
-    applied_waves = unpack(returned[0], place, None, 0, bands, planes)
+    returned.append(shifted(inverse(arrived[1], 0, half - 1, place, *spectrum)))
+    grams, place = lax.optimization_barrier((grams, place))
+    returned.append(shifted(inverse(arrived[1], half - 1, 1, place, *spectrum)))
+    grams, applied_waves = lax.optimization_barrier((grams, applied_waves))
     full_matrix = overlap(
         met_space, space_weights, per // met_space.shape[1], scale, grams
     )
@@ -545,8 +554,8 @@
     )
     subspace = lax.all_to_all(blocks, ("band", "ga"), 0, 0, tiled=True).sum(0)
 
-    place, subspace = lax.optimization_barrier((place, subspace))
     applied_waves = unpack(returned[1], place, applied_waves, half, bands, planes)
+    applied_waves = unpack(returned[2], place, applied_waves, own_bands - 1, bands, planes)
     return (applied_waves, subspace)
 
 

time: 257 us -> 249 us (0.969)
  waiting for transfers between devices: 70.9 us -> 57.3 us
  Pallas kernels: 102 us -> 106 us
  starting transfers between devices: 59.9 us -> 62.5 us
    ppermute x12 -> x15, waiting for transfers between devices: 23.9 us -> 50.1 us  [shifted(): lax.ppermute(message, 'ga', [(i, i ^ s) for i in range(groups)])]
    all_to_all x1, waiting for transfers between devices: 20.7 us -> 1.38 us  [shards(): subspace = lax.all_to_all(blocks, ('band', 'ga'), 0, 0, tiled=True).sum(0)]
    all_to_all x1, waiting for transfers between devices: 12.2 us -> 2.56 us  [shards(): met_waves = lax.all_to_all(mixed, 'band', 0, 0, tiled=True)]
    ppermute x12 -> x15, starting transfers between devices: 28.4 us -> 37.3 us  [shifted(): lax.ppermute(message, 'ga', [(i, i ^ s) for i in range(groups)])]
    all_to_all x1, starting transfers between devices: 12 us -> 3.94 us  [shards(): potential = lax.all_to_all(copies, 'band', 0, 0, tiled=True).reshape(NX, NY)]
    all_to_all x1, waiting for transfers between devices: 10.4 us -> 3.29 us  [shards(): potential = lax.all_to_all(copies, 'band', 0, 0, tiled=True).reshape(NX, NY)]
    all_to_all x1, waiting for transfers between devices: 3.67 us -> 0.01 us  [shards(): met_space = lax.all_to_all(mixed, 'band', 0, 0, tiled=True)]
    pallas_call x2 -> x3, Pallas kernels: 9.27 us -> 11.9 us  [unpack(): pl.pallas_call(functools.partial(unpack_body, groups), grid=(2, halves, c...]
  transfers between devices with their start and end apart: 17 -> 20, of which waited for: 7 -> 8; matrix products, arithmetic and copies ran while one was open for 6% -> 5% of each run, Pallas kernels for 38% -> 43%
where the time goes in v4:
time: 249 us; the launch traced here: 248 us
  Pallas kernels  106 us (43%)
  starting transfers between devices  62.5 us (25%)
  waiting for transfers between devices  57.3 us (23%)
  local copies, waits for them, and re-layouts  10.9 us (4%)
  other arithmetic  9.79 us (4%)
    ppermute x15, waiting for transfers between devices, shifted(): lax.ppermute(message, 'ga', [(i, i ^ s) for i in range(groups)])  50.1 us
    ppermute x15, starting transfers between devices, shifted(): lax.ppermute(message, 'ga', [(i, i ^ s) for i in range(groups)])  37.3 us
    pallas_call x3, Pallas kernels, inverse(): pl.pallas_call(functools.partial(inverse_body, groups), grid=(bands // st...  21.2 us
    pallas_call x2, Pallas kernels, overlap(): pl.pallas_call(functools.partial(overlap_body, scale, per), in_specs=[who...  17.9 us
    pallas_call x2, Pallas kernels, forward(): pl.pallas_call(functools.partial(forward_body, groups), grid=(bands // st...  16.3 us
    pallas_call x1, Pallas kernels, own_share(): pl.pallas_call(functools.partial(charges_body, planes, slab_rows), in_spe...  12 us
    pallas_call x3, Pallas kernels, unpack(): pl.pallas_call(functools.partial(unpack_body, groups), grid=(2, halves, c...  11.9 us
    pallas_call x1, Pallas kernels, mix_waves(): pl.pallas_call(mix_waves_body, grid=(shares,), in_specs=[pl.BlockSpec((2,...  10 us
  transfers between devices with their start and end apart: 20, of which 8 were waited for; matrix products, arithmetic and copies ran while one was open for 5% of the time, Pallas kernels for 43%

profile of v4, /device:TPU:0, one launch (start us, length us, event | category | flops | bytes accessed | tf_op | source)
XLA Modules:
  0.0 247.5 jit_solution(5407148406044213694)
XLA Ops:
  3.4 7.3 %all-to-all-start = ((f32[32,8,256]{2,1,0:T(8,128)}), f32[32,8,256]{2,1,0:T(8,128)S(1)}, u32[]{:S(2)}, u32[]{:S(2)}) async-start(f32[32,8,256]{2,1,0:T(8,128)} %pad_maximum_fusion.4), calls=%async_computation | async-start | bytes 524288 | tf_op jit(solution)/shard_map/all_to_all | solution.py:481
  10.7 3.5 %pack_planes.2 = (bf16[2,4,96,384]{3,2,1,0:T(8,128)(2,1)}, bf16[2,4,96,384]{3,2,1,0:T(8,128)(2,1)}, bf16[2,4,96,384]{3,2,1,0:T(8,128)(2,1)}, bf16[2,4,96,384]{3,2,1,0:T(8,128)(2,1)}) custom-call(s32[1]{0:T(128)} %bitcast.place, bf16[2,8,4,36864]{3,2,1,0:T(4,128)(2,1)} %w_ref.1), custom_call_target="tpu_custom_call" | custom-call | bytes 36900 | tf_op jit(solution)/shard_map/pack_planes/pallas_call | solution.py:69
  15.9 2.4 collective-permute-start.1
  18.6 3.5 %pack_planes.3 = (bf16[2,4,96,384]{3,2,1,0:T(8,128)(2,1)}, bf16[2,4,96,384]{3,2,1,0:T(8,128)(2,1)}, bf16[2,4,96,384]{3,2,1,0:T(8,128)(2,1)}, bf16[2,4,96,384]{3,2,1,0:T(8,128)(2,1)}) custom-call(s32[1]{0:T(128)} %bitcast.place, bf16[2,8,4,36864]{3,2,1,0:T(4,128)(2,1)} %w_ref.1), custom_call_target="tpu_custom_call" | custom-call | bytes 36900 | tf_op jit(solution)/shard_map/pack_planes/pallas_call | solution.py:69
  22.1 10.0 %mix_waves.1 = bf16[8,768,384]{2,1,0:T(8,128)(2,1)} custom-call(bf16[2,8,4,36864]{3,2,1,0:T(4,128)(2,1)} %w_ref.1), custom_call_target="tpu_custom_call" | custom-call | bytes 36900 | tf_op jit(solution)/shard_map/mix_waves/pallas_call | solution.py:112
  33.8 12.0 %charge_potential.1.w_ref = f32[48,384]{1,0:T(8,128)} custom-call(s32[2]{0:T(128)} %pad_add_fusion.place, f32[32,8,256]{2,1,0:T(8,128)} %copy-done.7, f32[48,384]{1,0:T(8,128)} %reshape.105.i_ref), custom_call_target="tpu_custom_call" | custom-call | bytes 36900 | tf_op jit(solution)/shard_map/charge_potential/pallas_call | solution.py:444
  47.5 3.9 %all-to-all-start.1 = ((f32[8,48,384]{2,1,0:T(8,128)}), f32[8,48,384]{2,1,0:T(8,128)S(1)}, u32[]{:S(2)}, u32[]{:S(2)}) async-start(f32[8,48,384]{2,1,0:T(8,128)} %broadcast_in_dim.15), calls=%async_computation.1 | async-start | bytes 1179648 | tf_op jit(solution)/shard_map/all_to_all | solution.py:486
  51.4 7.1 %collective-permute-done.1.refs_2_ = bf16[2,4,96,384]{3,2,1,0:T(8,128)(2,1)S(1)} collective-permute-done((bf16[2,4,96,384]{3,2,1,0:T(8,128)(2,1)}, bf16[2,4,96,384]{3,2,1,0:T(8,128)(2,1)S(1)}, u32[]{:S(2)}, u32[]{:S(2)}) %collective-permute-start.1) | collective-permute-done | bytes 589856 | tf_op jit(solution)/shard_map/ppermute | solution.py:361
  58.6 3.3 %all-to-all-done.1 = f32[8,48,384]{2,1,0:T(8,128)S(1)} async-done(((f32[8,48,384]{2,1,0:T(8,128)}), f32[8,48,384]{2,1,0:T(8,128)S(1)}, u32[]{:S(2)}, u32[]{:S(2)}) %all-to-all-start.1) | async-done | bytes 589856 | tf_op jit(solution)/shard_map/all_to_all | solution.py:486
  62.7 4.8 %all-to-all-start.2 = ((bf16[8,768,384]{2,1,0:T(8,128)(2,1)}), bf16[8,768,384]{2,1,0:T(8,128)(2,1)}, u32[]{:S(2)}, u32[]{:S(2)}) async-start(bf16[8,768,384]{2,1,0:T(8,128)(2,1)} %mix_waves.1), calls=%async_computation.2 | async-start | bytes 9437184 | tf_op jit(solution)/shard_map/all_to_all | solution.py:493
  67.5 9.6 %collective-permute-start.3 = (bf16[2,4,96,384]{3,2,1,0:T(8,128)(2,1)}, bf16[2,4,96,384]{3,2,1,0:T(8,128)(2,1)S(1)}, u32[]{:S(2)}, u32[]{:S(2)}) collective-permute-start(bf16[2,4,96,384]{3,2,1,0:T(8,128)(2,1)} %get-tuple-element.70), channel_id=1, source_target_pairs={{0,1},{1,0},{2,3},{3,2},{4,5},{5,4},{6,7},{7,6},{8,9},{9,8},{10,11... | collective-permute-start | bytes 1769480 | tf_op jit(solution)/shard_map/ppermute | solution.py:361
  79.6 2.6 %fusion.7 = bf16[384,384]{1,0:T(8,128)(2,1)S(1)} fusion(s32[384]{0:T(512)S(1)} %iota.13), kind=kLoop, calls=%fused_computation.18 | loop fusion | flops 2064384 | bytes 296448 | tf_op jit(solution)/shard_map/neg | solution.py:496
  82.1 2.9 %multiply_convert_fusion = (bf16[384,384]{1,0:T(8,128)(2,1)S(1)}, bf16[384,384]{1,0:T(8,128)(2,1)S(1)}) fusion(s32[384]{0:T(512)S(1)} %iota.13), kind=kLoop, calls=%fused_computation.9 | loop fusion | flops 1916928 | bytes 591360 | tf_op jit(solution)/shard_map/convert_element_type | solution.py:25
  86.5 8.1 %forward.2.refs_4_.s_ref = bf16[4,2,384,384]{3,2,1,0:T(8,128)(2,1)} custom-call(s32[1]{0:T(128)} %bitcast.place, bf16[2,4,96,384]{3,2,1,0:T(8,128)(2,1)} %get-tuple-element.74.refs_0_, bf16[2,4,96,384]{3,2,1,0:T(8,128)(2,1)} %copy-done.4, bf16[2,4,96,384]{3,2,1,0:T(8,128)(2,1)} %copy-done.5, bf16[2,4,96,384]{3,2,1,0:T(8,128)(2,1)} %copy-done.6, ...), custom_call_target="tpu_custom_call" | custom-call | bytes 36900 | tf_op jit(solution)/shard_map/forward/pallas_call | solution.py:229
  94.7 4.9 %mix_space.2.refs_0_ = bf16[8,2,384,384]{3,2,1,0:T(8,128)(2,1)} custom-call(bf16[4,2,384,384]{3,2,1,0:T(8,128)(2,1)} %forward.2.refs_4_.s_ref), custom_call_target="tpu_custom_call" | custom-call | bytes 36900 | tf_op jit(solution)/shard_map/mix_space/pallas_call | solution.py:156
  99.5 8.9 %inverse.3 = (bf16[2,4,96,384]{3,2,1,0:T(8,128)(2,1)}, bf16[2,4,96,384]{3,2,1,0:T(8,128)(2,1)}, bf16[2,4,96,384]{3,2,1,0:T(8,128)(2,1)}, bf16[2,4,96,384]{3,2,1,0:T(8,128)(2,1)}) custom-call(s32[1]{0:T(128)} %bitcast.place, bf16[2,4,96,384]{3,2,1,0:T(8,128)(2,1)} %get-tuple-element.74.refs_0_, bf16[2,4,96,384]{3,2,1,0:T(8,128)(2,1)} %copy-done.4, ...), custom_call_target="tpu_custom_call" | custom-call | bytes 36900 | tf_op jit(solution)/shard_map/inverse/pallas_call | solution.py:274
  108.5 11.0 %collective-permute-done.4.refs_2_ = bf16[2,4,96,384]{3,2,1,0:T(8,128)(2,1)S(1)} collective-permute-done((bf16[2,4,96,384]{3,2,1,0:T(8,128)(2,1)S(1)}, bf16[2,4,96,384]{3,2,1,0:T(8,128)(2,1)S(1)}, u32[]{:S(2)}, u32[]{:S(2)}) %collective-permute-start.4) | collective-permute-done | bytes 589856 | tf_op jit(solution)/shard_map/ppermute | solution.py:361
  119.5 2.6 %all-to-all-done.2 = bf16[8,768,384]{2,1,0:T(8,128)(2,1)} async-done(((bf16[8,768,384]{2,1,0:T(8,128)(2,1)}), bf16[8,768,384]{2,1,0:T(8,128)(2,1)}, u32[]{:S(2)}, u32[]{:S(2)}) %all-to-all-start.2) | async-done | bytes 4718624 | tf_op jit(solution)/shard_map/all_to_all | solution.py:493
  122.1 10.0 %collective-permute-start.13 = (bf16[2,4,96,384]{3,2,1,0:T(8,128)(2,1)}, bf16[2,4,96,384]{3,2,1,0:T(8,128)(2,1)S(1)}, u32[]{:S(2)}, u32[]{:S(2)}) collective-permute-start(bf16[2,4,96,384]{3,2,1,0:T(8,128)(2,1)} %get-tuple-element.102), channel_id=1, source_target_pairs={{0,2},{1,3},{2,0},{3,1},{4,6},{5,7},{6,4},{7,5},{8,10},{9,11},{10,... | collective-permute-start | bytes 1769480 | tf_op jit(solution)/shard_map/ppermute | solution.py:361
  132.0 8.2 %forward.3.refs_4_.s_ref = bf16[4,2,384,384]{3,2,1,0:T(8,128)(2,1)} custom-call(s32[1]{0:T(128)} %bitcast.place, bf16[2,4,96,384]{3,2,1,0:T(8,128)(2,1)} %get-tuple-element.86.refs_0_, bf16[2,4,96,384]{3,2,1,0:T(8,128)(2,1)} %copy-done.1, bf16[2,4,96,384]{3,2,1,0:T(8,128)(2,1)} %copy-done.2, bf16[2,4,96,384]{3,2,1,0:T(8,128)(2,1)} %copy-done.3, ...), custom_call_target="tpu_custom_call" | custom-call | bytes 36900 | tf_op jit(solution)/shard_map/forward/pallas_call | solution.py:229
  140.2 4.8 %mix_space.3 = bf16[8,2,384,384]{3,2,1,0:T(8,128)(2,1)} custom-call(bf16[4,2,384,384]{3,2,1,0:T(8,128)(2,1)} %forward.3.refs_4_.s_ref, bf16[8,2,384,384]{3,2,1,0:T(8,128)(2,1)} %mix_space.2.refs_0_), custom_call_target="tpu_custom_call", output_to_operand_aliasing={{}: (1, {})} | custom-call | bytes 36900 | tf_op jit(solution)/shard_map/mix_space/pallas_call | solution.py:156
  145.0 12.5 %collective-permute-done.13.refs_2_ = bf16[2,4,96,384]{3,2,1,0:T(8,128)(2,1)S(1)} collective-permute-done((bf16[2,4,96,384]{3,2,1,0:T(8,128)(2,1)}, bf16[2,4,96,384]{3,2,1,0:T(8,128)(2,1)S(1)}, u32[]{:S(2)}, u32[]{:S(2)}) %collective-permute-start.13) | collective-permute-done | bytes 589856 | tf_op jit(solution)/shard_map/ppermute | solution.py:361
  158.3 4.8 %all-to-all-start.3 = ((bf16[8,2,384,384]{3,2,1,0:T(8,128)(2,1)}), bf16[8,2,384,384]{3,2,1,0:T(8,128)(2,1)}, u32[]{:S(2)}, u32[]{:S(2)}) async-start(bf16[8,2,384,384]{3,2,1,0:T(8,128)(2,1)} %mix_space.3), calls=%async_computation.3 | async-start | bytes 9437184 | tf_op jit(solution)/shard_map/all_to_all | solution.py:517
  165.2 7.7 %inverse.5 = (bf16[2,3,96,384]{3,2,1,0:T(8,128)(2,1)}, bf16[2,3,96,384]{3,2,1,0:T(8,128)(2,1)}, bf16[2,3,96,384]{3,2,1,0:T(8,128)(2,1)}, bf16[2,3,96,384]{3,2,1,0:T(8,128)(2,1)}) custom-call(s32[1]{0:T(128)} %bitcast.place, bf16[2,4,96,384]{3,2,1,0:T(8,128)(2,1)} %get-tuple-element.86.refs_0_, bf16[2,4,96,384]{3,2,1,0:T(8,128)(2,1)} %copy-done.1, ...), custom_call_target="tpu_custom_call" | custom-call | bytes 36900 | tf_op jit(solution)/shard_map/inverse/pallas_call | solution.py:274
  178.1 8.9 %overlap.2.refs_0_ = f32[2,64,64]{2,1,0:T(8,128)} custom-call(bf16[8,1,768,384]{3,2,1,0:T(8,128)(2,1)} %bitcast.9.z_ref, f32[48,384]{1,0:T(8,128)} %reshape.107.w_ref), custom_call_target="tpu_custom_call" | custom-call | bytes 29520000 | tf_op jit(solution)/shard_map/overlap/pallas_call | solution.py:346
  187.0 4.6 %inverse.4 = (bf16[2,1,96,384]{3,2,1,0:T(8,128)(2,1)}, bf16[2,1,96,384]{3,2,1,0:T(8,128)(2,1)}, bf16[2,1,96,384]{3,2,1,0:T(8,128)(2,1)}, bf16[2,1,96,384]{3,2,1,0:T(8,128)(2,1)}) custom-call(s32[1]{0:T(128)} %bitcast.place, bf16[2,4,96,384]{3,2,1,0:T(8,128)(2,1)} %get-tuple-element.86.refs_0_, bf16[2,4,96,384]{3,2,1,0:T(8,128)(2,1)} %copy-done.1, ...), custom_call_target="tpu_custom_call" | custom-call | bytes 36900 | tf_op jit(solution)/shard_map/inverse/pallas_call | solution.py:274
  191.6 17.9 %collective-permute-done.9.refs_1_ = bf16[2,3,96,384]{3,2,1,0:T(8,128)(2,1)S(1)} collective-permute-done((bf16[2,3,96,384]{3,2,1,0:T(8,128)(2,1)}, bf16[2,3,96,384]{3,2,1,0:T(8,128)(2,1)S(1)}, u32[]{:S(2)}, u32[]{:S(2)}) %collective-permute-start.9) | collective-permute-done | bytes 442400 | tf_op jit(solution)/shard_map/ppermute | solution.py:361
  209.5 2.5 collective-permute-start.7
  213.9 4.6 %unpack_planes.3.refs_4_ = bf16[2,8,4,36864]{3,2,1,0:T(4,128)(2,1)} custom-call(s32[1]{0:T(128)} %bitcast.place, bf16[2,4,96,384]{3,2,1,0:T(8,128)(2,1)} %get-tuple-element.99.refs_0_, bf16[2,4,96,384]{3,2,1,0:T(8,128)(2,1)} %copy-done.9, bf16[2,4,96,384]{3,2,1,0:T(8,128)(2,1)} %copy-done.8, bf16[2,4,96,384]{3,2,1,0:T(8,128)(2,1)} %copy-done.10), custom_call_target="tpu_custom_call" | custom-call | bytes 17712000 | tf_op jit(solution)/shard_map/unpack_planes/pallas_call | solution.py:195
  218.5 9.0 %overlap.3 = f32[2,64,64]{2,1,0:T(8,128)} custom-call(bf16[8,2,384,384]{3,2,1,0:T(8,128)(2,1)} %all-to-all-done.3.z_ref, f32[48,384]{1,0:T(8,128)} %charge_potential.1.w_ref, f32[2,64,64]{2,1,0:T(8,128)} %overlap.2.refs_0_), custom_call_target="tpu_custom_call" | custom-call | bytes 29520000 | tf_op jit(solution)/shard_map/overlap/pallas_call | solution.py:346
  229.3 4.3 %all-to-all-start.4 = ((f32[32,1,256]{2,1,0:T(1,128)}), f32[32,1,256]{2,1,0:T(1,128)S(1)}, u32[]{:S(2)}, u32[]{:S(2)}) async-start(f32[32,1,256]{2,1,0:T(1,128)} %reshape.110), calls=%async_computation.4 | async-start | bytes 65536 | tf_op jit(solution)/shard_map/all_to_all | solution.py:555
  234.5 5.2 %unpack_planes.4.refs_4_ = bf16[2,8,4,36864]{3,2,1,0:T(4,128)(2,1)} custom-call(s32[1]{0:T(128)} %bitcast.place, bf16[2,3,96,384]{3,2,1,0:T(8,128)(2,1)} %get-tuple-element.94.refs_0_, bf16[2,3,96,384]{3,2,1,0:T(8,128)(2,1)} %copy-done.11, bf16[2,3,96,384]{3,2,1,0:T(8,128)(2,1)} %copy-done.12, ...), custom_call_target="tpu_custom_call", output_to_operand_aliasing={{}: (5, {})} | custom-call | bytes 13283999 | tf_op jit(solution)/shard_map/unpack_planes/pallas_call | solution.py:195
  (107 shorter events, 33.3 us)
Async XLA Ops:
  3.4 29.3 %all-to-all-start = ((f32[32,8,256]{2,1,0:T(8,128)}), f32[32,8,256]{2,1,0:T(8,128)S(1)}, u32[]{:S(2)}, u32[]{:S(2)}) async-start(f32[32,8,256]{2,1,0:T(8,128)} %pad_maximum_fusion.4), calls=%async_computation | async-start | bytes 524288 | tf_op jit(solution)/shard_map/all_to_all | solution.py:481
  14.2 37.2 %collective-permute-start = (bf16[2,4,96,384]{3,2,1,0:T(8,128)(2,1)}, bf16[2,4,96,384]{3,2,1,0:T(8,128)(2,1)S(1)}, u32[]{:S(2)}, u32[]{:S(2)}) collective-permute-start(bf16[2,4,96,384]{3,2,1,0:T(8,128)(2,1)} %get-tuple-element.56), channel_id=1, source_target_pairs={{0,1},{1,0},{2,3},{3,2},{4,5},{5,4},{6,7},{7,6},{8,9},{9,8},{10,11... | collective-permute-start | bytes 1769480 | tf_op jit(solution)/shard_map/ppermute | solution.py:361
  15.9 42.6 %collective-permute-start.1 = (bf16[2,4,96,384]{3,2,1,0:T(8,128)(2,1)}, bf16[2,4,96,384]{3,2,1,0:T(8,128)(2,1)S(1)}, u32[]{:S(2)}, u32[]{:S(2)}) collective-permute-start(bf16[2,4,96,384]{3,2,1,0:T(8,128)(2,1)} %get-tuple-element.57), channel_id=1, source_target_pairs={{0,2},{1,3},{2,0},{3,1},{4,6},{5,7},{6,4},{7,5},{8,10},{9,11},{10,... | collective-permute-start | bytes 1769480 | tf_op jit(solution)/shard_map/ppermute | solution.py:361
  18.4 40.2 %collective-permute-start.2 = (bf16[2,4,96,384]{3,2,1,0:T(8,128)(2,1)}, bf16[2,4,96,384]{3,2,1,0:T(8,128)(2,1)S(1)}, u32[]{:S(2)}, u32[]{:S(2)}) collective-permute-start(bf16[2,4,96,384]{3,2,1,0:T(8,128)(2,1)} %get-tuple-element.58), channel_id=1, source_target_pairs={{0,3},{1,2},{2,1},{3,0},{4,7},{5,6},{6,5},{7,4},{8,11},{9,10},{10,... | collective-permute-start | bytes 1769480 | tf_op jit(solution)/shard_map/ppermute | solution.py:361
  47.5 14.4 %all-to-all-start.1 = ((f32[8,48,384]{2,1,0:T(8,128)}), f32[8,48,384]{2,1,0:T(8,128)S(1)}, u32[]{:S(2)}, u32[]{:S(2)}) async-start(f32[8,48,384]{2,1,0:T(8,128)} %broadcast_in_dim.15), calls=%async_computation.1 | async-start | bytes 1179648 | tf_op jit(solution)/shard_map/all_to_all | solution.py:486
  51.4 10.5 %copy-start.4 = (bf16[2,4,96,384]{3,2,1,0:T(8,128)(2,1)}, bf16[2,4,96,384]{3,2,1,0:T(8,128)(2,1)S(1)}, u32[]{:S(2)}) copy-start(bf16[2,4,96,384]{3,2,1,0:T(8,128)(2,1)S(1)} %collective-permute-done.refs_1_) | copy-start | bytes 1769476
  58.5 3.3 %copy-start.5 = (bf16[2,4,96,384]{3,2,1,0:T(8,128)(2,1)}, bf16[2,4,96,384]{3,2,1,0:T(8,128)(2,1)S(1)}, u32[]{:S(2)}) copy-start(bf16[2,4,96,384]{3,2,1,0:T(8,128)(2,1)S(1)} %collective-permute-done.1.refs_2_) | copy-start | bytes 1769476
  58.6 3.3 %copy-start.6 = (bf16[2,4,96,384]{3,2,1,0:T(8,128)(2,1)}, bf16[2,4,96,384]{3,2,1,0:T(8,128)(2,1)S(1)}, u32[]{:S(2)}) copy-start(bf16[2,4,96,384]{3,2,1,0:T(8,128)(2,1)S(1)} %collective-permute-done.2.refs_3_) | copy-start | bytes 1769476
  61.9 15.3 %copy-start.22 = (bf16[2,4,96,384]{3,2,1,0:T(8,128)(2,1)S(1)}, bf16[2,4,96,384]{3,2,1,0:T(8,128)(2,1)}, u32[]{:S(2)}) copy-start(bf16[2,4,96,384]{3,2,1,0:T(8,128)(2,1)} %get-tuple-element.71) | copy-start | bytes 1769476
  61.9 15.7 %copy-start.21 = (bf16[2,4,96,384]{3,2,1,0:T(8,128)(2,1)S(1)}, bf16[2,4,96,384]{3,2,1,0:T(8,128)(2,1)}, u32[]{:S(2)}) copy-start(bf16[2,4,96,384]{3,2,1,0:T(8,128)(2,1)} %get-tuple-element.72) | copy-start | bytes 1769476
  62.7 59.4 %all-to-all-start.2 = ((bf16[8,768,384]{2,1,0:T(8,128)(2,1)}), bf16[8,768,384]{2,1,0:T(8,128)(2,1)}, u32[]{:S(2)}, u32[]{:S(2)}) async-start(bf16[8,768,384]{2,1,0:T(8,128)(2,1)} %mix_waves.1), calls=%async_computation.2 | async-start | bytes 9437184 | tf_op jit(solution)/shard_map/all_to_all | solution.py:493
  67.5 40.9 %collective-permute-start.3 = (bf16[2,4,96,384]{3,2,1,0:T(8,128)(2,1)}, bf16[2,4,96,384]{3,2,1,0:T(8,128)(2,1)S(1)}, u32[]{:S(2)}, u32[]{:S(2)}) collective-permute-start(bf16[2,4,96,384]{3,2,1,0:T(8,128)(2,1)} %get-tuple-element.70), channel_id=1, source_target_pairs={{0,1},{1,0},{2,3},{3,2},{4,5},{5,4},{6,7},{7,6},{8,9},{9,8},{10,11... | collective-permute-start | bytes 1769480 | tf_op jit(solution)/shard_map/ppermute | solution.py:361
  77.1 42.4 %collective-permute-start.4 = (bf16[2,4,96,384]{3,2,1,0:T(8,128)(2,1)S(1)}, bf16[2,4,96,384]{3,2,1,0:T(8,128)(2,1)S(1)}, u32[]{:S(2)}, u32[]{:S(2)}) collective-permute-start(bf16[2,4,96,384]{3,2,1,0:T(8,128)(2,1)S(1)} %copy-done.22), channel_id=1, source_target_pairs={{0,2},{1,3},{2,0},{3,1},{4,6},{5,7},{6,4},{7,5},{8,10},{9,11},{10,... | collective-permute-start | bytes 1769480 | tf_op jit(solution)/shard_map/ppermute | solution.py:361
  77.6 41.9 %collective-permute-start.5 = (bf16[2,4,96,384]{3,2,1,0:T(8,128)(2,1)S(1)}, bf16[2,4,96,384]{3,2,1,0:T(8,128)(2,1)S(1)}, u32[]{:S(2)}, u32[]{:S(2)}) collective-permute-start(bf16[2,4,96,384]{3,2,1,0:T(8,128)(2,1)S(1)} %copy-done.21), channel_id=1, source_target_pairs={{0,3},{1,2},{2,1},{3,0},{4,7},{5,6},{6,5},{7,4},{8,11},{9,10},{10,... | collective-permute-start | bytes 1769480 | tf_op jit(solution)/shard_map/ppermute | solution.py:361
  108.5 23.6 %copy-start.1 = (bf16[2,4,96,384]{3,2,1,0:T(8,128)(2,1)}, bf16[2,4,96,384]{3,2,1,0:T(8,128)(2,1)S(1)}, u32[]{:S(2)}) copy-start(bf16[2,4,96,384]{3,2,1,0:T(8,128)(2,1)S(1)} %collective-permute-done.3.refs_1_) | copy-start | bytes 1769476
  119.5 12.5 %copy-start.2 = (bf16[2,4,96,384]{3,2,1,0:T(8,128)(2,1)}, bf16[2,4,96,384]{3,2,1,0:T(8,128)(2,1)S(1)}, u32[]{:S(2)}) copy-start(bf16[2,4,96,384]{3,2,1,0:T(8,128)(2,1)S(1)} %collective-permute-done.4.refs_2_) | copy-start | bytes 1769476
  119.5 12.5 %copy-start.3 = (bf16[2,4,96,384]{3,2,1,0:T(8,128)(2,1)}, bf16[2,4,96,384]{3,2,1,0:T(8,128)(2,1)S(1)}, u32[]{:S(2)}) copy-start(bf16[2,4,96,384]{3,2,1,0:T(8,128)(2,1)S(1)} %collective-permute-done.5.refs_3_) | copy-start | bytes 1769476
  122.1 35.4 %collective-permute-start.13 = (bf16[2,4,96,384]{3,2,1,0:T(8,128)(2,1)}, bf16[2,4,96,384]{3,2,1,0:T(8,128)(2,1)S(1)}, u32[]{:S(2)}, u32[]{:S(2)}) collective-permute-start(bf16[2,4,96,384]{3,2,1,0:T(8,128)(2,1)} %get-tuple-element.102), channel_id=1, source_target_pairs={{0,2},{1,3},{2,0},{3,1},{4,6},{5,7},{6,4},{7,5},{8,10},{9,11},{10,... | collective-permute-start | bytes 1769480 | tf_op jit(solution)/shard_map/ppermute | solution.py:361
  145.0 18.2 %copy-start.20 = (bf16[2,4,96,384]{3,2,1,0:T(8,128)(2,1)S(1)}, bf16[2,4,96,384]{3,2,1,0:T(8,128)(2,1)}, u32[]{:S(2)}) copy-start(bf16[2,4,96,384]{3,2,1,0:T(8,128)(2,1)} %get-tuple-element.104) | copy-start | bytes 1769476
  158.3 60.2 %all-to-all-start.3 = ((bf16[8,2,384,384]{3,2,1,0:T(8,128)(2,1)}), bf16[8,2,384,384]{3,2,1,0:T(8,128)(2,1)}, u32[]{:S(2)}, u32[]{:S(2)}) async-start(bf16[8,2,384,384]{3,2,1,0:T(8,128)(2,1)} %mix_space.3), calls=%async_computation.3 | async-start | bytes 9437184 | tf_op jit(solution)/shard_map/all_to_all | solution.py:517
  163.1 46.3 %collective-permute-start.12 = (bf16[2,4,96,384]{3,2,1,0:T(8,128)(2,1)}, bf16[2,4,96,384]{3,2,1,0:T(8,128)(2,1)S(1)}, u32[]{:S(2)}, u32[]{:S(2)}) collective-permute-start(bf16[2,4,96,384]{3,2,1,0:T(8,128)(2,1)} %get-tuple-element.100), channel_id=1, source_target_pairs={{0,1},{1,0},{2,3},{3,2},{4,5},{5,4},{6,7},{7,6},{8,9},{9,8},{10,11... | collective-permute-start | bytes 1769480 | tf_op jit(solution)/shard_map/ppermute | solution.py:361
  163.2 48.7 %collective-permute-start.14 = (bf16[2,4,96,384]{3,2,1,0:T(8,128)(2,1)S(1)}, bf16[2,4,96,384]{3,2,1,0:T(8,128)(2,1)S(1)}, u32[]{:S(2)}, u32[]{:S(2)}) collective-permute-start(bf16[2,4,96,384]{3,2,1,0:T(8,128)(2,1)S(1)} %copy-done.20), channel_id=1, source_target_pairs={{0,3},{1,2},{2,1},{3,0},{4,7},{5,6},{6,5},{7,4},{8,11},{9,10},{10,... | collective-permute-start | bytes 1769480 | tf_op jit(solution)/shard_map/ppermute | solution.py:361
  173.0 36.5 %collective-permute-start.9 = (bf16[2,3,96,384]{3,2,1,0:T(8,128)(2,1)}, bf16[2,3,96,384]{3,2,1,0:T(8,128)(2,1)S(1)}, u32[]{:S(2)}, u32[]{:S(2)}) collective-permute-start(bf16[2,3,96,384]{3,2,1,0:T(8,128)(2,1)} %get-tuple-element.95), channel_id=1, source_target_pairs={{0,1},{1,0},{2,3},{3,2},{4,5},{5,4},{6,7},{7,6},{8,9},{9,8},{10,11... | collective-permute-start | bytes 1327112 | tf_op jit(solution)/shard_map/ppermute | solution.py:361
  174.0 59.6 %collective-permute-start.10 = (bf16[2,3,96,384]{3,2,1,0:T(8,128)(2,1)}, bf16[2,3,96,384]{3,2,1,0:T(8,128)(2,1)S(1)}, u32[]{:S(2)}, u32[]{:S(2)}) collective-permute-start(bf16[2,3,96,384]{3,2,1,0:T(8,128)(2,1)} %get-tuple-element.96), channel_id=1, source_target_pairs={{0,2},{1,3},{2,0},{3,1},{4,6},{5,7},{6,4},{7,5},{8,10},{9,11},{10,... | collective-permute-start | bytes 1327112 | tf_op jit(solution)/shard_map/ppermute | solution.py:361
  175.4 58.2 %collective-permute-start.11 = (bf16[2,3,96,384]{3,2,1,0:T(8,128)(2,1)}, bf16[2,3,96,384]{3,2,1,0:T(8,128)(2,1)S(1)}, u32[]{:S(2)}, u32[]{:S(2)}) collective-permute-start(bf16[2,3,96,384]{3,2,1,0:T(8,128)(2,1)} %get-tuple-element.97), channel_id=1, source_target_pairs={{0,3},{1,2},{2,1},{3,0},{4,7},{5,6},{6,5},{7,4},{8,11},{9,10},{10,... | collective-permute-start | bytes 1327112 | tf_op jit(solution)/shard_map/ppermute | solution.py:361
  209.4 24.2 %copy-start.11 = (bf16[2,3,96,384]{3,2,1,0:T(8,128)(2,1)}, bf16[2,3,96,384]{3,2,1,0:T(8,128)(2,1)S(1)}, u32[]{:S(2)}) copy-start(bf16[2,3,96,384]{3,2,1,0:T(8,128)(2,1)S(1)} %collective-permute-done.9.refs_1_) | copy-start | bytes 1327108
  209.4 30.3 %collective-permute-start.6 = (bf16[2,1,96,384]{3,2,1,0:T(8,128)(2,1)}, bf16[2,1,96,384]{3,2,1,0:T(8,128)(2,1)S(1)}, u32[]{:S(2)}, u32[]{:S(2)}) collective-permute-start(bf16[2,1,96,384]{3,2,1,0:T(8,128)(2,1)} %get-tuple-element.91), channel_id=1, source_target_pairs={{0,1},{1,0},{2,3},{3,2},{4,5},{5,4},{6,7},{7,6},{8,9},{9,8},{10,11... | collective-permute-start | bytes 442376 | tf_op jit(solution)/shard_map/ppermute | solution.py:361
  209.5 4.4 %copy-start.9 = (bf16[2,4,96,384]{3,2,1,0:T(8,128)(2,1)}, bf16[2,4,96,384]{3,2,1,0:T(8,128)(2,1)S(1)}, u32[]{:S(2)}) copy-start(bf16[2,4,96,384]{3,2,1,0:T(8,128)(2,1)S(1)} %collective-permute-done.12.refs_1_) | copy-start | bytes 1769476
  209.5 31.9 %collective-permute-start.7 = (bf16[2,1,96,384]{3,2,1,0:T(8,128)(2,1)}, bf16[2,1,96,384]{3,2,1,0:T(8,128)(2,1)S(1)}, u32[]{:S(2)}, u32[]{:S(2)}) collective-permute-start(bf16[2,1,96,384]{3,2,1,0:T(8,128)(2,1)} %get-tuple-element.92), channel_id=1, source_target_pairs={{0,2},{1,3},{2,0},{3,1},{4,6},{5,7},{6,4},{7,5},{8,10},{9,11},{10,... | collective-permute-start | bytes 442376 | tf_op jit(solution)/shard_map/ppermute | solution.py:361
  211.9 1.9 copy-start.10
  211.9 29.4 %collective-permute-start.8 = (bf16[2,1,96,384]{3,2,1,0:T(8,128)(2,1)}, bf16[2,1,96,384]{3,2,1,0:T(8,128)(2,1)S(1)}, u32[]{:S(2)}, u32[]{:S(2)}) collective-permute-start(bf16[2,1,96,384]{3,2,1,0:T(8,128)(2,1)} %get-tuple-element.93), channel_id=1, source_target_pairs={{0,3},{1,2},{2,1},{3,0},{4,7},{5,6},{6,5},{7,4},{8,11},{9,10},{10,... | collective-permute-start | bytes 442376 | tf_op jit(solution)/shard_map/ppermute | solution.py:361
  229.3 16.3 %all-to-all-start.4 = ((f32[32,1,256]{2,1,0:T(1,128)}), f32[32,1,256]{2,1,0:T(1,128)S(1)}, u32[]{:S(2)}, u32[]{:S(2)}) async-start(f32[32,1,256]{2,1,0:T(1,128)} %reshape.110), calls=%async_computation.4 | async-start | bytes 65536 | tf_op jit(solution)/shard_map/all_to_all | solution.py:555
  (11 other events, 13.1 us)

commit v5 on v4

--- a/solution.py
+++ b/solution.py
@@ -397,7 +397,7 @@
             preferred_element_type=jnp.float32,
         )
 
-    o_ref[...] = i_ref[...] + total[...].T[: o_ref.shape[0]]
+    o_ref[...] = (total[...] + i_ref[...]).T[: o_ref.shape[0]]
 
 
 def potential_message(ionic_field, point_charge, charge_place, charge_slab, planes, halves):
@@ -413,8 +413,10 @@
     charges = jnp.concatenate(
         [charge_place, point_charge[None], charge_slab[:, 0][None].astype(jnp.float32)], axis=0
     )
-    ionic = ionic_field.T.reshape(planes, band_groups, band_groups, piece)
-    ionic = lax.dynamic_index_in_dim(ionic, band_at, 2, keepdims=False)
+    own_rows = slab_rows // band_groups
+    ionic = lax.dynamic_slice_in_dim(ionic_field, band_at * own_rows, own_rows, 0)
+    ionic = ionic.reshape(own_rows, planes, band_groups, share).transpose(1, 2, 0, 3)
+    ionic = ionic.reshape(planes, band_groups, piece)
     ionic = jnp.broadcast_to(
         ionic.transpose(1, 0, 2)[:, :, None], (band_groups, planes, halves, piece)
     )
@@ -438,8 +440,8 @@
     spare = message.shape[1] - 5
     band_at = lax.axis_index("band")
     ionic = message[:, 5:].reshape(band_groups, ga_count, spare * atoms)[:, :, :piece]
-    ionic = ionic.transpose(1, 0, 2).reshape(ga_count, share, slab_rows)
-    ionic = ionic.transpose(1, 0, 2).reshape(share, NY)
+    ionic = ionic.transpose(1, 0, 2).reshape(NY, share)
+    ionic = jnp.pad(ionic, ((0, 0), (0, LANES - share)))
     place = jnp.stack([band_at * share, lax.axis_index("ga") // halves]).astype(jnp.int32)
     return pl.pallas_call(
         functools.partial(charges_body, planes, slab_rows),

time: 249 us -> 250 us (level)
    unnamed x49 -> x40, local copies, waits for them, and re-layouts: 4.18 us -> 5.17 us
where the time goes in v5:
time: 250 us; the launch traced here: 249 us
  Pallas kernels  106 us (42%)
  starting transfers between devices  62.9 us (25%)
  waiting for transfers between devices  57.4 us (23%)
  other arithmetic  11.1 us (4%)
  local copies, waits for them, and re-layouts  10.6 us (4%)
    ppermute x15, waiting for transfers between devices, shifted(): lax.ppermute(message, 'ga', [(i, i ^ s) for i in range(groups)])  50.5 us
    ppermute x15, starting transfers between devices, shifted(): lax.ppermute(message, 'ga', [(i, i ^ s) for i in range(groups)])  37.7 us
    pallas_call x3, Pallas kernels, inverse(): pl.pallas_call(functools.partial(inverse_body, groups), grid=(bands // st...  21.2 us
    pallas_call x2, Pallas kernels, overlap(): pl.pallas_call(functools.partial(overlap_body, scale, per), in_specs=[who...  17.9 us
    pallas_call x2, Pallas kernels, forward(): pl.pallas_call(functools.partial(forward_body, groups), grid=(bands // st...  16.3 us
    pallas_call x1, Pallas kernels, own_share(): pl.pallas_call(functools.partial(charges_body, planes, slab_rows), in_spe...  12 us
    pallas_call x3, Pallas kernels, unpack(): pl.pallas_call(functools.partial(unpack_body, groups), grid=(2, halves, c...  11.9 us
    pallas_call x1, Pallas kernels, mix_waves(): pl.pallas_call(mix_waves_body, grid=(shares,), in_specs=[pl.BlockSpec((2,...  10 us
  transfers between devices with their start and end apart: 20, of which 8 were waited for; matrix products, arithmetic and copies ran while one was open for 5% of the time, Pallas kernels for 43%

profile of v5, /device:TPU:0, one launch (start us, length us, event | category | flops | bytes accessed | tf_op | source)
XLA Modules:
  0.0 249.0 jit_solution(12332997908757173407)
XLA Ops:
  4.4 7.3 %all-to-all-start = ((f32[32,8,256]{2,1,0:T(8,128)}), f32[32,8,256]{2,1,0:T(8,128)S(1)}, u32[]{:S(2)}, u32[]{:S(2)}) async-start(f32[32,8,256]{2,1,0:T(8,128)} %pad_maximum_fusion.4), calls=%async_computation | async-start | bytes 524288 | tf_op jit(solution)/shard_map/all_to_all | solution.py:483
  11.7 3.5 %pack_planes.2 = (bf16[2,4,96,384]{3,2,1,0:T(8,128)(2,1)}, bf16[2,4,96,384]{3,2,1,0:T(8,128)(2,1)}, bf16[2,4,96,384]{3,2,1,0:T(8,128)(2,1)}, bf16[2,4,96,384]{3,2,1,0:T(8,128)(2,1)}) custom-call(s32[1]{0:T(128)} %bitcast.place, bf16[2,8,4,36864]{3,2,1,0:T(4,128)(2,1)} %w_ref.1), custom_call_target="tpu_custom_call" | custom-call | bytes 36900 | tf_op jit(solution)/shard_map/pack_planes/pallas_call | solution.py:69
  17.0 2.4 collective-permute-start.1
  19.6 3.5 %pack_planes.3 = (bf16[2,4,96,384]{3,2,1,0:T(8,128)(2,1)}, bf16[2,4,96,384]{3,2,1,0:T(8,128)(2,1)}, bf16[2,4,96,384]{3,2,1,0:T(8,128)(2,1)}, bf16[2,4,96,384]{3,2,1,0:T(8,128)(2,1)}) custom-call(s32[1]{0:T(128)} %bitcast.place, bf16[2,8,4,36864]{3,2,1,0:T(4,128)(2,1)} %w_ref.1), custom_call_target="tpu_custom_call" | custom-call | bytes 36900 | tf_op jit(solution)/shard_map/pack_planes/pallas_call | solution.py:69
  23.1 10.0 %mix_waves.1 = bf16[8,768,384]{2,1,0:T(8,128)(2,1)} custom-call(bf16[2,8,4,36864]{3,2,1,0:T(4,128)(2,1)} %w_ref.1), custom_call_target="tpu_custom_call" | custom-call | bytes 36900 | tf_op jit(solution)/shard_map/mix_waves/pallas_call | solution.py:112
  34.7 12.0 %charge_potential.1.w_ref = f32[48,384]{1,0:T(8,128)} custom-call(s32[2]{0:T(128)} %pad_add_fusion.place, f32[32,8,256]{2,1,0:T(8,128)} %copy-done.8, f32[384,128]{1,0:T(8,128)} %pad.9.i_ref), custom_call_target="tpu_custom_call" | custom-call | bytes 36900 | tf_op jit(solution)/shard_map/charge_potential/pallas_call | solution.py:446
  48.4 3.9 %all-to-all-start.1 = ((f32[8,48,384]{2,1,0:T(8,128)}), f32[8,48,384]{2,1,0:T(8,128)S(1)}, u32[]{:S(2)}, u32[]{:S(2)}) async-start(f32[8,48,384]{2,1,0:T(8,128)} %broadcast_in_dim.15), calls=%async_computation.1 | async-start | bytes 1179648 | tf_op jit(solution)/shard_map/all_to_all | solution.py:488
  52.4 7.2 %collective-permute-done.1.refs_2_ = bf16[2,4,96,384]{3,2,1,0:T(8,128)(2,1)S(1)} collective-permute-done((bf16[2,4,96,384]{3,2,1,0:T(8,128)(2,1)}, bf16[2,4,96,384]{3,2,1,0:T(8,128)(2,1)S(1)}, u32[]{:S(2)}, u32[]{:S(2)}) %collective-permute-start.1) | collective-permute-done | bytes 589856 | tf_op jit(solution)/shard_map/ppermute | solution.py:361
  59.6 3.2 %all-to-all-done.1 = f32[8,48,384]{2,1,0:T(8,128)S(1)} async-done(((f32[8,48,384]{2,1,0:T(8,128)}), f32[8,48,384]{2,1,0:T(8,128)S(1)}, u32[]{:S(2)}, u32[]{:S(2)}) %all-to-all-start.1) | async-done | bytes 589856 | tf_op jit(solution)/shard_map/all_to_all | solution.py:488
  63.6 4.8 %all-to-all-start.2 = ((bf16[8,768,384]{2,1,0:T(8,128)(2,1)}), bf16[8,768,384]{2,1,0:T(8,128)(2,1)}, u32[]{:S(2)}, u32[]{:S(2)}) async-start(bf16[8,768,384]{2,1,0:T(8,128)(2,1)} %mix_waves.1), calls=%async_computation.2 | async-start | bytes 9437184 | tf_op jit(solution)/shard_map/all_to_all | solution.py:495
  68.5 9.7 %collective-permute-start.3 = (bf16[2,4,96,384]{3,2,1,0:T(8,128)(2,1)}, bf16[2,4,96,384]{3,2,1,0:T(8,128)(2,1)S(1)}, u32[]{:S(2)}, u32[]{:S(2)}) collective-permute-start(bf16[2,4,96,384]{3,2,1,0:T(8,128)(2,1)} %get-tuple-element.70), channel_id=1, source_target_pairs={{0,1},{1,0},{2,3},{3,2},{4,5},{5,4},{6,7},{7,6},{8,9},{9,8},{10,11... | collective-permute-start | bytes 1769480 | tf_op jit(solution)/shard_map/ppermute | solution.py:361
  80.6 2.6 %fusion.7 = bf16[384,384]{1,0:T(8,128)(2,1)S(1)} fusion(s32[384]{0:T(512)S(1)} %iota.13), kind=kLoop, calls=%fused_computation.17 | loop fusion | flops 2064384 | bytes 296448 | tf_op jit(solution)/shard_map/neg | solution.py:498
  83.2 2.9 %multiply_convert_fusion = (bf16[384,384]{1,0:T(8,128)(2,1)S(1)}, bf16[384,384]{1,0:T(8,128)(2,1)S(1)}) fusion(s32[384]{0:T(512)S(1)} %iota.13), kind=kLoop, calls=%fused_computation.9 | loop fusion | flops 1916928 | bytes 591360 | tf_op jit(solution)/shard_map/convert_element_type | solution.py:25
  87.6 8.1 %forward.2.refs_4_.s_ref = bf16[4,2,384,384]{3,2,1,0:T(8,128)(2,1)} custom-call(s32[1]{0:T(128)} %bitcast.place, bf16[2,4,96,384]{3,2,1,0:T(8,128)(2,1)} %get-tuple-element.74.refs_0_, bf16[2,4,96,384]{3,2,1,0:T(8,128)(2,1)} %copy-done.5, bf16[2,4,96,384]{3,2,1,0:T(8,128)(2,1)} %copy-done.6, bf16[2,4,96,384]{3,2,1,0:T(8,128)(2,1)} %copy-done.7, ...), custom_call_target="tpu_custom_call" | custom-call | bytes 36900 | tf_op jit(solution)/shard_map/forward/pallas_call | solution.py:229
  95.7 4.9 %mix_space.2.refs_0_ = bf16[8,2,384,384]{3,2,1,0:T(8,128)(2,1)} custom-call(bf16[4,2,384,384]{3,2,1,0:T(8,128)(2,1)} %forward.2.refs_4_.s_ref), custom_call_target="tpu_custom_call" | custom-call | bytes 36900 | tf_op jit(solution)/shard_map/mix_space/pallas_call | solution.py:156
  100.6 9.0 %inverse.3 = (bf16[2,4,96,384]{3,2,1,0:T(8,128)(2,1)}, bf16[2,4,96,384]{3,2,1,0:T(8,128)(2,1)}, bf16[2,4,96,384]{3,2,1,0:T(8,128)(2,1)}, bf16[2,4,96,384]{3,2,1,0:T(8,128)(2,1)}) custom-call(s32[1]{0:T(128)} %bitcast.place, bf16[2,4,96,384]{3,2,1,0:T(8,128)(2,1)} %get-tuple-element.74.refs_0_, bf16[2,4,96,384]{3,2,1,0:T(8,128)(2,1)} %copy-done.5, ...), custom_call_target="tpu_custom_call" | custom-call | bytes 36900 | tf_op jit(solution)/shard_map/inverse/pallas_call | solution.py:274
  109.6 11.2 %collective-permute-done.4.refs_2_ = bf16[2,4,96,384]{3,2,1,0:T(8,128)(2,1)S(1)} collective-permute-done((bf16[2,4,96,384]{3,2,1,0:T(8,128)(2,1)}, bf16[2,4,96,384]{3,2,1,0:T(8,128)(2,1)S(1)}, u32[]{:S(2)}, u32[]{:S(2)}) %collective-permute-start.4) | collective-permute-done | bytes 589856 | tf_op jit(solution)/shard_map/ppermute | solution.py:361
  120.8 2.3 all-to-all-done.2
  123.0 10.3 %collective-permute-start.13 = (bf16[2,4,96,384]{3,2,1,0:T(8,128)(2,1)}, bf16[2,4,96,384]{3,2,1,0:T(8,128)(2,1)S(1)}, u32[]{:S(2)}, u32[]{:S(2)}) collective-permute-start(bf16[2,4,96,384]{3,2,1,0:T(8,128)(2,1)} %get-tuple-element.102), channel_id=1, source_target_pairs={{0,2},{1,3},{2,0},{3,1},{4,6},{5,7},{6,4},{7,5},{8,10},{9,11},{10,... | collective-permute-start | bytes 1769480 | tf_op jit(solution)/shard_map/ppermute | solution.py:361
  133.3 8.2 %forward.3.refs_4_.s_ref = bf16[4,2,384,384]{3,2,1,0:T(8,128)(2,1)} custom-call(s32[1]{0:T(128)} %bitcast.place, bf16[2,4,96,384]{3,2,1,0:T(8,128)(2,1)} %get-tuple-element.86.refs_0_, bf16[2,4,96,384]{3,2,1,0:T(8,128)(2,1)} %copy-done.2, bf16[2,4,96,384]{3,2,1,0:T(8,128)(2,1)} %copy-done.3, bf16[2,4,96,384]{3,2,1,0:T(8,128)(2,1)} %copy-done.4, ...), custom_call_target="tpu_custom_call" | custom-call | bytes 36900 | tf_op jit(solution)/shard_map/forward/pallas_call | solution.py:229
  141.5 4.9 %mix_space.3 = bf16[8,2,384,384]{3,2,1,0:T(8,128)(2,1)} custom-call(bf16[4,2,384,384]{3,2,1,0:T(8,128)(2,1)} %forward.3.refs_4_.s_ref, bf16[8,2,384,384]{3,2,1,0:T(8,128)(2,1)} %mix_space.2.refs_0_), custom_call_target="tpu_custom_call", output_to_operand_aliasing={{}: (1, {})} | custom-call | bytes 36900 | tf_op jit(solution)/shard_map/mix_space/pallas_call | solution.py:156
  146.3 12.4 %collective-permute-done.13.refs_2_ = bf16[2,4,96,384]{3,2,1,0:T(8,128)(2,1)S(1)} collective-permute-done((bf16[2,4,96,384]{3,2,1,0:T(8,128)(2,1)}, bf16[2,4,96,384]{3,2,1,0:T(8,128)(2,1)S(1)}, u32[]{:S(2)}, u32[]{:S(2)}) %collective-permute-start.13) | collective-permute-done | bytes 589856 | tf_op jit(solution)/shard_map/ppermute | solution.py:361
  159.6 4.8 %all-to-all-start.3 = ((bf16[8,2,384,384]{3,2,1,0:T(8,128)(2,1)}), bf16[8,2,384,384]{3,2,1,0:T(8,128)(2,1)}, u32[]{:S(2)}, u32[]{:S(2)}) async-start(bf16[8,2,384,384]{3,2,1,0:T(8,128)(2,1)} %mix_space.3), calls=%async_computation.3 | async-start | bytes 9437184 | tf_op jit(solution)/shard_map/all_to_all | solution.py:519
  166.5 7.7 %inverse.5 = (bf16[2,3,96,384]{3,2,1,0:T(8,128)(2,1)}, bf16[2,3,96,384]{3,2,1,0:T(8,128)(2,1)}, bf16[2,3,96,384]{3,2,1,0:T(8,128)(2,1)}, bf16[2,3,96,384]{3,2,1,0:T(8,128)(2,1)}) custom-call(s32[1]{0:T(128)} %bitcast.place, bf16[2,4,96,384]{3,2,1,0:T(8,128)(2,1)} %get-tuple-element.86.refs_0_, bf16[2,4,96,384]{3,2,1,0:T(8,128)(2,1)} %copy-done.2, ...), custom_call_target="tpu_custom_call" | custom-call | bytes 36900 | tf_op jit(solution)/shard_map/inverse/pallas_call | solution.py:274
  179.4 8.9 %overlap.2.refs_0_ = f32[2,64,64]{2,1,0:T(8,128)} custom-call(bf16[8,1,768,384]{3,2,1,0:T(8,128)(2,1)} %bitcast.8.z_ref, f32[48,384]{1,0:T(8,128)} %reshape.107.w_ref), custom_call_target="tpu_custom_call" | custom-call | bytes 29520000 | tf_op jit(solution)/shard_map/overlap/pallas_call | solution.py:346
  188.3 4.5 %inverse.4 = (bf16[2,1,96,384]{3,2,1,0:T(8,128)(2,1)}, bf16[2,1,96,384]{3,2,1,0:T(8,128)(2,1)}, bf16[2,1,96,384]{3,2,1,0:T(8,128)(2,1)}, bf16[2,1,96,384]{3,2,1,0:T(8,128)(2,1)}) custom-call(s32[1]{0:T(128)} %bitcast.place, bf16[2,4,96,384]{3,2,1,0:T(8,128)(2,1)} %get-tuple-element.86.refs_0_, bf16[2,4,96,384]{3,2,1,0:T(8,128)(2,1)} %copy-done.2, ...), custom_call_target="tpu_custom_call" | custom-call | bytes 36900 | tf_op jit(solution)/shard_map/inverse/pallas_call | solution.py:274
  192.8 17.8 %collective-permute-done.9.refs_1_ = bf16[2,3,96,384]{3,2,1,0:T(8,128)(2,1)S(1)} collective-permute-done((bf16[2,3,96,384]{3,2,1,0:T(8,128)(2,1)}, bf16[2,3,96,384]{3,2,1,0:T(8,128)(2,1)S(1)}, u32[]{:S(2)}, u32[]{:S(2)}) %collective-permute-start.9) | collective-permute-done | bytes 442400 | tf_op jit(solution)/shard_map/ppermute | solution.py:361
  210.6 2.5 collective-permute-start.7
  215.0 4.6 %unpack_planes.3.refs_4_ = bf16[2,8,4,36864]{3,2,1,0:T(4,128)(2,1)} custom-call(s32[1]{0:T(128)} %bitcast.place, bf16[2,4,96,384]{3,2,1,0:T(8,128)(2,1)} %get-tuple-element.99.refs_0_, bf16[2,4,96,384]{3,2,1,0:T(8,128)(2,1)} %copy-done.10, bf16[2,4,96,384]{3,2,1,0:T(8,128)(2,1)} %copy-done.9, bf16[2,4,96,384]{3,2,1,0:T(8,128)(2,1)} %copy-done.11), custom_call_target="tpu_custom_call" | custom-call | bytes 17712000 | tf_op jit(solution)/shard_map/unpack_planes/pallas_call | solution.py:195
  219.7 9.0 %overlap.3 = f32[2,64,64]{2,1,0:T(8,128)} custom-call(bf16[8,2,384,384]{3,2,1,0:T(8,128)(2,1)} %all-to-all-done.3.z_ref, f32[48,384]{1,0:T(8,128)} %charge_potential.1.w_ref, f32[2,64,64]{2,1,0:T(8,128)} %overlap.2.refs_0_), custom_call_target="tpu_custom_call" | custom-call | bytes 29520000 | tf_op jit(solution)/shard_map/overlap/pallas_call | solution.py:346
  230.4 4.4 %all-to-all-start.4 = ((f32[32,1,256]{2,1,0:T(1,128)}), f32[32,1,256]{2,1,0:T(1,128)S(1)}, u32[]{:S(2)}, u32[]{:S(2)}) async-start(f32[32,1,256]{2,1,0:T(1,128)} %reshape.110), calls=%async_computation.4 | async-start | bytes 65536 | tf_op jit(solution)/shard_map/all_to_all | solution.py:557
  235.7 5.2 %unpack_planes.4.refs_4_ = bf16[2,8,4,36864]{3,2,1,0:T(4,128)(2,1)} custom-call(s32[1]{0:T(128)} %bitcast.place, bf16[2,3,96,384]{3,2,1,0:T(8,128)(2,1)} %get-tuple-element.94.refs_0_, bf16[2,3,96,384]{3,2,1,0:T(8,128)(2,1)} %copy-done.12, bf16[2,3,96,384]{3,2,1,0:T(8,128)(2,1)} %copy-done.13, ...), custom_call_target="tpu_custom_call", output_to_operand_aliasing={{}: (5, {})} | custom-call | bytes 13283999 | tf_op jit(solution)/shard_map/unpack_planes/pallas_call | solution.py:195
  (98 shorter events, 34.5 us)
Async XLA Ops:
  0.6 1.1 copy-start
  4.4 29.3 %all-to-all-start = ((f32[32,8,256]{2,1,0:T(8,128)}), f32[32,8,256]{2,1,0:T(8,128)S(1)}, u32[]{:S(2)}, u32[]{:S(2)}) async-start(f32[32,8,256]{2,1,0:T(8,128)} %pad_maximum_fusion.4), calls=%async_computation | async-start | bytes 524288 | tf_op jit(solution)/shard_map/all_to_all | solution.py:483
  15.2 37.1 %collective-permute-start = (bf16[2,4,96,384]{3,2,1,0:T(8,128)(2,1)}, bf16[2,4,96,384]{3,2,1,0:T(8,128)(2,1)S(1)}, u32[]{:S(2)}, u32[]{:S(2)}) collective-permute-start(bf16[2,4,96,384]{3,2,1,0:T(8,128)(2,1)} %get-tuple-element.56), channel_id=1, source_target_pairs={{0,1},{1,0},{2,3},{3,2},{4,5},{5,4},{6,7},{7,6},{8,9},{9,8},{10,11... | collective-permute-start | bytes 1769480 | tf_op jit(solution)/shard_map/ppermute | solution.py:361
  17.0 42.6 %collective-permute-start.1 = (bf16[2,4,96,384]{3,2,1,0:T(8,128)(2,1)}, bf16[2,4,96,384]{3,2,1,0:T(8,128)(2,1)S(1)}, u32[]{:S(2)}, u32[]{:S(2)}) collective-permute-start(bf16[2,4,96,384]{3,2,1,0:T(8,128)(2,1)} %get-tuple-element.57), channel_id=1, source_target_pairs={{0,2},{1,3},{2,0},{3,1},{4,6},{5,7},{6,4},{7,5},{8,10},{9,11},{10,... | collective-permute-start | bytes 1769480 | tf_op jit(solution)/shard_map/ppermute | solution.py:361
  19.4 40.2 %collective-permute-start.2 = (bf16[2,4,96,384]{3,2,1,0:T(8,128)(2,1)}, bf16[2,4,96,384]{3,2,1,0:T(8,128)(2,1)S(1)}, u32[]{:S(2)}, u32[]{:S(2)}) collective-permute-start(bf16[2,4,96,384]{3,2,1,0:T(8,128)(2,1)} %get-tuple-element.58), channel_id=1, source_target_pairs={{0,3},{1,2},{2,1},{3,0},{4,7},{5,6},{6,5},{7,4},{8,11},{9,10},{10,... | collective-permute-start | bytes 1769480 | tf_op jit(solution)/shard_map/ppermute | solution.py:361
  48.4 14.4 %all-to-all-start.1 = ((f32[8,48,384]{2,1,0:T(8,128)}), f32[8,48,384]{2,1,0:T(8,128)S(1)}, u32[]{:S(2)}, u32[]{:S(2)}) async-start(f32[8,48,384]{2,1,0:T(8,128)} %broadcast_in_dim.15), calls=%async_computation.1 | async-start | bytes 1179648 | tf_op jit(solution)/shard_map/all_to_all | solution.py:488
  52.4 10.5 %copy-start.5 = (bf16[2,4,96,384]{3,2,1,0:T(8,128)(2,1)}, bf16[2,4,96,384]{3,2,1,0:T(8,128)(2,1)S(1)}, u32[]{:S(2)}) copy-start(bf16[2,4,96,384]{3,2,1,0:T(8,128)(2,1)S(1)} %collective-permute-done.refs_1_) | copy-start | bytes 1769476
  59.6 3.2 %copy-start.6 = (bf16[2,4,96,384]{3,2,1,0:T(8,128)(2,1)}, bf16[2,4,96,384]{3,2,1,0:T(8,128)(2,1)S(1)}, u32[]{:S(2)}) copy-start(bf16[2,4,96,384]{3,2,1,0:T(8,128)(2,1)S(1)} %collective-permute-done.1.refs_2_) | copy-start | bytes 1769476
  59.6 3.2 %copy-start.7 = (bf16[2,4,96,384]{3,2,1,0:T(8,128)(2,1)}, bf16[2,4,96,384]{3,2,1,0:T(8,128)(2,1)S(1)}, u32[]{:S(2)}) copy-start(bf16[2,4,96,384]{3,2,1,0:T(8,128)(2,1)S(1)} %collective-permute-done.2.refs_3_) | copy-start | bytes 1769476
  62.8 15.8 %copy-start.18 = (bf16[2,4,96,384]{3,2,1,0:T(8,128)(2,1)S(1)}, bf16[2,4,96,384]{3,2,1,0:T(8,128)(2,1)}, u32[]{:S(2)}) copy-start(bf16[2,4,96,384]{3,2,1,0:T(8,128)(2,1)} %get-tuple-element.72) | copy-start | bytes 1769476
  63.6 59.4 %all-to-all-start.2 = ((bf16[8,768,384]{2,1,0:T(8,128)(2,1)}), bf16[8,768,384]{2,1,0:T(8,128)(2,1)}, u32[]{:S(2)}, u32[]{:S(2)}) async-start(bf16[8,768,384]{2,1,0:T(8,128)(2,1)} %mix_waves.1), calls=%async_computation.2 | async-start | bytes 9437184 | tf_op jit(solution)/shard_map/all_to_all | solution.py:495
  68.5 41.1 %collective-permute-start.3 = (bf16[2,4,96,384]{3,2,1,0:T(8,128)(2,1)}, bf16[2,4,96,384]{3,2,1,0:T(8,128)(2,1)S(1)}, u32[]{:S(2)}, u32[]{:S(2)}) collective-permute-start(bf16[2,4,96,384]{3,2,1,0:T(8,128)(2,1)} %get-tuple-element.70), channel_id=1, source_target_pairs={{0,1},{1,0},{2,3},{3,2},{4,5},{5,4},{6,7},{7,6},{8,9},{9,8},{10,11... | collective-permute-start | bytes 1769480 | tf_op jit(solution)/shard_map/ppermute | solution.py:361
  78.1 42.6 %collective-permute-start.4 = (bf16[2,4,96,384]{3,2,1,0:T(8,128)(2,1)}, bf16[2,4,96,384]{3,2,1,0:T(8,128)(2,1)S(1)}, u32[]{:S(2)}, u32[]{:S(2)}) collective-permute-start(bf16[2,4,96,384]{3,2,1,0:T(8,128)(2,1)} %get-tuple-element.71), channel_id=1, source_target_pairs={{0,2},{1,3},{2,0},{3,1},{4,6},{5,7},{6,4},{7,5},{8,10},{9,11},{10,... | collective-permute-start | bytes 1769480 | tf_op jit(solution)/shard_map/ppermute | solution.py:361
  78.6 42.1 %collective-permute-start.5 = (bf16[2,4,96,384]{3,2,1,0:T(8,128)(2,1)S(1)}, bf16[2,4,96,384]{3,2,1,0:T(8,128)(2,1)S(1)}, u32[]{:S(2)}, u32[]{:S(2)}) collective-permute-start(bf16[2,4,96,384]{3,2,1,0:T(8,128)(2,1)S(1)} %copy-done.18), channel_id=1, source_target_pairs={{0,3},{1,2},{2,1},{3,0},{4,7},{5,6},{6,5},{7,4},{8,11},{9,10},{10,... | collective-permute-start | bytes 1769480 | tf_op jit(solution)/shard_map/ppermute | solution.py:361
  109.6 23.7 %copy-start.2 = (bf16[2,4,96,384]{3,2,1,0:T(8,128)(2,1)}, bf16[2,4,96,384]{3,2,1,0:T(8,128)(2,1)S(1)}, u32[]{:S(2)}) copy-start(bf16[2,4,96,384]{3,2,1,0:T(8,128)(2,1)S(1)} %collective-permute-done.3.refs_1_) | copy-start | bytes 1769476
  120.8 12.5 %copy-start.3 = (bf16[2,4,96,384]{3,2,1,0:T(8,128)(2,1)}, bf16[2,4,96,384]{3,2,1,0:T(8,128)(2,1)S(1)}, u32[]{:S(2)}) copy-start(bf16[2,4,96,384]{3,2,1,0:T(8,128)(2,1)S(1)} %collective-permute-done.4.refs_2_) | copy-start | bytes 1769476
  120.8 12.5 %copy-start.4 = (bf16[2,4,96,384]{3,2,1,0:T(8,128)(2,1)}, bf16[2,4,96,384]{3,2,1,0:T(8,128)(2,1)S(1)}, u32[]{:S(2)}) copy-start(bf16[2,4,96,384]{3,2,1,0:T(8,128)(2,1)S(1)} %collective-permute-done.5.refs_3_) | copy-start | bytes 1769476
  123.0 35.7 %collective-permute-start.13 = (bf16[2,4,96,384]{3,2,1,0:T(8,128)(2,1)}, bf16[2,4,96,384]{3,2,1,0:T(8,128)(2,1)S(1)}, u32[]{:S(2)}, u32[]{:S(2)}) collective-permute-start(bf16[2,4,96,384]{3,2,1,0:T(8,128)(2,1)} %get-tuple-element.102), channel_id=1, source_target_pairs={{0,2},{1,3},{2,0},{3,1},{4,6},{5,7},{6,4},{7,5},{8,10},{9,11},{10,... | collective-permute-start | bytes 1769480 | tf_op jit(solution)/shard_map/ppermute | solution.py:361
  159.6 60.1 %all-to-all-start.3 = ((bf16[8,2,384,384]{3,2,1,0:T(8,128)(2,1)}), bf16[8,2,384,384]{3,2,1,0:T(8,128)(2,1)}, u32[]{:S(2)}, u32[]{:S(2)}) async-start(bf16[8,2,384,384]{3,2,1,0:T(8,128)(2,1)} %mix_space.3), calls=%async_computation.3 | async-start | bytes 9437184 | tf_op jit(solution)/shard_map/all_to_all | solution.py:519
  164.4 46.2 %collective-permute-start.12 = (bf16[2,4,96,384]{3,2,1,0:T(8,128)(2,1)}, bf16[2,4,96,384]{3,2,1,0:T(8,128)(2,1)S(1)}, u32[]{:S(2)}, u32[]{:S(2)}) collective-permute-start(bf16[2,4,96,384]{3,2,1,0:T(8,128)(2,1)} %get-tuple-element.100), channel_id=1, source_target_pairs={{0,1},{1,0},{2,3},{3,2},{4,5},{5,4},{6,7},{7,6},{8,9},{9,8},{10,11... | collective-permute-start | bytes 1769480 | tf_op jit(solution)/shard_map/ppermute | solution.py:361
  164.5 48.6 %collective-permute-start.14 = (bf16[2,4,96,384]{3,2,1,0:T(8,128)(2,1)}, bf16[2,4,96,384]{3,2,1,0:T(8,128)(2,1)S(1)}, u32[]{:S(2)}, u32[]{:S(2)}) collective-permute-start(bf16[2,4,96,384]{3,2,1,0:T(8,128)(2,1)} %get-tuple-element.104), channel_id=1, source_target_pairs={{0,3},{1,2},{2,1},{3,0},{4,7},{5,6},{6,5},{7,4},{8,11},{9,10},{10,... | collective-permute-start | bytes 1769480 | tf_op jit(solution)/shard_map/ppermute | solution.py:361
  174.2 36.4 %collective-permute-start.9 = (bf16[2,3,96,384]{3,2,1,0:T(8,128)(2,1)}, bf16[2,3,96,384]{3,2,1,0:T(8,128)(2,1)S(1)}, u32[]{:S(2)}, u32[]{:S(2)}) collective-permute-start(bf16[2,3,96,384]{3,2,1,0:T(8,128)(2,1)} %get-tuple-element.95), channel_id=1, source_target_pairs={{0,1},{1,0},{2,3},{3,2},{4,5},{5,4},{6,7},{7,6},{8,9},{9,8},{10,11... | collective-permute-start | bytes 1327112 | tf_op jit(solution)/shard_map/ppermute | solution.py:361
  175.3 59.5 %collective-permute-start.10 = (bf16[2,3,96,384]{3,2,1,0:T(8,128)(2,1)}, bf16[2,3,96,384]{3,2,1,0:T(8,128)(2,1)S(1)}, u32[]{:S(2)}, u32[]{:S(2)}) collective-permute-start(bf16[2,3,96,384]{3,2,1,0:T(8,128)(2,1)} %get-tuple-element.96), channel_id=1, source_target_pairs={{0,2},{1,3},{2,0},{3,1},{4,6},{5,7},{6,4},{7,5},{8,10},{9,11},{10,... | collective-permute-start | bytes 1327112 | tf_op jit(solution)/shard_map/ppermute | solution.py:361
  176.7 58.1 %collective-permute-start.11 = (bf16[2,3,96,384]{3,2,1,0:T(8,128)(2,1)}, bf16[2,3,96,384]{3,2,1,0:T(8,128)(2,1)S(1)}, u32[]{:S(2)}, u32[]{:S(2)}) collective-permute-start(bf16[2,3,96,384]{3,2,1,0:T(8,128)(2,1)} %get-tuple-element.97), channel_id=1, source_target_pairs={{0,3},{1,2},{2,1},{3,0},{4,7},{5,6},{6,5},{7,4},{8,11},{9,10},{10,... | collective-permute-start | bytes 1327112 | tf_op jit(solution)/shard_map/ppermute | solution.py:361
  210.6 24.2 %copy-start.12 = (bf16[2,3,96,384]{3,2,1,0:T(8,128)(2,1)}, bf16[2,3,96,384]{3,2,1,0:T(8,128)(2,1)S(1)}, u32[]{:S(2)}) copy-start(bf16[2,3,96,384]{3,2,1,0:T(8,128)(2,1)S(1)} %collective-permute-done.9.refs_1_) | copy-start | bytes 1327108
  210.6 30.3 %collective-permute-start.6 = (bf16[2,1,96,384]{3,2,1,0:T(8,128)(2,1)}, bf16[2,1,96,384]{3,2,1,0:T(8,128)(2,1)S(1)}, u32[]{:S(2)}, u32[]{:S(2)}) collective-permute-start(bf16[2,1,96,384]{3,2,1,0:T(8,128)(2,1)} %get-tuple-element.91), channel_id=1, source_target_pairs={{0,1},{1,0},{2,3},{3,2},{4,5},{5,4},{6,7},{7,6},{8,9},{9,8},{10,11... | collective-permute-start | bytes 442376 | tf_op jit(solution)/shard_map/ppermute | solution.py:361
  210.6 4.4 %copy-start.10 = (bf16[2,4,96,384]{3,2,1,0:T(8,128)(2,1)}, bf16[2,4,96,384]{3,2,1,0:T(8,128)(2,1)S(1)}, u32[]{:S(2)}) copy-start(bf16[2,4,96,384]{3,2,1,0:T(8,128)(2,1)S(1)} %collective-permute-done.12.refs_1_) | copy-start | bytes 1769476
  210.6 32.2 %collective-permute-start.7 = (bf16[2,1,96,384]{3,2,1,0:T(8,128)(2,1)}, bf16[2,1,96,384]{3,2,1,0:T(8,128)(2,1)S(1)}, u32[]{:S(2)}, u32[]{:S(2)}) collective-permute-start(bf16[2,1,96,384]{3,2,1,0:T(8,128)(2,1)} %get-tuple-element.92), channel_id=1, source_target_pairs={{0,2},{1,3},{2,0},{3,1},{4,6},{5,7},{6,4},{7,5},{8,10},{9,11},{10,... | collective-permute-start | bytes 442376 | tf_op jit(solution)/shard_map/ppermute | solution.py:361
  213.1 1.9 copy-start.11
  213.1 29.7 %collective-permute-start.8 = (bf16[2,1,96,384]{3,2,1,0:T(8,128)(2,1)}, bf16[2,1,96,384]{3,2,1,0:T(8,128)(2,1)S(1)}, u32[]{:S(2)}, u32[]{:S(2)}) collective-permute-start(bf16[2,1,96,384]{3,2,1,0:T(8,128)(2,1)} %get-tuple-element.93), channel_id=1, source_target_pairs={{0,3},{1,2},{2,1},{3,0},{4,7},{5,6},{6,5},{7,4},{8,11},{9,10},{10,... | collective-permute-start | bytes 442376 | tf_op jit(solution)/shard_map/ppermute | solution.py:361
  230.4 16.6 %all-to-all-start.4 = ((f32[32,1,256]{2,1,0:T(1,128)}), f32[32,1,256]{2,1,0:T(1,128)S(1)}, u32[]{:S(2)}, u32[]{:S(2)}) async-start(f32[32,1,256]{2,1,0:T(1,128)} %reshape.110), calls=%async_computation.4 | async-start | bytes 65536 | tf_op jit(solution)/shard_map/all_to_all | solution.py:557
  240.9 1.9 copy-start.15
  (7 other events, 5.7 us)

commit v6 on v4

--- a/solution.py
+++ b/solution.py
@@ -36,6 +36,10 @@
 
 def dot(left, right):
     return jnp.dot(left, right, preferred_element_type=jnp.float32)
+
+
+def partners(groups):
+    return [0, *range(groups // 2, groups), *range(1, groups // 2)]
 
 
 def step_of(count):
@@ -58,8 +62,8 @@
             split = source[0, i].reshape(planes, rows, NY)
             for p in range(planes):
                 held[p * halves + h, i] = split[p]
-    for s, message in enumerate(messages):
-        message[0] = held[place[0] ^ s]
+    for partner, message in zip(partners(groups), messages):
+        message[0] = held[place[0] ^ partner]
 
 
 def pack(waves, place, first, count, rows, groups):
@@ -169,8 +173,8 @@
 def unpack_body(groups, place, *refs):
     messages, o_ref, held = refs[:groups], refs[-2], refs[-1]
     halves, planes, count, rows, _ = held.shape
-    for s, message in enumerate(messages):
-        source = place[0] ^ s
+    for partner, message in zip(partners(groups), messages):
+        source = place[0] ^ partner
         held[lax.rem(source, halves), source // halves] = message[0]
     half = pl.program_id(1)
     for i in range(count):
@@ -210,8 +214,8 @@
 
 def forward_body(groups, place, *refs):
     messages, (f_ref, b_ref, s_ref, held) = refs[:groups], refs[groups:]
-    for s, message in enumerate(messages):
-        held[place[0] ^ s] = message[...]
+    for partner, message in zip(partners(groups), messages):
+        held[place[0] ^ partner] = message[...]
     for i in range(held.shape[2]):
         parts = [held[:, c, i].reshape(NX, NY) for c in range(2)]
         first = dot(jnp.concatenate(parts, axis=1), f_ref[...]).astype(jnp.bfloat16)
@@ -249,8 +253,8 @@
     freq_x = frequency(lax.broadcasted_iota(jnp.int32, (NX, 1), 0), NX)
     freq_y = frequency(lax.broadcasted_iota(jnp.int32, (1, NY), 1), NY)
     kinetic = 2.0 * (freq_x * freq_x / (NX * NX) + freq_y * freq_y / (NY * NY))
-    for s, message in enumerate(messages):
-        held[place[0] ^ s] = message[...]
+    for partner, message in zip(partners(groups), messages):
+        held[place[0] ^ partner] = message[...]
     for i in range(held.shape[2]):
         weighted = jnp.concatenate(
             [v_ref[...] * s_ref[i, c].astype(jnp.float32) for c in range(2)], axis=0
@@ -261,8 +265,8 @@
             wide = held[:, c, i].reshape(NX, NY).astype(jnp.float32)
             applied = kinetic * wide + recip[:, c * NY : (c + 1) * NY]
             held[:, c, i] = applied.astype(jnp.bfloat16).reshape(groups, rows, NY)
-    for s, result in enumerate(results):
-        result[...] = held[place[0] ^ s]
+    for partner, result in zip(partners(groups), results):
+        result[...] = held[place[0] ^ partner]
 
 
 def inverse(messages, base, bands, place, in_space, potential, forth, back):
@@ -358,8 +362,10 @@
 def shifted(messages):
     groups = len(messages)
     return [
-        lax.ppermute(message, "ga", [(i, i ^ s) for i in range(groups)]) if s else message
-        for s, message in enumerate(messages)
+        lax.ppermute(message, "ga", [(i, i ^ partner) for i in range(groups)])
+        if partner
+        else message
+        for partner, message in zip(partners(groups), messages)
     ]
 
 
@@ -509,8 +515,7 @@
     returned = [shifted(result)]
     in_space.append(forward(arrived[1], place, forth, back))
     mixed = mix_space(in_space[1], 1, mixed, shares)
-    middle = ga_count // 2
-    mixed, returned[0][middle] = lax.optimization_barrier((mixed, returned[0][middle]))
+    mixed, returned[0][1] = lax.optimization_barrier((mixed, returned[0][1]))
     if halves > 1:
         mixed = mixed.reshape(band_groups, halves, -1, NY)
         mixed = lax.all_to_all(mixed, "ga", 1, 1, axis_index_groups=pairs, tiled=True)

time: 249 us -> 259 us (1.040)
  waiting for transfers between devices: 57.3 us -> 73.5 us
  starting transfers between devices: 62.5 us -> 56 us
    ppermute x15, starting transfers between devices: 37.3 us -> 18.5 us  [shifted(): lax.ppermute(message, 'ga', [(i, i ^ partner) for i in range(groups)])]
    all_to_all x1, starting transfers between devices: 3.94 us -> 16.3 us  [shards(): potential = lax.all_to_all(copies, 'band', 0, 0, tiled=True).reshape(NX, NY)]
    all_to_all x1, waiting for transfers between devices: 2.56 us -> 11.6 us  [shards(): met_waves = lax.all_to_all(mixed, 'band', 0, 0, tiled=True)]
    all_to_all x1, waiting for transfers between devices: 3.29 us -> 10.4 us  [shards(): potential = lax.all_to_all(copies, 'band', 0, 0, tiled=True).reshape(NX, NY)]
  transfers between devices with their start and end apart: 20 -> 20, of which waited for: 8 -> 6; matrix products, arithmetic and copies ran while one was open for 5% -> 5% of each run, Pallas kernels for 43% -> 41%
where the time goes in v6:
time: 259 us; the launch traced here: 257 us
  Pallas kernels  106 us (41%)
  waiting for transfers between devices  73.5 us (28%)
  starting transfers between devices  56 us (22%)
  local copies, waits for them, and re-layouts  11 us (4%)
  other arithmetic  9.79 us (4%)
    ppermute x15, waiting for transfers between devices, shifted(): lax.ppermute(message, 'ga', [(i, i ^ partner) for i in range(groups)])  51.5 us
    pallas_call x3, Pallas kernels, inverse(): pl.pallas_call(functools.partial(inverse_body, groups), grid=(bands // st...  21.2 us
    ppermute x15, starting transfers between devices, shifted(): lax.ppermute(message, 'ga', [(i, i ^ partner) for i in range(groups)])  18.5 us
    pallas_call x2, Pallas kernels, overlap(): pl.pallas_call(functools.partial(overlap_body, scale, per), in_specs=[who...  17.9 us
    all_to_all x1, starting transfers between devices, shards(): potential = lax.all_to_all(copies, 'band', 0, 0, tiled=True).reshape(NX, NY)  16.3 us
    pallas_call x2, Pallas kernels, forward(): pl.pallas_call(functools.partial(forward_body, groups), grid=(bands // st...  16.3 us
    pallas_call x1, Pallas kernels, own_share(): pl.pallas_call(functools.partial(charges_body, planes, slab_rows), in_spe...  12 us
    pallas_call x3, Pallas kernels, unpack(): pl.pallas_call(functools.partial(unpack_body, groups), grid=(2, halves, c...  11.9 us
  transfers between devices with their start and end apart: 20, of which 6 were waited for; matrix products, arithmetic and copies ran while one was open for 5% of the time, Pallas kernels for 41%

profile of v6, /device:TPU:0, one launch (start us, length us, event | category | flops | bytes accessed | tf_op | source)
XLA Modules:
  0.0 257.3 jit_solution(13666096940744504140)
XLA Ops:
  3.4 7.3 %all-to-all-start = ((f32[32,8,256]{2,1,0:T(8,128)}), f32[32,8,256]{2,1,0:T(8,128)S(1)}, u32[]{:S(2)}, u32[]{:S(2)}) async-start(f32[32,8,256]{2,1,0:T(8,128)} %pad_maximum_fusion.4), calls=%async_computation | async-start | bytes 524288 | tf_op jit(solution)/shard_map/all_to_all | solution.py:487
  10.7 3.5 %pack_planes.2 = (bf16[2,4,96,384]{3,2,1,0:T(8,128)(2,1)}, bf16[2,4,96,384]{3,2,1,0:T(8,128)(2,1)}, bf16[2,4,96,384]{3,2,1,0:T(8,128)(2,1)}, bf16[2,4,96,384]{3,2,1,0:T(8,128)(2,1)}) custom-call(s32[1]{0:T(128)} %bitcast.place, bf16[2,8,4,36864]{3,2,1,0:T(4,128)(2,1)} %w_ref.1), custom_call_target="tpu_custom_call" | custom-call | bytes 36900 | tf_op jit(solution)/shard_map/pack_planes/pallas_call | solution.py:73
  14.2 2.7 %collective-permute-start = (bf16[2,4,96,384]{3,2,1,0:T(8,128)(2,1)}, bf16[2,4,96,384]{3,2,1,0:T(8,128)(2,1)S(1)}, u32[]{:S(2)}, u32[]{:S(2)}) collective-permute-start(bf16[2,4,96,384]{3,2,1,0:T(8,128)(2,1)} %get-tuple-element.56), channel_id=1, source_target_pairs={{0,2},{1,3},{2,0},{3,1},{4,6},{5,7},{6,4},{7,5},{8,10},{9,11},{10,... | collective-permute-start | bytes 1769480 | tf_op jit(solution)/shard_map/ppermute | solution.py:365
  18.4 3.5 %pack_planes.3 = (bf16[2,4,96,384]{3,2,1,0:T(8,128)(2,1)}, bf16[2,4,96,384]{3,2,1,0:T(8,128)(2,1)}, bf16[2,4,96,384]{3,2,1,0:T(8,128)(2,1)}, bf16[2,4,96,384]{3,2,1,0:T(8,128)(2,1)}) custom-call(s32[1]{0:T(128)} %bitcast.place, bf16[2,8,4,36864]{3,2,1,0:T(4,128)(2,1)} %w_ref.1), custom_call_target="tpu_custom_call" | custom-call | bytes 36900 | tf_op jit(solution)/shard_map/pack_planes/pallas_call | solution.py:73
  21.9 10.0 %mix_waves.1 = bf16[8,768,384]{2,1,0:T(8,128)(2,1)} custom-call(bf16[2,8,4,36864]{3,2,1,0:T(4,128)(2,1)} %w_ref.1), custom_call_target="tpu_custom_call" | custom-call | bytes 36900 | tf_op jit(solution)/shard_map/mix_waves/pallas_call | solution.py:116
  33.6 12.0 %charge_potential.1.w_ref = f32[48,384]{1,0:T(8,128)} custom-call(s32[2]{0:T(128)} %pad_add_fusion.place, f32[32,8,256]{2,1,0:T(8,128)} %copy-done.7, f32[48,384]{1,0:T(8,128)} %reshape.105.i_ref), custom_call_target="tpu_custom_call" | custom-call | bytes 36900 | tf_op jit(solution)/shard_map/charge_potential/pallas_call | solution.py:450
  47.3 16.3 %all-to-all-start.1 = ((f32[8,48,384]{2,1,0:T(8,128)}), f32[8,48,384]{2,1,0:T(8,128)S(1)}, u32[]{:S(2)}, u32[]{:S(2)}) async-start(f32[8,48,384]{2,1,0:T(8,128)} %broadcast_in_dim.15), calls=%async_computation.1 | async-start | bytes 1179648 | tf_op jit(solution)/shard_map/all_to_all | solution.py:492
  63.6 10.4 %all-to-all-done.1 = f32[8,48,384]{2,1,0:T(8,128)S(1)} async-done(((f32[8,48,384]{2,1,0:T(8,128)}), f32[8,48,384]{2,1,0:T(8,128)S(1)}, u32[]{:S(2)}, u32[]{:S(2)}) %all-to-all-start.1) | async-done | bytes 589856 | tf_op jit(solution)/shard_map/all_to_all | solution.py:492
  74.8 4.8 %all-to-all-start.2 = ((bf16[8,768,384]{2,1,0:T(8,128)(2,1)}), bf16[8,768,384]{2,1,0:T(8,128)(2,1)}, u32[]{:S(2)}, u32[]{:S(2)}) async-start(bf16[8,768,384]{2,1,0:T(8,128)(2,1)} %mix_waves.1), calls=%async_computation.2 | async-start | bytes 9437184 | tf_op jit(solution)/shard_map/all_to_all | solution.py:499
  79.9 3.4 %collective-permute-start.4 = (bf16[2,4,96,384]{3,2,1,0:T(8,128)(2,1)S(1)}, bf16[2,4,96,384]{3,2,1,0:T(8,128)(2,1)S(1)}, u32[]{:S(2)}, u32[]{:S(2)}) collective-permute-start(bf16[2,4,96,384]{3,2,1,0:T(8,128)(2,1)S(1)} %copy-done.22), channel_id=1, source_target_pairs={{0,3},{1,2},{2,1},{3,0},{4,7},{5,6},{6,5},{7,4},{8,11},{9,10},{10,... | collective-permute-start | bytes 1769480 | tf_op jit(solution)/shard_map/ppermute | solution.py:365
  83.2 2.6 fusion.7
  85.8 2.9 %multiply_convert_fusion = (bf16[384,384]{1,0:T(8,128)(2,1)S(1)}, bf16[384,384]{1,0:T(8,128)(2,1)S(1)}) fusion(s32[384]{0:T(512)S(1)} %iota.13), kind=kLoop, calls=%fused_computation.9 | loop fusion | flops 1916928 | bytes 591360 | tf_op jit(solution)/shard_map/convert_element_type | solution.py:25
  90.2 8.1 %forward.2.refs_4_.s_ref = bf16[4,2,384,384]{3,2,1,0:T(8,128)(2,1)} custom-call(s32[1]{0:T(128)} %bitcast.place, bf16[2,4,96,384]{3,2,1,0:T(8,128)(2,1)} %get-tuple-element.74.refs_0_, bf16[2,4,96,384]{3,2,1,0:T(8,128)(2,1)} %copy-done.4, bf16[2,4,96,384]{3,2,1,0:T(8,128)(2,1)} %copy-done.5, bf16[2,4,96,384]{3,2,1,0:T(8,128)(2,1)} %copy-done.6, ...), custom_call_target="tpu_custom_call" | custom-call | bytes 36900 | tf_op jit(solution)/shard_map/forward/pallas_call | solution.py:233
  98.4 4.9 %mix_space.2.refs_0_ = bf16[8,2,384,384]{3,2,1,0:T(8,128)(2,1)} custom-call(bf16[4,2,384,384]{3,2,1,0:T(8,128)(2,1)} %forward.2.refs_4_.s_ref), custom_call_target="tpu_custom_call" | custom-call | bytes 36900 | tf_op jit(solution)/shard_map/mix_space/pallas_call | solution.py:160
  103.2 8.9 %inverse.3 = (bf16[2,4,96,384]{3,2,1,0:T(8,128)(2,1)}, bf16[2,4,96,384]{3,2,1,0:T(8,128)(2,1)}, bf16[2,4,96,384]{3,2,1,0:T(8,128)(2,1)}, bf16[2,4,96,384]{3,2,1,0:T(8,128)(2,1)}) custom-call(s32[1]{0:T(128)} %bitcast.place, bf16[2,4,96,384]{3,2,1,0:T(8,128)(2,1)} %get-tuple-element.74.refs_0_, bf16[2,4,96,384]{3,2,1,0:T(8,128)(2,1)} %copy-done.4, ...), custom_call_target="tpu_custom_call" | custom-call | bytes 36900 | tf_op jit(solution)/shard_map/inverse/pallas_call | solution.py:278
  112.1 10.0 %collective-permute-done.3.refs_1_ = bf16[2,4,96,384]{3,2,1,0:T(8,128)(2,1)S(1)} collective-permute-done((bf16[2,4,96,384]{3,2,1,0:T(8,128)(2,1)}, bf16[2,4,96,384]{3,2,1,0:T(8,128)(2,1)S(1)}, u32[]{:S(2)}, u32[]{:S(2)}) %collective-permute-start.3) | collective-permute-done | bytes 589856 | tf_op jit(solution)/shard_map/ppermute | solution.py:365
  122.6 11.6 %all-to-all-done.2 = bf16[8,768,384]{2,1,0:T(8,128)(2,1)} async-done(((bf16[8,768,384]{2,1,0:T(8,128)(2,1)}), bf16[8,768,384]{2,1,0:T(8,128)(2,1)}, u32[]{:S(2)}, u32[]{:S(2)}) %all-to-all-start.2) | async-done | bytes 4718624 | tf_op jit(solution)/shard_map/all_to_all | solution.py:499
  134.4 8.1 %forward.3.refs_4_.s_ref = bf16[4,2,384,384]{3,2,1,0:T(8,128)(2,1)} custom-call(s32[1]{0:T(128)} %bitcast.place, bf16[2,4,96,384]{3,2,1,0:T(8,128)(2,1)} %get-tuple-element.86.refs_0_, bf16[2,4,96,384]{3,2,1,0:T(8,128)(2,1)} %copy-done.1, bf16[2,4,96,384]{3,2,1,0:T(8,128)(2,1)} %copy-done.2, bf16[2,4,96,384]{3,2,1,0:T(8,128)(2,1)} %copy-done.3, ...), custom_call_target="tpu_custom_call" | custom-call | bytes 36900 | tf_op jit(solution)/shard_map/forward/pallas_call | solution.py:233
  142.5 4.8 %mix_space.3 = bf16[8,2,384,384]{3,2,1,0:T(8,128)(2,1)} custom-call(bf16[4,2,384,384]{3,2,1,0:T(8,128)(2,1)} %forward.3.refs_4_.s_ref, bf16[8,2,384,384]{3,2,1,0:T(8,128)(2,1)} %mix_space.2.refs_0_), custom_call_target="tpu_custom_call", output_to_operand_aliasing={{}: (1, {})} | custom-call | bytes 36900 | tf_op jit(solution)/shard_map/mix_space/pallas_call | solution.py:160
  147.4 13.1 %collective-permute-done.12.refs_1_ = bf16[2,4,96,384]{3,2,1,0:T(8,128)(2,1)S(1)} collective-permute-done((bf16[2,4,96,384]{3,2,1,0:T(8,128)(2,1)}, bf16[2,4,96,384]{3,2,1,0:T(8,128)(2,1)S(1)}, u32[]{:S(2)}, u32[]{:S(2)}) %collective-permute-start.12) | collective-permute-done | bytes 589856 | tf_op jit(solution)/shard_map/ppermute | solution.py:365
  161.2 4.8 %all-to-all-start.3 = ((bf16[8,2,384,384]{3,2,1,0:T(8,128)(2,1)}), bf16[8,2,384,384]{3,2,1,0:T(8,128)(2,1)}, u32[]{:S(2)}, u32[]{:S(2)}) async-start(bf16[8,2,384,384]{3,2,1,0:T(8,128)(2,1)} %mix_space.3), calls=%async_computation.3 | async-start | bytes 9437184 | tf_op jit(solution)/shard_map/all_to_all | solution.py:522
  166.1 2.7 %collective-permute-start.13 = (bf16[2,4,96,384]{3,2,1,0:T(8,128)(2,1)}, bf16[2,4,96,384]{3,2,1,0:T(8,128)(2,1)S(1)}, u32[]{:S(2)}, u32[]{:S(2)}) collective-permute-start(bf16[2,4,96,384]{3,2,1,0:T(8,128)(2,1)} %get-tuple-element.103), channel_id=1, source_target_pairs={{0,3},{1,2},{2,1},{3,0},{4,7},{5,6},{6,5},{7,4},{8,11},{9,10},{10,... | collective-permute-start | bytes 1769480 | tf_op jit(solution)/shard_map/ppermute | solution.py:365
  168.8 7.7 %inverse.5 = (bf16[2,3,96,384]{3,2,1,0:T(8,128)(2,1)}, bf16[2,3,96,384]{3,2,1,0:T(8,128)(2,1)}, bf16[2,3,96,384]{3,2,1,0:T(8,128)(2,1)}, bf16[2,3,96,384]{3,2,1,0:T(8,128)(2,1)}) custom-call(s32[1]{0:T(128)} %bitcast.place, bf16[2,4,96,384]{3,2,1,0:T(8,128)(2,1)} %get-tuple-element.86.refs_0_, bf16[2,4,96,384]{3,2,1,0:T(8,128)(2,1)} %copy-done.1, ...), custom_call_target="tpu_custom_call" | custom-call | bytes 36900 | tf_op jit(solution)/shard_map/inverse/pallas_call | solution.py:278
  178.3 2.6 %collective-permute-start.10 = (bf16[2,3,96,384]{3,2,1,0:T(8,128)(2,1)}, bf16[2,3,96,384]{3,2,1,0:T(8,128)(2,1)S(1)}, u32[]{:S(2)}, u32[]{:S(2)}) collective-permute-start(bf16[2,3,96,384]{3,2,1,0:T(8,128)(2,1)} %get-tuple-element.96), channel_id=1, source_target_pairs={{0,3},{1,2},{2,1},{3,0},{4,7},{5,6},{6,5},{7,4},{8,11},{9,10},{10,... | collective-permute-start | bytes 1327112 | tf_op jit(solution)/shard_map/ppermute | solution.py:365
  181.7 8.9 %overlap.2.refs_0_ = f32[2,64,64]{2,1,0:T(8,128)} custom-call(bf16[8,1,768,384]{3,2,1,0:T(8,128)(2,1)} %bitcast.9.z_ref, f32[48,384]{1,0:T(8,128)} %reshape.107.w_ref), custom_call_target="tpu_custom_call" | custom-call | bytes 29520000 | tf_op jit(solution)/shard_map/overlap/pallas_call | solution.py:350
  190.6 4.6 %inverse.4 = (bf16[2,1,96,384]{3,2,1,0:T(8,128)(2,1)}, bf16[2,1,96,384]{3,2,1,0:T(8,128)(2,1)}, bf16[2,1,96,384]{3,2,1,0:T(8,128)(2,1)}, bf16[2,1,96,384]{3,2,1,0:T(8,128)(2,1)}) custom-call(s32[1]{0:T(128)} %bitcast.place, bf16[2,4,96,384]{3,2,1,0:T(8,128)(2,1)} %get-tuple-element.86.refs_0_, bf16[2,4,96,384]{3,2,1,0:T(8,128)(2,1)} %copy-done.1, ...), custom_call_target="tpu_custom_call" | custom-call | bytes 36900 | tf_op jit(solution)/shard_map/inverse/pallas_call | solution.py:278
  195.1 27.9 %collective-permute-done.9.refs_1_ = bf16[2,3,96,384]{3,2,1,0:T(8,128)(2,1)S(1)} collective-permute-done((bf16[2,3,96,384]{3,2,1,0:T(8,128)(2,1)}, bf16[2,3,96,384]{3,2,1,0:T(8,128)(2,1)S(1)}, u32[]{:S(2)}, u32[]{:S(2)}) %collective-permute-start.9) | collective-permute-done | bytes 442400 | tf_op jit(solution)/shard_map/ppermute | solution.py:365
  224.3 2.3 collective-permute-start.8
  226.6 4.6 %unpack_planes.3.refs_4_ = bf16[2,8,4,36864]{3,2,1,0:T(4,128)(2,1)} custom-call(s32[1]{0:T(128)} %bitcast.place, bf16[2,4,96,384]{3,2,1,0:T(8,128)(2,1)} %get-tuple-element.99.refs_0_, bf16[2,4,96,384]{3,2,1,0:T(8,128)(2,1)} %copy-done.8, bf16[2,4,96,384]{3,2,1,0:T(8,128)(2,1)} %copy-done.9, bf16[2,4,96,384]{3,2,1,0:T(8,128)(2,1)} %copy-done.10), custom_call_target="tpu_custom_call" | custom-call | bytes 17712000 | tf_op jit(solution)/shard_map/unpack_planes/pallas_call | solution.py:199
  231.2 9.0 %overlap.3 = f32[2,64,64]{2,1,0:T(8,128)} custom-call(bf16[8,2,384,384]{3,2,1,0:T(8,128)(2,1)} %all-to-all-done.3.z_ref, f32[48,384]{1,0:T(8,128)} %charge_potential.1.w_ref, f32[2,64,64]{2,1,0:T(8,128)} %overlap.2.refs_0_), custom_call_target="tpu_custom_call" | custom-call | bytes 29520000 | tf_op jit(solution)/shard_map/overlap/pallas_call | solution.py:350
  242.0 4.3 %all-to-all-start.4 = ((f32[32,1,256]{2,1,0:T(1,128)}), f32[32,1,256]{2,1,0:T(1,128)S(1)}, u32[]{:S(2)}, u32[]{:S(2)}) async-start(f32[32,1,256]{2,1,0:T(1,128)} %reshape.110), calls=%async_computation.4 | async-start | bytes 65536 | tf_op jit(solution)/shard_map/all_to_all | solution.py:560
  247.3 5.2 %unpack_planes.4.refs_4_ = bf16[2,8,4,36864]{3,2,1,0:T(4,128)(2,1)} custom-call(s32[1]{0:T(128)} %bitcast.place, bf16[2,3,96,384]{3,2,1,0:T(8,128)(2,1)} %get-tuple-element.94.refs_0_, bf16[2,3,96,384]{3,2,1,0:T(8,128)(2,1)} %copy-done.11, bf16[2,3,96,384]{3,2,1,0:T(8,128)(2,1)} %copy-done.12, ...), custom_call_target="tpu_custom_call", output_to_operand_aliasing={{}: (5, {})} | custom-call | bytes 13283999 | tf_op jit(solution)/shard_map/unpack_planes/pallas_call | solution.py:199
  (107 shorter events, 22.8 us)
Async XLA Ops:
  3.4 29.1 %all-to-all-start = ((f32[32,8,256]{2,1,0:T(8,128)}), f32[32,8,256]{2,1,0:T(8,128)S(1)}, u32[]{:S(2)}, u32[]{:S(2)}) async-start(f32[32,8,256]{2,1,0:T(8,128)} %pad_maximum_fusion.4), calls=%async_computation | async-start | bytes 524288 | tf_op jit(solution)/shard_map/all_to_all | solution.py:487
  14.2 49.4 %collective-permute-start = (bf16[2,4,96,384]{3,2,1,0:T(8,128)(2,1)}, bf16[2,4,96,384]{3,2,1,0:T(8,128)(2,1)S(1)}, u32[]{:S(2)}, u32[]{:S(2)}) collective-permute-start(bf16[2,4,96,384]{3,2,1,0:T(8,128)(2,1)} %get-tuple-element.56), channel_id=1, source_target_pairs={{0,2},{1,3},{2,0},{3,1},{4,6},{5,7},{6,4},{7,5},{8,10},{9,11},{10,... | collective-permute-start | bytes 1769480 | tf_op jit(solution)/shard_map/ppermute | solution.py:365
  16.8 46.7 %collective-permute-start.1 = (bf16[2,4,96,384]{3,2,1,0:T(8,128)(2,1)}, bf16[2,4,96,384]{3,2,1,0:T(8,128)(2,1)S(1)}, u32[]{:S(2)}, u32[]{:S(2)}) collective-permute-start(bf16[2,4,96,384]{3,2,1,0:T(8,128)(2,1)} %get-tuple-element.57), channel_id=1, source_target_pairs={{0,3},{1,2},{2,1},{3,0},{4,7},{5,6},{6,5},{7,4},{8,11},{9,10},{10,... | collective-permute-start | bytes 1769480 | tf_op jit(solution)/shard_map/ppermute | solution.py:365
  18.3 45.3 %collective-permute-start.2 = (bf16[2,4,96,384]{3,2,1,0:T(8,128)(2,1)}, bf16[2,4,96,384]{3,2,1,0:T(8,128)(2,1)S(1)}, u32[]{:S(2)}, u32[]{:S(2)}) collective-permute-start(bf16[2,4,96,384]{3,2,1,0:T(8,128)(2,1)} %get-tuple-element.58), channel_id=1, source_target_pairs={{0,1},{1,0},{2,3},{3,2},{4,5},{5,4},{6,7},{7,6},{8,9},{9,8},{10,11... | collective-permute-start | bytes 1769480 | tf_op jit(solution)/shard_map/ppermute | solution.py:365
  47.3 26.7 %all-to-all-start.1 = ((f32[8,48,384]{2,1,0:T(8,128)}), f32[8,48,384]{2,1,0:T(8,128)S(1)}, u32[]{:S(2)}, u32[]{:S(2)}) async-start(f32[8,48,384]{2,1,0:T(8,128)} %broadcast_in_dim.15), calls=%async_computation.1 | async-start | bytes 1179648 | tf_op jit(solution)/shard_map/all_to_all | solution.py:492
  63.6 10.5 %copy-start.4 = (bf16[2,4,96,384]{3,2,1,0:T(8,128)(2,1)}, bf16[2,4,96,384]{3,2,1,0:T(8,128)(2,1)S(1)}, u32[]{:S(2)}) copy-start(bf16[2,4,96,384]{3,2,1,0:T(8,128)(2,1)S(1)} %collective-permute-done.refs_1_) | copy-start | bytes 1769476
  63.6 10.4 %copy-start.5 = (bf16[2,4,96,384]{3,2,1,0:T(8,128)(2,1)}, bf16[2,4,96,384]{3,2,1,0:T(8,128)(2,1)S(1)}, u32[]{:S(2)}) copy-start(bf16[2,4,96,384]{3,2,1,0:T(8,128)(2,1)S(1)} %collective-permute-done.1.refs_2_) | copy-start | bytes 1769476
  63.6 10.4 %copy-start.6 = (bf16[2,4,96,384]{3,2,1,0:T(8,128)(2,1)}, bf16[2,4,96,384]{3,2,1,0:T(8,128)(2,1)S(1)}, u32[]{:S(2)}) copy-start(bf16[2,4,96,384]{3,2,1,0:T(8,128)(2,1)S(1)} %collective-permute-done.2.refs_3_) | copy-start | bytes 1769476
  74.0 5.9 %copy-start.22 = (bf16[2,4,96,384]{3,2,1,0:T(8,128)(2,1)S(1)}, bf16[2,4,96,384]{3,2,1,0:T(8,128)(2,1)}, u32[]{:S(2)}) copy-start(bf16[2,4,96,384]{3,2,1,0:T(8,128)(2,1)} %get-tuple-element.71) | copy-start | bytes 1769476
  74.0 9.2 %copy-start.21 = (bf16[2,4,96,384]{3,2,1,0:T(8,128)(2,1)S(1)}, bf16[2,4,96,384]{3,2,1,0:T(8,128)(2,1)}, u32[]{:S(2)}) copy-start(bf16[2,4,96,384]{3,2,1,0:T(8,128)(2,1)} %get-tuple-element.72) | copy-start | bytes 1769476
  74.8 59.4 %all-to-all-start.2 = ((bf16[8,768,384]{2,1,0:T(8,128)(2,1)}), bf16[8,768,384]{2,1,0:T(8,128)(2,1)}, u32[]{:S(2)}, u32[]{:S(2)}) async-start(bf16[8,768,384]{2,1,0:T(8,128)(2,1)} %mix_waves.1), calls=%async_computation.2 | async-start | bytes 9437184 | tf_op jit(solution)/shard_map/all_to_all | solution.py:499
  79.7 42.5 %collective-permute-start.3 = (bf16[2,4,96,384]{3,2,1,0:T(8,128)(2,1)}, bf16[2,4,96,384]{3,2,1,0:T(8,128)(2,1)S(1)}, u32[]{:S(2)}, u32[]{:S(2)}) collective-permute-start(bf16[2,4,96,384]{3,2,1,0:T(8,128)(2,1)} %get-tuple-element.70), channel_id=1, source_target_pairs={{0,2},{1,3},{2,0},{3,1},{4,6},{5,7},{6,4},{7,5},{8,10},{9,11},{10,... | collective-permute-start | bytes 1769480 | tf_op jit(solution)/shard_map/ppermute | solution.py:365
  79.9 42.3 %collective-permute-start.4 = (bf16[2,4,96,384]{3,2,1,0:T(8,128)(2,1)S(1)}, bf16[2,4,96,384]{3,2,1,0:T(8,128)(2,1)S(1)}, u32[]{:S(2)}, u32[]{:S(2)}) collective-permute-start(bf16[2,4,96,384]{3,2,1,0:T(8,128)(2,1)S(1)} %copy-done.22), channel_id=1, source_target_pairs={{0,3},{1,2},{2,1},{3,0},{4,7},{5,6},{6,5},{7,4},{8,11},{9,10},{10,... | collective-permute-start | bytes 1769480 | tf_op jit(solution)/shard_map/ppermute | solution.py:365
  83.2 39.4 %collective-permute-start.5 = (bf16[2,4,96,384]{3,2,1,0:T(8,128)(2,1)S(1)}, bf16[2,4,96,384]{3,2,1,0:T(8,128)(2,1)S(1)}, u32[]{:S(2)}, u32[]{:S(2)}) collective-permute-start(bf16[2,4,96,384]{3,2,1,0:T(8,128)(2,1)S(1)} %copy-done.21), channel_id=1, source_target_pairs={{0,1},{1,0},{2,3},{3,2},{4,5},{5,4},{6,7},{7,6},{8,9},{9,8},{10,11... | collective-permute-start | bytes 1769480 | tf_op jit(solution)/shard_map/ppermute | solution.py:365
  122.2 12.2 %copy-start.1 = (bf16[2,4,96,384]{3,2,1,0:T(8,128)(2,1)}, bf16[2,4,96,384]{3,2,1,0:T(8,128)(2,1)S(1)}, u32[]{:S(2)}) copy-start(bf16[2,4,96,384]{3,2,1,0:T(8,128)(2,1)S(1)} %collective-permute-done.3.refs_1_) | copy-start | bytes 1769476
  122.2 12.2 %copy-start.2 = (bf16[2,4,96,384]{3,2,1,0:T(8,128)(2,1)}, bf16[2,4,96,384]{3,2,1,0:T(8,128)(2,1)S(1)}, u32[]{:S(2)}) copy-start(bf16[2,4,96,384]{3,2,1,0:T(8,128)(2,1)S(1)} %collective-permute-done.4.refs_2_) | copy-start | bytes 1769476
  122.6 11.7 %copy-start.3 = (bf16[2,4,96,384]{3,2,1,0:T(8,128)(2,1)}, bf16[2,4,96,384]{3,2,1,0:T(8,128)(2,1)S(1)}, u32[]{:S(2)}) copy-start(bf16[2,4,96,384]{3,2,1,0:T(8,128)(2,1)S(1)} %collective-permute-done.5.refs_3_) | copy-start | bytes 1769476
  134.2 26.2 %collective-permute-start.12 = (bf16[2,4,96,384]{3,2,1,0:T(8,128)(2,1)}, bf16[2,4,96,384]{3,2,1,0:T(8,128)(2,1)S(1)}, u32[]{:S(2)}, u32[]{:S(2)}) collective-permute-start(bf16[2,4,96,384]{3,2,1,0:T(8,128)(2,1)} %get-tuple-element.101), channel_id=1, source_target_pairs={{0,2},{1,3},{2,0},{3,1},{4,6},{5,7},{6,4},{7,5},{8,10},{9,11},{10,... | collective-permute-start | bytes 1769480 | tf_op jit(solution)/shard_map/ppermute | solution.py:365
  147.4 21.4 %copy-start.20 = (bf16[2,4,96,384]{3,2,1,0:T(8,128)(2,1)S(1)}, bf16[2,4,96,384]{3,2,1,0:T(8,128)(2,1)}, u32[]{:S(2)}) copy-start(bf16[2,4,96,384]{3,2,1,0:T(8,128)(2,1)} %get-tuple-element.104) | copy-start | bytes 1769476
  161.2 70.0 %all-to-all-start.3 = ((bf16[8,2,384,384]{3,2,1,0:T(8,128)(2,1)}), bf16[8,2,384,384]{3,2,1,0:T(8,128)(2,1)}, u32[]{:S(2)}, u32[]{:S(2)}) async-start(bf16[8,2,384,384]{3,2,1,0:T(8,128)(2,1)} %mix_space.3), calls=%async_computation.3 | async-start | bytes 9437184 | tf_op jit(solution)/shard_map/all_to_all | solution.py:522
  166.1 57.0 %collective-permute-start.13 = (bf16[2,4,96,384]{3,2,1,0:T(8,128)(2,1)}, bf16[2,4,96,384]{3,2,1,0:T(8,128)(2,1)S(1)}, u32[]{:S(2)}, u32[]{:S(2)}) collective-permute-start(bf16[2,4,96,384]{3,2,1,0:T(8,128)(2,1)} %get-tuple-element.103), channel_id=1, source_target_pairs={{0,3},{1,2},{2,1},{3,0},{4,7},{5,6},{6,5},{7,4},{8,11},{9,10},{10,... | collective-permute-start | bytes 1769480 | tf_op jit(solution)/shard_map/ppermute | solution.py:365
  168.8 55.5 %collective-permute-start.14 = (bf16[2,4,96,384]{3,2,1,0:T(8,128)(2,1)S(1)}, bf16[2,4,96,384]{3,2,1,0:T(8,128)(2,1)S(1)}, u32[]{:S(2)}, u32[]{:S(2)}) collective-permute-start(bf16[2,4,96,384]{3,2,1,0:T(8,128)(2,1)S(1)} %copy-done.20), channel_id=1, source_target_pairs={{0,1},{1,0},{2,3},{3,2},{4,5},{5,4},{6,7},{7,6},{8,9},{9,8},{10,11... | collective-permute-start | bytes 1769480 | tf_op jit(solution)/shard_map/ppermute | solution.py:365
  176.5 46.5 %collective-permute-start.9 = (bf16[2,3,96,384]{3,2,1,0:T(8,128)(2,1)}, bf16[2,3,96,384]{3,2,1,0:T(8,128)(2,1)S(1)}, u32[]{:S(2)}, u32[]{:S(2)}) collective-permute-start(bf16[2,3,96,384]{3,2,1,0:T(8,128)(2,1)} %get-tuple-element.95), channel_id=1, source_target_pairs={{0,2},{1,3},{2,0},{3,1},{4,6},{5,7},{6,4},{7,5},{8,10},{9,11},{10,... | collective-permute-start | bytes 1327112 | tf_op jit(solution)/shard_map/ppermute | solution.py:365
  178.3 68.1 %collective-permute-start.10 = (bf16[2,3,96,384]{3,2,1,0:T(8,128)(2,1)}, bf16[2,3,96,384]{3,2,1,0:T(8,128)(2,1)S(1)}, u32[]{:S(2)}, u32[]{:S(2)}) collective-permute-start(bf16[2,3,96,384]{3,2,1,0:T(8,128)(2,1)} %get-tuple-element.96), channel_id=1, source_target_pairs={{0,3},{1,2},{2,1},{3,0},{4,7},{5,6},{6,5},{7,4},{8,11},{9,10},{10,... | collective-permute-start | bytes 1327112 | tf_op jit(solution)/shard_map/ppermute | solution.py:365
  180.9 65.4 %collective-permute-start.11 = (bf16[2,3,96,384]{3,2,1,0:T(8,128)(2,1)}, bf16[2,3,96,384]{3,2,1,0:T(8,128)(2,1)S(1)}, u32[]{:S(2)}, u32[]{:S(2)}) collective-permute-start(bf16[2,3,96,384]{3,2,1,0:T(8,128)(2,1)} %get-tuple-element.97), channel_id=1, source_target_pairs={{0,1},{1,0},{2,3},{3,2},{4,5},{5,4},{6,7},{7,6},{8,9},{9,8},{10,11... | collective-permute-start | bytes 1327112 | tf_op jit(solution)/shard_map/ppermute | solution.py:365
  223.1 23.3 %copy-start.11 = (bf16[2,3,96,384]{3,2,1,0:T(8,128)(2,1)}, bf16[2,3,96,384]{3,2,1,0:T(8,128)(2,1)S(1)}, u32[]{:S(2)}) copy-start(bf16[2,3,96,384]{3,2,1,0:T(8,128)(2,1)S(1)} %collective-permute-done.9.refs_1_) | copy-start | bytes 1327108
  223.1 29.4 %collective-permute-start.6 = (bf16[2,1,96,384]{3,2,1,0:T(8,128)(2,1)}, bf16[2,1,96,384]{3,2,1,0:T(8,128)(2,1)S(1)}, u32[]{:S(2)}, u32[]{:S(2)}) collective-permute-start(bf16[2,1,96,384]{3,2,1,0:T(8,128)(2,1)} %get-tuple-element.91), channel_id=1, source_target_pairs={{0,2},{1,3},{2,0},{3,1},{4,6},{5,7},{6,4},{7,5},{8,10},{9,11},{10,... | collective-permute-start | bytes 442376 | tf_op jit(solution)/shard_map/ppermute | solution.py:365
  223.1 3.5 %copy-start.9 = (bf16[2,4,96,384]{3,2,1,0:T(8,128)(2,1)}, bf16[2,4,96,384]{3,2,1,0:T(8,128)(2,1)S(1)}, u32[]{:S(2)}) copy-start(bf16[2,4,96,384]{3,2,1,0:T(8,128)(2,1)S(1)} %collective-permute-done.13.refs_2_) | copy-start | bytes 1769476
  223.1 29.4 %collective-permute-start.7 = (bf16[2,1,96,384]{3,2,1,0:T(8,128)(2,1)}, bf16[2,1,96,384]{3,2,1,0:T(8,128)(2,1)S(1)}, u32[]{:S(2)}, u32[]{:S(2)}) collective-permute-start(bf16[2,1,96,384]{3,2,1,0:T(8,128)(2,1)} %get-tuple-element.92), channel_id=1, source_target_pairs={{0,3},{1,2},{2,1},{3,0},{4,7},{5,6},{6,5},{7,4},{8,11},{9,10},{10,... | collective-permute-start | bytes 442376 | tf_op jit(solution)/shard_map/ppermute | solution.py:365
  224.3 2.3 copy-start.10
  224.3 28.2 %collective-permute-start.8 = (bf16[2,1,96,384]{3,2,1,0:T(8,128)(2,1)}, bf16[2,1,96,384]{3,2,1,0:T(8,128)(2,1)S(1)}, u32[]{:S(2)}, u32[]{:S(2)}) collective-permute-start(bf16[2,1,96,384]{3,2,1,0:T(8,128)(2,1)} %get-tuple-element.93), channel_id=1, source_target_pairs={{0,1},{1,0},{2,3},{3,2},{4,5},{5,4},{6,7},{7,6},{8,9},{9,8},{10,11... | collective-permute-start | bytes 442376 | tf_op jit(solution)/shard_map/ppermute | solution.py:365
  242.0 13.3 %all-to-all-start.4 = ((f32[32,1,256]{2,1,0:T(1,128)}), f32[32,1,256]{2,1,0:T(1,128)S(1)}, u32[]{:S(2)}, u32[]{:S(2)}) async-start(f32[32,1,256]{2,1,0:T(1,128)} %reshape.110), calls=%async_computation.4 | async-start | bytes 65536 | tf_op jit(solution)/shard_map/all_to_all | solution.py:560
  (11 other events, 12.2 us)

commit v7 on v4

--- a/solution.py
+++ b/solution.py
@@ -202,7 +202,7 @@
         out_shape=jax.ShapeDtypeStruct((2, bands, planes, rows * NY), jnp.bfloat16),
         scratch_shapes=[pltpu.VMEM((halves, planes, step, rows, NY), jnp.bfloat16)],
         input_output_aliases=aliases,
-        compiler_params=pltpu.CompilerParams(vmem_limit_bytes=56 << 20),
+        compiler_params=pltpu.CompilerParams(vmem_limit_bytes=12 << 20),
         cost_estimate=lasting(1.2 * count),
         name="unpack_planes",
     )(*operands)
@@ -550,9 +550,10 @@
     col_width = all_bands // ga_count
     blocks = full_matrix.reshape(2, band_groups, bands, ga_count, col_width)
     blocks = blocks.transpose(1, 3, 0, 2, 4).reshape(
-        band_groups * ga_count, 2, bands, col_width
+        band_groups * ga_count, 2, bands * col_width
     )
     subspace = lax.all_to_all(blocks, ("band", "ga"), 0, 0, tiled=True).sum(0)
+    subspace = subspace.reshape(2, bands, col_width)
 
     applied_waves = unpack(returned[1], place, applied_waves, half, bands, planes)
     applied_waves = unpack(returned[2], place, applied_waves, own_bands - 1, bands, planes)

time: 249 us -> 247 us (level)
  waiting for transfers between devices: 57.3 us -> 65.4 us
  Pallas kernels: 106 us -> 101 us
    pallas_call x3, Pallas kernels: 11.9 us -> 6.76 us  [unpack(): pl.pallas_call(functools.partial(unpack_body, groups), grid=(2, halves, c...]
    ppermute x15, waiting for transfers between devices: 50.1 us -> 55.1 us  [shifted(): lax.ppermute(message, 'ga', [(i, i ^ s) for i in range(groups)])]
    unnamed x49 -> x33, local copies, waits for them, and re-layouts: 4.18 us -> 0.85 us
  transfers between devices with their start and end apart: 20 -> 20, of which waited for: 8 -> 9; matrix products, arithmetic and copies ran while one was open for 5% -> 5% of each run, Pallas kernels for 43% -> 41%
where the time goes in v7:
time: 247 us; the launch traced here: 246 us
  Pallas kernels  101 us (41%)
  waiting for transfers between devices  65.4 us (26%)
  starting transfers between devices  61.2 us (25%)
  other arithmetic  8.55 us (3%)
  local copies, waits for them, and re-layouts  8.52 us (3%)
    ppermute x15, waiting for transfers between devices, shifted(): lax.ppermute(message, 'ga', [(i, i ^ s) for i in range(groups)])  55.1 us
    ppermute x15, starting transfers between devices, shifted(): lax.ppermute(message, 'ga', [(i, i ^ s) for i in range(groups)])  37.1 us
    pallas_call x3, Pallas kernels, inverse(): pl.pallas_call(functools.partial(inverse_body, groups), grid=(bands // st...  21.3 us
    pallas_call x2, Pallas kernels, overlap(): pl.pallas_call(functools.partial(overlap_body, scale, per), in_specs=[who...  17.9 us
    pallas_call x2, Pallas kernels, forward(): pl.pallas_call(functools.partial(forward_body, groups), grid=(bands // st...  16.3 us
    pallas_call x1, Pallas kernels, own_share(): pl.pallas_call(functools.partial(charges_body, planes, slab_rows), in_spe...  12 us
    pallas_call x1, Pallas kernels, mix_waves(): pl.pallas_call(mix_waves_body, grid=(shares,), in_specs=[pl.BlockSpec((2,...  10 us
    pallas_call x2, Pallas kernels, mix_space(): pl.pallas_call(mix_space_body, grid=(NX // rows,), in_specs=in_specs, out...  9.75 us
  transfers between devices with their start and end apart: 20, of which 9 were waited for; matrix products, arithmetic and copies ran while one was open for 5% of the time, Pallas kernels for 41%

profile of v7, /device:TPU:0, one launch (start us, length us, event | category | flops | bytes accessed | tf_op | source)
XLA Modules:
  0.0 245.7 jit_solution(4246773625992079200)
XLA Ops:
  3.4 7.3 %all-to-all-start = ((f32[32,8,256]{2,1,0:T(8,128)}), f32[32,8,256]{2,1,0:T(8,128)S(1)}, u32[]{:S(2)}, u32[]{:S(2)}) async-start(f32[32,8,256]{2,1,0:T(8,128)} %pad_maximum_fusion.4), calls=%async_computation | async-start | bytes 524288 | tf_op jit(solution)/shard_map/all_to_all | solution.py:481
  10.7 3.5 %pack_planes.2 = (bf16[2,4,96,384]{3,2,1,0:T(8,128)(2,1)}, bf16[2,4,96,384]{3,2,1,0:T(8,128)(2,1)}, bf16[2,4,96,384]{3,2,1,0:T(8,128)(2,1)}, bf16[2,4,96,384]{3,2,1,0:T(8,128)(2,1)}) custom-call(s32[1]{0:T(128)} %bitcast.place, bf16[2,8,4,36864]{3,2,1,0:T(4,128)(2,1)} %w_ref.1), custom_call_target="tpu_custom_call" | custom-call | bytes 36900 | tf_op jit(solution)/shard_map/pack_planes/pallas_call | solution.py:69
  18.6 3.5 %pack_planes.3 = (bf16[2,4,96,384]{3,2,1,0:T(8,128)(2,1)}, bf16[2,4,96,384]{3,2,1,0:T(8,128)(2,1)}, bf16[2,4,96,384]{3,2,1,0:T(8,128)(2,1)}, bf16[2,4,96,384]{3,2,1,0:T(8,128)(2,1)}) custom-call(s32[1]{0:T(128)} %bitcast.place, bf16[2,8,4,36864]{3,2,1,0:T(4,128)(2,1)} %w_ref.1), custom_call_target="tpu_custom_call" | custom-call | bytes 36900 | tf_op jit(solution)/shard_map/pack_planes/pallas_call | solution.py:69
  22.1 10.0 %mix_waves.1 = bf16[8,768,384]{2,1,0:T(8,128)(2,1)} custom-call(bf16[2,8,4,36864]{3,2,1,0:T(4,128)(2,1)} %w_ref.1), custom_call_target="tpu_custom_call" | custom-call | bytes 36900 | tf_op jit(solution)/shard_map/mix_waves/pallas_call | solution.py:112
  33.8 12.0 %charge_potential.1.w_ref = f32[48,384]{1,0:T(8,128)} custom-call(s32[2]{0:T(128)} %pad_add_fusion.place, f32[32,8,256]{2,1,0:T(8,128)} %copy-done.10, f32[48,384]{1,0:T(8,128)} %reshape.108.i_ref), custom_call_target="tpu_custom_call" | custom-call | bytes 36900 | tf_op jit(solution)/shard_map/charge_potential/pallas_call | solution.py:444
  47.5 3.9 %all-to-all-start.1 = ((f32[8,48,384]{2,1,0:T(8,128)}), f32[8,48,384]{2,1,0:T(8,128)S(1)}, u32[]{:S(2)}, u32[]{:S(2)}) async-start(f32[8,48,384]{2,1,0:T(8,128)} %broadcast_in_dim.15), calls=%async_computation.1 | async-start | bytes 1179648 | tf_op jit(solution)/shard_map/all_to_all | solution.py:486
  51.5 7.1 %collective-permute-done.1.refs_2_ = bf16[2,4,96,384]{3,2,1,0:T(8,128)(2,1)S(1)} collective-permute-done((bf16[2,4,96,384]{3,2,1,0:T(8,128)(2,1)}, bf16[2,4,96,384]{3,2,1,0:T(8,128)(2,1)S(1)}, u32[]{:S(2)}, u32[]{:S(2)}) %collective-permute-start.1) | collective-permute-done | bytes 589856 | tf_op jit(solution)/shard_map/ppermute | solution.py:361
  58.6 3.4 %all-to-all-done.1 = f32[8,48,384]{2,1,0:T(8,128)S(1)} async-done(((f32[8,48,384]{2,1,0:T(8,128)}), f32[8,48,384]{2,1,0:T(8,128)S(1)}, u32[]{:S(2)}, u32[]{:S(2)}) %all-to-all-start.1) | async-done | bytes 589856 | tf_op jit(solution)/shard_map/all_to_all | solution.py:486
  62.8 4.8 %all-to-all-start.2 = ((bf16[8,768,384]{2,1,0:T(8,128)(2,1)}), bf16[8,768,384]{2,1,0:T(8,128)(2,1)}, u32[]{:S(2)}, u32[]{:S(2)}) async-start(bf16[8,768,384]{2,1,0:T(8,128)(2,1)} %mix_waves.1), calls=%async_computation.2 | async-start | bytes 9437184 | tf_op jit(solution)/shard_map/all_to_all | solution.py:493
  67.6 9.5 %collective-permute-start.3 = (bf16[2,4,96,384]{3,2,1,0:T(8,128)(2,1)}, bf16[2,4,96,384]{3,2,1,0:T(8,128)(2,1)S(1)}, u32[]{:S(2)}, u32[]{:S(2)}) collective-permute-start(bf16[2,4,96,384]{3,2,1,0:T(8,128)(2,1)} %get-tuple-element.70), channel_id=1, source_target_pairs={{0,1},{1,0},{2,3},{3,2},{4,5},{5,4},{6,7},{7,6},{8,9},{9,8},{10,11... | collective-permute-start | bytes 1769480 | tf_op jit(solution)/shard_map/ppermute | solution.py:361
  79.5 2.6 %fusion.7 = bf16[384,384]{1,0:T(8,128)(2,1)S(1)} fusion(s32[384]{0:T(512)S(1)} %iota.13), kind=kLoop, calls=%fused_computation.19 | loop fusion | flops 2064384 | bytes 296448 | tf_op jit(solution)/shard_map/neg | solution.py:496
  82.1 2.9 %multiply_convert_fusion = (bf16[384,384]{1,0:T(8,128)(2,1)S(1)}, bf16[384,384]{1,0:T(8,128)(2,1)S(1)}) fusion(s32[384]{0:T(512)S(1)} %iota.13), kind=kLoop, calls=%fused_computation.9 | loop fusion | flops 1916928 | bytes 591360 | tf_op jit(solution)/shard_map/convert_element_type | solution.py:25
  86.5 8.1 %forward.2.refs_4_.s_ref = bf16[4,2,384,384]{3,2,1,0:T(8,128)(2,1)} custom-call(s32[1]{0:T(128)} %bitcast.place, bf16[2,4,96,384]{3,2,1,0:T(8,128)(2,1)} %get-tuple-element.74.refs_0_, bf16[2,4,96,384]{3,2,1,0:T(8,128)(2,1)} %copy-done.7, bf16[2,4,96,384]{3,2,1,0:T(8,128)(2,1)} %copy-done.8, bf16[2,4,96,384]{3,2,1,0:T(8,128)(2,1)} %copy-done.9, ...), custom_call_target="tpu_custom_call" | custom-call | bytes 36900 | tf_op jit(solution)/shard_map/forward/pallas_call | solution.py:229
  94.6 4.9 %mix_space.2.refs_0_ = bf16[8,2,384,384]{3,2,1,0:T(8,128)(2,1)} custom-call(bf16[4,2,384,384]{3,2,1,0:T(8,128)(2,1)} %forward.2.refs_4_.s_ref), custom_call_target="tpu_custom_call" | custom-call | bytes 36900 | tf_op jit(solution)/shard_map/mix_space/pallas_call | solution.py:156
  99.5 8.9 %inverse.3 = (bf16[2,4,96,384]{3,2,1,0:T(8,128)(2,1)}, bf16[2,4,96,384]{3,2,1,0:T(8,128)(2,1)}, bf16[2,4,96,384]{3,2,1,0:T(8,128)(2,1)}, bf16[2,4,96,384]{3,2,1,0:T(8,128)(2,1)}) custom-call(s32[1]{0:T(128)} %bitcast.place, bf16[2,4,96,384]{3,2,1,0:T(8,128)(2,1)} %get-tuple-element.74.refs_0_, bf16[2,4,96,384]{3,2,1,0:T(8,128)(2,1)} %copy-done.7, ...), custom_call_target="tpu_custom_call" | custom-call | bytes 36900 | tf_op jit(solution)/shard_map/inverse/pallas_call | solution.py:274
  108.5 11.0 %collective-permute-done.4.refs_2_ = bf16[2,4,96,384]{3,2,1,0:T(8,128)(2,1)S(1)} collective-permute-done((bf16[2,4,96,384]{3,2,1,0:T(8,128)(2,1)S(1)}, bf16[2,4,96,384]{3,2,1,0:T(8,128)(2,1)S(1)}, u32[]{:S(2)}, u32[]{:S(2)}) %collective-permute-start.4) | collective-permute-done | bytes 589856 | tf_op jit(solution)/shard_map/ppermute | solution.py:361
  119.5 2.6 %all-to-all-done.2 = bf16[8,768,384]{2,1,0:T(8,128)(2,1)} async-done(((bf16[8,768,384]{2,1,0:T(8,128)(2,1)}), bf16[8,768,384]{2,1,0:T(8,128)(2,1)}, u32[]{:S(2)}, u32[]{:S(2)}) %all-to-all-start.2) | async-done | bytes 4718624 | tf_op jit(solution)/shard_map/all_to_all | solution.py:493
  122.1 9.9 %collective-permute-start.13 = (bf16[2,4,96,384]{3,2,1,0:T(8,128)(2,1)}, bf16[2,4,96,384]{3,2,1,0:T(8,128)(2,1)S(1)}, u32[]{:S(2)}, u32[]{:S(2)}) collective-permute-start(bf16[2,4,96,384]{3,2,1,0:T(8,128)(2,1)} %get-tuple-element.102), channel_id=1, source_target_pairs={{0,2},{1,3},{2,0},{3,1},{4,6},{5,7},{6,4},{7,5},{8,10},{9,11},{10,... | collective-permute-start | bytes 1769480 | tf_op jit(solution)/shard_map/ppermute | solution.py:361
  132.0 8.2 %forward.3.refs_4_.s_ref = bf16[4,2,384,384]{3,2,1,0:T(8,128)(2,1)} custom-call(s32[1]{0:T(128)} %bitcast.place, bf16[2,4,96,384]{3,2,1,0:T(8,128)(2,1)} %get-tuple-element.86.refs_0_, bf16[2,4,96,384]{3,2,1,0:T(8,128)(2,1)} %copy-done.4, bf16[2,4,96,384]{3,2,1,0:T(8,128)(2,1)} %copy-done.5, bf16[2,4,96,384]{3,2,1,0:T(8,128)(2,1)} %copy-done.6, ...), custom_call_target="tpu_custom_call" | custom-call | bytes 36900 | tf_op jit(solution)/shard_map/forward/pallas_call | solution.py:229
  140.2 4.9 %mix_space.3 = bf16[8,2,384,384]{3,2,1,0:T(8,128)(2,1)} custom-call(bf16[4,2,384,384]{3,2,1,0:T(8,128)(2,1)} %forward.3.refs_4_.s_ref, bf16[8,2,384,384]{3,2,1,0:T(8,128)(2,1)} %mix_space.2.refs_0_), custom_call_target="tpu_custom_call", output_to_operand_aliasing={{}: (1, {})} | custom-call | bytes 36900 | tf_op jit(solution)/shard_map/mix_space/pallas_call | solution.py:156
  145.1 12.4 %collective-permute-done.13.refs_2_ = bf16[2,4,96,384]{3,2,1,0:T(8,128)(2,1)S(1)} collective-permute-done((bf16[2,4,96,384]{3,2,1,0:T(8,128)(2,1)}, bf16[2,4,96,384]{3,2,1,0:T(8,128)(2,1)S(1)}, u32[]{:S(2)}, u32[]{:S(2)}) %collective-permute-start.13) | collective-permute-done | bytes 589856 | tf_op jit(solution)/shard_map/ppermute | solution.py:361
  157.5 4.9 %all-to-all-start.3 = ((bf16[8,2,384,384]{3,2,1,0:T(8,128)(2,1)}), bf16[8,2,384,384]{3,2,1,0:T(8,128)(2,1)}, u32[]{:S(2)}, u32[]{:S(2)}) async-start(bf16[8,2,384,384]{3,2,1,0:T(8,128)(2,1)} %mix_space.3), calls=%async_computation.3 | async-start | bytes 9437184 | tf_op jit(solution)/shard_map/all_to_all | solution.py:517
  164.4 7.7 %inverse.5 = (bf16[2,3,96,384]{3,2,1,0:T(8,128)(2,1)}, bf16[2,3,96,384]{3,2,1,0:T(8,128)(2,1)}, bf16[2,3,96,384]{3,2,1,0:T(8,128)(2,1)}, bf16[2,3,96,384]{3,2,1,0:T(8,128)(2,1)}) custom-call(s32[1]{0:T(128)} %bitcast.place, bf16[2,4,96,384]{3,2,1,0:T(8,128)(2,1)} %get-tuple-element.86.refs_0_, bf16[2,4,96,384]{3,2,1,0:T(8,128)(2,1)} %copy-done.4, ...), custom_call_target="tpu_custom_call" | custom-call | bytes 36900 | tf_op jit(solution)/shard_map/inverse/pallas_call | solution.py:274
  177.3 8.9 %overlap.2.refs_0_ = f32[2,64,64]{2,1,0:T(8,128)} custom-call(bf16[8,1,768,384]{3,2,1,0:T(8,128)(2,1)} %bitcast.9.z_ref, f32[48,384]{1,0:T(8,128)} %reshape.110.w_ref), custom_call_target="tpu_custom_call" | custom-call | bytes 29520000 | tf_op jit(solution)/shard_map/overlap/pallas_call | solution.py:346
  186.2 4.6 %inverse.4 = (bf16[2,1,96,384]{3,2,1,0:T(8,128)(2,1)}, bf16[2,1,96,384]{3,2,1,0:T(8,128)(2,1)}, bf16[2,1,96,384]{3,2,1,0:T(8,128)(2,1)}, bf16[2,1,96,384]{3,2,1,0:T(8,128)(2,1)}) custom-call(s32[1]{0:T(128)} %bitcast.place, bf16[2,4,96,384]{3,2,1,0:T(8,128)(2,1)} %get-tuple-element.86.refs_0_, bf16[2,4,96,384]{3,2,1,0:T(8,128)(2,1)} %copy-done.4, ...), custom_call_target="tpu_custom_call" | custom-call | bytes 36900 | tf_op jit(solution)/shard_map/inverse/pallas_call | solution.py:274
  190.8 17.7 %collective-permute-done.9.refs_1_ = bf16[2,3,96,384]{3,2,1,0:T(8,128)(2,1)S(1)} collective-permute-done((bf16[2,3,96,384]{3,2,1,0:T(8,128)(2,1)}, bf16[2,3,96,384]{3,2,1,0:T(8,128)(2,1)S(1)}, u32[]{:S(2)}, u32[]{:S(2)}) %collective-permute-start.9) | collective-permute-done | bytes 442400 | tf_op jit(solution)/shard_map/ppermute | solution.py:361
  212.9 2.7 %unpack_planes.3.refs_4_ = bf16[2,8,4,36864]{3,2,1,0:T(4,128)(2,1)} custom-call(s32[1]{0:T(128)} %bitcast.place, bf16[2,4,96,384]{3,2,1,0:T(8,128)(2,1)S(1)} %copy-done, bf16[2,4,96,384]{3,2,1,0:T(8,128)(2,1)S(1)} %collective-permute-done.12.refs_1_, bf16[2,4,96,384]{3,2,1,0:T(8,128)(2,1)S(1)} %collective-permute-done.13.refs_2_, ...), custom_call_target="tpu_custom_call" | custom-call | bytes 17712000 | tf_op jit(solution)/shard_map/unpack_planes/pallas_call | solution.py:195
  216.9 9.0 %overlap.3 = f32[2,64,64]{2,1,0:T(8,128)} custom-call(bf16[8,2,384,384]{3,2,1,0:T(8,128)(2,1)} %all-to-all-done.3.z_ref, f32[48,384]{1,0:T(8,128)} %charge_potential.1.w_ref, f32[2,64,64]{2,1,0:T(8,128)} %overlap.2.refs_0_), custom_call_target="tpu_custom_call" | custom-call | bytes 29520000 | tf_op jit(solution)/shard_map/overlap/pallas_call | solution.py:346
  227.6 3.2 %all-to-all-start.4 = ((f32[32,2,128]{2,1,0:T(2,128)}), f32[32,2,128]{2,1,0:T(2,128)S(1)}, u32[]{:S(2)}, u32[]{:S(2)}) async-start(f32[32,2,128]{2,1,0:T(2,128)} %copy.28), calls=%async_computation.4 | async-start | bytes 65536 | tf_op jit(solution)/shard_map/all_to_all | solution.py:555
  230.9 2.9 %unpack_planes.4.refs_4_ = bf16[2,8,4,36864]{3,2,1,0:T(4,128)(2,1)} custom-call(s32[1]{0:T(128)} %bitcast.place, bf16[2,3,96,384]{3,2,1,0:T(8,128)(2,1)S(1)} %copy-done.1, bf16[2,3,96,384]{3,2,1,0:T(8,128)(2,1)S(1)} %collective-permute-done.9.refs_1_, bf16[2,3,96,384]{3,2,1,0:T(8,128)(2,1)S(1)} %collective-permute-done.10.refs_2_, ...), custom_call_target="tpu_custom_call", output_to_operand_aliasing={{}: (5, {})} | custom-call | bytes 13283999 | tf_op jit(solution)/shard_map/unpack_planes/pallas_call | solution.py:195
  233.8 6.9 %collective-permute-done.7.refs_2_ = bf16[2,1,96,384]{3,2,1,0:T(8,128)(2,1)S(1)} collective-permute-done((bf16[2,1,96,384]{3,2,1,0:T(8,128)(2,1)}, bf16[2,1,96,384]{3,2,1,0:T(8,128)(2,1)S(1)}, u32[]{:S(2)}, u32[]{:S(2)}) %collective-permute-start.7) | collective-permute-done | bytes 147488 | tf_op jit(solution)/shard_map/ppermute | solution.py:361
  241.8 3.1 %all-to-all-done.4 = f32[32,2,128]{2,1,0:T(2,128)S(1)} async-done(((f32[32,2,128]{2,1,0:T(2,128)}), f32[32,2,128]{2,1,0:T(2,128)S(1)}, u32[]{:S(2)}, u32[]{:S(2)}) %all-to-all-start.4) | async-done | bytes 32800 | tf_op jit(solution)/shard_map/all_to_all | solution.py:555
  (92 shorter events, 31.7 us)
Async XLA Ops:
  0.6 1.9 copy-start.12
  3.4 29.4 %all-to-all-start = ((f32[32,8,256]{2,1,0:T(8,128)}), f32[32,8,256]{2,1,0:T(8,128)S(1)}, u32[]{:S(2)}, u32[]{:S(2)}) async-start(f32[32,8,256]{2,1,0:T(8,128)} %pad_maximum_fusion.4), calls=%async_computation | async-start | bytes 524288 | tf_op jit(solution)/shard_map/all_to_all | solution.py:481
  14.2 37.3 %collective-permute-start = (bf16[2,4,96,384]{3,2,1,0:T(8,128)(2,1)}, bf16[2,4,96,384]{3,2,1,0:T(8,128)(2,1)S(1)}, u32[]{:S(2)}, u32[]{:S(2)}) collective-permute-start(bf16[2,4,96,384]{3,2,1,0:T(8,128)(2,1)} %get-tuple-element.56), channel_id=1, source_target_pairs={{0,1},{1,0},{2,3},{3,2},{4,5},{5,4},{6,7},{7,6},{8,9},{9,8},{10,11... | collective-permute-start | bytes 1769480 | tf_op jit(solution)/shard_map/ppermute | solution.py:361
  16.0 42.6 %collective-permute-start.1 = (bf16[2,4,96,384]{3,2,1,0:T(8,128)(2,1)}, bf16[2,4,96,384]{3,2,1,0:T(8,128)(2,1)S(1)}, u32[]{:S(2)}, u32[]{:S(2)}) collective-permute-start(bf16[2,4,96,384]{3,2,1,0:T(8,128)(2,1)} %get-tuple-element.57), channel_id=1, source_target_pairs={{0,2},{1,3},{2,0},{3,1},{4,6},{5,7},{6,4},{7,5},{8,10},{9,11},{10,... | collective-permute-start | bytes 1769480 | tf_op jit(solution)/shard_map/ppermute | solution.py:361
  18.4 40.2 %collective-permute-start.2 = (bf16[2,4,96,384]{3,2,1,0:T(8,128)(2,1)}, bf16[2,4,96,384]{3,2,1,0:T(8,128)(2,1)S(1)}, u32[]{:S(2)}, u32[]{:S(2)}) collective-permute-start(bf16[2,4,96,384]{3,2,1,0:T(8,128)(2,1)} %get-tuple-element.58), channel_id=1, source_target_pairs={{0,3},{1,2},{2,1},{3,0},{4,7},{5,6},{6,5},{7,4},{8,11},{9,10},{10,... | collective-permute-start | bytes 1769480 | tf_op jit(solution)/shard_map/ppermute | solution.py:361
  47.5 14.4 %all-to-all-start.1 = ((f32[8,48,384]{2,1,0:T(8,128)}), f32[8,48,384]{2,1,0:T(8,128)S(1)}, u32[]{:S(2)}, u32[]{:S(2)}) async-start(f32[8,48,384]{2,1,0:T(8,128)} %broadcast_in_dim.15), calls=%async_computation.1 | async-start | bytes 1179648 | tf_op jit(solution)/shard_map/all_to_all | solution.py:486
  51.5 10.5 %copy-start.7 = (bf16[2,4,96,384]{3,2,1,0:T(8,128)(2,1)}, bf16[2,4,96,384]{3,2,1,0:T(8,128)(2,1)S(1)}, u32[]{:S(2)}) copy-start(bf16[2,4,96,384]{3,2,1,0:T(8,128)(2,1)S(1)} %collective-permute-done.refs_1_) | copy-start | bytes 1769476
  58.6 3.4 %copy-start.8 = (bf16[2,4,96,384]{3,2,1,0:T(8,128)(2,1)}, bf16[2,4,96,384]{3,2,1,0:T(8,128)(2,1)S(1)}, u32[]{:S(2)}) copy-start(bf16[2,4,96,384]{3,2,1,0:T(8,128)(2,1)S(1)} %collective-permute-done.1.refs_2_) | copy-start | bytes 1769476
  58.6 3.4 %copy-start.9 = (bf16[2,4,96,384]{3,2,1,0:T(8,128)(2,1)}, bf16[2,4,96,384]{3,2,1,0:T(8,128)(2,1)S(1)}, u32[]{:S(2)}) copy-start(bf16[2,4,96,384]{3,2,1,0:T(8,128)(2,1)S(1)} %collective-permute-done.2.refs_3_) | copy-start | bytes 1769476
  61.9 15.1 %copy-start.15 = (bf16[2,4,96,384]{3,2,1,0:T(8,128)(2,1)S(1)}, bf16[2,4,96,384]{3,2,1,0:T(8,128)(2,1)}, u32[]{:S(2)}) copy-start(bf16[2,4,96,384]{3,2,1,0:T(8,128)(2,1)} %get-tuple-element.71) | copy-start | bytes 1769476
  61.9 15.6 %copy-start.14 = (bf16[2,4,96,384]{3,2,1,0:T(8,128)(2,1)S(1)}, bf16[2,4,96,384]{3,2,1,0:T(8,128)(2,1)}, u32[]{:S(2)}) copy-start(bf16[2,4,96,384]{3,2,1,0:T(8,128)(2,1)} %get-tuple-element.72) | copy-start | bytes 1769476
  62.8 59.4 %all-to-all-start.2 = ((bf16[8,768,384]{2,1,0:T(8,128)(2,1)}), bf16[8,768,384]{2,1,0:T(8,128)(2,1)}, u32[]{:S(2)}, u32[]{:S(2)}) async-start(bf16[8,768,384]{2,1,0:T(8,128)(2,1)} %mix_waves.1), calls=%async_computation.2 | async-start | bytes 9437184 | tf_op jit(solution)/shard_map/all_to_all | solution.py:493
  67.6 40.9 %collective-permute-start.3 = (bf16[2,4,96,384]{3,2,1,0:T(8,128)(2,1)}, bf16[2,4,96,384]{3,2,1,0:T(8,128)(2,1)S(1)}, u32[]{:S(2)}, u32[]{:S(2)}) collective-permute-start(bf16[2,4,96,384]{3,2,1,0:T(8,128)(2,1)} %get-tuple-element.70), channel_id=1, source_target_pairs={{0,1},{1,0},{2,3},{3,2},{4,5},{5,4},{6,7},{7,6},{8,9},{9,8},{10,11... | collective-permute-start | bytes 1769480 | tf_op jit(solution)/shard_map/ppermute | solution.py:361
  77.1 42.4 %collective-permute-start.4 = (bf16[2,4,96,384]{3,2,1,0:T(8,128)(2,1)S(1)}, bf16[2,4,96,384]{3,2,1,0:T(8,128)(2,1)S(1)}, u32[]{:S(2)}, u32[]{:S(2)}) collective-permute-start(bf16[2,4,96,384]{3,2,1,0:T(8,128)(2,1)S(1)} %copy-done.15), channel_id=1, source_target_pairs={{0,2},{1,3},{2,0},{3,1},{4,6},{5,7},{6,4},{7,5},{8,10},{9,11},{10,... | collective-permute-start | bytes 1769480 | tf_op jit(solution)/shard_map/ppermute | solution.py:361
  77.6 41.9 %collective-permute-start.5 = (bf16[2,4,96,384]{3,2,1,0:T(8,128)(2,1)S(1)}, bf16[2,4,96,384]{3,2,1,0:T(8,128)(2,1)S(1)}, u32[]{:S(2)}, u32[]{:S(2)}) collective-permute-start(bf16[2,4,96,384]{3,2,1,0:T(8,128)(2,1)S(1)} %copy-done.14), channel_id=1, source_target_pairs={{0,3},{1,2},{2,1},{3,0},{4,7},{5,6},{6,5},{7,4},{8,11},{9,10},{10,... | collective-permute-start | bytes 1769480 | tf_op jit(solution)/shard_map/ppermute | solution.py:361
  108.5 23.5 %copy-start.4 = (bf16[2,4,96,384]{3,2,1,0:T(8,128)(2,1)}, bf16[2,4,96,384]{3,2,1,0:T(8,128)(2,1)S(1)}, u32[]{:S(2)}) copy-start(bf16[2,4,96,384]{3,2,1,0:T(8,128)(2,1)S(1)} %collective-permute-done.3.refs_1_) | copy-start | bytes 1769476
  119.5 12.5 %copy-start.5 = (bf16[2,4,96,384]{3,2,1,0:T(8,128)(2,1)}, bf16[2,4,96,384]{3,2,1,0:T(8,128)(2,1)S(1)}, u32[]{:S(2)}) copy-start(bf16[2,4,96,384]{3,2,1,0:T(8,128)(2,1)S(1)} %collective-permute-done.4.refs_2_) | copy-start | bytes 1769476
  119.5 12.5 %copy-start.6 = (bf16[2,4,96,384]{3,2,1,0:T(8,128)(2,1)}, bf16[2,4,96,384]{3,2,1,0:T(8,128)(2,1)S(1)}, u32[]{:S(2)}) copy-start(bf16[2,4,96,384]{3,2,1,0:T(8,128)(2,1)S(1)} %collective-permute-done.5.refs_3_) | copy-start | bytes 1769476
  122.1 35.4 %collective-permute-start.13 = (bf16[2,4,96,384]{3,2,1,0:T(8,128)(2,1)}, bf16[2,4,96,384]{3,2,1,0:T(8,128)(2,1)S(1)}, u32[]{:S(2)}, u32[]{:S(2)}) collective-permute-start(bf16[2,4,96,384]{3,2,1,0:T(8,128)(2,1)} %get-tuple-element.102), channel_id=1, source_target_pairs={{0,2},{1,3},{2,0},{3,1},{4,6},{5,7},{6,4},{7,5},{8,10},{9,11},{10,... | collective-permute-start | bytes 1769480 | tf_op jit(solution)/shard_map/ppermute | solution.py:361
  157.5 59.4 %all-to-all-start.3 = ((bf16[8,2,384,384]{3,2,1,0:T(8,128)(2,1)}), bf16[8,2,384,384]{3,2,1,0:T(8,128)(2,1)}, u32[]{:S(2)}, u32[]{:S(2)}) async-start(bf16[8,2,384,384]{3,2,1,0:T(8,128)(2,1)} %mix_space.3), calls=%async_computation.3 | async-start | bytes 9437184 | tf_op jit(solution)/shard_map/all_to_all | solution.py:517
  162.3 46.2 %collective-permute-start.12 = (bf16[2,4,96,384]{3,2,1,0:T(8,128)(2,1)}, bf16[2,4,96,384]{3,2,1,0:T(8,128)(2,1)S(1)}, u32[]{:S(2)}, u32[]{:S(2)}) collective-permute-start(bf16[2,4,96,384]{3,2,1,0:T(8,128)(2,1)} %get-tuple-element.100), channel_id=1, source_target_pairs={{0,1},{1,0},{2,3},{3,2},{4,5},{5,4},{6,7},{7,6},{8,9},{9,8},{10,11... | collective-permute-start | bytes 1769480 | tf_op jit(solution)/shard_map/ppermute | solution.py:361
  162.4 48.6 %collective-permute-start.14 = (bf16[2,4,96,384]{3,2,1,0:T(8,128)(2,1)}, bf16[2,4,96,384]{3,2,1,0:T(8,128)(2,1)S(1)}, u32[]{:S(2)}, u32[]{:S(2)}) collective-permute-start(bf16[2,4,96,384]{3,2,1,0:T(8,128)(2,1)} %get-tuple-element.104), channel_id=1, source_target_pairs={{0,3},{1,2},{2,1},{3,0},{4,7},{5,6},{6,5},{7,4},{8,11},{9,10},{10,... | collective-permute-start | bytes 1769480 | tf_op jit(solution)/shard_map/ppermute | solution.py:361
  172.2 36.4 %collective-permute-start.9 = (bf16[2,3,96,384]{3,2,1,0:T(8,128)(2,1)}, bf16[2,3,96,384]{3,2,1,0:T(8,128)(2,1)S(1)}, u32[]{:S(2)}, u32[]{:S(2)}) collective-permute-start(bf16[2,3,96,384]{3,2,1,0:T(8,128)(2,1)} %get-tuple-element.95), channel_id=1, source_target_pairs={{0,1},{1,0},{2,3},{3,2},{4,5},{5,4},{6,7},{7,6},{8,9},{9,8},{10,11... | collective-permute-start | bytes 1327112 | tf_op jit(solution)/shard_map/ppermute | solution.py:361
  173.3 57.6 %collective-permute-start.10 = (bf16[2,3,96,384]{3,2,1,0:T(8,128)(2,1)}, bf16[2,3,96,384]{3,2,1,0:T(8,128)(2,1)S(1)}, u32[]{:S(2)}, u32[]{:S(2)}) collective-permute-start(bf16[2,3,96,384]{3,2,1,0:T(8,128)(2,1)} %get-tuple-element.96), channel_id=1, source_target_pairs={{0,2},{1,3},{2,0},{3,1},{4,6},{5,7},{6,4},{7,5},{8,10},{9,11},{10,... | collective-permute-start | bytes 1327112 | tf_op jit(solution)/shard_map/ppermute | solution.py:361
  174.7 56.2 %collective-permute-start.11 = (bf16[2,3,96,384]{3,2,1,0:T(8,128)(2,1)}, bf16[2,3,96,384]{3,2,1,0:T(8,128)(2,1)S(1)}, u32[]{:S(2)}, u32[]{:S(2)}) collective-permute-start(bf16[2,3,96,384]{3,2,1,0:T(8,128)(2,1)} %get-tuple-element.97), channel_id=1, source_target_pairs={{0,3},{1,2},{2,1},{3,0},{4,7},{5,6},{6,5},{7,4},{8,11},{9,10},{10,... | collective-permute-start | bytes 1327112 | tf_op jit(solution)/shard_map/ppermute | solution.py:361
  186.2 26.7 %copy-start = (bf16[2,4,96,384]{3,2,1,0:T(8,128)(2,1)S(1)}, bf16[2,4,96,384]{3,2,1,0:T(8,128)(2,1)}, u32[]{:S(2)}) copy-start(bf16[2,4,96,384]{3,2,1,0:T(8,128)(2,1)} %get-tuple-element.99.refs_0_) | copy-start | bytes 1769476
  208.5 25.3 %collective-permute-start.6 = (bf16[2,1,96,384]{3,2,1,0:T(8,128)(2,1)}, bf16[2,1,96,384]{3,2,1,0:T(8,128)(2,1)S(1)}, u32[]{:S(2)}, u32[]{:S(2)}) collective-permute-start(bf16[2,1,96,384]{3,2,1,0:T(8,128)(2,1)} %get-tuple-element.91), channel_id=1, source_target_pairs={{0,1},{1,0},{2,3},{3,2},{4,5},{5,4},{6,7},{7,6},{8,9},{9,8},{10,11... | collective-permute-start | bytes 442376 | tf_op jit(solution)/shard_map/ppermute | solution.py:361
  208.5 32.2 %collective-permute-start.7 = (bf16[2,1,96,384]{3,2,1,0:T(8,128)(2,1)}, bf16[2,1,96,384]{3,2,1,0:T(8,128)(2,1)S(1)}, u32[]{:S(2)}, u32[]{:S(2)}) collective-permute-start(bf16[2,1,96,384]{3,2,1,0:T(8,128)(2,1)} %get-tuple-element.92), channel_id=1, source_target_pairs={{0,2},{1,3},{2,0},{3,1},{4,6},{5,7},{6,4},{7,5},{8,10},{9,11},{10,... | collective-permute-start | bytes 442376 | tf_op jit(solution)/shard_map/ppermute | solution.py:361
  211.0 29.7 %collective-permute-start.8 = (bf16[2,1,96,384]{3,2,1,0:T(8,128)(2,1)}, bf16[2,1,96,384]{3,2,1,0:T(8,128)(2,1)S(1)}, u32[]{:S(2)}, u32[]{:S(2)}) collective-permute-start(bf16[2,1,96,384]{3,2,1,0:T(8,128)(2,1)} %get-tuple-element.93), channel_id=1, source_target_pairs={{0,3},{1,2},{2,1},{3,0},{4,7},{5,6},{6,5},{7,4},{8,11},{9,10},{10,... | collective-permute-start | bytes 442376 | tf_op jit(solution)/shard_map/ppermute | solution.py:361
  215.7 15.2 %copy-start.1 = (bf16[2,3,96,384]{3,2,1,0:T(8,128)(2,1)S(1)}, bf16[2,3,96,384]{3,2,1,0:T(8,128)(2,1)}, u32[]{:S(2)}) copy-start(bf16[2,3,96,384]{3,2,1,0:T(8,128)(2,1)} %get-tuple-element.94.refs_0_) | copy-start | bytes 1327108
  227.6 17.3 %all-to-all-start.4 = ((f32[32,2,128]{2,1,0:T(2,128)}), f32[32,2,128]{2,1,0:T(2,128)S(1)}, u32[]{:S(2)}, u32[]{:S(2)}) async-start(f32[32,2,128]{2,1,0:T(2,128)} %copy.28), calls=%async_computation.4 | async-start | bytes 65536 | tf_op jit(solution)/shard_map/all_to_all | solution.py:555
  230.9 9.9 %copy-start.2 = (bf16[2,1,96,384]{3,2,1,0:T(8,128)(2,1)S(1)}, bf16[2,1,96,384]{3,2,1,0:T(8,128)(2,1)}, u32[]{:S(2)}) copy-start(bf16[2,1,96,384]{3,2,1,0:T(8,128)(2,1)} %get-tuple-element.90.refs_0_) | copy-start | bytes 442372
  (4 other events, 5.7 us)

commit v8 on v7

--- a/solution.py
+++ b/solution.py
@@ -542,7 +542,6 @@
     returned.append(shifted(inverse(arrived[1], 0, half - 1, place, *spectrum)))
     grams, place = lax.optimization_barrier((grams, place))
     returned.append(shifted(inverse(arrived[1], half - 1, 1, place, *spectrum)))
-    grams, applied_waves = lax.optimization_barrier((grams, applied_waves))
     full_matrix = overlap(
         met_space, space_weights, per // met_space.shape[1], scale, grams
     )

time: 247 us -> 248 us (level)
  waiting for transfers between devices: 65.4 us -> 58.1 us
  local copies, waits for them, and re-layouts: 8.52 us -> 13.3 us
  Pallas kernels: 101 us -> 104 us
    ppermute x15, waiting for transfers between devices: 55.1 us -> 48.4 us  [shifted(): lax.ppermute(message, 'ga', [(i, i ^ s) for i in range(groups)])]
    all_to_all x1, waiting for transfers between devices: 3.11 us -> 0.01 us  [shards(): subspace = lax.all_to_all(blocks, ('band', 'ga'), 0, 0, tiled=True).sum(0)]
    pallas_call x3, Pallas kernels: 6.76 us -> 9.59 us  [unpack(): pl.pallas_call(functools.partial(unpack_body, groups), grid=(2, halves, c...]
    all_to_all x1, waiting for transfers between devices: 1.2 us -> 3.83 us  [shards(): met_space = lax.all_to_all(mixed, 'band', 0, 0, tiled=True)]
  transfers between devices with their start and end apart: 20 -> 20, of which waited for: 9 -> 7; matrix products, arithmetic and copies ran while one was open for 5% -> 7% of each run, Pallas kernels for 41% -> 42%
where the time goes in v8:
time: 248 us; the launch traced here: 247 us
  Pallas kernels  104 us (42%)
  starting transfers between devices  61.4 us (25%)
  waiting for transfers between devices  58.1 us (23%)
  local copies, waits for them, and re-layouts  13.3 us (5%)
  other arithmetic  9.3 us (4%)
    ppermute x15, waiting for transfers between devices, shifted(): lax.ppermute(message, 'ga', [(i, i ^ s) for i in range(groups)])  48.4 us
    ppermute x15, starting transfers between devices, shifted(): lax.ppermute(message, 'ga', [(i, i ^ s) for i in range(groups)])  37.3 us
    pallas_call x3, Pallas kernels, inverse(): pl.pallas_call(functools.partial(inverse_body, groups), grid=(bands // st...  21.2 us
    pallas_call x2, Pallas kernels, overlap(): pl.pallas_call(functools.partial(overlap_body, scale, per), in_specs=[who...  17.9 us
    pallas_call x2, Pallas kernels, forward(): pl.pallas_call(functools.partial(forward_body, groups), grid=(bands // st...  16.3 us
    pallas_call x1, Pallas kernels, own_share(): pl.pallas_call(functools.partial(charges_body, planes, slab_rows), in_spe...  12 us
    pallas_call x1, Pallas kernels, mix_waves(): pl.pallas_call(mix_waves_body, grid=(shares,), in_specs=[pl.BlockSpec((2,...  10.1 us
    pallas_call x2, Pallas kernels, mix_space(): pl.pallas_call(mix_space_body, grid=(NX // rows,), in_specs=in_specs, out...  9.68 us
  transfers between devices with their start and end apart: 20, of which 7 were waited for; matrix products, arithmetic and copies ran while one was open for 7% of the time, Pallas kernels for 42%

profile of v8, /device:TPU:0, one launch (start us, length us, event | category | flops | bytes accessed | tf_op | source)
XLA Modules:
  0.0 246.7 jit_solution(15593840917594691930)
XLA Ops:
  3.4 7.3 %all-to-all-start = ((f32[32,8,256]{2,1,0:T(8,128)}), f32[32,8,256]{2,1,0:T(8,128)S(1)}, u32[]{:S(2)}, u32[]{:S(2)}) async-start(f32[32,8,256]{2,1,0:T(8,128)} %pad_maximum_fusion.4), calls=%async_computation | async-start | bytes 524288 | tf_op jit(solution)/shard_map/all_to_all | solution.py:481
  10.7 3.5 %pack_planes.2 = (bf16[2,4,96,384]{3,2,1,0:T(8,128)(2,1)}, bf16[2,4,96,384]{3,2,1,0:T(8,128)(2,1)}, bf16[2,4,96,384]{3,2,1,0:T(8,128)(2,1)}, bf16[2,4,96,384]{3,2,1,0:T(8,128)(2,1)}) custom-call(s32[1]{0:T(128)} %bitcast.place, bf16[2,8,4,36864]{3,2,1,0:T(4,128)(2,1)} %w_ref.1), custom_call_target="tpu_custom_call" | custom-call | bytes 36900 | tf_op jit(solution)/shard_map/pack_planes/pallas_call | solution.py:69
  18.6 3.5 %pack_planes.3 = (bf16[2,4,96,384]{3,2,1,0:T(8,128)(2,1)}, bf16[2,4,96,384]{3,2,1,0:T(8,128)(2,1)}, bf16[2,4,96,384]{3,2,1,0:T(8,128)(2,1)}, bf16[2,4,96,384]{3,2,1,0:T(8,128)(2,1)}) custom-call(s32[1]{0:T(128)} %bitcast.place, bf16[2,8,4,36864]{3,2,1,0:T(4,128)(2,1)} %w_ref.1), custom_call_target="tpu_custom_call" | custom-call | bytes 36900 | tf_op jit(solution)/shard_map/pack_planes/pallas_call | solution.py:69
  22.1 10.1 %mix_waves.1 = bf16[8,768,384]{2,1,0:T(8,128)(2,1)} custom-call(bf16[2,8,4,36864]{3,2,1,0:T(4,128)(2,1)} %w_ref.1), custom_call_target="tpu_custom_call" | custom-call | bytes 36900 | tf_op jit(solution)/shard_map/mix_waves/pallas_call | solution.py:112
  33.8 12.0 %charge_potential.1.w_ref = f32[48,384]{1,0:T(8,128)} custom-call(s32[2]{0:T(128)} %pad_add_fusion.place, f32[32,8,256]{2,1,0:T(8,128)} %copy-done.10, f32[48,384]{1,0:T(8,128)} %reshape.108.i_ref), custom_call_target="tpu_custom_call" | custom-call | bytes 36900 | tf_op jit(solution)/shard_map/charge_potential/pallas_call | solution.py:444
  47.5 3.9 %all-to-all-start.1 = ((f32[8,48,384]{2,1,0:T(8,128)}), f32[8,48,384]{2,1,0:T(8,128)S(1)}, u32[]{:S(2)}, u32[]{:S(2)}) async-start(f32[8,48,384]{2,1,0:T(8,128)} %broadcast_in_dim.15), calls=%async_computation.1 | async-start | bytes 1179648 | tf_op jit(solution)/shard_map/all_to_all | solution.py:486
  51.5 7.1 %collective-permute-done.1.refs_2_ = bf16[2,4,96,384]{3,2,1,0:T(8,128)(2,1)S(1)} collective-permute-done((bf16[2,4,96,384]{3,2,1,0:T(8,128)(2,1)}, bf16[2,4,96,384]{3,2,1,0:T(8,128)(2,1)S(1)}, u32[]{:S(2)}, u32[]{:S(2)}) %collective-permute-start.1) | collective-permute-done | bytes 589856 | tf_op jit(solution)/shard_map/ppermute | solution.py:361
  58.6 3.3 %all-to-all-done.1 = f32[8,48,384]{2,1,0:T(8,128)S(1)} async-done(((f32[8,48,384]{2,1,0:T(8,128)}), f32[8,48,384]{2,1,0:T(8,128)S(1)}, u32[]{:S(2)}, u32[]{:S(2)}) %all-to-all-start.1) | async-done | bytes 589856 | tf_op jit(solution)/shard_map/all_to_all | solution.py:486
  62.7 4.8 %all-to-all-start.2 = ((bf16[8,768,384]{2,1,0:T(8,128)(2,1)}), bf16[8,768,384]{2,1,0:T(8,128)(2,1)}, u32[]{:S(2)}, u32[]{:S(2)}) async-start(bf16[8,768,384]{2,1,0:T(8,128)(2,1)} %mix_waves.1), calls=%async_computation.2 | async-start | bytes 9437184 | tf_op jit(solution)/shard_map/all_to_all | solution.py:493
  67.6 9.6 %collective-permute-start.3 = (bf16[2,4,96,384]{3,2,1,0:T(8,128)(2,1)}, bf16[2,4,96,384]{3,2,1,0:T(8,128)(2,1)S(1)}, u32[]{:S(2)}, u32[]{:S(2)}) collective-permute-start(bf16[2,4,96,384]{3,2,1,0:T(8,128)(2,1)} %get-tuple-element.68), channel_id=1, source_target_pairs={{0,1},{1,0},{2,3},{3,2},{4,5},{5,4},{6,7},{7,6},{8,9},{9,8},{10,11... | collective-permute-start | bytes 1769480 | tf_op jit(solution)/shard_map/ppermute | solution.py:361
  79.6 2.6 %fusion.7 = bf16[384,384]{1,0:T(8,128)(2,1)S(1)} fusion(s32[384]{0:T(512)S(1)} %iota.13), kind=kLoop, calls=%fused_computation.19 | loop fusion | flops 2064384 | bytes 296448 | tf_op jit(solution)/shard_map/neg | solution.py:496
  82.2 2.9 %multiply_convert_fusion = (bf16[384,384]{1,0:T(8,128)(2,1)S(1)}, bf16[384,384]{1,0:T(8,128)(2,1)S(1)}) fusion(s32[384]{0:T(512)S(1)} %iota.13), kind=kLoop, calls=%fused_computation.9 | loop fusion | flops 1916928 | bytes 591360 | tf_op jit(solution)/shard_map/convert_element_type | solution.py:25
  86.6 8.1 %forward.2.refs_4_.s_ref = bf16[4,2,384,384]{3,2,1,0:T(8,128)(2,1)} custom-call(s32[1]{0:T(128)} %bitcast.place, bf16[2,4,96,384]{3,2,1,0:T(8,128)(2,1)} %get-tuple-element.72.refs_0_, bf16[2,4,96,384]{3,2,1,0:T(8,128)(2,1)} %copy-done.7, bf16[2,4,96,384]{3,2,1,0:T(8,128)(2,1)} %copy-done.8, bf16[2,4,96,384]{3,2,1,0:T(8,128)(2,1)} %copy-done.9, ...), custom_call_target="tpu_custom_call" | custom-call | bytes 36900 | tf_op jit(solution)/shard_map/forward/pallas_call | solution.py:229
  94.8 4.8 %mix_space.2.refs_0_ = bf16[8,2,384,384]{3,2,1,0:T(8,128)(2,1)} custom-call(bf16[4,2,384,384]{3,2,1,0:T(8,128)(2,1)} %forward.2.refs_4_.s_ref), custom_call_target="tpu_custom_call" | custom-call | bytes 36900 | tf_op jit(solution)/shard_map/mix_space/pallas_call | solution.py:156
  99.6 9.0 %inverse.3 = (bf16[2,4,96,384]{3,2,1,0:T(8,128)(2,1)}, bf16[2,4,96,384]{3,2,1,0:T(8,128)(2,1)}, bf16[2,4,96,384]{3,2,1,0:T(8,128)(2,1)}, bf16[2,4,96,384]{3,2,1,0:T(8,128)(2,1)}) custom-call(s32[1]{0:T(128)} %bitcast.place, bf16[2,4,96,384]{3,2,1,0:T(8,128)(2,1)} %get-tuple-element.72.refs_0_, bf16[2,4,96,384]{3,2,1,0:T(8,128)(2,1)} %copy-done.7, ...), custom_call_target="tpu_custom_call" | custom-call | bytes 36900 | tf_op jit(solution)/shard_map/inverse/pallas_call | solution.py:274
  108.6 11.0 %collective-permute-done.4.refs_2_ = bf16[2,4,96,384]{3,2,1,0:T(8,128)(2,1)S(1)} collective-permute-done((bf16[2,4,96,384]{3,2,1,0:T(8,128)(2,1)S(1)}, bf16[2,4,96,384]{3,2,1,0:T(8,128)(2,1)S(1)}, u32[]{:S(2)}, u32[]{:S(2)}) %collective-permute-start.4) | collective-permute-done | bytes 589856 | tf_op jit(solution)/shard_map/ppermute | solution.py:361
  119.6 2.6 %all-to-all-done.2 = bf16[8,768,384]{2,1,0:T(8,128)(2,1)} async-done(((bf16[8,768,384]{2,1,0:T(8,128)(2,1)}), bf16[8,768,384]{2,1,0:T(8,128)(2,1)}, u32[]{:S(2)}, u32[]{:S(2)}) %all-to-all-start.2) | async-done | bytes 4718624 | tf_op jit(solution)/shard_map/all_to_all | solution.py:493
  122.1 10.0 %collective-permute-start.13 = (bf16[2,4,96,384]{3,2,1,0:T(8,128)(2,1)}, bf16[2,4,96,384]{3,2,1,0:T(8,128)(2,1)S(1)}, u32[]{:S(2)}, u32[]{:S(2)}) collective-permute-start(bf16[2,4,96,384]{3,2,1,0:T(8,128)(2,1)} %get-tuple-element.99), channel_id=1, source_target_pairs={{0,2},{1,3},{2,0},{3,1},{4,6},{5,7},{6,4},{7,5},{8,10},{9,11},{10,... | collective-permute-start | bytes 1769480 | tf_op jit(solution)/shard_map/ppermute | solution.py:361
  132.1 8.2 %forward.3.refs_4_.s_ref = bf16[4,2,384,384]{3,2,1,0:T(8,128)(2,1)} custom-call(s32[1]{0:T(128)} %bitcast.place, bf16[2,4,96,384]{3,2,1,0:T(8,128)(2,1)} %get-tuple-element.84.refs_0_, bf16[2,4,96,384]{3,2,1,0:T(8,128)(2,1)} %copy-done.4, bf16[2,4,96,384]{3,2,1,0:T(8,128)(2,1)} %copy-done.5, bf16[2,4,96,384]{3,2,1,0:T(8,128)(2,1)} %copy-done.6, ...), custom_call_target="tpu_custom_call" | custom-call | bytes 36900 | tf_op jit(solution)/shard_map/forward/pallas_call | solution.py:229
  140.3 4.8 %mix_space.3 = bf16[8,2,384,384]{3,2,1,0:T(8,128)(2,1)} custom-call(bf16[4,2,384,384]{3,2,1,0:T(8,128)(2,1)} %forward.3.refs_4_.s_ref, bf16[8,2,384,384]{3,2,1,0:T(8,128)(2,1)} %mix_space.2.refs_0_), custom_call_target="tpu_custom_call", output_to_operand_aliasing={{}: (1, {})} | custom-call | bytes 36900 | tf_op jit(solution)/shard_map/mix_space/pallas_call | solution.py:156
  145.1 12.5 %collective-permute-done.13.refs_2_ = bf16[2,4,96,384]{3,2,1,0:T(8,128)(2,1)S(1)} collective-permute-done((bf16[2,4,96,384]{3,2,1,0:T(8,128)(2,1)}, bf16[2,4,96,384]{3,2,1,0:T(8,128)(2,1)S(1)}, u32[]{:S(2)}, u32[]{:S(2)}) %collective-permute-start.13) | collective-permute-done | bytes 589856 | tf_op jit(solution)/shard_map/ppermute | solution.py:361
  157.6 4.8 %all-to-all-start.3 = ((bf16[8,2,384,384]{3,2,1,0:T(8,128)(2,1)}), bf16[8,2,384,384]{3,2,1,0:T(8,128)(2,1)}, u32[]{:S(2)}, u32[]{:S(2)}) async-start(bf16[8,2,384,384]{3,2,1,0:T(8,128)(2,1)} %mix_space.3), calls=%async_computation.3 | async-start | bytes 9437184 | tf_op jit(solution)/shard_map/all_to_all | solution.py:517
  164.5 7.7 %inverse.5 = (bf16[2,3,96,384]{3,2,1,0:T(8,128)(2,1)}, bf16[2,3,96,384]{3,2,1,0:T(8,128)(2,1)}, bf16[2,3,96,384]{3,2,1,0:T(8,128)(2,1)}, bf16[2,3,96,384]{3,2,1,0:T(8,128)(2,1)}) custom-call(s32[1]{0:T(128)} %bitcast.place, bf16[2,4,96,384]{3,2,1,0:T(8,128)(2,1)} %get-tuple-element.84.refs_0_, bf16[2,4,96,384]{3,2,1,0:T(8,128)(2,1)} %copy-done.4, ...), custom_call_target="tpu_custom_call" | custom-call | bytes 36900 | tf_op jit(solution)/shard_map/inverse/pallas_call | solution.py:274
  177.4 8.9 %overlap.2.refs_0_ = f32[2,64,64]{2,1,0:T(8,128)} custom-call(bf16[8,1,768,384]{3,2,1,0:T(8,128)(2,1)} %bitcast.9.z_ref, f32[48,384]{1,0:T(8,128)} %reshape.110.w_ref), custom_call_target="tpu_custom_call" | custom-call | bytes 29520000 | tf_op jit(solution)/shard_map/overlap/pallas_call | solution.py:346
  186.3 4.5 %inverse.4 = (bf16[2,1,96,384]{3,2,1,0:T(8,128)(2,1)}, bf16[2,1,96,384]{3,2,1,0:T(8,128)(2,1)}, bf16[2,1,96,384]{3,2,1,0:T(8,128)(2,1)}, bf16[2,1,96,384]{3,2,1,0:T(8,128)(2,1)}) custom-call(s32[1]{0:T(128)} %bitcast.place, bf16[2,4,96,384]{3,2,1,0:T(8,128)(2,1)} %get-tuple-element.84.refs_0_, bf16[2,4,96,384]{3,2,1,0:T(8,128)(2,1)} %copy-done.4, ...), custom_call_target="tpu_custom_call" | custom-call | bytes 36900 | tf_op jit(solution)/shard_map/inverse/pallas_call | solution.py:274
  190.9 17.8 %collective-permute-done.9.refs_1_ = bf16[2,3,96,384]{3,2,1,0:T(8,128)(2,1)S(1)} collective-permute-done((bf16[2,3,96,384]{3,2,1,0:T(8,128)(2,1)}, bf16[2,3,96,384]{3,2,1,0:T(8,128)(2,1)S(1)}, u32[]{:S(2)}, u32[]{:S(2)}) %collective-permute-start.9) | collective-permute-done | bytes 442400 | tf_op jit(solution)/shard_map/ppermute | solution.py:361
  208.7 2.5 %collective-permute-start.7 = (bf16[2,1,96,384]{3,2,1,0:T(8,128)(2,1)}, bf16[2,1,96,384]{3,2,1,0:T(8,128)(2,1)S(1)}, u32[]{:S(2)}, u32[]{:S(2)}) collective-permute-start(bf16[2,1,96,384]{3,2,1,0:T(8,128)(2,1)} %get-tuple-element.90), channel_id=1, source_target_pairs={{0,2},{1,3},{2,0},{3,1},{4,6},{5,7},{6,4},{7,5},{8,10},{9,11},{10,... | collective-permute-start | bytes 442376 | tf_op jit(solution)/shard_map/ppermute | solution.py:361
  213.1 3.8 %all-to-all-done.3.z_ref = bf16[8,2,384,384]{3,2,1,0:T(8,128)(2,1)} async-done(((bf16[8,2,384,384]{3,2,1,0:T(8,128)(2,1)}), bf16[8,2,384,384]{3,2,1,0:T(8,128)(2,1)}, u32[]{:S(2)}, u32[]{:S(2)}) %all-to-all-start.3) | async-done | bytes 4718624 | tf_op jit(solution)/shard_map/all_to_all | solution.py:517
  216.9 9.0 %overlap.3 = f32[2,64,64]{2,1,0:T(8,128)} custom-call(bf16[8,2,384,384]{3,2,1,0:T(8,128)(2,1)} %all-to-all-done.3.z_ref, f32[48,384]{1,0:T(8,128)} %charge_potential.1.w_ref, f32[2,64,64]{2,1,0:T(8,128)} %overlap.2.refs_0_), custom_call_target="tpu_custom_call" | custom-call | bytes 29520000 | tf_op jit(solution)/shard_map/overlap/pallas_call | solution.py:346
  232.4 3.2 %all-to-all-start.4 = ((f32[32,2,128]{2,1,0:T(2,128)}), f32[32,2,128]{2,1,0:T(2,128)}, u32[]{:S(2)}, u32[]{:S(2)}) async-start(f32[32,2,128]{2,1,0:T(2,128)} %copy.28), calls=%async_computation.4 | async-start | bytes 65536 | tf_op jit(solution)/shard_map/all_to_all | solution.py:554
  235.6 2.8 %unpack_planes.3.refs_4_ = bf16[2,8,4,36864]{3,2,1,0:T(4,128)(2,1)} custom-call(s32[1]{0:T(128)} %bitcast.place, bf16[2,4,96,384]{3,2,1,0:T(8,128)(2,1)S(1)} %copy-done, bf16[2,4,96,384]{3,2,1,0:T(8,128)(2,1)S(1)} %collective-permute-done.12.refs_1_, bf16[2,4,96,384]{3,2,1,0:T(8,128)(2,1)S(1)} %collective-permute-done.13.refs_2_, ...), custom_call_target="tpu_custom_call" | custom-call | bytes 17712000 | tf_op jit(solution)/shard_map/unpack_planes/pallas_call | solution.py:195
  238.4 4.8 %unpack_planes.4.refs_4_ = bf16[2,8,4,36864]{3,2,1,0:T(4,128)(2,1)} custom-call(s32[1]{0:T(128)} %bitcast.place, bf16[2,3,96,384]{3,2,1,0:T(8,128)(2,1)S(1)} %copy-done.1, bf16[2,3,96,384]{3,2,1,0:T(8,128)(2,1)S(1)} %collective-permute-done.9.refs_1_, bf16[2,3,96,384]{3,2,1,0:T(8,128)(2,1)S(1)} %collective-permute-done.10.refs_2_, ...), custom_call_target="tpu_custom_call", output_to_operand_aliasing={{}: (5, {})} | custom-call | bytes 13283999 | tf_op jit(solution)/shard_map/unpack_planes/pallas_call | solution.py:195
  (94 shorter events, 34.4 us)
Async XLA Ops:
  3.4 29.4 %all-to-all-start = ((f32[32,8,256]{2,1,0:T(8,128)}), f32[32,8,256]{2,1,0:T(8,128)S(1)}, u32[]{:S(2)}, u32[]{:S(2)}) async-start(f32[32,8,256]{2,1,0:T(8,128)} %pad_maximum_fusion.4), calls=%async_computation | async-start | bytes 524288 | tf_op jit(solution)/shard_map/all_to_all | solution.py:481
  14.2 37.2 %collective-permute-start = (bf16[2,4,96,384]{3,2,1,0:T(8,128)(2,1)}, bf16[2,4,96,384]{3,2,1,0:T(8,128)(2,1)S(1)}, u32[]{:S(2)}, u32[]{:S(2)}) collective-permute-start(bf16[2,4,96,384]{3,2,1,0:T(8,128)(2,1)} %get-tuple-element.54), channel_id=1, source_target_pairs={{0,1},{1,0},{2,3},{3,2},{4,5},{5,4},{6,7},{7,6},{8,9},{9,8},{10,11... | collective-permute-start | bytes 1769480 | tf_op jit(solution)/shard_map/ppermute | solution.py:361
  16.0 42.6 %collective-permute-start.1 = (bf16[2,4,96,384]{3,2,1,0:T(8,128)(2,1)}, bf16[2,4,96,384]{3,2,1,0:T(8,128)(2,1)S(1)}, u32[]{:S(2)}, u32[]{:S(2)}) collective-permute-start(bf16[2,4,96,384]{3,2,1,0:T(8,128)(2,1)} %get-tuple-element.55), channel_id=1, source_target_pairs={{0,2},{1,3},{2,0},{3,1},{4,6},{5,7},{6,4},{7,5},{8,10},{9,11},{10,... | collective-permute-start | bytes 1769480 | tf_op jit(solution)/shard_map/ppermute | solution.py:361
  18.4 40.2 %collective-permute-start.2 = (bf16[2,4,96,384]{3,2,1,0:T(8,128)(2,1)}, bf16[2,4,96,384]{3,2,1,0:T(8,128)(2,1)S(1)}, u32[]{:S(2)}, u32[]{:S(2)}) collective-permute-start(bf16[2,4,96,384]{3,2,1,0:T(8,128)(2,1)} %get-tuple-element.56), channel_id=1, source_target_pairs={{0,3},{1,2},{2,1},{3,0},{4,7},{5,6},{6,5},{7,4},{8,11},{9,10},{10,... | collective-permute-start | bytes 1769480 | tf_op jit(solution)/shard_map/ppermute | solution.py:361
  47.5 14.4 %all-to-all-start.1 = ((f32[8,48,384]{2,1,0:T(8,128)}), f32[8,48,384]{2,1,0:T(8,128)S(1)}, u32[]{:S(2)}, u32[]{:S(2)}) async-start(f32[8,48,384]{2,1,0:T(8,128)} %broadcast_in_dim.15), calls=%async_computation.1 | async-start | bytes 1179648 | tf_op jit(solution)/shard_map/all_to_all | solution.py:486
  51.5 10.5 %copy-start.7 = (bf16[2,4,96,384]{3,2,1,0:T(8,128)(2,1)}, bf16[2,4,96,384]{3,2,1,0:T(8,128)(2,1)S(1)}, u32[]{:S(2)}) copy-start(bf16[2,4,96,384]{3,2,1,0:T(8,128)(2,1)S(1)} %collective-permute-done.refs_1_) | copy-start | bytes 1769476
  58.6 3.3 %copy-start.8 = (bf16[2,4,96,384]{3,2,1,0:T(8,128)(2,1)}, bf16[2,4,96,384]{3,2,1,0:T(8,128)(2,1)S(1)}, u32[]{:S(2)}) copy-start(bf16[2,4,96,384]{3,2,1,0:T(8,128)(2,1)S(1)} %collective-permute-done.1.refs_2_) | copy-start | bytes 1769476
  58.6 3.3 %copy-start.9 = (bf16[2,4,96,384]{3,2,1,0:T(8,128)(2,1)}, bf16[2,4,96,384]{3,2,1,0:T(8,128)(2,1)S(1)}, u32[]{:S(2)}) copy-start(bf16[2,4,96,384]{3,2,1,0:T(8,128)(2,1)S(1)} %collective-permute-done.2.refs_3_) | copy-start | bytes 1769476
  61.9 15.2 %copy-start.16 = (bf16[2,4,96,384]{3,2,1,0:T(8,128)(2,1)S(1)}, bf16[2,4,96,384]{3,2,1,0:T(8,128)(2,1)}, u32[]{:S(2)}) copy-start(bf16[2,4,96,384]{3,2,1,0:T(8,128)(2,1)} %get-tuple-element.69) | copy-start | bytes 1769476
  61.9 15.8 %copy-start.15 = (bf16[2,4,96,384]{3,2,1,0:T(8,128)(2,1)S(1)}, bf16[2,4,96,384]{3,2,1,0:T(8,128)(2,1)}, u32[]{:S(2)}) copy-start(bf16[2,4,96,384]{3,2,1,0:T(8,128)(2,1)} %get-tuple-element.70) | copy-start | bytes 1769476
  62.7 59.4 %all-to-all-start.2 = ((bf16[8,768,384]{2,1,0:T(8,128)(2,1)}), bf16[8,768,384]{2,1,0:T(8,128)(2,1)}, u32[]{:S(2)}, u32[]{:S(2)}) async-start(bf16[8,768,384]{2,1,0:T(8,128)(2,1)} %mix_waves.1), calls=%async_computation.2 | async-start | bytes 9437184 | tf_op jit(solution)/shard_map/all_to_all | solution.py:493
  67.6 41.0 %collective-permute-start.3 = (bf16[2,4,96,384]{3,2,1,0:T(8,128)(2,1)}, bf16[2,4,96,384]{3,2,1,0:T(8,128)(2,1)S(1)}, u32[]{:S(2)}, u32[]{:S(2)}) collective-permute-start(bf16[2,4,96,384]{3,2,1,0:T(8,128)(2,1)} %get-tuple-element.68), channel_id=1, source_target_pairs={{0,1},{1,0},{2,3},{3,2},{4,5},{5,4},{6,7},{7,6},{8,9},{9,8},{10,11... | collective-permute-start | bytes 1769480 | tf_op jit(solution)/shard_map/ppermute | solution.py:361
  77.2 42.4 %collective-permute-start.4 = (bf16[2,4,96,384]{3,2,1,0:T(8,128)(2,1)S(1)}, bf16[2,4,96,384]{3,2,1,0:T(8,128)(2,1)S(1)}, u32[]{:S(2)}, u32[]{:S(2)}) collective-permute-start(bf16[2,4,96,384]{3,2,1,0:T(8,128)(2,1)S(1)} %copy-done.16), channel_id=1, source_target_pairs={{0,2},{1,3},{2,0},{3,1},{4,6},{5,7},{6,4},{7,5},{8,10},{9,11},{10,... | collective-permute-start | bytes 1769480 | tf_op jit(solution)/shard_map/ppermute | solution.py:361
  77.7 41.9 %collective-permute-start.5 = (bf16[2,4,96,384]{3,2,1,0:T(8,128)(2,1)S(1)}, bf16[2,4,96,384]{3,2,1,0:T(8,128)(2,1)S(1)}, u32[]{:S(2)}, u32[]{:S(2)}) collective-permute-start(bf16[2,4,96,384]{3,2,1,0:T(8,128)(2,1)S(1)} %copy-done.15), channel_id=1, source_target_pairs={{0,3},{1,2},{2,1},{3,0},{4,7},{5,6},{6,5},{7,4},{8,11},{9,10},{10,... | collective-permute-start | bytes 1769480 | tf_op jit(solution)/shard_map/ppermute | solution.py:361
  108.6 23.6 %copy-start.4 = (bf16[2,4,96,384]{3,2,1,0:T(8,128)(2,1)}, bf16[2,4,96,384]{3,2,1,0:T(8,128)(2,1)S(1)}, u32[]{:S(2)}) copy-start(bf16[2,4,96,384]{3,2,1,0:T(8,128)(2,1)S(1)} %collective-permute-done.3.refs_1_) | copy-start | bytes 1769476
  119.6 12.6 %copy-start.5 = (bf16[2,4,96,384]{3,2,1,0:T(8,128)(2,1)}, bf16[2,4,96,384]{3,2,1,0:T(8,128)(2,1)S(1)}, u32[]{:S(2)}) copy-start(bf16[2,4,96,384]{3,2,1,0:T(8,128)(2,1)S(1)} %collective-permute-done.4.refs_2_) | copy-start | bytes 1769476
  119.6 12.6 %copy-start.6 = (bf16[2,4,96,384]{3,2,1,0:T(8,128)(2,1)}, bf16[2,4,96,384]{3,2,1,0:T(8,128)(2,1)S(1)}, u32[]{:S(2)}) copy-start(bf16[2,4,96,384]{3,2,1,0:T(8,128)(2,1)S(1)} %collective-permute-done.5.refs_3_) | copy-start | bytes 1769476
  122.1 35.5 %collective-permute-start.13 = (bf16[2,4,96,384]{3,2,1,0:T(8,128)(2,1)}, bf16[2,4,96,384]{3,2,1,0:T(8,128)(2,1)S(1)}, u32[]{:S(2)}, u32[]{:S(2)}) collective-permute-start(bf16[2,4,96,384]{3,2,1,0:T(8,128)(2,1)} %get-tuple-element.99), channel_id=1, source_target_pairs={{0,2},{1,3},{2,0},{3,1},{4,6},{5,7},{6,4},{7,5},{8,10},{9,11},{10,... | collective-permute-start | bytes 1769480 | tf_op jit(solution)/shard_map/ppermute | solution.py:361
  145.1 17.4 %copy-start.14 = (bf16[2,4,96,384]{3,2,1,0:T(8,128)(2,1)S(1)}, bf16[2,4,96,384]{3,2,1,0:T(8,128)(2,1)}, u32[]{:S(2)}) copy-start(bf16[2,4,96,384]{3,2,1,0:T(8,128)(2,1)} %get-tuple-element.101) | copy-start | bytes 1769476
  157.6 59.4 %all-to-all-start.3 = ((bf16[8,2,384,384]{3,2,1,0:T(8,128)(2,1)}), bf16[8,2,384,384]{3,2,1,0:T(8,128)(2,1)}, u32[]{:S(2)}, u32[]{:S(2)}) async-start(bf16[8,2,384,384]{3,2,1,0:T(8,128)(2,1)} %mix_space.3), calls=%async_computation.3 | async-start | bytes 9437184 | tf_op jit(solution)/shard_map/all_to_all | solution.py:517
  162.4 46.3 %collective-permute-start.12 = (bf16[2,4,96,384]{3,2,1,0:T(8,128)(2,1)}, bf16[2,4,96,384]{3,2,1,0:T(8,128)(2,1)S(1)}, u32[]{:S(2)}, u32[]{:S(2)}) collective-permute-start(bf16[2,4,96,384]{3,2,1,0:T(8,128)(2,1)} %get-tuple-element.97), channel_id=1, source_target_pairs={{0,1},{1,0},{2,3},{3,2},{4,5},{5,4},{6,7},{7,6},{8,9},{9,8},{10,11... | collective-permute-start | bytes 1769480 | tf_op jit(solution)/shard_map/ppermute | solution.py:361
  162.5 48.7 %collective-permute-start.14 = (bf16[2,4,96,384]{3,2,1,0:T(8,128)(2,1)S(1)}, bf16[2,4,96,384]{3,2,1,0:T(8,128)(2,1)S(1)}, u32[]{:S(2)}, u32[]{:S(2)}) collective-permute-start(bf16[2,4,96,384]{3,2,1,0:T(8,128)(2,1)S(1)} %copy-done.14), channel_id=1, source_target_pairs={{0,3},{1,2},{2,1},{3,0},{4,7},{5,6},{6,5},{7,4},{8,11},{9,10},{10,... | collective-permute-start | bytes 1769480 | tf_op jit(solution)/shard_map/ppermute | solution.py:361
  172.2 36.5 %collective-permute-start.9 = (bf16[2,3,96,384]{3,2,1,0:T(8,128)(2,1)}, bf16[2,3,96,384]{3,2,1,0:T(8,128)(2,1)S(1)}, u32[]{:S(2)}, u32[]{:S(2)}) collective-permute-start(bf16[2,3,96,384]{3,2,1,0:T(8,128)(2,1)} %get-tuple-element.93), channel_id=1, source_target_pairs={{0,1},{1,0},{2,3},{3,2},{4,5},{5,4},{6,7},{7,6},{8,9},{9,8},{10,11... | collective-permute-start | bytes 1327112 | tf_op jit(solution)/shard_map/ppermute | solution.py:361
  173.3 65.1 %collective-permute-start.10 = (bf16[2,3,96,384]{3,2,1,0:T(8,128)(2,1)}, bf16[2,3,96,384]{3,2,1,0:T(8,128)(2,1)S(1)}, u32[]{:S(2)}, u32[]{:S(2)}) collective-permute-start(bf16[2,3,96,384]{3,2,1,0:T(8,128)(2,1)} %get-tuple-element.94), channel_id=1, source_target_pairs={{0,2},{1,3},{2,0},{3,1},{4,6},{5,7},{6,4},{7,5},{8,10},{9,11},{10,... | collective-permute-start | bytes 1327112 | tf_op jit(solution)/shard_map/ppermute | solution.py:361
  174.7 63.6 %collective-permute-start.11 = (bf16[2,3,96,384]{3,2,1,0:T(8,128)(2,1)}, bf16[2,3,96,384]{3,2,1,0:T(8,128)(2,1)}, u32[]{:S(2)}, u32[]{:S(2)}) collective-permute-start(bf16[2,3,96,384]{3,2,1,0:T(8,128)(2,1)} %get-tuple-element.95), channel_id=1, source_target_pairs={{0,3},{1,2},{2,1},{3,0},{4,7},{5,6},{6,5},{7,4},{8,11},{9,10},{10,... | collective-permute-start | bytes 1327112 | tf_op jit(solution)/shard_map/ppermute | solution.py:361
  208.7 34.5 %collective-permute-start.6 = (bf16[2,1,96,384]{3,2,1,0:T(8,128)(2,1)}, bf16[2,1,96,384]{3,2,1,0:T(8,128)(2,1)S(1)}, u32[]{:S(2)}, u32[]{:S(2)}) collective-permute-start(bf16[2,1,96,384]{3,2,1,0:T(8,128)(2,1)} %get-tuple-element.89), channel_id=1, source_target_pairs={{0,1},{1,0},{2,3},{3,2},{4,5},{5,4},{6,7},{7,6},{8,9},{9,8},{10,11... | collective-permute-start | bytes 442376 | tf_op jit(solution)/shard_map/ppermute | solution.py:361
  208.7 34.5 %collective-permute-start.7 = (bf16[2,1,96,384]{3,2,1,0:T(8,128)(2,1)}, bf16[2,1,96,384]{3,2,1,0:T(8,128)(2,1)S(1)}, u32[]{:S(2)}, u32[]{:S(2)}) collective-permute-start(bf16[2,1,96,384]{3,2,1,0:T(8,128)(2,1)} %get-tuple-element.90), channel_id=1, source_target_pairs={{0,2},{1,3},{2,0},{3,1},{4,6},{5,7},{6,4},{7,5},{8,10},{9,11},{10,... | collective-permute-start | bytes 442376 | tf_op jit(solution)/shard_map/ppermute | solution.py:361
  211.2 24.4 %copy-start = (bf16[2,4,96,384]{3,2,1,0:T(8,128)(2,1)S(1)}, bf16[2,4,96,384]{3,2,1,0:T(8,128)(2,1)}, u32[]{:S(2)}) copy-start(bf16[2,4,96,384]{3,2,1,0:T(8,128)(2,1)} %get-tuple-element.96.refs_0_) | copy-start | bytes 1769476
  211.2 32.0 %collective-permute-start.8 = (bf16[2,1,96,384]{3,2,1,0:T(8,128)(2,1)}, bf16[2,1,96,384]{3,2,1,0:T(8,128)(2,1)}, u32[]{:S(2)}, u32[]{:S(2)}) collective-permute-start(bf16[2,1,96,384]{3,2,1,0:T(8,128)(2,1)} %get-tuple-element.91), channel_id=1, source_target_pairs={{0,3},{1,2},{2,1},{3,0},{4,7},{5,6},{6,5},{7,4},{8,11},{9,10},{10,... | collective-permute-start | bytes 442376 | tf_op jit(solution)/shard_map/ppermute | solution.py:361
  232.4 12.9 %all-to-all-start.4 = ((f32[32,2,128]{2,1,0:T(2,128)}), f32[32,2,128]{2,1,0:T(2,128)}, u32[]{:S(2)}, u32[]{:S(2)}) async-start(f32[32,2,128]{2,1,0:T(2,128)} %copy.28), calls=%async_computation.4 | async-start | bytes 65536 | tf_op jit(solution)/shard_map/all_to_all | solution.py:554
  235.6 2.8 %copy-start.1 = (bf16[2,3,96,384]{3,2,1,0:T(8,128)(2,1)S(1)}, bf16[2,3,96,384]{3,2,1,0:T(8,128)(2,1)}, u32[]{:S(2)}) copy-start(bf16[2,3,96,384]{3,2,1,0:T(8,128)(2,1)} %get-tuple-element.92.refs_0_) | copy-start | bytes 1327108
  238.4 4.8 %copy-start.2 = (bf16[2,1,96,384]{3,2,1,0:T(8,128)(2,1)S(1)}, bf16[2,1,96,384]{3,2,1,0:T(8,128)(2,1)}, u32[]{:S(2)}) copy-start(bf16[2,1,96,384]{3,2,1,0:T(8,128)(2,1)} %get-tuple-element.88.refs_0_) | copy-start | bytes 442372
  (5 other events, 7.6 us)
